TPU v7x, 128 devices: a whole 4x4x4 slice. The times are simulated.
128 devices in a mesh: rep: 16 (over z, x), tp: 8 (over y, core).
Axes of the slice: x: 4, y: 4, z: 4, core: 2. Of those that a mesh axis runs over, the one named last changes fastest.
Arguments:
- activations: bfloat16 [16384, 8192], P('rep'), may hold values from -6 to 6
- token_adapter_index: int32 [16384, 1], P('rep'), may hold values from 0 to 31; in each aligned block of 1024 rows (0 to 1023, 1024 to 2047, ...) at most 64 rows name the same one
- query_matrix: bfloat16 [8192, 4096], P(None, 'tp'), may hold values from -0.0625 to 0.0625
- adapter_down_factor: bfloat16 [32, 8192, 64], P('rep', 'tp'), may hold values from -0.0625 to 0.0625
- adapter_up_factor: bfloat16 [32, 64, 4096], P('rep', None, 'tp'), may hold values from -0.75 to 0.75
Outputs:
- queries: bfloat16 [16384, 4096], P('rep', 'tp')
Inputs may be any that keep to these rules, and one draw needn't show every extreme that they name: `token_adapter_index`: in the rows of one replica (1024 tokens), no adapter appears more than 64 times, and one appears exactly 64 times; every adapter appears somewhere.
All inputs are finite; a program needn't handle non-finite values.
Results may differ from a plain program's by a relative error of at most 0.0036.
Values may be sent and summed in bfloat16 or wider, within the bound.
No kernel may reach another device: no remote copies, remote signals or barrier semaphores. Data moves between devices by JAX's collectives and lax.ppermute only.
A program may use at most 128 MiB of HBM per device.

v0:
```python
import jax
import jax.numpy as jnp
from jax import lax
from jax.sharding import PartitionSpec as P

adapter_scale = 0.5


def slot_table(ident, adapter_table, most):
    onehot = (ident[:, None] == jnp.arange(adapter_table, dtype=jnp.int32)[None, :]).astype(
        jnp.int32
    )
    rank = jnp.sum((jnp.cumsum(onehot, axis=0) - onehot) * onehot, axis=1)
    return ident * most + rank


def per_device(
    activations, token_adapter_index, query_matrix, adapter_down_factor, adapter_up_factor
):
    replicas = lax.axis_size("rep")
    owned_adapters = adapter_down_factor.shape[0]
    adapter_table = owned_adapters * replicas
    token_rows = activations.shape[0]
    most = 2 * token_rows // adapter_table
    width = activations.shape[1] // lax.axis_size("tp")
    ident = token_adapter_index[:, 0]
    slots = slot_table(ident, adapter_table, most)
    local = lax.dynamic_slice_in_dim(activations, lax.axis_index("tp") * width, width, 1)
    buffer = (
        jnp.zeros((adapter_table * most, width), jnp.bfloat16).at[slots].set(local, mode="drop")
    )
    buffer = buffer.reshape(adapter_table, most, width)
    received = lax.all_to_all(buffer, "rep", split_axis=0, concat_axis=0, tiled=True)
    count = received.shape[1]
    grouped_tokens = received.reshape(replicas, owned_adapters, count, width)
    partial_down = jnp.einsum(
        "ieht,etz->iehz", grouped_tokens, adapter_down_factor, preferred_element_type=jnp.float32
    )
    reduced_sum = lax.psum(partial_down, "tp").astype(jnp.bfloat16)
    expanded_rows = jnp.einsum(
        "nlue,ley->nluy", reduced_sum, adapter_up_factor, preferred_element_type=jnp.float32
    )
    expanded_rows = expanded_rows.astype(jnp.bfloat16).reshape(replicas * owned_adapters, count, -1)
    returned = lax.all_to_all(expanded_rows, "rep", split_axis=0, concat_axis=0, tiled=True)
    token_delta = returned.reshape(adapter_table * most, -1)[slots]
    base_output = jnp.dot(activations, query_matrix, preferred_element_type=jnp.float32)
    return (base_output + adapter_scale * token_delta.astype(jnp.float32)).astype(jnp.bfloat16)


def solution(mesh):
    in_specs = (
        P("rep", None),
        P("rep", None),
        P(None, "tp"),
        P("rep", "tp", None),
        P("rep", None, "tp"),
    )
    out_specs = P("rep", "tp")
    return jax.shard_map(
        per_device, mesh=mesh, in_specs=in_specs, out_specs=out_specs, check_vma=False
    )
```

profile of v0, /device:TPU:0, one launch (start us, length us, event | category | flops | bytes accessed | tf_op | source)
XLA Modules:
  0.0 186.4 jit_solution(548503389294389397)
XLA Ops:
  0.0 0.0 copy-start
  0.0 0.7 fusion.14
  0.7 9.0 %reduce-window.6 = s32[32,8,128]{2,1,0:T(8,128)S(1)} reduce-window(s32[32,8,128]{2,1,0:T(8,128)S(1)} %fusion.14, s32[]{:T(128)} %constant.10.clone.1), window={size=1x1x128 pad=0_0x0_0x127_0}, to_apply=%region_0.0 | reduce-window | flops 4161536 | bytes 262148 | tf_op jit(solution)/shard_map/reduce-window
  9.8 0.1 slice.10
  9.9 0.1 copy.6
  10.0 0.1 copy.7
  10.1 0.1 broadcast_add_fusion
  10.2 0.7 fusion.12
  10.9 0.7 compare_select_fusion
  11.7 8.6 %scatter_custom_fusion = bf16[2048,1024]{1,0:T(8,128)(2,1)} fusion(s32[1024]{0:T(1024)S(1)} %bitcast.53, bf16[1024,8192]{1,0:T(8,128)(2,1)} %param.5, s32[]{:T(128)} %constant.10.clone.1, s32[]{:T(128)S(6)} %select_n.9, bf16[]{:T(256)} %constant.8.clone.1), kind=kCustom, calls=%fused_computation.6 | custom fusion | bytes 6292484 | tf_op jit(solution)/shard_map/scatter | solution.py:30
  20.2 58.8 %all_to_all.10 = bf16[32,64,1024]{2,1,0:T(8,128)(2,1)S(1)} all-to-all(bf16[32,64,1024]{2,1,0:T(8,128)(2,1)} %bitcast.45), channel_id=1, replica_groups=mesh['rep'=16,'tp'=8] {'rep'}, dimensions={0} | all-to-all | bytes 8388608 | tf_op jit(solution)/shard_map/all_to_all | solution.py:33
  79.0 0.0 copy-done
  79.0 0.0 copy-start.1
  79.0 1.2 fusion.5
  80.3 51.4 %all-reduce.1 = bf16[16,2,64,64]{3,2,0,1:T(8,128)(2,1)S(1)} all-reduce(f32[16,2,64,64]{3,2,0,1:T(8,128)S(1)} %fusion.5), channel_id=1, replica_groups=mesh['rep'=16,'tp'=8] {'tp'}, use_global_device_ids=true, to_apply=%region_4.5 | all-reduce | flops 131072 | bytes 786432 | tf_op jit(solution)/shard_map/psum | solution.py:39
  131.7 0.0 copy-done.1
  131.7 0.7 convert_bitcast_fusion
  132.3 1.6 copy.8
  133.9 3.7 %all-to-all-start.1 = ((bf16[32,64,512]{2,1,0:T(8,128)(2,1)}), bf16[32,64,512]{2,1,0:T(8,128)(2,1)S(1)}, u32[]{:S(2)}, u32[]{:S(2)}) async-start(bf16[32,64,512]{2,1,0:T(8,128)(2,1)} %bitcast.46), calls=%async_computation.1 | async-start | bytes 4194304 | tf_op jit(solution)/shard_map/all_to_all | solution.py:44
  137.7 29.2 %all-to-all-done.1 = bf16[32,64,512]{2,1,0:T(8,128)(2,1)S(1)} async-done(((bf16[32,64,512]{2,1,0:T(8,128)(2,1)}), bf16[32,64,512]{2,1,0:T(8,128)(2,1)S(1)}, u32[]{:S(2)}, u32[]{:S(2)}) %all-to-all-start.1) | async-done | bytes 2097184 | tf_op jit(solution)/shard_map/all_to_all | solution.py:44
  166.9 4.0 %gather_fusion = bf16[1024,512]{1,0:T(8,128)(2,1)S(1)} fusion(bf16[2048,512]{1,0:T(8,128)(2,1)S(1)} %bitcast.44, s32[1024]{0:T(1024)S(1)} %broadcast_clamp_fusion), kind=kCustom, calls=%fused_computation | custom fusion | bytes 2101248 | tf_op jit(solution)/shard_map/gather | solution.py:45
  170.9 15.6 %add_convert_fusion = bf16[1024,512]{1,0:T(8,128)(2,1)} fusion(bf16[1024,512]{1,0:T(8,128)(2,1)S(1)} %gather_fusion, bf16[1024,8192]{1,0:T(8,128)(2,1)} %param.5, bf16[8192,512]{1,0:T(8,128)(2,1)} %param.7), kind=kOutput, calls=%fused_computation.4 | convolution fusion | flops 8592031744 | bytes 27262976 | tf_op jit(solution)/shard_map/dot_general | solution.py:46
  (3 shorter events, 0.0 us)
Async XLA Ops:
  0.0 79.0 %copy-start = (bf16[2,1024,64]{1,2,0:T(8,128)(2,1)S(1)}, bf16[2,1024,64]{1,2,0:T(8,128)(2,1)}, u32[]{:S(2)}) copy-start(bf16[2,1024,64]{1,2,0:T(8,128)(2,1)} %param.8) | copy-start | bytes 786436
  79.0 52.6 %copy-start.1 = (bf16[2,64,512]{2,1,0:T(8,128)(2,1)S(1)}, bf16[2,64,512]{2,1,0:T(8,128)(2,1)}, u32[]{:S(2)}) copy-start(bf16[2,64,512]{2,1,0:T(8,128)(2,1)} %param.9) | copy-start | bytes 393220
  133.9 33.0 %all-to-all-start.1 = ((bf16[32,64,512]{2,1,0:T(8,128)(2,1)}), bf16[32,64,512]{2,1,0:T(8,128)(2,1)S(1)}, u32[]{:S(2)}, u32[]{:S(2)}) async-start(bf16[32,64,512]{2,1,0:T(8,128)(2,1)} %bitcast.46), calls=%async_computation.1 | async-start | bytes 4194304 | tf_op jit(solution)/shard_map/all_to_all | solution.py:44
where the time goes:
time: 187 us; the launch traced here: 186 us
  blocking collectives  110 us (59%)
  waiting for transfers between devices  29.2 us (16%)
  matrix products  17.5 us (9%)
  local copies, waits for them, and re-layouts  14.4 us (8%)
  other arithmetic  11.3 us (6%)
  starting transfers between devices  3.72 us (2%)
    all_to_all x1, blocking collectives, per_device(): lax.all_to_all(buffer, 'rep', split_axis=0, concat_axis=0, tiled=True)  58.8 us
    psum x1, blocking collectives, per_device(): reduced_sum = lax.psum(partial_down, 'tp').astype(jnp.bfloat16)  51.4 us
    all_to_all x1, waiting for transfers between devices, per_device(): lax.all_to_all(expanded_rows, 'rep', split_axis=0, concat_axis=0, tiled=T...  29.2 us
    dot_general x1, matrix products, per_device(): jnp.dot(activations, query_matrix, preferred_element_type=jnp.float32)  15.6 us
    another operation x3, other arithmetic  9.15 us
    scatter x1, local copies, waits for them, and re-layouts, per_device(): jnp.zeros((adapter_table * most, width), jnp.bfloat16).at[slots]  8.56 us
    gather x1, local copies, waits for them, and re-layouts, per_device(): token_delta = returned.reshape(adapter_table * most, -1)[slots]  3.96 us
  transfers between devices with their start and end apart: 1, of which 1 were waited for; matrix products, arithmetic and copies ran while one was open for 0% of the time, Pallas kernels for 0%

commit v1 on v0

v1 whole, which is shorter than its diff:
```python
import functools

import jax
import jax.numpy as jnp
from jax import lax
from jax.experimental import pallas as pl
from jax.experimental.pallas import tpu as pltpu
from jax.sharding import PartitionSpec as P

BF, F32 = jnp.bfloat16, jnp.float32
AXES = ("rep", "tp")
RING = 4
adapter_scale = 0.5


def device_of(x, y, z, c):
    return (z % RING * RING + x % RING) * 2 * RING + y % RING * 2 + c


def every(f):
    return [
        (device_of(x, y, z, c), device_of(*f(x, y, z, c)))
        for z in range(RING)
        for x in range(RING)
        for y in range(RING)
        for c in range(2)
    ]


def first(a, d):
    return lax.ppermute(
        a, AXES, every(lambda x, y, z, c: (x, y, z + d, c) if c else (x + d, y, z, c))
    )


def second(a, d):
    return lax.ppermute(
        a, AXES, every(lambda x, y, z, c: (x + d, y, z, c) if c else (x, y, z + d, c))
    )


def other_core(a):
    return lax.ppermute(a, AXES, every(lambda x, y, z, c: (x, y, z, 1 - c)))


def pair(a, step):
    def to(x, y, z, c):
        return (x, (y ^ 1) if (c + step) % 2 == 0 else (3 - y), z, c)
    return lax.ppermute(a, AXES, every(to))


def params():
    return pltpu.CompilerParams(vmem_limit_bytes=48 << 20)


def base_kernel(x_ref, w_ref, o_ref):
    p = jnp.dot(x_ref[...], w_ref[...], preferred_element_type=F32)

    @pl.when(pl.program_id(0) == 0)
    def _():
        o_ref[...] = p

    @pl.when(pl.program_id(0) > 0)
    def _():
        o_ref[...] += p


def base_product(x, w, depth=2048):
    m, k = x.shape
    n = w.shape[1]
    return pl.pallas_call(
        base_kernel,
        grid=(k // depth,),
        in_specs=[
            pl.BlockSpec((m, depth), lambda i: (0, i)),
            pl.BlockSpec((depth, n), lambda i: (i, 0)),
        ],
        out_specs=pl.BlockSpec((m, n), lambda i: (0, 0)),
        out_shape=jax.ShapeDtypeStruct((m, n), F32),
        compiler_params=params(),
        cost_estimate=pl.CostEstimate(
            flops=2 * m * n * k, bytes_accessed=2 * (m * k + k * n) + 4 * m * n, transcendentals=0
        ),
        name="base",
    )(x, w)


def shrink_kernel(counts, has_sum, last, s_ref, code_ref, x_ref, *refs):
    a_refs, refs = refs[: len(counts)], refs[len(counts):]
    o_ref = refs[-1]
    code = code_ref[...]
    total = refs[0][...] if has_sum else None
    at = 0
    for a_ref, count in zip(a_refs, counts):
        p = lax.dot_general(
            x_ref[...], a_ref[...], (((1,), (1,)), ((), ())), preferred_element_type=F32
        )
        for j in range(count):
            term = jnp.where(code == s_ref[at + j], p[:, 128 * j : 128 * j + 128], 0.0)
            total = term if total is None else total + term
        at += count
    if last:
        half = total.shape[0] // 2
        folded = total + pltpu.roll(total, 64, 1)
        lane = lax.broadcasted_iota(jnp.int32, (half, 128), 1)
        o_ref[...] = jnp.where(lane < 64, folded[:half], folded[half:])
    else:
        o_ref[...] = total


def shrink(code, where, ids, x, parts, total, last, name):
    m, width = x.shape[0], parts[0].shape[1]
    width = min(width, 1024)
    counts = tuple(a.shape[0] // 128 for a in parts)
    nb = sum(counts)
    s = jnp.concatenate([ids, where[None]])
    whole = lambda i, s: (0, 0)
    specs = [pl.BlockSpec((m, 128), whole), pl.BlockSpec((m, width), lambda i, s: (0, s[nb]))]
    specs += [pl.BlockSpec((a.shape[0], width), whole) for a in parts]
    args = [s, code, x, *parts]
    if total is not None:
        specs.append(pl.BlockSpec((m, 128), whole))
        args.append(total)
    rows = m // 2 if last else m
    return pl.pallas_call(
        functools.partial(shrink_kernel, counts, total is not None, last),
        grid_spec=pltpu.PrefetchScalarGridSpec(
            num_scalar_prefetch=1,
            grid=(1,),
            in_specs=specs,
            out_specs=pl.BlockSpec((rows, 128), whole),
        ),
        out_shape=jax.ShapeDtypeStruct((rows, 128), F32),
        compiler_params=params(),
        cost_estimate=pl.CostEstimate(
            flops=2 * m * width * nb * 128, bytes_accessed=2 * m * width + 256 * nb * width, transcendentals=0
        ),
        name=name,
    )(*args)


def expand_kernel(counts, s_ref, code_ref, mine_ref, other_ref, base_ref, *refs):
    b_refs, o_ref = refs[:-1], refs[-1]
    code = code_ref[...]
    packed = mine_ref[...] + other_ref[...]
    lane = lax.broadcasted_iota(jnp.int32, packed.shape, 1)
    left = (lane < 64) == (pl.program_id(0) < pl.num_programs(0) // 2)
    rows = jnp.where(left, packed, pltpu.roll(packed, 64, 1))
    delta, at = None, 0
    for b_ref, count in zip(b_refs, counts):
        spread = jnp.concatenate(
            [jnp.where(code == s_ref[at + j], rows, 0.0).astype(BF) for j in range(count)], axis=1
        )
        d = jnp.dot(spread, b_ref[...], preferred_element_type=F32)
        delta = d if delta is None else delta + d
        at += count
    delta = delta.astype(BF).astype(F32)
    o_ref[...] = (base_ref[...] + adapter_scale * delta).astype(BF)


def expand(code, ids, mine, other, base, parts, block=256):
    m, n = base.shape
    counts = tuple(b.shape[0] // 128 for b in parts)
    steps = m // block
    row = lambda i, s: (i, 0)
    packed = pl.BlockSpec((block, 128), lambda i, s: (i % (steps // 2), 0))
    specs = [pl.BlockSpec((block, 128), row), packed, packed, pl.BlockSpec((block, n), row)]
    specs += [pl.BlockSpec((b.shape[0], n), lambda i, s: (0, 0)) for b in parts]
    return pl.pallas_call(
        functools.partial(expand_kernel, counts),
        grid_spec=pltpu.PrefetchScalarGridSpec(
            num_scalar_prefetch=1,
            grid=(steps,),
            in_specs=specs,
            out_specs=pl.BlockSpec((block, n), row),
        ),
        out_shape=jax.ShapeDtypeStruct((m, n), BF),
        compiler_params=params(),
        cost_estimate=pl.CostEstimate(
            flops=2 * m * n * 128 * sum(counts), bytes_accessed=6 * m * n, transcendentals=0
        ),
        name="expand",
    )(ids, code, mine, other, base, *parts)


def per_device(activations, token_adapter_index, query_matrix, down, up):
    m = activations.shape[0]
    rep, tp = lax.axis_index("rep"), lax.axis_index("tp")
    core = tp % 2
    hops = jnp.array([0, -1, 1, 2], jnp.int32)
    z, x = rep // RING, rep % RING
    zs, xs = (z + hops) % RING, (x + hops) % RING
    ids = jnp.where(core == 0, zs[:, None] * RING + xs[None, :], zs[None, :] * RING + xs[:, None])
    ids = ids.reshape(16)
    ident = token_adapter_index
    side = lax.broadcasted_iota(jnp.int32, (m, 128), 1) // 64
    code = jnp.where(ident % 2 == side, ident // 2, -1)

    down = jnp.swapaxes(down, 1, 2).reshape(128, -1)
    up = up.reshape(128, -1)

    def gather_first(a):
        return jnp.concatenate([a, first(a, 1), first(a, -1), first(a, 2)], axis=0)

    def gather_second(a):
        half = a.shape[0] // 2
        before, after = second(a, 1), second(a, -1)
        far = (second(before[:half], 1), second(after[half:], -1))
        return before, after, far

    both = gather_first(jnp.concatenate([down, up], axis=1))
    width = down.shape[1]
    d0, u0 = both[:, :width], both[:, width:]
    d1, d2, d3 = gather_second(d0)
    u1, u2, u3 = gather_second(u0)
    base = base_product(activations, query_matrix)
    total = shrink(code, tp, ids[:12], activations, [d0, d1, d2], None, False, "shrink_near")
    total = shrink(code, tp, ids[12:], activations, d3, total, True, "shrink_far")
    total = total + other_core(total)
    total = total + pair(total, 0)
    other = pair(total, 1)
    return expand(code, ids, total, other, base, [u0, u1, u2, *u3])


def solution(mesh):
    in_specs = (
        P("rep", None),
        P("rep", None),
        P(None, "tp"),
        P("rep", "tp", None),
        P("rep", None, "tp"),
    )
    return jax.shard_map(
        per_device, mesh=mesh, in_specs=in_specs, out_specs=P("rep", "tp"), check_vma=False
    )
```

time: 187 us -> 81.7 us (0.44)
  blocking collectives: 110 us -> 0 us
  Pallas kernels: 0 us -> 26.7 us
  starting transfers between devices: 3.72 us -> 24.2 us
  matrix products: 17.5 us -> 0 us
  local copies, waits for them, and re-layouts: 14.4 us -> 4.04 us
  other arithmetic: 11.3 us -> 3.55 us
  waiting for transfers between devices: 29.2 us -> 22.8 us
    all_to_all x1 -> x0, blocking collectives: 58.8 us -> none  [per_device(): lax.all_to_all(buffer, 'rep', split_axis=0, concat_axis=0, tiled=True)]
    psum x1 -> x0, blocking collectives: 51.4 us -> none  [per_device(): reduced_sum = lax.psum(partial_down, 'tp').astype(jnp.bfloat16)]
    all_to_all x1 -> x0, waiting for transfers between devices: 29.2 us -> none  [per_device(): lax.all_to_all(expanded_rows, 'rep', split_axis=0, concat_axis=0, tiled=T...]
    pallas_call x0 -> x4, Pallas kernels: none -> 26.7 us  [the longest x1 13.3 us: base_product(): pl.pallas_call(base_kernel, grid=(k // depth,), in_specs=[pl.BlockSpec((m...]
    ppermute x0 -> x14, starting transfers between devices: none -> 24.2 us  [the longest x8 14.1 us: second(): lax.ppermute(a, AXES, every(lambda x, y, z, c: (x + d, y, z, c) if c else...]
    ppermute x0 -> x14, waiting for transfers between devices: none -> 22.8 us  [the longest x8 12.2 us: second(): lax.ppermute(a, AXES, every(lambda x, y, z, c: (x + d, y, z, c) if c else...]
    dot_general x3 -> x0, matrix products: 17.5 us -> none  [the longest x1 15.6 us: per_device(): jnp.dot(activations, query_matrix, preferred_element_type=jnp.float32)]
    another operation x3 -> x0, other arithmetic: 9.15 us -> none
  transfers between devices with their start and end apart: 1 -> 14, of which waited for: 1 -> 6; matrix products, arithmetic and copies ran while one was open for 0% -> 3% of each run, Pallas kernels for 0% -> 27%
where the time goes in v1:
time: 81.7 us; the launch traced here: 81.5 us
  Pallas kernels  26.7 us (33%)
  starting transfers between devices  24.2 us (30%)
  waiting for transfers between devices  22.8 us (28%)
  local copies, waits for them, and re-layouts  4.04 us (5%)
  other arithmetic  3.55 us (4%)
    ppermute x8, starting transfers between devices, second(): lax.ppermute(a, AXES, every(lambda x, y, z, c: (x + d, y, z, c) if c else...  14.1 us
    pallas_call x1, Pallas kernels, base_product(): pl.pallas_call(base_kernel, grid=(k // depth,), in_specs=[pl.BlockSpec((m...  13.3 us
    ppermute x8, waiting for transfers between devices, second(): lax.ppermute(a, AXES, every(lambda x, y, z, c: (x + d, y, z, c) if c else...  12.2 us
    pallas_call x2, Pallas kernels, shrink(): pl.pallas_call(functools.partial(shrink_kernel, counts, total is not None...  9.1 us
    ppermute x3, waiting for transfers between devices, first(): lax.ppermute(a, AXES, every(lambda x, y, z, c: (x, y, z + d, c) if c else...  8.3 us
    ppermute x3, starting transfers between devices, first(): lax.ppermute(a, AXES, every(lambda x, y, z, c: (x, y, z + d, c) if c else...  5.2 us
    ppermute x2, starting transfers between devices, pair(): return lax.ppermute(a, AXES, every(to))  4.75 us
    pallas_call x1, Pallas kernels, expand(): pl.pallas_call(functools.partial(expand_kernel, counts), grid_spec=pltpu....  4.38 us
  transfers between devices with their start and end apart: 14, of which 6 were waited for; matrix products, arithmetic and copies ran while one was open for 3% of the time, Pallas kernels for 27%

profile of v1, /device:TPU:0, one launch (start us, length us, event | category | flops | bytes accessed | tf_op | source)
XLA Modules:
  0.0 81.5 jit_solution(8840195622013971802)
XLA Ops:
  0.0 0.0 copy-start.4
  0.0 1.1 %pad_maximum_fusion.2 = bf16[128,1536]{1,0:T(8,128)(2,1)S(1)} fusion(bf16[128,512]{1,0:T(8,128)(2,1)} %bitcast.13, bf16[128,1024]{1,0:T(8,128)(2,1)} %bitcast.10), kind=kLoop, calls=%fused_computation.4 | loop fusion | flops 786432 | bytes 786432 | tf_op jit(solution)/shard_map/concatenate | solution.py:211
  1.1 1.6 %collective-permute-start = (bf16[128,1536]{1,0:T(8,128)(2,1)S(1)}, bf16[128,1536]{1,0:T(8,128)(2,1)S(1)}, u32[]{:S(2)}, u32[]{:S(2)}) collective-permute-start(bf16[128,1536]{1,0:T(8,128)(2,1)S(1)} %pad_maximum_fusion.2), channel_id=1, source_target_pairs={{0,8},{1,33},{2,10},{3,35},{4,12},{5,37},{6,14},{7,39},{8,16},{9,4... | collective-permute-start | bytes 1179656 | tf_op jit(solution)/shard_map/ppermute | solution.py:31
  2.7 1.7 %collective-permute-start.1 = (bf16[128,1536]{1,0:T(8,128)(2,1)S(1)}, bf16[128,1536]{1,0:T(8,128)(2,1)S(1)}, u32[]{:S(2)}, u32[]{:S(2)}) collective-permute-start(bf16[128,1536]{1,0:T(8,128)(2,1)S(1)} %pad_maximum_fusion.2), channel_id=1, source_target_pairs={{0,24},{1,97},{2,26},{3,99},{4,28},{5,101},{6,30},{7,103},{8,0},{9... | collective-permute-start | bytes 1179656 | tf_op jit(solution)/shard_map/ppermute | solution.py:31
  4.4 1.9 %collective-permute-start.2 = (bf16[128,1536]{1,0:T(8,128)(2,1)S(1)}, bf16[128,1536]{1,0:T(8,128)(2,1)S(1)}, u32[]{:S(2)}, u32[]{:S(2)}) collective-permute-start(bf16[128,1536]{1,0:T(8,128)(2,1)S(1)} %pad_maximum_fusion.2), channel_id=1, source_target_pairs={{0,16},{1,65},{2,18},{3,67},{4,20},{5,69},{6,22},{7,71},{8,24},{9,... | collective-permute-start | bytes 1179656 | tf_op jit(solution)/shard_map/ppermute | solution.py:31
  6.3 0.7 fusion.2
  6.9 0.1 add_select_fusion
  7.0 0.1 slice.36
  7.1 3.0 %collective-permute-done = bf16[128,1536]{1,0:T(8,128)(2,1)S(1)} collective-permute-done((bf16[128,1536]{1,0:T(8,128)(2,1)S(1)}, bf16[128,1536]{1,0:T(8,128)(2,1)S(1)}, u32[]{:S(2)}, u32[]{:S(2)}) %collective-permute-start) | collective-permute-done | bytes 393248 | tf_op jit(solution)/shard_map/ppermute | solution.py:31
  10.1 0.4 collective-permute-done.1
  10.5 4.9 %collective-permute-done.2 = bf16[128,1536]{1,0:T(8,128)(2,1)S(1)} collective-permute-done((bf16[128,1536]{1,0:T(8,128)(2,1)S(1)}, bf16[128,1536]{1,0:T(8,128)(2,1)S(1)}, u32[]{:S(2)}, u32[]{:S(2)}) %collective-permute-start.2) | collective-permute-done | bytes 393248 | tf_op jit(solution)/shard_map/ppermute | solution.py:31
  15.4 1.1 %pad_maximum_fusion = bf16[512,1536]{1,0:T(8,128)(2,1)S(1)} fusion(bf16[128,1536]{1,0:T(8,128)(2,1)S(1)} %collective-permute-done.2, bf16[128,1536]{1,0:T(8,128)(2,1)S(1)} %collective-permute-done.1, bf16[128,1536]{1,0:T(8,128)(2,1)S(1)} %collective-permute-done, bf16[128,512]{1,0:T(8,128)(2,1)} %bitcast.14, bf16[128,1024]{1,0:T(8,128)(2,1)} %bitcast.11), kind=kLoop, calls=%fused_computation | loop fusion | flops 7864320 | bytes 3145728 | tf_op jit(solution)/shard_map/concatenate | solution.py:203
  16.5 0.0 copy-start.2
  16.5 0.0 copy-start.3
  16.6 0.1 slice.40.refs_0_
  16.7 2.0 %collective-permute-start.3 = (bf16[512,1024]{1,0:T(8,128)(2,1)S(1)}, bf16[512,1024]{1,0:T(8,128)(2,1)S(1)}, u32[]{:S(2)}, u32[]{:S(2)}) collective-permute-start(bf16[512,1024]{1,0:T(8,128)(2,1)S(1)} %slice.40.refs_0_), channel_id=1, source_target_pairs={{0,32},{1,9},{2,34},{3,11},{4,36},{5,13},{6,38},{7,15},{8,40},{9,1... | collective-permute-start | bytes 3145736 | tf_op jit(solution)/shard_map/ppermute | solution.py:37
  18.7 2.2 %collective-permute-start.5 = (bf16[512,1024]{1,0:T(8,128)(2,1)S(1)}, bf16[512,1024]{1,0:T(8,128)(2,1)S(1)}, u32[]{:S(2)}, u32[]{:S(2)}) collective-permute-start(bf16[512,1024]{1,0:T(8,128)(2,1)S(1)} %slice.40.refs_0_), channel_id=1, source_target_pairs={{0,96},{1,25},{2,98},{3,27},{4,100},{5,29},{6,102},{7,31},{8,104},... | collective-permute-start | bytes 3145736 | tf_op jit(solution)/shard_map/ppermute | solution.py:37
  20.9 0.1 pad_add_fusion.1.s_ref
  21.0 0.0 copy-done.4
  21.0 0.3 fusion.code_ref
  21.4 12.2 %collective-permute-done.3.refs_1_ = bf16[512,1024]{1,0:T(8,128)(2,1)S(1)} collective-permute-done((bf16[512,1024]{1,0:T(8,128)(2,1)S(1)}, bf16[512,1024]{1,0:T(8,128)(2,1)S(1)}, u32[]{:S(2)}, u32[]{:S(2)}) %collective-permute-start.3) | collective-permute-done | bytes 1048608 | tf_op jit(solution)/shard_map/ppermute | solution.py:37
  33.6 0.1 collective-permute-start.4
  33.7 0.0 collective-permute-done.5.refs_2_
  33.8 3.3 %collective-permute-start.6 = (bf16[256,1024]{1,0:T(8,128)(2,1)S(1)}, bf16[256,1024]{1,0:T(8,128)(2,1)S(1)}, u32[]{:S(2)}, u32[]{:S(2)}) collective-permute-start(bf16[256,1024]{1,0:T(8,128)(2,1)S(1)} %slice.42), channel_id=1, source_target_pairs={{0,96},{1,25},{2,98},{3,27},{4,100},{5,29},{6,102},{7,31},{8,104},... | collective-permute-start | bytes 1572872 | tf_op jit(solution)/shard_map/ppermute | solution.py:37
  37.0 0.1 pad_add_fusion.s_ref
  37.1 0.0 copy-done.2
  37.1 0.0 copy-done.3
  37.2 0.1 collective-permute-start.10
  37.3 3.2 %collective-permute-start.11 = (bf16[512,512]{1,0:T(8,128)(2,1)S(1)}, bf16[512,512]{1,0:T(8,128)(2,1)S(1)}, u32[]{:S(2)}, u32[]{:S(2)}) collective-permute-start(bf16[512,512]{1,0:T(8,128)(2,1)S(1)} %pad_maximum_fusion.1.refs_0_), channel_id=1, source_target_pairs={{0,96},{1,25},{2,98},{3,27},{4,100},{5,29},{6,102},{7,31},{8,104},... | collective-permute-start | bytes 1572872 | tf_op jit(solution)/shard_map/ppermute | solution.py:37
  40.5 5.6 %shrink_near.1.refs_2_ = f32[1024,128]{1,0:T(8,128)S(1)} custom-call(s32[13]{0:T(128)S(1)} %pad_add_fusion.1.s_ref, s32[1024,128]{1,0:T(8,128)S(1)} %fusion.code_ref, bf16[1024,8192]{1,0:T(8,128)(2,1)} %x_ref.5, bf16[512,1024]{1,0:T(8,128)(2,1)S(1)} %slice.40.refs_0_, bf16[512,1024]{1,0:T(8,128)(2,1)S(1)} %collective-permute-done.3.refs_1_, ...), custom_call_target="tpu_custom_call" | custom-call | flops 3221225472 | bytes 5242880 | tf_op jit(solution)/shard_map/shrink_near/pallas_call | solution.py:125
  46.1 0.0 collective-permute-done.4.refs_0_
  46.1 0.0 collective-permute-done.6.refs_1_
  46.1 3.5 %shrink_far.1 = f32[512,128]{1,0:T(8,128)S(1)} custom-call(s32[5]{0:T(128)S(1)} %pad_add_fusion.s_ref, s32[1024,128]{1,0:T(8,128)S(1)} %fusion.code_ref, bf16[1024,8192]{1,0:T(8,128)(2,1)} %x_ref.5, bf16[256,1024]{1,0:T(8,128)(2,1)S(1)} %collective-permute-done.4.refs_0_, bf16[256,1024]{1,0:T(8,128)(2,1)S(1)} %collective-permute-done.6.refs_1_, ...), custom_call_target="tpu_custom_call" | custom-call | flops 1073741824 | bytes 3145728 | tf_op jit(solution)/shard_map/shrink_far/pallas_call | solution.py:125
  49.6 0.1 collective-permute-start.7
  49.7 1.5 %collective-permute-done.7 = f32[512,128]{1,0:T(8,128)S(1)} collective-permute-done((f32[512,128]{1,0:T(8,128)S(1)}, f32[512,128]{1,0:T(8,128)S(1)}, u32[]{:S(2)}, u32[]{:S(2)}) %collective-permute-start.7) | collective-permute-done | bytes 262176 | tf_op jit(solution)/shard_map/ppermute | solution.py:43
  51.3 1.7 %collective-permute-start.8 = (f32[512,128]{1,0:T(8,128)S(1)}, f32[512,128]{1,0:T(8,128)S(1)}, u32[]{:S(2)}, u32[]{:S(2)}) collective-permute-start(f32[512,128]{1,0:T(8,128)S(1)} %add.90), channel_id=1, source_target_pairs={{0,2},{1,7},{2,0},{3,5},{4,6},{5,3},{6,4},{7,1},{8,10},{9,15},{10,... | collective-permute-start | bytes 786440 | tf_op jit(solution)/shard_map/ppermute | solution.py:49
  52.9 0.0 collective-permute-done.10.refs_1_
  52.9 0.1 collective-permute-start.12
  53.0 0.0 collective-permute-done.11.refs_2_
  53.0 0.7 slice.44
  53.7 3.2 %collective-permute-start.13 = (bf16[256,512]{1,0:T(8,128)(2,1)}, bf16[256,512]{1,0:T(8,128)(2,1)S(1)}, u32[]{:S(2)}, u32[]{:S(2)}) collective-permute-start(bf16[256,512]{1,0:T(8,128)(2,1)} %slice.44), channel_id=1, source_target_pairs={{0,96},{1,25},{2,98},{3,27},{4,100},{5,29},{6,102},{7,31},{8,104},... | collective-permute-start | bytes 786440 | tf_op jit(solution)/shard_map/ppermute | solution.py:37
  57.0 0.7 collective-permute-done.8
  57.7 3.1 %collective-permute-start.9 = (f32[512,128]{1,0:T(8,128)S(1)}, f32[512,128]{1,0:T(8,128)S(1)}, u32[]{:S(2)}, u32[]{:S(2)}) collective-permute-start(f32[512,128]{1,0:T(8,128)S(1)} %add.91.mine_ref), channel_id=1, source_target_pairs={{0,6},{1,3},{2,4},{3,1},{4,2},{5,7},{6,0},{7,5},{8,14},{9,11},{10,... | collective-permute-start | bytes 786440 | tf_op jit(solution)/shard_map/ppermute | solution.py:49
  60.8 13.3 %base.1.base_ref = f32[1024,512]{1,0:T(8,128)S(1)} custom-call(bf16[1024,8192]{1,0:T(8,128)(2,1)} %x_ref.5, bf16[8192,512]{1,0:T(8,128)(2,1)} %w_ref.1), custom_call_target="tpu_custom_call" | custom-call | flops 8589934592 | bytes 27262976 | tf_op jit(solution)/shard_map/base/pallas_call | solution.py:71
  74.1 0.0 copy-start
  74.1 1.3 %copy-done = f32[1024,512]{1,0:T(8,128)} copy-done((f32[1024,512]{1,0:T(8,128)}, f32[1024,512]{1,0:T(8,128)S(1)}, u32[]{:S(2)}) %copy-start) | copy-done | bytes 2097176
  75.4 0.1 select_n.64.s_ref
  75.5 0.0 collective-permute-done.12.refs_3_
  75.5 0.0 collective-permute-done.13.refs_4_
  75.5 0.0 collective-permute-done.9.other_ref
  75.5 0.0 copy-start.1
  75.5 1.6 %copy-done.1 = f32[1024,512]{1,0:T(8,128)S(1)} copy-done((f32[1024,512]{1,0:T(8,128)S(1)}, f32[1024,512]{1,0:T(8,128)}, u32[]{:S(2)}) %copy-start.1) | copy-done | bytes 2097176
  77.1 4.4 %expand.1 = bf16[1024,512]{1,0:T(8,128)(2,1)} custom-call(s32[16]{0:T(128)S(1)} %select_n.64.s_ref, s32[1024,128]{1,0:T(8,128)S(1)} %fusion.code_ref, f32[512,128]{1,0:T(8,128)S(1)} %add.91.mine_ref, f32[512,128]{1,0:T(8,128)S(1)} %collective-permute-done.9.other_ref, f32[1024,512]{1,0:T(8,128)S(1)} %copy-done.1, ...), custom_call_target="tpu_custom_call" | custom-call | flops 2147483648 | bytes 3145728 | tf_op jit(solution)/shard_map/expand/pallas_call | solution.py:169
  (11 shorter events, 0.2 us)
Async XLA Ops:
  0.0 21.0 %copy-start.4 = (s32[1024,1]{0,1:T(1,128)S(1)}, s32[1024,1]{0,1:T(1,128)}, u32[]{:S(2)}) copy-start(s32[1024,1]{0,1:T(1,128)} %param.7) | copy-start | bytes 12292
  1.1 9.1 %collective-permute-start = (bf16[128,1536]{1,0:T(8,128)(2,1)S(1)}, bf16[128,1536]{1,0:T(8,128)(2,1)S(1)}, u32[]{:S(2)}, u32[]{:S(2)}) collective-permute-start(bf16[128,1536]{1,0:T(8,128)(2,1)S(1)} %pad_maximum_fusion.2), channel_id=1, source_target_pairs={{0,8},{1,33},{2,10},{3,35},{4,12},{5,37},{6,14},{7,39},{8,16},{9,4... | collective-permute-start | bytes 1179656 | tf_op jit(solution)/shard_map/ppermute | solution.py:31
  2.7 7.8 %collective-permute-start.1 = (bf16[128,1536]{1,0:T(8,128)(2,1)S(1)}, bf16[128,1536]{1,0:T(8,128)(2,1)S(1)}, u32[]{:S(2)}, u32[]{:S(2)}) collective-permute-start(bf16[128,1536]{1,0:T(8,128)(2,1)S(1)} %pad_maximum_fusion.2), channel_id=1, source_target_pairs={{0,24},{1,97},{2,26},{3,99},{4,28},{5,101},{6,30},{7,103},{8,0},{9... | collective-permute-start | bytes 1179656 | tf_op jit(solution)/shard_map/ppermute | solution.py:31
  4.4 11.0 %collective-permute-start.2 = (bf16[128,1536]{1,0:T(8,128)(2,1)S(1)}, bf16[128,1536]{1,0:T(8,128)(2,1)S(1)}, u32[]{:S(2)}, u32[]{:S(2)}) collective-permute-start(bf16[128,1536]{1,0:T(8,128)(2,1)S(1)} %pad_maximum_fusion.2), channel_id=1, source_target_pairs={{0,16},{1,65},{2,18},{3,67},{4,20},{5,69},{6,22},{7,71},{8,24},{9,... | collective-permute-start | bytes 1179656 | tf_op jit(solution)/shard_map/ppermute | solution.py:31
  16.5 20.6 %copy-start.2 = (bf16[2,1024,64]{1,2,0:T(8,128)(2,1)S(1)}, bf16[2,1024,64]{1,2,0:T(8,128)(2,1)}, u32[]{:S(2)}) copy-start(bf16[2,1024,64]{1,2,0:T(8,128)(2,1)} %param.9) | copy-start | bytes 786436
  16.5 20.6 %copy-start.3 = (bf16[2,64,512]{2,1,0:T(8,128)(2,1)S(1)}, bf16[2,64,512]{2,1,0:T(8,128)(2,1)}, u32[]{:S(2)}) copy-start(bf16[2,64,512]{2,1,0:T(8,128)(2,1)} %param.10) | copy-start | bytes 393220
  16.7 16.9 %collective-permute-start.3 = (bf16[512,1024]{1,0:T(8,128)(2,1)S(1)}, bf16[512,1024]{1,0:T(8,128)(2,1)S(1)}, u32[]{:S(2)}, u32[]{:S(2)}) collective-permute-start(bf16[512,1024]{1,0:T(8,128)(2,1)S(1)} %slice.40.refs_0_), channel_id=1, source_target_pairs={{0,32},{1,9},{2,34},{3,11},{4,36},{5,13},{6,38},{7,15},{8,40},{9,1... | collective-permute-start | bytes 3145736 | tf_op jit(solution)/shard_map/ppermute | solution.py:37
  18.7 15.0 %collective-permute-start.5 = (bf16[512,1024]{1,0:T(8,128)(2,1)S(1)}, bf16[512,1024]{1,0:T(8,128)(2,1)S(1)}, u32[]{:S(2)}, u32[]{:S(2)}) collective-permute-start(bf16[512,1024]{1,0:T(8,128)(2,1)S(1)} %slice.40.refs_0_), channel_id=1, source_target_pairs={{0,96},{1,25},{2,98},{3,27},{4,100},{5,29},{6,102},{7,31},{8,104},... | collective-permute-start | bytes 3145736 | tf_op jit(solution)/shard_map/ppermute | solution.py:37
  33.6 12.4 %collective-permute-start.4 = (bf16[256,1024]{1,0:T(8,128)(2,1)S(1)}, bf16[256,1024]{1,0:T(8,128)(2,1)S(1)}, u32[]{:S(2)}, u32[]{:S(2)}) collective-permute-start(bf16[256,1024]{1,0:T(8,128)(2,1)S(1)} %slice.41), channel_id=1, source_target_pairs={{0,32},{1,9},{2,34},{3,11},{4,36},{5,13},{6,38},{7,15},{8,40},{9,1... | collective-permute-start | bytes 1572872 | tf_op jit(solution)/shard_map/ppermute | solution.py:37
  33.8 12.3 %collective-permute-start.6 = (bf16[256,1024]{1,0:T(8,128)(2,1)S(1)}, bf16[256,1024]{1,0:T(8,128)(2,1)S(1)}, u32[]{:S(2)}, u32[]{:S(2)}) collective-permute-start(bf16[256,1024]{1,0:T(8,128)(2,1)S(1)} %slice.42), channel_id=1, source_target_pairs={{0,96},{1,25},{2,98},{3,27},{4,100},{5,29},{6,102},{7,31},{8,104},... | collective-permute-start | bytes 1572872 | tf_op jit(solution)/shard_map/ppermute | solution.py:37
  37.2 15.7 %collective-permute-start.10 = (bf16[512,512]{1,0:T(8,128)(2,1)S(1)}, bf16[512,512]{1,0:T(8,128)(2,1)S(1)}, u32[]{:S(2)}, u32[]{:S(2)}) collective-permute-start(bf16[512,512]{1,0:T(8,128)(2,1)S(1)} %pad_maximum_fusion.1.refs_0_), channel_id=1, source_target_pairs={{0,32},{1,9},{2,34},{3,11},{4,36},{5,13},{6,38},{7,15},{8,40},{9,1... | collective-permute-start | bytes 1572872 | tf_op jit(solution)/shard_map/ppermute | solution.py:37
  37.3 15.8 %collective-permute-start.11 = (bf16[512,512]{1,0:T(8,128)(2,1)S(1)}, bf16[512,512]{1,0:T(8,128)(2,1)S(1)}, u32[]{:S(2)}, u32[]{:S(2)}) collective-permute-start(bf16[512,512]{1,0:T(8,128)(2,1)S(1)} %pad_maximum_fusion.1.refs_0_), channel_id=1, source_target_pairs={{0,96},{1,25},{2,98},{3,27},{4,100},{5,29},{6,102},{7,31},{8,104},... | collective-permute-start | bytes 1572872 | tf_op jit(solution)/shard_map/ppermute | solution.py:37
  49.6 1.6 %collective-permute-start.7 = (f32[512,128]{1,0:T(8,128)S(1)}, f32[512,128]{1,0:T(8,128)S(1)}, u32[]{:S(2)}, u32[]{:S(2)}) collective-permute-start(f32[512,128]{1,0:T(8,128)S(1)} %shrink_far.1), channel_id=1, source_target_pairs={{0,1},{1,0},{2,3},{3,2},{4,5},{5,4},{6,7},{7,6},{8,9},{9,8},{10,11... | collective-permute-start | bytes 786440 | tf_op jit(solution)/shard_map/ppermute | solution.py:43
  51.3 6.5 %collective-permute-start.8 = (f32[512,128]{1,0:T(8,128)S(1)}, f32[512,128]{1,0:T(8,128)S(1)}, u32[]{:S(2)}, u32[]{:S(2)}) collective-permute-start(f32[512,128]{1,0:T(8,128)S(1)} %add.90), channel_id=1, source_target_pairs={{0,2},{1,7},{2,0},{3,5},{4,6},{5,3},{6,4},{7,1},{8,10},{9,15},{10,... | collective-permute-start | bytes 786440 | tf_op jit(solution)/shard_map/ppermute | solution.py:49
  52.9 22.6 %collective-permute-start.12 = (bf16[256,512]{1,0:T(8,128)(2,1)S(1)}, bf16[256,512]{1,0:T(8,128)(2,1)S(1)}, u32[]{:S(2)}, u32[]{:S(2)}) collective-permute-start(bf16[256,512]{1,0:T(8,128)(2,1)S(1)} %slice.43), channel_id=1, source_target_pairs={{0,32},{1,9},{2,34},{3,11},{4,36},{5,13},{6,38},{7,15},{8,40},{9,1... | collective-permute-start | bytes 786440 | tf_op jit(solution)/shard_map/ppermute | solution.py:37
  53.7 21.8 %collective-permute-start.13 = (bf16[256,512]{1,0:T(8,128)(2,1)}, bf16[256,512]{1,0:T(8,128)(2,1)S(1)}, u32[]{:S(2)}, u32[]{:S(2)}) collective-permute-start(bf16[256,512]{1,0:T(8,128)(2,1)} %slice.44), channel_id=1, source_target_pairs={{0,96},{1,25},{2,98},{3,27},{4,100},{5,29},{6,102},{7,31},{8,104},... | collective-permute-start | bytes 786440 | tf_op jit(solution)/shard_map/ppermute | solution.py:37
  57.7 17.8 %collective-permute-start.9 = (f32[512,128]{1,0:T(8,128)S(1)}, f32[512,128]{1,0:T(8,128)S(1)}, u32[]{:S(2)}, u32[]{:S(2)}) collective-permute-start(f32[512,128]{1,0:T(8,128)S(1)} %add.91.mine_ref), channel_id=1, source_target_pairs={{0,6},{1,3},{2,4},{3,1},{4,2},{5,7},{6,0},{7,5},{8,14},{9,11},{10,... | collective-permute-start | bytes 786440 | tf_op jit(solution)/shard_map/ppermute | solution.py:49
  74.1 1.3 %copy-start = (f32[1024,512]{1,0:T(8,128)}, f32[1024,512]{1,0:T(8,128)S(1)}, u32[]{:S(2)}) copy-start(f32[1024,512]{1,0:T(8,128)S(1)} %base.1.base_ref) | copy-start | bytes 6291460
  75.5 1.6 %copy-start.1 = (f32[1024,512]{1,0:T(8,128)S(1)}, f32[1024,512]{1,0:T(8,128)}, u32[]{:S(2)}) copy-start(f32[1024,512]{1,0:T(8,128)} %copy-done) | copy-start | bytes 6291460

commit v2 on v1

--- a/solution.py
+++ b/solution.py
@@ -108,29 +108,17 @@
         o_ref[...] = total
 
 
-def shrink(code, where, ids, x, parts, total, last, name):
-    m, width = x.shape[0], parts[0].shape[1]
-    width = min(width, 1024)
+def shrink(code, ids, x, parts, total, last, name):
+    m, width = x.shape
     counts = tuple(a.shape[0] // 128 for a in parts)
     nb = sum(counts)
-    s = jnp.concatenate([ids, where[None]])
-    whole = lambda i, s: (0, 0)
-    specs = [pl.BlockSpec((m, 128), whole), pl.BlockSpec((m, width), lambda i, s: (0, s[nb]))]
-    specs += [pl.BlockSpec((a.shape[0], width), whole) for a in parts]
-    args = [s, code, x, *parts]
-    if total is not None:
-        specs.append(pl.BlockSpec((m, 128), whole))
-        args.append(total)
-    rows = m // 2 if last else m
+    args = [ids, code, x, *parts] + ([] if total is None else [total])
+    vmem = pl.BlockSpec(memory_space=pltpu.VMEM)
     return pl.pallas_call(
         functools.partial(shrink_kernel, counts, total is not None, last),
-        grid_spec=pltpu.PrefetchScalarGridSpec(
-            num_scalar_prefetch=1,
-            grid=(1,),
-            in_specs=specs,
-            out_specs=pl.BlockSpec((rows, 128), whole),
-        ),
-        out_shape=jax.ShapeDtypeStruct((rows, 128), F32),
+        in_specs=[pl.BlockSpec(memory_space=pltpu.SMEM)] + [vmem] * (len(args) - 1),
+        out_specs=vmem,
+        out_shape=jax.ShapeDtypeStruct((m // 2 if last else m, 128), F32),
         compiler_params=params(),
         cost_estimate=pl.CostEstimate(
             flops=2 * m * width * nb * 128, bytes_accessed=2 * m * width + 256 * nb * width, transcendentals=0
@@ -203,19 +191,25 @@
         return jnp.concatenate([a, first(a, 1), first(a, -1), first(a, 2)], axis=0)
 
     def gather_second(a):
-        half = a.shape[0] // 2
-        before, after = second(a, 1), second(a, -1)
-        far = (second(before[:half], 1), second(after[half:], -1))
-        return before, after, far
-
-    both = gather_first(jnp.concatenate([down, up], axis=1))
+        return second(a, 1), second(a, -1)
+
+    def forward(before, after):
+        half = before.shape[0] // 2
+        return second(before[:half], 1), second(after[half:], -1)
+
     width = down.shape[1]
-    d0, u0 = both[:, :width], both[:, width:]
-    d1, d2, d3 = gather_second(d0)
-    u1, u2, u3 = gather_second(u0)
+    here = lax.dynamic_slice_in_dim(activations, tp * width, width, 1)
+    d0 = gather_first(down)
+    u0 = gather_first(up)
+    d0, here, code = lax.optimization_barrier((d0, here, code))
+    d1, d2 = gather_second(d0)
     base = base_product(activations, query_matrix)
-    total = shrink(code, tp, ids[:12], activations, [d0, d1, d2], None, False, "shrink_near")
-    total = shrink(code, tp, ids[12:], activations, d3, total, True, "shrink_far")
+    d1, d2, base = lax.optimization_barrier((d1, d2, base))
+    d3 = forward(d1, d2)
+    u1, u2 = gather_second(u0)
+    total = shrink(code, ids[:12], here, [d0, d1, d2], None, False, "shrink_near")
+    total = shrink(code, ids[12:], here, d3, total, True, "shrink_far")
+    u3 = forward(u1, u2)
     total = total + other_core(total)
     total = total + pair(total, 0)
     other = pair(total, 1)

time: 81.7 us -> 77 us (0.942)
  waiting for transfers between devices: 22.8 us -> 7.42 us
  local copies, waits for them, and re-layouts: 4.04 us -> 13.3 us
  starting transfers between devices: 24.2 us -> 27.8 us
  Pallas kernels: 26.7 us -> 24.8 us
    ppermute x8, waiting for transfers between devices: 12.2 us -> 0.02 us  [second(): lax.ppermute(a, AXES, every(lambda x, y, z, c: (x + d, y, z, c) if c else...]
    ppermute x3 -> x6, waiting for transfers between devices: 8.3 us -> 0.02 us  [first(): lax.ppermute(a, AXES, every(lambda x, y, z, c: (x, y, z + d, c) if c else...]
    ppermute x2, waiting for transfers between devices: 0.74 us -> 5.86 us  [pair(): return lax.ppermute(a, AXES, every(to))]
    unnamed x10 -> x24, local copies, waits for them, and re-layouts: 2.93 us -> 7.2 us
    ppermute x3 -> x6, starting transfers between devices: 5.2 us -> 8.87 us  [first(): lax.ppermute(a, AXES, every(lambda x, y, z, c: (x, y, z + d, c) if c else...]
    dynamic_slice x0 -> x1, local copies, waits for them, and re-layouts: none -> 3.16 us  [per_device(): here = lax.dynamic_slice_in_dim(activations, tp * width, width, 1)]
    pallas_call x2, Pallas kernels: 9.1 us -> 7.21 us  [shrink(): pl.pallas_call(functools.partial(shrink_kernel, counts, total is not None...]
    slice x6 -> x5, local copies, waits for them, and re-layouts: 0.95 us -> 2.77 us  [the longest x4 2.77 us: forward(): return (second(before[:half], 1), second(after[half:], -1))]
  transfers between devices with their start and end apart: 14 -> 17, of which waited for: 6 -> 3; matrix products, arithmetic and copies ran while one was open for 3% -> 12% of each run, Pallas kernels for 27% -> 27%
where the time goes in v2:
time: 77 us; the launch traced here: 76.6 us
  starting transfers between devices  27.8 us (36%)
  Pallas kernels  24.8 us (32%)
  local copies, waits for them, and re-layouts  13.3 us (17%)
  waiting for transfers between devices  7.42 us (10%)
  other arithmetic  2.91 us (4%)
    ppermute x8, starting transfers between devices, second(): lax.ppermute(a, AXES, every(lambda x, y, z, c: (x + d, y, z, c) if c else...  14.2 us
    pallas_call x1, Pallas kernels, base_product(): pl.pallas_call(base_kernel, grid=(k // depth,), in_specs=[pl.BlockSpec((m...  13.3 us
    ppermute x6, starting transfers between devices, first(): lax.ppermute(a, AXES, every(lambda x, y, z, c: (x, y, z + d, c) if c else...  8.87 us
    pallas_call x2, Pallas kernels, shrink(): pl.pallas_call(functools.partial(shrink_kernel, counts, total is not None...  7.21 us
    unnamed x24, local copies, waits for them, and re-layouts  7.2 us
    ppermute x2, waiting for transfers between devices, pair(): return lax.ppermute(a, AXES, every(to))  5.86 us
    ppermute x2, starting transfers between devices, pair(): return lax.ppermute(a, AXES, every(to))  4.73 us
    pallas_call x1, Pallas kernels, expand(): pl.pallas_call(functools.partial(expand_kernel, counts), grid_spec=pltpu....  4.36 us
  transfers between devices with their start and end apart: 17, of which 3 were waited for; matrix products, arithmetic and copies ran while one was open for 12% of the time, Pallas kernels for 27%

profile of v2, /device:TPU:0, one launch (start us, length us, event | category | flops | bytes accessed | tf_op | source)
XLA Modules:
  0.0 76.6 jit_solution(13298834252151919713)
XLA Ops:
  0.0 1.6 %collective-permute-start = (bf16[128,1024]{1,0:T(8,128)(2,1)}, bf16[128,1024]{1,0:T(8,128)(2,1)S(1)}, u32[]{:S(2)}, u32[]{:S(2)}) collective-permute-start(bf16[128,1024]{1,0:T(8,128)(2,1)} %bitcast.9), channel_id=1, source_target_pairs={{0,8},{1,33},{2,10},{3,35},{4,12},{5,37},{6,14},{7,39},{8,16},{9,4... | collective-permute-start | bytes 786440 | tf_op jit(solution)/shard_map/ppermute | solution.py:31
  1.6 1.7 %collective-permute-start.1 = (bf16[128,1024]{1,0:T(8,128)(2,1)}, bf16[128,1024]{1,0:T(8,128)(2,1)S(1)}, u32[]{:S(2)}, u32[]{:S(2)}) collective-permute-start(bf16[128,1024]{1,0:T(8,128)(2,1)} %bitcast.10), channel_id=1, source_target_pairs={{0,24},{1,97},{2,26},{3,99},{4,28},{5,101},{6,30},{7,103},{8,0},{9... | collective-permute-start | bytes 786440 | tf_op jit(solution)/shard_map/ppermute | solution.py:31
  3.2 1.9 %collective-permute-start.2 = (bf16[128,1024]{1,0:T(8,128)(2,1)}, bf16[128,1024]{1,0:T(8,128)(2,1)S(1)}, u32[]{:S(2)}, u32[]{:S(2)}) collective-permute-start(bf16[128,1024]{1,0:T(8,128)(2,1)} %bitcast.11), channel_id=1, source_target_pairs={{0,16},{1,65},{2,18},{3,67},{4,20},{5,69},{6,22},{7,71},{8,24},{9,... | collective-permute-start | bytes 786440 | tf_op jit(solution)/shard_map/ppermute | solution.py:31
  5.1 0.6 collective-permute-start.10
  5.7 2.6 %collective-permute-start.11 = (bf16[128,512]{1,0:T(8,128)(2,1)}, bf16[128,512]{1,0:T(8,128)(2,1)S(1)}, u32[]{:S(2)}, u32[]{:S(2)}) collective-permute-start(bf16[128,512]{1,0:T(8,128)(2,1)} %bitcast.14), channel_id=1, source_target_pairs={{0,24},{1,97},{2,26},{3,99},{4,28},{5,101},{6,30},{7,103},{8,0},{9... | collective-permute-start | bytes 393224 | tf_op jit(solution)/shard_map/ppermute | solution.py:31
  8.4 0.7 and_select_fusion.1
  9.1 0.7 and_select_fusion
  9.8 0.0 copy-start.10
  9.8 0.0 copy-start.9
  9.8 3.2 %constant_dynamic-slice_fusion.x_ref = bf16[1024,1024]{1,0:T(8,128)(2,1)} fusion(bf16[1024,8192]{1,0:T(8,128)(2,1)} %x_ref.1, s32[]{:T(128)S(6)} %select_n.68), kind=kLoop, calls=%fused_computation.25 | loop fusion | bytes 4194308 | tf_op jit(solution)/shard_map/dynamic_slice | solution.py:201
  13.0 0.3 fusion.code_ref
  13.4 0.0 collective-permute-done
  13.4 0.0 copy-done.10
  13.4 0.5 collective-permute-start.12
  13.9 0.0 collective-permute-done.1
  13.9 0.0 collective-permute-done.2
  13.9 0.0 copy-done.9
  13.9 0.1 pad_maximum_fusion.refs_0_
  14.0 2.1 %collective-permute-start.3 = (bf16[512,1024]{1,0:T(8,128)(2,1)S(1)}, bf16[512,1024]{1,0:T(8,128)(2,1)S(1)}, u32[]{:S(2)}, u32[]{:S(2)}) collective-permute-start(bf16[512,1024]{1,0:T(8,128)(2,1)S(1)} %pad_maximum_fusion.refs_0_), channel_id=1, source_target_pairs={{0,32},{1,9},{2,34},{3,11},{4,36},{5,13},{6,38},{7,15},{8,40},{9,1... | collective-permute-start | bytes 3145736 | tf_op jit(solution)/shard_map/ppermute | solution.py:37
  16.0 2.2 %collective-permute-start.4 = (bf16[512,1024]{1,0:T(8,128)(2,1)S(1)}, bf16[512,1024]{1,0:T(8,128)(2,1)}, u32[]{:S(2)}, u32[]{:S(2)}) collective-permute-start(bf16[512,1024]{1,0:T(8,128)(2,1)S(1)} %pad_maximum_fusion.refs_0_), channel_id=1, source_target_pairs={{0,96},{1,25},{2,98},{3,27},{4,100},{5,29},{6,102},{7,31},{8,104},... | collective-permute-start | bytes 3145736 | tf_op jit(solution)/shard_map/ppermute | solution.py:37
  18.2 0.0 copy-done.11
  18.3 0.1 add_select_fusion
  18.3 13.3 %base.1.base_ref = f32[1024,512]{1,0:T(8,128)S(1)} custom-call(bf16[1024,8192]{1,0:T(8,128)(2,1)} %x_ref.1, bf16[8192,512]{1,0:T(8,128)(2,1)} %w_ref.1), custom_call_target="tpu_custom_call" | custom-call | flops 8589934592 | bytes 27262976 | tf_op jit(solution)/shard_map/base/pallas_call | solution.py:71
  31.6 0.0 copy-start.7
  31.6 1.3 %copy-done.7 = f32[1024,512]{1,0:T(8,128)} copy-done((f32[1024,512]{1,0:T(8,128)}, f32[1024,512]{1,0:T(8,128)S(1)}, u32[]{:S(2)}) %copy-start.7) | copy-done | bytes 2097176
  32.9 0.0 collective-permute-done.3.refs_1_
  32.9 0.0 collective-permute-done.4.refs_2_
  32.9 0.8 %slice.26 = bf16[256,1024]{1,0:T(8,128)(2,1)} slice(bf16[512,1024]{1,0:T(8,128)(2,1)S(1)} %collective-permute-done.3.refs_1_), slice={[0:256], [0:1024]} | slice | bytes 1048576 | tf_op jit(solution)/shard_map/slice | solution.py:198
  33.8 1.0 %copy-done.1 = bf16[512,1024]{1,0:T(8,128)(2,1)} copy-done((bf16[512,1024]{1,0:T(8,128)(2,1)}, bf16[512,1024]{1,0:T(8,128)(2,1)S(1)}, u32[]{:S(2)}) %copy-start.1) | copy-done | bytes 1048600
  34.7 0.0 collective-permute-start.5
  34.8 1.9 %slice.27 = bf16[256,1024]{1,0:T(8,128)(2,1)} slice(bf16[512,1024]{1,0:T(8,128)(2,1)} %collective-permute-done.4.refs_2_), slice={[256:512], [0:1024]} | slice | bytes 1048576 | tf_op jit(solution)/shard_map/slice | solution.py:198
  36.6 3.2 %collective-permute-start.6 = (bf16[256,1024]{1,0:T(8,128)(2,1)}, bf16[256,1024]{1,0:T(8,128)(2,1)S(1)}, u32[]{:S(2)}, u32[]{:S(2)}) collective-permute-start(bf16[256,1024]{1,0:T(8,128)(2,1)} %slice.27), channel_id=1, source_target_pairs={{0,96},{1,25},{2,98},{3,27},{4,100},{5,29},{6,102},{7,31},{8,104},... | collective-permute-start | bytes 1572872 | tf_op jit(solution)/shard_map/ppermute | solution.py:37
  39.9 0.1 slice.29.s_ref
  40.0 0.0 collective-permute-done.10
  40.0 0.0 collective-permute-done.11
  40.0 0.0 collective-permute-done.12
  40.0 0.9 %pad_maximum_fusion.1.refs_0_ = bf16[512,512]{1,0:T(8,128)(2,1)S(1)} fusion(bf16[128,512]{1,0:T(8,128)(2,1)} %collective-permute-done.12, bf16[128,512]{1,0:T(8,128)(2,1)S(1)} %collective-permute-done.11, bf16[128,512]{1,0:T(8,128)(2,1)S(1)} %collective-permute-done.10, bf16[128,512]{1,0:T(8,128)(2,1)S(1)} %bitcast.16), kind=kLoop, calls=%fused_computation.1 | loop fusion | flops 2097152 | bytes 1048576 | tf_op jit(solution)/shard_map/concatenate | solution.py:191
  40.9 0.0 copy-start
  40.9 0.1 collective-permute-start.13
  41.0 3.2 %collective-permute-start.14 = (bf16[512,512]{1,0:T(8,128)(2,1)S(1)}, bf16[512,512]{1,0:T(8,128)(2,1)S(1)}, u32[]{:S(2)}, u32[]{:S(2)}) collective-permute-start(bf16[512,512]{1,0:T(8,128)(2,1)S(1)} %pad_maximum_fusion.1.refs_0_), channel_id=1, source_target_pairs={{0,96},{1,25},{2,98},{3,27},{4,100},{5,29},{6,102},{7,31},{8,104},... | collective-permute-start | bytes 1572872 | tf_op jit(solution)/shard_map/ppermute | solution.py:37
  44.2 1.2 %copy-done.2 = bf16[512,1024]{1,0:T(8,128)(2,1)S(1)} copy-done((bf16[512,1024]{1,0:T(8,128)(2,1)S(1)}, bf16[512,1024]{1,0:T(8,128)(2,1)}, u32[]{:S(2)}) %copy-start.2) | copy-done | bytes 1048600
  45.5 5.3 %shrink_near.1.refs_2_ = f32[1024,128]{1,0:T(8,128)S(1)} custom-call(s32[12]{0:T(128)S(1)} %slice.29.s_ref, s32[1024,128]{1,0:T(8,128)S(1)} %fusion.code_ref, bf16[1024,1024]{1,0:T(8,128)(2,1)} %constant_dynamic-slice_fusion.x_ref, bf16[512,1024]{1,0:T(8,128)(2,1)S(1)} %pad_maximum_fusion.refs_0_, bf16[512,1024]{1,0:T(8,128)(2,1)S(1)} %copy-done.2, ...), custom_call_target="tpu_custom_call" | custom-call | flops 3221225472 | bytes 5242880 | tf_op jit(solution)/shard_map/shrink_near/pallas_call | solution.py:117
  50.8 0.0 collective-permute-done.5.refs_0_
  50.8 0.0 collective-permute-done.6.refs_1_
  50.8 0.0 copy-done
  50.8 1.9 %shrink_far.1 = f32[512,128]{1,0:T(8,128)S(1)} custom-call(s32[4]{0:T(128)S(1)} %slice_bitcast_fusion.s_ref, s32[1024,128]{1,0:T(8,128)S(1)} %fusion.code_ref, bf16[1024,1024]{1,0:T(8,128)(2,1)S(1)} %copy-done, bf16[256,1024]{1,0:T(8,128)(2,1)S(1)} %collective-permute-done.5.refs_0_, bf16[256,1024]{1,0:T(8,128)(2,1)S(1)} %collective-permute-done.6.refs_1_, ...), custom_call_target="tpu_custom_call" | custom-call | flops 1073741824 | bytes 3145728 | tf_op jit(solution)/shard_map/shrink_far/pallas_call | solution.py:117
  52.7 0.1 collective-permute-start.7
  52.8 1.5 %collective-permute-done.7 = f32[512,128]{1,0:T(8,128)S(1)} collective-permute-done((f32[512,128]{1,0:T(8,128)S(1)}, f32[512,128]{1,0:T(8,128)S(1)}, u32[]{:S(2)}, u32[]{:S(2)}) %collective-permute-start.7) | collective-permute-done | bytes 262176 | tf_op jit(solution)/shard_map/ppermute | solution.py:43
  54.4 1.7 %collective-permute-start.8 = (f32[512,128]{1,0:T(8,128)S(1)}, f32[512,128]{1,0:T(8,128)S(1)}, u32[]{:S(2)}, u32[]{:S(2)}) collective-permute-start(f32[512,128]{1,0:T(8,128)S(1)} %add.94), channel_id=1, source_target_pairs={{0,2},{1,7},{2,0},{3,5},{4,6},{5,3},{6,4},{7,1},{8,10},{9,15},{10,... | collective-permute-start | bytes 786440 | tf_op jit(solution)/shard_map/ppermute | solution.py:49
  56.0 0.0 collective-permute-done.13.refs_1_
  56.0 0.1 collective-permute-start.15
  56.1 0.0 collective-permute-done.14.refs_2_
  56.2 3.3 %collective-permute-start.16 = (bf16[256,512]{1,0:T(8,128)(2,1)S(1)}, bf16[256,512]{1,0:T(8,128)(2,1)S(1)}, u32[]{:S(2)}, u32[]{:S(2)}) collective-permute-start(bf16[256,512]{1,0:T(8,128)(2,1)S(1)} %slice.33), channel_id=1, source_target_pairs={{0,96},{1,25},{2,98},{3,27},{4,100},{5,29},{6,102},{7,31},{8,104},... | collective-permute-start | bytes 786440 | tf_op jit(solution)/shard_map/ppermute | solution.py:37
  59.4 1.4 %collective-permute-done.8 = f32[512,128]{1,0:T(8,128)S(1)} collective-permute-done((f32[512,128]{1,0:T(8,128)S(1)}, f32[512,128]{1,0:T(8,128)S(1)}, u32[]{:S(2)}, u32[]{:S(2)}) %collective-permute-start.8) | collective-permute-done | bytes 262176 | tf_op jit(solution)/shard_map/ppermute | solution.py:49
  60.8 0.0 copy-done.3
  60.9 3.1 %collective-permute-start.9 = (f32[512,128]{1,0:T(8,128)S(1)}, f32[512,128]{1,0:T(8,128)S(1)}, u32[]{:S(2)}, u32[]{:S(2)}) collective-permute-start(f32[512,128]{1,0:T(8,128)S(1)} %add.95.mine_ref), channel_id=1, source_target_pairs={{0,6},{1,3},{2,4},{3,1},{4,2},{5,7},{6,0},{7,5},{8,14},{9,11},{10,... | collective-permute-start | bytes 786440 | tf_op jit(solution)/shard_map/ppermute | solution.py:49
  63.9 0.1 select_n.67.s_ref
  64.0 0.0 collective-permute-done.15.refs_3_
  64.0 0.0 collective-permute-done.16.refs_4_
  64.0 4.5 %collective-permute-done.9.other_ref = f32[512,128]{1,0:T(8,128)S(1)} collective-permute-done((f32[512,128]{1,0:T(8,128)S(1)}, f32[512,128]{1,0:T(8,128)S(1)}, u32[]{:S(2)}, u32[]{:S(2)}) %collective-permute-start.9) | collective-permute-done | bytes 262176 | tf_op jit(solution)/shard_map/ppermute | solution.py:49
  68.5 1.0 %copy-done.4 = bf16[512,512]{1,0:T(8,128)(2,1)S(1)} copy-done((bf16[512,512]{1,0:T(8,128)(2,1)S(1)}, bf16[512,512]{1,0:T(8,128)(2,1)}, u32[]{:S(2)}) %copy-start.4) | copy-done | bytes 524312
  69.6 1.0 %copy-done.6 = bf16[512,512]{1,0:T(8,128)(2,1)S(1)} copy-done((bf16[512,512]{1,0:T(8,128)(2,1)S(1)}, bf16[512,512]{1,0:T(8,128)(2,1)}, u32[]{:S(2)}) %copy-start.6) | copy-done | bytes 524312
  70.6 1.6 %copy-done.8 = f32[1024,512]{1,0:T(8,128)S(1)} copy-done((f32[1024,512]{1,0:T(8,128)S(1)}, f32[1024,512]{1,0:T(8,128)}, u32[]{:S(2)}) %copy-start.8) | copy-done | bytes 2097176
  72.2 4.4 %expand.1 = bf16[1024,512]{1,0:T(8,128)(2,1)} custom-call(s32[16]{0:T(128)S(1)} %select_n.67.s_ref, s32[1024,128]{1,0:T(8,128)S(1)} %fusion.code_ref, f32[512,128]{1,0:T(8,128)S(1)} %add.95.mine_ref, f32[512,128]{1,0:T(8,128)S(1)} %collective-permute-done.9.other_ref, f32[1024,512]{1,0:T(8,128)S(1)} %copy-done.8, ...), custom_call_target="tpu_custom_call" | custom-call | flops 2147483648 | bytes 3145728 | tf_op jit(solution)/shard_map/expand/pallas_call | solution.py:157
  (17 shorter events, 0.1 us)
Async XLA Ops:
  0.0 13.4 %collective-permute-start = (bf16[128,1024]{1,0:T(8,128)(2,1)}, bf16[128,1024]{1,0:T(8,128)(2,1)S(1)}, u32[]{:S(2)}, u32[]{:S(2)}) collective-permute-start(bf16[128,1024]{1,0:T(8,128)(2,1)} %bitcast.9), channel_id=1, source_target_pairs={{0,8},{1,33},{2,10},{3,35},{4,12},{5,37},{6,14},{7,39},{8,16},{9,4... | collective-permute-start | bytes 786440 | tf_op jit(solution)/shard_map/ppermute | solution.py:31
  1.6 12.3 %collective-permute-start.1 = (bf16[128,1024]{1,0:T(8,128)(2,1)}, bf16[128,1024]{1,0:T(8,128)(2,1)S(1)}, u32[]{:S(2)}, u32[]{:S(2)}) collective-permute-start(bf16[128,1024]{1,0:T(8,128)(2,1)} %bitcast.10), channel_id=1, source_target_pairs={{0,24},{1,97},{2,26},{3,99},{4,28},{5,101},{6,30},{7,103},{8,0},{9... | collective-permute-start | bytes 786440 | tf_op jit(solution)/shard_map/ppermute | solution.py:31
  3.2 10.6 %collective-permute-start.2 = (bf16[128,1024]{1,0:T(8,128)(2,1)}, bf16[128,1024]{1,0:T(8,128)(2,1)S(1)}, u32[]{:S(2)}, u32[]{:S(2)}) collective-permute-start(bf16[128,1024]{1,0:T(8,128)(2,1)} %bitcast.11), channel_id=1, source_target_pairs={{0,16},{1,65},{2,18},{3,67},{4,20},{5,69},{6,22},{7,71},{8,24},{9,... | collective-permute-start | bytes 786440 | tf_op jit(solution)/shard_map/ppermute | solution.py:31
  5.1 34.8 %collective-permute-start.10 = (bf16[128,512]{1,0:T(8,128)(2,1)}, bf16[128,512]{1,0:T(8,128)(2,1)S(1)}, u32[]{:S(2)}, u32[]{:S(2)}) collective-permute-start(bf16[128,512]{1,0:T(8,128)(2,1)} %bitcast.13), channel_id=1, source_target_pairs={{0,8},{1,33},{2,10},{3,35},{4,12},{5,37},{6,14},{7,39},{8,16},{9,4... | collective-permute-start | bytes 393224 | tf_op jit(solution)/shard_map/ppermute | solution.py:31
  5.7 34.2 %collective-permute-start.11 = (bf16[128,512]{1,0:T(8,128)(2,1)}, bf16[128,512]{1,0:T(8,128)(2,1)S(1)}, u32[]{:S(2)}, u32[]{:S(2)}) collective-permute-start(bf16[128,512]{1,0:T(8,128)(2,1)} %bitcast.14), channel_id=1, source_target_pairs={{0,24},{1,97},{2,26},{3,99},{4,28},{5,101},{6,30},{7,103},{8,0},{9... | collective-permute-start | bytes 393224 | tf_op jit(solution)/shard_map/ppermute | solution.py:31
  9.8 3.6 %copy-start.10 = (bf16[2,64,512]{2,1,0:T(8,128)(2,1)S(1)}, bf16[2,64,512]{2,1,0:T(8,128)(2,1)}, u32[]{:S(2)}) copy-start(bf16[2,64,512]{2,1,0:T(8,128)(2,1)} %param.10) | copy-start | bytes 393220
  9.8 4.1 %copy-start.9 = (bf16[2,1024,64]{1,2,0:T(8,128)(2,1)S(1)}, bf16[2,1024,64]{1,2,0:T(8,128)(2,1)}, u32[]{:S(2)}) copy-start(bf16[2,1024,64]{1,2,0:T(8,128)(2,1)} %param.9) | copy-start | bytes 786436
  13.0 5.3 %copy-start.11 = (s32[4]{0:T(128)S(1)}, s32[4]{0:T(128)}, u32[]{:S(2)}) copy-start(s32[4]{0:T(128)} %constant.101.clone) | copy-start | bytes 52
  13.4 26.6 %collective-permute-start.12 = (bf16[128,512]{1,0:T(8,128)(2,1)S(1)}, bf16[128,512]{1,0:T(8,128)(2,1)}, u32[]{:S(2)}, u32[]{:S(2)}) collective-permute-start(bf16[128,512]{1,0:T(8,128)(2,1)S(1)} %bitcast.15), channel_id=1, source_target_pairs={{0,16},{1,65},{2,18},{3,67},{4,20},{5,69},{6,22},{7,71},{8,24},{9,... | collective-permute-start | bytes 393224 | tf_op jit(solution)/shard_map/ppermute | solution.py:31
  14.0 19.0 %collective-permute-start.3 = (bf16[512,1024]{1,0:T(8,128)(2,1)S(1)}, bf16[512,1024]{1,0:T(8,128)(2,1)S(1)}, u32[]{:S(2)}, u32[]{:S(2)}) collective-permute-start(bf16[512,1024]{1,0:T(8,128)(2,1)S(1)} %pad_maximum_fusion.refs_0_), channel_id=1, source_target_pairs={{0,32},{1,9},{2,34},{3,11},{4,36},{5,13},{6,38},{7,15},{8,40},{9,1... | collective-permute-start | bytes 3145736 | tf_op jit(solution)/shard_map/ppermute | solution.py:37
  16.0 16.9 %collective-permute-start.4 = (bf16[512,1024]{1,0:T(8,128)(2,1)S(1)}, bf16[512,1024]{1,0:T(8,128)(2,1)}, u32[]{:S(2)}, u32[]{:S(2)}) collective-permute-start(bf16[512,1024]{1,0:T(8,128)(2,1)S(1)} %pad_maximum_fusion.refs_0_), channel_id=1, source_target_pairs={{0,96},{1,25},{2,98},{3,27},{4,100},{5,29},{6,102},{7,31},{8,104},... | collective-permute-start | bytes 3145736 | tf_op jit(solution)/shard_map/ppermute | solution.py:37
  31.6 1.3 %copy-start.7 = (f32[1024,512]{1,0:T(8,128)}, f32[1024,512]{1,0:T(8,128)S(1)}, u32[]{:S(2)}) copy-start(f32[1024,512]{1,0:T(8,128)S(1)} %base.1.base_ref) | copy-start | bytes 6291460
  33.8 1.0 %copy-start.1 = (bf16[512,1024]{1,0:T(8,128)(2,1)}, bf16[512,1024]{1,0:T(8,128)(2,1)S(1)}, u32[]{:S(2)}) copy-start(bf16[512,1024]{1,0:T(8,128)(2,1)S(1)} %collective-permute-done.3.refs_1_) | copy-start | bytes 3145732
  34.7 16.0 %collective-permute-start.5 = (bf16[256,1024]{1,0:T(8,128)(2,1)}, bf16[256,1024]{1,0:T(8,128)(2,1)S(1)}, u32[]{:S(2)}, u32[]{:S(2)}) collective-permute-start(bf16[256,1024]{1,0:T(8,128)(2,1)} %slice.26), channel_id=1, source_target_pairs={{0,32},{1,9},{2,34},{3,11},{4,36},{5,13},{6,38},{7,15},{8,40},{9,1... | collective-permute-start | bytes 1572872 | tf_op jit(solution)/shard_map/ppermute | solution.py:37
  36.6 14.2 %collective-permute-start.6 = (bf16[256,1024]{1,0:T(8,128)(2,1)}, bf16[256,1024]{1,0:T(8,128)(2,1)S(1)}, u32[]{:S(2)}, u32[]{:S(2)}) collective-permute-start(bf16[256,1024]{1,0:T(8,128)(2,1)} %slice.27), channel_id=1, source_target_pairs={{0,96},{1,25},{2,98},{3,27},{4,100},{5,29},{6,102},{7,31},{8,104},... | collective-permute-start | bytes 1572872 | tf_op jit(solution)/shard_map/ppermute | solution.py:37
  40.9 9.9 %copy-start = (bf16[1024,1024]{1,0:T(8,128)(2,1)S(1)}, bf16[1024,1024]{1,0:T(8,128)(2,1)}, u32[]{:S(2)}) copy-start(bf16[1024,1024]{1,0:T(8,128)(2,1)} %constant_dynamic-slice_fusion.x_ref) | copy-start | bytes 6291460
  40.9 15.1 %collective-permute-start.13 = (bf16[512,512]{1,0:T(8,128)(2,1)S(1)}, bf16[512,512]{1,0:T(8,128)(2,1)S(1)}, u32[]{:S(2)}, u32[]{:S(2)}) collective-permute-start(bf16[512,512]{1,0:T(8,128)(2,1)S(1)} %pad_maximum_fusion.1.refs_0_), channel_id=1, source_target_pairs={{0,32},{1,9},{2,34},{3,11},{4,36},{5,13},{6,38},{7,15},{8,40},{9,1... | collective-permute-start | bytes 1572872 | tf_op jit(solution)/shard_map/ppermute | solution.py:37
  41.0 15.1 %collective-permute-start.14 = (bf16[512,512]{1,0:T(8,128)(2,1)S(1)}, bf16[512,512]{1,0:T(8,128)(2,1)S(1)}, u32[]{:S(2)}, u32[]{:S(2)}) collective-permute-start(bf16[512,512]{1,0:T(8,128)(2,1)S(1)} %pad_maximum_fusion.1.refs_0_), channel_id=1, source_target_pairs={{0,96},{1,25},{2,98},{3,27},{4,100},{5,29},{6,102},{7,31},{8,104},... | collective-permute-start | bytes 1572872 | tf_op jit(solution)/shard_map/ppermute | solution.py:37
  44.2 1.2 %copy-start.2 = (bf16[512,1024]{1,0:T(8,128)(2,1)S(1)}, bf16[512,1024]{1,0:T(8,128)(2,1)}, u32[]{:S(2)}) copy-start(bf16[512,1024]{1,0:T(8,128)(2,1)} %copy-done.1) | copy-start | bytes 3145732
  52.7 1.6 %collective-permute-start.7 = (f32[512,128]{1,0:T(8,128)S(1)}, f32[512,128]{1,0:T(8,128)S(1)}, u32[]{:S(2)}, u32[]{:S(2)}) collective-permute-start(f32[512,128]{1,0:T(8,128)S(1)} %shrink_far.1), channel_id=1, source_target_pairs={{0,1},{1,0},{2,3},{3,2},{4,5},{5,4},{6,7},{7,6},{8,9},{9,8},{10,11... | collective-permute-start | bytes 786440 | tf_op jit(solution)/shard_map/ppermute | solution.py:43
  54.4 6.5 %collective-permute-start.8 = (f32[512,128]{1,0:T(8,128)S(1)}, f32[512,128]{1,0:T(8,128)S(1)}, u32[]{:S(2)}, u32[]{:S(2)}) collective-permute-start(f32[512,128]{1,0:T(8,128)S(1)} %add.94), channel_id=1, source_target_pairs={{0,2},{1,7},{2,0},{3,5},{4,6},{5,3},{6,4},{7,1},{8,10},{9,15},{10,... | collective-permute-start | bytes 786440 | tf_op jit(solution)/shard_map/ppermute | solution.py:49
  56.0 4.8 %copy-start.3 = (bf16[512,512]{1,0:T(8,128)(2,1)}, bf16[512,512]{1,0:T(8,128)(2,1)S(1)}, u32[]{:S(2)}) copy-start(bf16[512,512]{1,0:T(8,128)(2,1)S(1)} %collective-permute-done.13.refs_1_) | copy-start | bytes 1572868
  56.0 8.0 %collective-permute-start.15 = (bf16[256,512]{1,0:T(8,128)(2,1)S(1)}, bf16[256,512]{1,0:T(8,128)(2,1)S(1)}, u32[]{:S(2)}, u32[]{:S(2)}) collective-permute-start(bf16[256,512]{1,0:T(8,128)(2,1)S(1)} %slice.32), channel_id=1, source_target_pairs={{0,32},{1,9},{2,34},{3,11},{4,36},{5,13},{6,38},{7,15},{8,40},{9,1... | collective-permute-start | bytes 786440 | tf_op jit(solution)/shard_map/ppermute | solution.py:37
  56.1 4.7 %copy-start.5 = (bf16[512,512]{1,0:T(8,128)(2,1)}, bf16[512,512]{1,0:T(8,128)(2,1)S(1)}, u32[]{:S(2)}) copy-start(bf16[512,512]{1,0:T(8,128)(2,1)S(1)} %collective-permute-done.14.refs_2_) | copy-start | bytes 1572868
  56.2 7.8 %collective-permute-start.16 = (bf16[256,512]{1,0:T(8,128)(2,1)S(1)}, bf16[256,512]{1,0:T(8,128)(2,1)S(1)}, u32[]{:S(2)}, u32[]{:S(2)}) collective-permute-start(bf16[256,512]{1,0:T(8,128)(2,1)S(1)} %slice.33), channel_id=1, source_target_pairs={{0,96},{1,25},{2,98},{3,27},{4,100},{5,29},{6,102},{7,31},{8,104},... | collective-permute-start | bytes 786440 | tf_op jit(solution)/shard_map/ppermute | solution.py:37
  60.9 7.7 %collective-permute-start.9 = (f32[512,128]{1,0:T(8,128)S(1)}, f32[512,128]{1,0:T(8,128)S(1)}, u32[]{:S(2)}, u32[]{:S(2)}) collective-permute-start(f32[512,128]{1,0:T(8,128)S(1)} %add.95.mine_ref), channel_id=1, source_target_pairs={{0,6},{1,3},{2,4},{3,1},{4,2},{5,7},{6,0},{7,5},{8,14},{9,11},{10,... | collective-permute-start | bytes 786440 | tf_op jit(solution)/shard_map/ppermute | solution.py:49
  68.5 1.0 %copy-start.4 = (bf16[512,512]{1,0:T(8,128)(2,1)S(1)}, bf16[512,512]{1,0:T(8,128)(2,1)}, u32[]{:S(2)}) copy-start(bf16[512,512]{1,0:T(8,128)(2,1)} %copy-done.3) | copy-start | bytes 1572868
  69.6 1.0 %copy-start.6 = (bf16[512,512]{1,0:T(8,128)(2,1)S(1)}, bf16[512,512]{1,0:T(8,128)(2,1)}, u32[]{:S(2)}) copy-start(bf16[512,512]{1,0:T(8,128)(2,1)} %copy-done.5) | copy-start | bytes 1572868
  70.6 1.6 %copy-start.8 = (f32[1024,512]{1,0:T(8,128)S(1)}, f32[1024,512]{1,0:T(8,128)}, u32[]{:S(2)}) copy-start(f32[1024,512]{1,0:T(8,128)} %copy-done.7) | copy-start | bytes 6291460

commit v3 on v0

v3 whole, which is shorter than its diff:
```python
import functools

import jax
import jax.numpy as jnp
from jax import lax
from jax.experimental import pallas as pl
from jax.experimental.pallas import tpu as pltpu
from jax.sharding import PartitionSpec as P

BF, F32 = jnp.bfloat16, jnp.float32
AXES = ("rep", "tp")
RING = 4
HOPS = (0, -1, 1, 2)
adapter_scale = 0.5


def device_of(x, y, z, c):
    return (z % RING * RING + x % RING) * 2 * RING + y % RING * 2 + c


def every(f):
    return [
        (device_of(x, y, z, c), device_of(*f(x, y, z, c)))
        for z in range(RING)
        for x in range(RING)
        for y in range(RING)
        for c in range(2)
    ]


def first(a, d):
    return lax.ppermute(
        a, AXES, every(lambda x, y, z, c: (x, y, z + d, c) if c else (x + d, y, z, c))
    )


def second(a, d):
    return lax.ppermute(
        a, AXES, every(lambda x, y, z, c: (x + d, y, z, c) if c else (x, y, z + d, c))
    )


def other_core(a):
    return lax.ppermute(a, AXES, every(lambda x, y, z, c: (x, y, z, 1 - c)))


def pair(a, step):
    def to(x, y, z, c):
        return (x, (y ^ 1) if (c + step) % 2 == 0 else (3 - y), z, c)

    return lax.ppermute(a, AXES, every(to))


def params(mib):
    return pltpu.CompilerParams(vmem_limit_bytes=mib << 20)


def cost(flops, moved):
    return pl.CostEstimate(flops=flops, bytes_accessed=moved, transcendentals=0)


VMEM = pl.BlockSpec(memory_space=pltpu.VMEM)
HBM = pl.BlockSpec(memory_space=pltpu.HBM)


def owner(j, i):
    rep, core = lax.axis_index("rep"), lax.axis_index("tp") % 2
    dz, dx = jnp.where(core == 0, j, i), jnp.where(core == 0, i, j)
    return (rep // RING + dz + RING) % RING * RING + (rep % RING + dx + RING) % RING


def prep_kernel(ident_ref, x_ref, here_ref, code_ref, sem):
    width = here_ref.shape[1]
    at = pl.multiple_of(lax.axis_index("tp") * width, width)
    copy = pltpu.make_async_copy(x_ref.at[:, pl.ds(at, width)], here_ref, sem)
    copy.start()
    side = lax.broadcasted_iota(jnp.int32, (128, 128), 1) // 64
    for r in range(ident_ref.shape[0]):
        ident = jnp.broadcast_to(ident_ref[r : r + 1, :], (128, 128)).T
        code_ref[128 * r : 128 * r + 128, :] = jnp.where((ident & 1) == side, ident >> 1, -1)
    copy.wait()


def prepare(ident, x, width):
    m = x.shape[0]
    return pl.pallas_call(
        prep_kernel,
        in_specs=[VMEM, HBM],
        out_specs=[VMEM, VMEM],
        out_shape=[
            jax.ShapeDtypeStruct((m, width), BF),
            jax.ShapeDtypeStruct((m, 128), jnp.int32),
        ],
        scratch_shapes=[pltpu.SemaphoreType.DMA],
        compiler_params=params(50),
        cost_estimate=cost(0, 4 * m * width),
        name="prepare",
    )(ident.reshape(m // 128, 128), x)


def base_kernel(depths, block, x_ref, w_ref, o_ref, xb, wb, sems):
    copies, at = [], 0
    for i, depth in enumerate(depths):
        part = pl.ds(at, depth)
        copies.append(
            (
                part,
                pltpu.make_async_copy(w_ref.at[part], wb.at[part], sems.at[2 * i]),
                pltpu.make_async_copy(x_ref.at[:, part], xb.at[:, part], sems.at[2 * i + 1]),
            )
        )
        at += depth
    for _, *pair_of in copies:
        for copy in pair_of:
            copy.start()
    for i, (part, *pair_of) in enumerate(copies):
        for copy in pair_of:
            copy.wait()

        def rows(r, _):
            row = pl.ds(pl.multiple_of(r * block, block), block)
            p = jnp.dot(xb[row, part], wb[part, :], preferred_element_type=F32)
            o_ref[row, :] = p if i == 0 else o_ref[row, :] + p
            return 0

        lax.fori_loop(0, x_ref.shape[0] // block, rows, 0)


def base_product(x, w, depths=(1024, 2048, 2048, 2048, 1024), block=256):
    m, k = x.shape
    n = w.shape[1]
    return pl.pallas_call(
        functools.partial(base_kernel, depths, block),
        in_specs=[HBM, HBM],
        out_specs=VMEM,
        out_shape=jax.ShapeDtypeStruct((m, n), F32),
        scratch_shapes=[
            pltpu.VMEM((m, k), BF),
            pltpu.VMEM((k, n), BF),
            pltpu.SemaphoreType.DMA((2 * len(depths),)),
        ],
        compiler_params=params(30),
        cost_estimate=cost(2 * m * n * k, 2 * (m * k + k * n) + 4 * m * n),
        name="base",
    )(x, w)


def shrink_kernel(groups, has_sum, last, code_ref, x_ref, *refs):
    code = code_ref[...]
    refs = list(refs)
    total = None
    for j, sizes in groups:
        parts = [refs.pop(0)[...] for _ in sizes]
        a = parts[0] if len(parts) == 1 else jnp.concatenate(parts, axis=0)
        p = lax.dot_general(x_ref[...], a, (((1,), (1,)), ((), ())), preferred_element_type=F32)
        for k, i in enumerate(HOPS):
            term = jnp.where(code == owner(j, i), p[:, 128 * k : 128 * k + 128], 0.0)
            total = term if total is None else total + term
    if has_sum:
        total = total + refs.pop(0)[...]
    if not last:
        refs[0][...] = total
        return
    keep_ref, give_ref = refs
    half = total.shape[0] // 2
    folded = total + pltpu.roll(total, 64, 1)
    lane = lax.broadcasted_iota(jnp.int32, (half, 128), 1)
    packed = jnp.where(lane < 64, folded[:half], folded[half:])
    low, high = packed[: half // 2], packed[half // 2 :]
    core = lax.axis_index("tp") % 2
    keep_ref[...] = jnp.where(core == 0, low, high)
    give_ref[...] = jnp.where(core == 0, high, low)


def shrink(code, x, groups, total, last, name):
    m, width = x.shape
    args = [code, x] + [a for _, parts in groups for a in parts] + ([] if total is None else [total])
    rows = m // 4 if last else m
    shape = jax.ShapeDtypeStruct((rows, 128), F32)
    return pl.pallas_call(
        functools.partial(
            shrink_kernel, [(j, [a.shape[0] for a in p]) for j, p in groups], total is not None, last
        ),
        in_specs=[VMEM] * len(args),
        out_specs=[VMEM] * 2 if last else VMEM,
        out_shape=[shape] * 2 if last else shape,
        compiler_params=params(16),
        cost_estimate=cost(2 * m * width * 512 * len(groups), 2 * m * width),
        name=name,
    )(*args)


def expand_kernel(code_ref, mine_ref, other_ref, base_ref, *refs):
    b_refs, o_ref = refs[:-1], refs[-1]
    block = o_ref.shape[0]
    step = pl.program_id(0)
    at = pl.multiple_of(step * block, block)
    code = code_ref[pl.ds(at, block), :]
    mine = step % 2 == lax.axis_index("tp") % 2
    packed = jnp.where(mine, mine_ref[...].astype(F32), other_ref[...].astype(F32))
    lane = lax.broadcasted_iota(jnp.int32, packed.shape, 1)
    left = (lane < 64) == (step < 2)
    rows = jnp.where(left, packed, pltpu.roll(packed, 64, 1))
    delta = None
    for j, b_ref in zip(HOPS, b_refs):
        spread = jnp.concatenate(
            [jnp.where(code == owner(j, i), rows, 0.0).astype(BF) for i in HOPS], axis=1
        )
        d = jnp.dot(spread, b_ref[...], preferred_element_type=F32)
        delta = d if delta is None else delta + d
    delta = delta.astype(BF).astype(F32)
    o_ref[...] = (base_ref[pl.ds(at, block), :] + adapter_scale * delta).astype(BF)


def expand(code, mine, other, base, parts):
    m, n = base.shape
    block = m // 4
    args = [code, mine, other, base, *parts]
    return pl.pallas_call(
        expand_kernel,
        grid=(4,),
        in_specs=[VMEM] * len(args),
        out_specs=pl.BlockSpec((block, n), lambda i: (i, 0)),
        out_shape=jax.ShapeDtypeStruct((m, n), BF),
        compiler_params=params(16),
        cost_estimate=cost(2 * m * n * 2048, 6 * m * n),
        name="expand",
    )(*args)


def after(a, *others):
    return lax.optimization_barrier((a, others))[0]


def per_device(activations, token_adapter_index, query_matrix, down, up):
    down = jnp.swapaxes(down, 1, 2).reshape(128, -1)
    up = up.reshape(128, -1)

    near = [first(down, d) for d in (1, -1, 2)]
    own = [second(down, d) for d in (1, -1)]
    up_near = [first(up, d) for d in (1, -1, 2)]
    here, code = prepare(token_adapter_index, activations, down.shape[1])
    near, up_near, here, code = lax.optimization_barrier((near, up_near, here, code))
    rest = jnp.concatenate(near, axis=0)
    d0 = jnp.concatenate([down, *near], axis=0)
    sides = [second(rest, d) for d in (1, -1)]
    far = second(d0, 2)

    base = base_product(activations, query_matrix)
    total = shrink(code, here, [(0, [d0])], None, False, "shrink_own")
    u0 = after(jnp.concatenate([up, *up_near], axis=0), base)
    ups = [u0] + [second(u0, d) for d in (1, -1, 2)]

    sides, total, base = lax.optimization_barrier((sides, total, base))
    total = shrink(
        code, here, [(-1, [own[0], sides[0]]), (1, [own[1], sides[1]])], total, False, "shrink_near"
    )
    far, total = lax.optimization_barrier((far, total))
    keep, give = shrink(code, here, [(2, [far])], total, True, "shrink_far")
    keep = keep + other_core(give)
    keep = keep + pair(keep, 0)
    keep = keep + pair(keep, 1)
    mine, ups = lax.optimization_barrier((keep.astype(BF), ups))
    return expand(code, mine, other_core(mine), base, ups)


def solution(mesh):
    in_specs = (
        P("rep", None),
        P("rep", None),
        P(None, "tp"),
        P("rep", "tp", None),
        P("rep", None, "tp"),
    )
    return jax.shard_map(
        per_device, mesh=mesh, in_specs=in_specs, out_specs=P("rep", "tp"), check_vma=False
    )
```

time: 187 us -> 71.2 us (0.38)
  the two profiles are of different devices: /device:TPU:0 before, /device:TPU:15 now
where the time goes in v3:
time: 71.2 us; the launch traced here: 71.1 us
  Pallas kernels  24.5 us (34%)
  starting transfers between devices  23.4 us (33%)
  waiting for transfers between devices  22.1 us (31%)
  local copies, waits for them, and re-layouts  0.76 us (1%)
    pallas_call x1, Pallas kernels, base_product(): pl.pallas_call(functools.partial(base_kernel, depths, block), in_specs=[H...  13.7 us
    ppermute x8, waiting for transfers between devices, second(): lax.ppermute(a, AXES, every(lambda x, y, z, c: (x + d, y, z, c) if c else...  11.5 us
    ppermute x6, starting transfers between devices, first(): lax.ppermute(a, AXES, every(lambda x, y, z, c: (x, y, z + d, c) if c else...  7.91 us
    ppermute x8, starting transfers between devices, second(): lax.ppermute(a, AXES, every(lambda x, y, z, c: (x + d, y, z, c) if c else...  6.75 us
    ppermute x2, starting transfers between devices, other_core(): return lax.ppermute(a, AXES, every(lambda x, y, z, c: (x, y, z, 1 - c)))  5.87 us
    ppermute x2, waiting for transfers between devices, pair(): return lax.ppermute(a, AXES, every(to))  5.54 us
    pallas_call x3, Pallas kernels, shrink(): pl.pallas_call(functools.partial(shrink_kernel, [(j, [a.shape[0] for a in...  5.07 us
    ppermute x6, waiting for transfers between devices, first(): lax.ppermute(a, AXES, every(lambda x, y, z, c: (x, y, z + d, c) if c else...  4.16 us
  transfers between devices with their start and end apart: 18, of which 8 were waited for; matrix products, arithmetic and copies ran while one was open for 0% of the time, Pallas kernels for 27%

profile of v3, /device:TPU:15, one launch (start us, length us, event | category | flops | bytes accessed | tf_op | source)
XLA Modules:
  0.0 71.1 jit_solution(332758602951674959)
XLA Ops:
  0.0 1.6 %collective-permute-start.3 = (bf16[128,512]{1,0:T(8,128)(2,1)}, bf16[128,512]{1,0:T(8,128)(2,1)S(1)}, u32[]{:S(2)}, u32[]{:S(2)}) collective-permute-start(bf16[128,512]{1,0:T(8,128)(2,1)} %bitcast.12), channel_id=1, source_target_pairs={{0,8},{1,33},{2,10},{3,35},{4,12},{5,37},{6,14},{7,39},{8,16},{9,4... | collective-permute-start | bytes 393224 | tf_op jit(solution)/shard_map/ppermute | solution.py:32
  1.6 1.6 %collective-permute-start = (bf16[128,1024]{1,0:T(8,128)(2,1)}, bf16[128,1024]{1,0:T(8,128)(2,1)S(1)}, u32[]{:S(2)}, u32[]{:S(2)}) collective-permute-start(bf16[128,1024]{1,0:T(8,128)(2,1)} %bitcast.6), channel_id=1, source_target_pairs={{0,8},{1,33},{2,10},{3,35},{4,12},{5,37},{6,14},{7,39},{8,16},{9,4... | collective-permute-start | bytes 786440 | tf_op jit(solution)/shard_map/ppermute | solution.py:32
  3.3 1.0 %collective-permute-start.1 = (bf16[128,1024]{1,0:T(8,128)(2,1)}, bf16[128,1024]{1,0:T(8,128)(2,1)S(1)}, u32[]{:S(2)}, u32[]{:S(2)}) collective-permute-start(bf16[128,1024]{1,0:T(8,128)(2,1)} %bitcast.7), channel_id=1, source_target_pairs={{0,24},{1,97},{2,26},{3,99},{4,28},{5,101},{6,30},{7,103},{8,0},{9... | collective-permute-start | bytes 786440 | tf_op jit(solution)/shard_map/ppermute | solution.py:32
  4.3 2.1 %collective-permute-start.2 = (bf16[128,1024]{1,0:T(8,128)(2,1)}, bf16[128,1024]{1,0:T(8,128)(2,1)S(1)}, u32[]{:S(2)}, u32[]{:S(2)}) collective-permute-start(bf16[128,1024]{1,0:T(8,128)(2,1)} %bitcast.8), channel_id=1, source_target_pairs={{0,16},{1,65},{2,18},{3,67},{4,20},{5,69},{6,22},{7,71},{8,24},{9,... | collective-permute-start | bytes 786440 | tf_op jit(solution)/shard_map/ppermute | solution.py:32
  6.4 0.7 %collective-permute-start.4 = (bf16[128,512]{1,0:T(8,128)(2,1)}, bf16[128,512]{1,0:T(8,128)(2,1)S(1)}, u32[]{:S(2)}, u32[]{:S(2)}) collective-permute-start(bf16[128,512]{1,0:T(8,128)(2,1)} %bitcast.13), channel_id=1, source_target_pairs={{0,24},{1,97},{2,26},{3,99},{4,28},{5,101},{6,30},{7,103},{8,0},{9... | collective-permute-start | bytes 393224 | tf_op jit(solution)/shard_map/ppermute | solution.py:32
  7.1 0.0 collective-permute-done.3
  7.1 0.8 %collective-permute-start.5 = (bf16[128,512]{1,0:T(8,128)(2,1)}, bf16[128,512]{1,0:T(8,128)(2,1)S(1)}, u32[]{:S(2)}, u32[]{:S(2)}) collective-permute-start(bf16[128,512]{1,0:T(8,128)(2,1)} %bitcast.14), channel_id=1, source_target_pairs={{0,16},{1,65},{2,18},{3,67},{4,20},{5,69},{6,22},{7,71},{8,24},{9,... | collective-permute-start | bytes 393224 | tf_op jit(solution)/shard_map/ppermute | solution.py:32
  7.9 0.0 copy-start
  7.9 0.7 copy-done
  8.6 0.0 copy-start.2
  8.6 0.0 copy-start.1
  8.6 1.8 %prepare.1 = (bf16[1024,1024]{1,0:T(8,128)(2,1)S(1)}, s32[1024,128]{1,0:T(8,128)S(1)}) custom-call(s32[8,128]{1,0:T(8,128)S(1)} %bitcast.5, bf16[1024,8192]{1,0:T(8,128)(2,1)} %x_ref.3), custom_call_target="tpu_custom_call" | custom-call | bytes 4194304 | tf_op jit(solution)/shard_map/prepare/pallas_call | solution.py:86
  10.5 2.8 %collective-permute-done.4 = bf16[128,512]{1,0:T(8,128)(2,1)S(1)} collective-permute-done((bf16[128,512]{1,0:T(8,128)(2,1)}, bf16[128,512]{1,0:T(8,128)(2,1)S(1)}, u32[]{:S(2)}, u32[]{:S(2)}) %collective-permute-start.4) | collective-permute-done | bytes 131104 | tf_op jit(solution)/shard_map/ppermute | solution.py:32
  13.3 0.0 copy-done.2
  13.3 0.2 collective-permute-start.7
  13.5 1.4 %collective-permute-done.5 = bf16[128,512]{1,0:T(8,128)(2,1)S(1)} collective-permute-done((bf16[128,512]{1,0:T(8,128)(2,1)}, bf16[128,512]{1,0:T(8,128)(2,1)S(1)}, u32[]{:S(2)}, u32[]{:S(2)}) %collective-permute-start.5) | collective-permute-done | bytes 131104 | tf_op jit(solution)/shard_map/ppermute | solution.py:32
  14.8 0.3 collective-permute-start.10
  15.1 0.0 collective-permute-done
  15.1 0.0 collective-permute-done.1
  15.1 0.0 collective-permute-done.2
  15.1 0.1 pad_maximum_fusion.refs_0_
  15.2 2.5 %collective-permute-start.8 = (bf16[384,1024]{1,0:T(8,128)(2,1)S(1)}, bf16[384,1024]{1,0:T(8,128)(2,1)S(1)}, u32[]{:S(2)}, u32[]{:S(2)}) collective-permute-start(bf16[384,1024]{1,0:T(8,128)(2,1)S(1)} %constant_dynamic-update-slice_fusion), channel_id=1, source_target_pairs={{0,32},{1,9},{2,34},{3,11},{4,36},{5,13},{6,38},{7,15},{8,40},{9,1... | collective-permute-start | bytes 2359304 | tf_op jit(solution)/shard_map/ppermute | solution.py:38
  17.7 0.0 collective-permute-start.9
  17.7 1.3 %collective-permute-start.6 = (bf16[512,1024]{1,0:T(8,128)(2,1)S(1)}, bf16[512,1024]{1,0:T(8,128)(2,1)S(1)}, u32[]{:S(2)}, u32[]{:S(2)}) collective-permute-start(bf16[512,1024]{1,0:T(8,128)(2,1)S(1)} %pad_maximum_fusion.refs_0_), channel_id=1, source_target_pairs={{0,64},{1,17},{2,66},{3,19},{4,68},{5,21},{6,70},{7,23},{8,72},{9,... | collective-permute-start | bytes 3145736 | tf_op jit(solution)/shard_map/ppermute | solution.py:38
  19.0 0.0 copy-done.1
  19.0 13.7 %base.1.base_ref = f32[1024,512]{1,0:T(8,128)S(1)} custom-call(bf16[1024,8192]{1,0:T(8,128)(2,1)} %x_ref.3, bf16[8192,512]{1,0:T(8,128)(2,1)S(1)} %copy-done.1), custom_call_target="tpu_custom_call" | custom-call | flops 8589934592 | bytes 27262976 | tf_op jit(solution)/shard_map/base/pallas_call | solution.py:132
  32.8 1.3 %shrink_own.1.refs_4_ = f32[1024,128]{1,0:T(8,128)S(1)} custom-call(s32[1024,128]{1,0:T(8,128)S(1)} %get-tuple-element.31.code_ref, bf16[1024,1024]{1,0:T(8,128)(2,1)S(1)} %get-tuple-element.32.x_ref, bf16[512,1024]{1,0:T(8,128)(2,1)S(1)} %pad_maximum_fusion.refs_0_), custom_call_target="tpu_custom_call" | custom-call | flops 1073741824 | bytes 2097152 | tf_op jit(solution)/shard_map/shrink_own/pallas_call | solution.py:180
  34.1 3.8 %collective-permute-done.8.refs_1_ = bf16[384,1024]{1,0:T(8,128)(2,1)S(1)} collective-permute-done((bf16[384,1024]{1,0:T(8,128)(2,1)S(1)}, bf16[384,1024]{1,0:T(8,128)(2,1)S(1)}, u32[]{:S(2)}, u32[]{:S(2)}) %collective-permute-start.8) | collective-permute-done | bytes 786464 | tf_op jit(solution)/shard_map/ppermute | solution.py:38
  37.9 3.4 %collective-permute-done.9.refs_3_ = bf16[384,1024]{1,0:T(8,128)(2,1)S(1)} collective-permute-done((bf16[384,1024]{1,0:T(8,128)(2,1)S(1)}, bf16[384,1024]{1,0:T(8,128)(2,1)S(1)}, u32[]{:S(2)}, u32[]{:S(2)}) %collective-permute-start.9) | collective-permute-done | bytes 786464 | tf_op jit(solution)/shard_map/ppermute | solution.py:38
  41.3 0.0 collective-permute-done.7.refs_0_
  41.3 0.0 collective-permute-done.10.refs_2_
  41.3 2.4 %shrink_near.1.refs_1_ = f32[1024,128]{1,0:T(8,128)S(1)} custom-call(s32[1024,128]{1,0:T(8,128)S(1)} %get-tuple-element.31.code_ref, bf16[1024,1024]{1,0:T(8,128)(2,1)S(1)} %get-tuple-element.32.x_ref, bf16[128,1024]{1,0:T(8,128)(2,1)S(1)} %collective-permute-done.7.refs_0_, bf16[384,1024]{1,0:T(8,128)(2,1)S(1)} %collective-permute-done.8.refs_1_, ...), custom_call_target="tpu_custom_call" | custom-call | flops 2147483648 | bytes 2097152 | tf_op jit(solution)/shard_map/shrink_near/pallas_call | solution.py:180
  43.7 0.0 copy-start.3
  43.7 0.0 collective-permute-done.6.refs_0_
  43.7 1.4 %shrink_far.1 = (f32[256,128]{1,0:T(8,128)S(1)}, f32[256,128]{1,0:T(8,128)S(1)}) custom-call(s32[1024,128]{1,0:T(8,128)S(1)} %get-tuple-element.31.code_ref, bf16[1024,1024]{1,0:T(8,128)(2,1)S(1)} %get-tuple-element.32.x_ref, bf16[512,1024]{1,0:T(8,128)(2,1)S(1)} %collective-permute-done.6.refs_0_, f32[1024,128]{1,0:T(8,128)S(1)} %shrink_near.1.refs_1_), custom_call_target="tpu_custom_call" | custom-call | flops 1073741824 | bytes 2097152 | tf_op jit(solution)/shard_map/shrink_far/pallas_call | solution.py:180
  45.1 3.2 %collective-permute-start.11 = (f32[256,128]{1,0:T(8,128)S(1)}, f32[256,128]{1,0:T(8,128)S(1)}, u32[]{:S(2)}, u32[]{:S(2)}) collective-permute-start(f32[256,128]{1,0:T(8,128)S(1)} %get-tuple-element.42), channel_id=1, source_target_pairs={{0,1},{1,0},{2,3},{3,2},{4,5},{5,4},{6,7},{7,6},{8,9},{9,8},{10,11... | collective-permute-start | bytes 393224 | tf_op jit(solution)/shard_map/ppermute | solution.py:44
  48.3 0.0 copy-done.3
  48.3 0.1 collective-permute-start.14
  48.4 1.5 %collective-permute-start.15 = (bf16[512,512]{1,0:T(8,128)(2,1)S(1)}, bf16[512,512]{1,0:T(8,128)(2,1)S(1)}, u32[]{:S(2)}, u32[]{:S(2)}) collective-permute-start(bf16[512,512]{1,0:T(8,128)(2,1)S(1)} %pad_maximum_fusion.1.refs_0_), channel_id=1, source_target_pairs={{0,96},{1,25},{2,98},{3,27},{4,100},{5,29},{6,102},{7,31},{8,104},... | collective-permute-start | bytes 1572872 | tf_op jit(solution)/shard_map/ppermute | solution.py:38
  49.9 1.0 %collective-permute-start.16 = (bf16[512,512]{1,0:T(8,128)(2,1)S(1)}, bf16[512,512]{1,0:T(8,128)(2,1)S(1)}, u32[]{:S(2)}, u32[]{:S(2)}) collective-permute-start(bf16[512,512]{1,0:T(8,128)(2,1)S(1)} %pad_maximum_fusion.1.refs_0_), channel_id=1, source_target_pairs={{0,64},{1,17},{2,66},{3,19},{4,68},{5,21},{6,70},{7,23},{8,72},{9,... | collective-permute-start | bytes 1572872 | tf_op jit(solution)/shard_map/ppermute | solution.py:38
  50.9 0.0 collective-permute-done.11
  50.9 1.4 %collective-permute-start.12 = (f32[256,128]{1,0:T(8,128)S(1)}, f32[256,128]{1,0:T(8,128)S(1)}, u32[]{:S(2)}, u32[]{:S(2)}) collective-permute-start(f32[256,128]{1,0:T(8,128)S(1)} %add.9), channel_id=1, source_target_pairs={{0,2},{1,7},{2,0},{3,5},{4,6},{5,3},{6,4},{7,1},{8,10},{9,15},{10,... | collective-permute-start | bytes 393224 | tf_op jit(solution)/shard_map/ppermute | solution.py:51
  52.3 2.8 %collective-permute-done.12 = f32[256,128]{1,0:T(8,128)S(1)} collective-permute-done((f32[256,128]{1,0:T(8,128)S(1)}, f32[256,128]{1,0:T(8,128)S(1)}, u32[]{:S(2)}, u32[]{:S(2)}) %collective-permute-start.12) | collective-permute-done | bytes 131104 | tf_op jit(solution)/shard_map/ppermute | solution.py:51
  55.1 1.5 %collective-permute-start.13 = (f32[256,128]{1,0:T(8,128)S(1)}, f32[256,128]{1,0:T(8,128)S(1)}, u32[]{:S(2)}, u32[]{:S(2)}) collective-permute-start(f32[256,128]{1,0:T(8,128)S(1)} %add.10), channel_id=1, source_target_pairs={{0,6},{1,3},{2,4},{3,1},{4,2},{5,7},{6,0},{7,5},{8,14},{9,11},{10,... | collective-permute-start | bytes 393224 | tf_op jit(solution)/shard_map/ppermute | solution.py:51
  56.6 2.7 %collective-permute-done.13 = f32[256,128]{1,0:T(8,128)S(1)} collective-permute-done((f32[256,128]{1,0:T(8,128)S(1)}, f32[256,128]{1,0:T(8,128)S(1)}, u32[]{:S(2)}, u32[]{:S(2)}) %collective-permute-start.13) | collective-permute-done | bytes 131104 | tf_op jit(solution)/shard_map/ppermute | solution.py:51
  59.4 0.0 collective-permute-done.14.refs_1_
  59.4 4.2 %collective-permute-done.15.refs_2_ = bf16[512,512]{1,0:T(8,128)(2,1)S(1)} collective-permute-done((bf16[512,512]{1,0:T(8,128)(2,1)S(1)}, bf16[512,512]{1,0:T(8,128)(2,1)S(1)}, u32[]{:S(2)}, u32[]{:S(2)}) %collective-permute-start.15) | collective-permute-done | bytes 524320 | tf_op jit(solution)/shard_map/ppermute | solution.py:38
  63.6 0.0 collective-permute-done.16.refs_3_
  63.6 2.7 %collective-permute-start.17 = (bf16[256,128]{1,0:T(8,128)(2,1)S(1)}, bf16[256,128]{1,0:T(8,128)(2,1)S(1)}, u32[]{:S(2)}, u32[]{:S(2)}) collective-permute-start(bf16[256,128]{1,0:T(8,128)(2,1)S(1)} %add_convert_fusion.mine_ref), channel_id=1, source_target_pairs={{0,1},{1,0},{2,3},{3,2},{4,5},{5,4},{6,7},{7,6},{8,9},{9,8},{10,11... | collective-permute-start | bytes 196616 | tf_op jit(solution)/shard_map/ppermute | solution.py:44
  66.4 0.9 %collective-permute-done.17.other_ref = bf16[256,128]{1,0:T(8,128)(2,1)S(1)} collective-permute-done((bf16[256,128]{1,0:T(8,128)(2,1)S(1)}, bf16[256,128]{1,0:T(8,128)(2,1)S(1)}, u32[]{:S(2)}, u32[]{:S(2)}) %collective-permute-start.17) | collective-permute-done | bytes 65568 | tf_op jit(solution)/shard_map/ppermute | solution.py:44
  67.3 3.8 %expand.1 = bf16[1024,512]{1,0:T(8,128)(2,1)} custom-call(s32[1024,128]{1,0:T(8,128)S(1)} %get-tuple-element.31.code_ref, bf16[256,128]{1,0:T(8,128)(2,1)S(1)} %add_convert_fusion.mine_ref, bf16[256,128]{1,0:T(8,128)(2,1)S(1)} %collective-permute-done.17.other_ref, f32[1024,512]{1,0:T(8,128)S(1)} %base.1.base_ref, ...), custom_call_target="tpu_custom_call" | custom-call | flops 2147483648 | bytes 3145728 | tf_op jit(solution)/shard_map/expand/pallas_call | solution.py:219
  (7 shorter events, 0.1 us)
Async XLA Ops:
  0.0 7.1 %collective-permute-start.3 = (bf16[128,512]{1,0:T(8,128)(2,1)}, bf16[128,512]{1,0:T(8,128)(2,1)S(1)}, u32[]{:S(2)}, u32[]{:S(2)}) collective-permute-start(bf16[128,512]{1,0:T(8,128)(2,1)} %bitcast.12), channel_id=1, source_target_pairs={{0,8},{1,33},{2,10},{3,35},{4,12},{5,37},{6,14},{7,39},{8,16},{9,4... | collective-permute-start | bytes 393224 | tf_op jit(solution)/shard_map/ppermute | solution.py:32
  1.6 13.4 %collective-permute-start = (bf16[128,1024]{1,0:T(8,128)(2,1)}, bf16[128,1024]{1,0:T(8,128)(2,1)S(1)}, u32[]{:S(2)}, u32[]{:S(2)}) collective-permute-start(bf16[128,1024]{1,0:T(8,128)(2,1)} %bitcast.6), channel_id=1, source_target_pairs={{0,8},{1,33},{2,10},{3,35},{4,12},{5,37},{6,14},{7,39},{8,16},{9,4... | collective-permute-start | bytes 786440 | tf_op jit(solution)/shard_map/ppermute | solution.py:32
  3.3 11.8 %collective-permute-start.1 = (bf16[128,1024]{1,0:T(8,128)(2,1)}, bf16[128,1024]{1,0:T(8,128)(2,1)S(1)}, u32[]{:S(2)}, u32[]{:S(2)}) collective-permute-start(bf16[128,1024]{1,0:T(8,128)(2,1)} %bitcast.7), channel_id=1, source_target_pairs={{0,24},{1,97},{2,26},{3,99},{4,28},{5,101},{6,30},{7,103},{8,0},{9... | collective-permute-start | bytes 786440 | tf_op jit(solution)/shard_map/ppermute | solution.py:32
  4.3 10.8 %collective-permute-start.2 = (bf16[128,1024]{1,0:T(8,128)(2,1)}, bf16[128,1024]{1,0:T(8,128)(2,1)S(1)}, u32[]{:S(2)}, u32[]{:S(2)}) collective-permute-start(bf16[128,1024]{1,0:T(8,128)(2,1)} %bitcast.8), channel_id=1, source_target_pairs={{0,16},{1,65},{2,18},{3,67},{4,20},{5,69},{6,22},{7,71},{8,24},{9,... | collective-permute-start | bytes 786440 | tf_op jit(solution)/shard_map/ppermute | solution.py:32
  6.4 6.9 %collective-permute-start.4 = (bf16[128,512]{1,0:T(8,128)(2,1)}, bf16[128,512]{1,0:T(8,128)(2,1)S(1)}, u32[]{:S(2)}, u32[]{:S(2)}) collective-permute-start(bf16[128,512]{1,0:T(8,128)(2,1)} %bitcast.13), channel_id=1, source_target_pairs={{0,24},{1,97},{2,26},{3,99},{4,28},{5,101},{6,30},{7,103},{8,0},{9... | collective-permute-start | bytes 393224 | tf_op jit(solution)/shard_map/ppermute | solution.py:32
  7.1 7.7 %collective-permute-start.5 = (bf16[128,512]{1,0:T(8,128)(2,1)}, bf16[128,512]{1,0:T(8,128)(2,1)S(1)}, u32[]{:S(2)}, u32[]{:S(2)}) collective-permute-start(bf16[128,512]{1,0:T(8,128)(2,1)} %bitcast.14), channel_id=1, source_target_pairs={{0,16},{1,65},{2,18},{3,67},{4,20},{5,69},{6,22},{7,71},{8,24},{9,... | collective-permute-start | bytes 393224 | tf_op jit(solution)/shard_map/ppermute | solution.py:32
  7.9 0.7 copy-start
  8.6 4.7 %copy-start.2 = (bf16[2,1024,64]{1,2,0:T(8,128)(2,1)S(1)}, bf16[2,1024,64]{1,2,0:T(8,128)(2,1)}, u32[]{:S(2)}) copy-start(bf16[2,1024,64]{1,2,0:T(8,128)(2,1)} %param.8) | copy-start | bytes 786436
  8.6 10.4 %copy-start.1 = (bf16[8192,512]{1,0:T(8,128)(2,1)S(1)}, bf16[8192,512]{1,0:T(8,128)(2,1)}, u32[]{:S(2)}) copy-start(bf16[8192,512]{1,0:T(8,128)(2,1)} %w_ref.1) | copy-start | bytes 25165828
  13.3 28.1 %collective-permute-start.7 = (bf16[128,1024]{1,0:T(8,128)(2,1)S(1)}, bf16[128,1024]{1,0:T(8,128)(2,1)S(1)}, u32[]{:S(2)}, u32[]{:S(2)}) collective-permute-start(bf16[128,1024]{1,0:T(8,128)(2,1)S(1)} %bitcast.9), channel_id=1, source_target_pairs={{0,32},{1,9},{2,34},{3,11},{4,36},{5,13},{6,38},{7,15},{8,40},{9,1... | collective-permute-start | bytes 786440 | tf_op jit(solution)/shard_map/ppermute | solution.py:38
  14.8 26.5 %collective-permute-start.10 = (bf16[128,1024]{1,0:T(8,128)(2,1)S(1)}, bf16[128,1024]{1,0:T(8,128)(2,1)S(1)}, u32[]{:S(2)}, u32[]{:S(2)}) collective-permute-start(bf16[128,1024]{1,0:T(8,128)(2,1)S(1)} %bitcast.10), channel_id=1, source_target_pairs={{0,96},{1,25},{2,98},{3,27},{4,100},{5,29},{6,102},{7,31},{8,104},... | collective-permute-start | bytes 786440 | tf_op jit(solution)/shard_map/ppermute | solution.py:38
  15.2 22.7 %collective-permute-start.8 = (bf16[384,1024]{1,0:T(8,128)(2,1)S(1)}, bf16[384,1024]{1,0:T(8,128)(2,1)S(1)}, u32[]{:S(2)}, u32[]{:S(2)}) collective-permute-start(bf16[384,1024]{1,0:T(8,128)(2,1)S(1)} %constant_dynamic-update-slice_fusion), channel_id=1, source_target_pairs={{0,32},{1,9},{2,34},{3,11},{4,36},{5,13},{6,38},{7,15},{8,40},{9,1... | collective-permute-start | bytes 2359304 | tf_op jit(solution)/shard_map/ppermute | solution.py:38
  17.7 23.6 %collective-permute-start.9 = (bf16[384,1024]{1,0:T(8,128)(2,1)S(1)}, bf16[384,1024]{1,0:T(8,128)(2,1)S(1)}, u32[]{:S(2)}, u32[]{:S(2)}) collective-permute-start(bf16[384,1024]{1,0:T(8,128)(2,1)S(1)} %constant_dynamic-update-slice_fusion), channel_id=1, source_target_pairs={{0,96},{1,25},{2,98},{3,27},{4,100},{5,29},{6,102},{7,31},{8,104},... | collective-permute-start | bytes 2359304 | tf_op jit(solution)/shard_map/ppermute | solution.py:38
  17.7 26.0 %collective-permute-start.6 = (bf16[512,1024]{1,0:T(8,128)(2,1)S(1)}, bf16[512,1024]{1,0:T(8,128)(2,1)S(1)}, u32[]{:S(2)}, u32[]{:S(2)}) collective-permute-start(bf16[512,1024]{1,0:T(8,128)(2,1)S(1)} %pad_maximum_fusion.refs_0_), channel_id=1, source_target_pairs={{0,64},{1,17},{2,66},{3,19},{4,68},{5,21},{6,70},{7,23},{8,72},{9,... | collective-permute-start | bytes 3145736 | tf_op jit(solution)/shard_map/ppermute | solution.py:38
  43.7 4.6 %copy-start.3 = (bf16[2,64,512]{2,1,0:T(8,128)(2,1)S(1)}, bf16[2,64,512]{2,1,0:T(8,128)(2,1)}, u32[]{:S(2)}) copy-start(bf16[2,64,512]{2,1,0:T(8,128)(2,1)} %param.9) | copy-start | bytes 393220
  45.1 5.8 %collective-permute-start.11 = (f32[256,128]{1,0:T(8,128)S(1)}, f32[256,128]{1,0:T(8,128)S(1)}, u32[]{:S(2)}, u32[]{:S(2)}) collective-permute-start(f32[256,128]{1,0:T(8,128)S(1)} %get-tuple-element.42), channel_id=1, source_target_pairs={{0,1},{1,0},{2,3},{3,2},{4,5},{5,4},{6,7},{7,6},{8,9},{9,8},{10,11... | collective-permute-start | bytes 393224 | tf_op jit(solution)/shard_map/ppermute | solution.py:44
  48.3 11.1 %collective-permute-start.14 = (bf16[512,512]{1,0:T(8,128)(2,1)S(1)}, bf16[512,512]{1,0:T(8,128)(2,1)S(1)}, u32[]{:S(2)}, u32[]{:S(2)}) collective-permute-start(bf16[512,512]{1,0:T(8,128)(2,1)S(1)} %pad_maximum_fusion.1.refs_0_), channel_id=1, source_target_pairs={{0,32},{1,9},{2,34},{3,11},{4,36},{5,13},{6,38},{7,15},{8,40},{9,1... | collective-permute-start | bytes 1572872 | tf_op jit(solution)/shard_map/ppermute | solution.py:38
  48.4 15.2 %collective-permute-start.15 = (bf16[512,512]{1,0:T(8,128)(2,1)S(1)}, bf16[512,512]{1,0:T(8,128)(2,1)S(1)}, u32[]{:S(2)}, u32[]{:S(2)}) collective-permute-start(bf16[512,512]{1,0:T(8,128)(2,1)S(1)} %pad_maximum_fusion.1.refs_0_), channel_id=1, source_target_pairs={{0,96},{1,25},{2,98},{3,27},{4,100},{5,29},{6,102},{7,31},{8,104},... | collective-permute-start | bytes 1572872 | tf_op jit(solution)/shard_map/ppermute | solution.py:38
  49.9 13.8 %collective-permute-start.16 = (bf16[512,512]{1,0:T(8,128)(2,1)S(1)}, bf16[512,512]{1,0:T(8,128)(2,1)S(1)}, u32[]{:S(2)}, u32[]{:S(2)}) collective-permute-start(bf16[512,512]{1,0:T(8,128)(2,1)S(1)} %pad_maximum_fusion.1.refs_0_), channel_id=1, source_target_pairs={{0,64},{1,17},{2,66},{3,19},{4,68},{5,21},{6,70},{7,23},{8,72},{9,... | collective-permute-start | bytes 1572872 | tf_op jit(solution)/shard_map/ppermute | solution.py:38
  50.9 4.2 %collective-permute-start.12 = (f32[256,128]{1,0:T(8,128)S(1)}, f32[256,128]{1,0:T(8,128)S(1)}, u32[]{:S(2)}, u32[]{:S(2)}) collective-permute-start(f32[256,128]{1,0:T(8,128)S(1)} %add.9), channel_id=1, source_target_pairs={{0,2},{1,7},{2,0},{3,5},{4,6},{5,3},{6,4},{7,1},{8,10},{9,15},{10,... | collective-permute-start | bytes 393224 | tf_op jit(solution)/shard_map/ppermute | solution.py:51
  55.1 4.3 %collective-permute-start.13 = (f32[256,128]{1,0:T(8,128)S(1)}, f32[256,128]{1,0:T(8,128)S(1)}, u32[]{:S(2)}, u32[]{:S(2)}) collective-permute-start(f32[256,128]{1,0:T(8,128)S(1)} %add.10), channel_id=1, source_target_pairs={{0,6},{1,3},{2,4},{3,1},{4,2},{5,7},{6,0},{7,5},{8,14},{9,11},{10,... | collective-permute-start | bytes 393224 | tf_op jit(solution)/shard_map/ppermute | solution.py:51
  63.6 3.6 %collective-permute-start.17 = (bf16[256,128]{1,0:T(8,128)(2,1)S(1)}, bf16[256,128]{1,0:T(8,128)(2,1)S(1)}, u32[]{:S(2)}, u32[]{:S(2)}) collective-permute-start(bf16[256,128]{1,0:T(8,128)(2,1)S(1)} %add_convert_fusion.mine_ref), channel_id=1, source_target_pairs={{0,1},{1,0},{2,3},{3,2},{4,5},{5,4},{6,7},{7,6},{8,9},{9,8},{10,11... | collective-permute-start | bytes 196616 | tf_op jit(solution)/shard_map/ppermute | solution.py:44

commit v4 on v3

v4 whole, which is shorter than its diff:
```python
import functools

import jax
import jax.numpy as jnp
from jax import lax
from jax.experimental import pallas as pl
from jax.experimental.pallas import tpu as pltpu
from jax.sharding import PartitionSpec as P

BF, F32 = jnp.bfloat16, jnp.float32
AXES = ("rep", "tp")
RING = 4
HOPS = (0, -1, 1, 2)
adapter_scale = 0.5


def device_of(x, y, z, c):
    return (z % RING * RING + x % RING) * 2 * RING + y % RING * 2 + c


def every(f):
    return [
        (device_of(x, y, z, c), device_of(*f(x, y, z, c)))
        for z in range(RING)
        for x in range(RING)
        for y in range(RING)
        for c in range(2)
    ]


def first(a, d):
    return lax.ppermute(
        a, AXES, every(lambda x, y, z, c: (x, y, z + d, c) if c else (x + d, y, z, c))
    )


def second(a, d):
    return lax.ppermute(
        a, AXES, every(lambda x, y, z, c: (x + d, y, z, c) if c else (x, y, z + d, c))
    )


def other_core(a):
    return lax.ppermute(a, AXES, every(lambda x, y, z, c: (x, y, z, 1 - c)))


def pair(a, step):
    def to(x, y, z, c):
        return (x, (y ^ 1) if (c + step) % 2 == 0 else (3 - y), z, c)

    return lax.ppermute(a, AXES, every(to))


def params(mib):
    return pltpu.CompilerParams(vmem_limit_bytes=mib << 20)


def cost(flops, moved):
    return pl.CostEstimate(flops=flops, bytes_accessed=moved, transcendentals=0)


VMEM = pl.BlockSpec(memory_space=pltpu.VMEM)
HBM = pl.BlockSpec(memory_space=pltpu.HBM)


def owner(j, i):
    rep, core = lax.axis_index("rep"), lax.axis_index("tp") % 2
    dz, dx = jnp.where(core == 0, j, i), jnp.where(core == 0, i, j)
    return (rep // RING + dz + RING) % RING * RING + (rep % RING + dx + RING) % RING


def prep_kernel(ident_ref, x_ref, here_ref, code_ref, sem):
    width = here_ref.shape[1]
    at = pl.multiple_of(lax.axis_index("tp") * width, width)
    copy = pltpu.make_async_copy(x_ref.at[:, pl.ds(at, width)], here_ref, sem)
    copy.start()
    side = lax.broadcasted_iota(jnp.int32, (128, 128), 1) // 64
    for r in range(ident_ref.shape[0]):
        ident = jnp.broadcast_to(ident_ref[r : r + 1, :], (128, 128)).T
        code_ref[128 * r : 128 * r + 128, :] = jnp.where((ident & 1) == side, ident >> 1, -1)
    copy.wait()


def prepare(ident, x, width):
    m = x.shape[0]
    return pl.pallas_call(
        prep_kernel,
        in_specs=[VMEM, HBM],
        out_specs=[VMEM, VMEM],
        out_shape=[
            jax.ShapeDtypeStruct((m, width), BF),
            jax.ShapeDtypeStruct((m, 128), jnp.int32),
        ],
        scratch_shapes=[pltpu.SemaphoreType.DMA],
        compiler_params=params(50),
        cost_estimate=cost(0, 1 << 20),
        name="prepare",
    )(ident.reshape(m // 128, 128), x)


def base_kernel(at, x_ref, w_ref, o_ref, xb, sems):
    count = sems.shape[0]
    block = xb.shape[0] // count
    copies = []
    for i in range(count):
        rows = pl.ds(i * block, block)
        copies.append(
            pltpu.make_async_copy(x_ref.at[pl.ds(at + i * block, block)], xb.at[rows], sems.at[i])
        )
    for copy in copies:
        copy.start()
    for i, copy in enumerate(copies):
        copy.wait()
        rows = pl.ds(i * block, block)
        o_ref[rows, :] = jnp.dot(xb[rows, :], w_ref[...], preferred_element_type=F32)


def base_rows(x, w, at, rows, block=128):
    k, n = w.shape
    return pl.pallas_call(
        functools.partial(base_kernel, at),
        in_specs=[HBM, VMEM],
        out_specs=VMEM,
        out_shape=jax.ShapeDtypeStruct((rows, n), F32),
        scratch_shapes=[pltpu.VMEM((rows, k), BF), pltpu.SemaphoreType.DMA((rows // block,))],
        compiler_params=params(36),
        cost_estimate=cost(1 << 20, 1 << 20),
        name="base",
    )(x, w)


def shrink_kernel(groups, has_sum, last, code_ref, x_ref, *refs):
    code = code_ref[...]
    refs = list(refs)
    total = None
    for count, places in groups:
        parts = [refs.pop(0)[...] for _ in range(count)]
        a = parts[0] if count == 1 else jnp.concatenate(parts, axis=0)
        p = lax.dot_general(x_ref[...], a, (((1,), (1,)), ((), ())), preferred_element_type=F32)
        for k, (j, i) in enumerate(places):
            term = jnp.where(code == owner(j, i), p[:, 128 * k : 128 * k + 128], 0.0)
            total = term if total is None else total + term
    if has_sum:
        total = total + refs.pop(0)[...]
    if not last:
        refs[0][...] = total
        return
    keep_ref, give_ref = refs
    half = total.shape[0] // 2
    folded = total + pltpu.roll(total, 64, 1)
    lane = lax.broadcasted_iota(jnp.int32, (half, 128), 1)
    packed = jnp.where(lane < 64, folded[:half], folded[half:])
    low, high = packed[: half // 2], packed[half // 2 :]
    core = lax.axis_index("tp") % 2
    keep_ref[...] = jnp.where(core == 0, low, high)
    give_ref[...] = jnp.where(core == 0, high, low)


def shrink(code, x, groups, total, last, name):
    m = x.shape[0]
    args = [code, x] + [a for parts, _ in groups for a in parts] + ([] if total is None else [total])
    rows = m // 4 if last else m
    shape = jax.ShapeDtypeStruct((rows, 128), F32)
    return pl.pallas_call(
        functools.partial(
            shrink_kernel, [(len(parts), places) for parts, places in groups], total is not None, last
        ),
        in_specs=[VMEM] * len(args),
        out_specs=[VMEM] * 2 if last else VMEM,
        out_shape=[shape] * 2 if last else shape,
        compiler_params=params(16),
        cost_estimate=cost(1 << 20, 1 << 20),
        name=name,
    )(*args)


def expand_kernel(pieces, code_ref, mine_ref, other_ref, *refs):
    base_refs, b_refs, o_ref = refs[: len(pieces)], refs[len(pieces) : -1], refs[-1]
    block = o_ref.shape[0]
    step = pl.program_id(0)
    code = code_ref[pl.ds(pl.multiple_of(step * block, block), block), :]
    mine = step % 2 == lax.axis_index("tp") % 2
    packed = jnp.where(mine, mine_ref[...].astype(F32), other_ref[...].astype(F32))
    lane = lax.broadcasted_iota(jnp.int32, packed.shape, 1)
    left = (lane < 64) == (step < 2)
    rows = jnp.where(left, packed, pltpu.roll(packed, 64, 1))
    delta = None
    for j, b_ref in zip(HOPS, b_refs):
        spread = jnp.concatenate(
            [jnp.where(code == owner(j, i), rows, 0.0).astype(BF) for i in HOPS], axis=1
        )
        d = jnp.dot(spread, b_ref[...], preferred_element_type=F32)
        delta = d if delta is None else delta + d
    delta = delta.astype(BF).astype(F32)
    at = 0
    for size, base_ref in zip(pieces, base_refs):

        @pl.when((step * block >= at) & (step * block < at + size))
        def _(at=at, base_ref=base_ref):
            row = pl.ds(pl.multiple_of(step * block - at, block), block)
            o_ref[...] = (base_ref[row, :] + adapter_scale * delta).astype(BF)

        at += size


def expand(code, mine, other, bases, parts):
    n = bases[0].shape[1]
    pieces = [a.shape[0] for a in bases]
    m = sum(pieces)
    block = m // 4
    args = [code, mine, other, *bases, *parts]
    return pl.pallas_call(
        functools.partial(expand_kernel, pieces),
        grid=(4,),
        in_specs=[VMEM] * len(args),
        out_specs=pl.BlockSpec((block, n), lambda i: (i, 0)),
        out_shape=jax.ShapeDtypeStruct((m, n), BF),
        compiler_params=params(12),
        cost_estimate=cost(2 * m * n * 2048, 6 * m * n),
        name="expand",
    )(*args)


def tie(*arrays):
    return lax.optimization_barrier(arrays)


def per_device(activations, token_adapter_index, query_matrix, down, up):
    down = jnp.swapaxes(down, 1, 2).reshape(128, -1)
    up = up.reshape(128, -1)
    m, width = activations.shape[0], down.shape[1]

    both = jnp.concatenate([down, up], axis=1)
    before, after, far = [first(both, d) for d in (1, -1, 2)]
    here, code = prepare(token_adapter_index, activations, width)
    before, after, here, code = tie(before, after, here, code)
    close = jnp.concatenate([down, before[:, :width], after[:, :width]], axis=0)
    a_before, a_after = second(close, 1), second(close, -1)
    d_far = far[:, :width]
    b_before, b_after = second(d_far, 1), second(d_far, -1)
    d_own = jnp.concatenate([close, d_far], axis=0)
    d_opposite = second(d_own, 2)
    u_own = jnp.concatenate([up, before[:, width:], after[:, width:], far[:, width:]], axis=0)

    base = [base_rows(activations, query_matrix, 0, m // 2)]
    total = shrink(code, here, [([d_own], [(0, i) for i in HOPS])], None, False, "shrink_own")
    a_before, a_after, total, base[0] = tie(a_before, a_after, total, base[0])
    groups = [([a], [(j, 0), (j, -1), (j, 1)]) for a, j in ((a_before, -1), (a_after, 1))]
    total = shrink(code, here, groups, total, False, "shrink_near")
    u_own = tie(u_own, base[0])[0]
    ups = [u_own] + [second(u_own, d) for d in (1, -1, 2)]
    b_before, b_after, d_opposite, total = tie(b_before, b_after, d_opposite, total)
    groups = [([b_before, b_after], [(-1, 2), (1, 2)]), ([d_opposite], [(2, i) for i in HOPS])]
    keep, give = shrink(code, here, groups, total, True, "shrink_far")
    keep = keep + other_core(give)
    for step in range(2):
        at = m // 2 + step * (m // 4)
        there, piece = tie(pair(keep, step), base_rows(activations, query_matrix, at, m // 4))
        keep = keep + there
        base.append(piece)
    mine, *ups = tie(keep.astype(BF), *ups)
    return expand(code, mine, other_core(mine), base, ups)


def solution(mesh):
    in_specs = (
        P("rep", None),
        P("rep", None),
        P(None, "tp"),
        P("rep", "tp", None),
        P("rep", None, "tp"),
    )
    return jax.shard_map(
        per_device, mesh=mesh, in_specs=in_specs, out_specs=P("rep", "tp"), check_vma=False
    )
```

time: 71.2 us -> 70.4 us (0.989)
  the two profiles are of different devices: /device:TPU:15 before, /device:TPU:0 now
where the time goes in v4:
time: 70.4 us; the launch traced here: 69.2 us
  Pallas kernels  27.6 us (39%)
  starting transfers between devices  24.2 us (34%)
  waiting for transfers between devices  15 us (21%)
  other arithmetic  1.26 us (2%)
  local copies, waits for them, and re-layouts  0.94 us (1%)
    pallas_call x3, Pallas kernels, base_rows(): pl.pallas_call(functools.partial(base_kernel, at), in_specs=[HBM, VMEM],...  15.9 us
    ppermute x8, starting transfers between devices, second(): lax.ppermute(a, AXES, every(lambda x, y, z, c: (x + d, y, z, c) if c else...  14.9 us
    ppermute x8, waiting for transfers between devices, second(): lax.ppermute(a, AXES, every(lambda x, y, z, c: (x + d, y, z, c) if c else...  7.58 us
    ppermute x3, waiting for transfers between devices, first(): lax.ppermute(a, AXES, every(lambda x, y, z, c: (x, y, z + d, c) if c else...  6.14 us
    pallas_call x3, Pallas kernels, shrink(): pl.pallas_call(functools.partial(shrink_kernel, [(len(parts), places) for...  5.56 us
    ppermute x3, starting transfers between devices, first(): lax.ppermute(a, AXES, every(lambda x, y, z, c: (x, y, z + d, c) if c else...  5.2 us
    pallas_call x1, Pallas kernels, expand(): pl.pallas_call(functools.partial(expand_kernel, pieces), grid=(4,), in_sp...  4.03 us
    ppermute x2, starting transfers between devices, pair(): return lax.ppermute(a, AXES, every(to))  3.92 us
  transfers between devices with their start and end apart: 15, of which 7 were waited for; matrix products, arithmetic and copies ran while one was open for 0% of the time, Pallas kernels for 31%

profile of v4, /device:TPU:0, one launch (start us, length us, event | category | flops | bytes accessed | tf_op | source)
XLA Modules:
  0.0 69.2 jit_solution(6163909559496886701)
XLA Ops:
  0.0 1.0 %pad_maximum_fusion.3 = bf16[128,1536]{1,0:T(8,128)(2,1)S(1)} fusion(bf16[128,512]{1,0:T(8,128)(2,1)} %bitcast.11, bf16[128,1024]{1,0:T(8,128)(2,1)} %bitcast.8), kind=kLoop, calls=%fused_computation.3 | loop fusion | flops 786432 | bytes 786432 | tf_op jit(solution)/shard_map/concatenate | solution.py:233
  1.1 1.6 %collective-permute-start = (bf16[128,1536]{1,0:T(8,128)(2,1)S(1)}, bf16[128,1536]{1,0:T(8,128)(2,1)S(1)}, u32[]{:S(2)}, u32[]{:S(2)}) collective-permute-start(bf16[128,1536]{1,0:T(8,128)(2,1)S(1)} %pad_maximum_fusion.3), channel_id=1, source_target_pairs={{0,8},{1,33},{2,10},{3,35},{4,12},{5,37},{6,14},{7,39},{8,16},{9,4... | collective-permute-start | bytes 1179656 | tf_op jit(solution)/shard_map/ppermute | solution.py:32
  2.7 1.7 %collective-permute-start.1 = (bf16[128,1536]{1,0:T(8,128)(2,1)S(1)}, bf16[128,1536]{1,0:T(8,128)(2,1)S(1)}, u32[]{:S(2)}, u32[]{:S(2)}) collective-permute-start(bf16[128,1536]{1,0:T(8,128)(2,1)S(1)} %pad_maximum_fusion.3), channel_id=1, source_target_pairs={{0,24},{1,97},{2,26},{3,99},{4,28},{5,101},{6,30},{7,103},{8,0},{9... | collective-permute-start | bytes 1179656 | tf_op jit(solution)/shard_map/ppermute | solution.py:32
  4.4 1.9 %collective-permute-start.2 = (bf16[128,1536]{1,0:T(8,128)(2,1)S(1)}, bf16[128,1536]{1,0:T(8,128)(2,1)S(1)}, u32[]{:S(2)}, u32[]{:S(2)}) collective-permute-start(bf16[128,1536]{1,0:T(8,128)(2,1)S(1)} %pad_maximum_fusion.3), channel_id=1, source_target_pairs={{0,16},{1,65},{2,18},{3,67},{4,20},{5,69},{6,22},{7,71},{8,24},{9,... | collective-permute-start | bytes 1179656 | tf_op jit(solution)/shard_map/ppermute | solution.py:32
  6.3 0.0 slice-start
  6.3 0.0 copy-start
  6.3 0.8 %copy-done = s32[1024,1]{0,1:T(1,128)S(1)} copy-done((s32[1024,1]{0,1:T(1,128)S(1)}, s32[1024,1]{0,1:T(1,128)}, u32[]{:S(2)}) %copy-start) | copy-done | bytes 4120
  7.1 0.0 copy-start.1
  7.1 0.0 slice-start.1
  7.1 2.1 %prepare.1 = (bf16[1024,1024]{1,0:T(8,128)(2,1)S(1)}, s32[1024,128]{1,0:T(8,128)S(1)}) custom-call(s32[8,128]{1,0:T(8,128)S(1)} %bitcast.7, bf16[1024,8192]{1,0:T(8,128)(2,1)} %x_ref.7), custom_call_target="tpu_custom_call" | custom-call | bytes 1048576 | tf_op jit(solution)/shard_map/prepare/pallas_call | solution.py:86
  9.2 0.9 %collective-permute-done = bf16[128,1536]{1,0:T(8,128)(2,1)S(1)} collective-permute-done((bf16[128,1536]{1,0:T(8,128)(2,1)S(1)}, bf16[128,1536]{1,0:T(8,128)(2,1)S(1)}, u32[]{:S(2)}, u32[]{:S(2)}) %collective-permute-start) | collective-permute-done | bytes 393248 | tf_op jit(solution)/shard_map/ppermute | solution.py:32
  10.1 0.0 copy-start.3
  10.1 0.4 collective-permute-done.1
  10.5 0.0 copy-start.2
  10.5 4.9 %collective-permute-done.2 = bf16[128,1536]{1,0:T(8,128)(2,1)S(1)} collective-permute-done((bf16[128,1536]{1,0:T(8,128)(2,1)S(1)}, bf16[128,1536]{1,0:T(8,128)(2,1)S(1)}, u32[]{:S(2)}, u32[]{:S(2)}) %collective-permute-start.2) | collective-permute-done | bytes 393248 | tf_op jit(solution)/shard_map/ppermute | solution.py:32
  15.4 0.0 copy-start.4
  15.4 0.0 copy-done.1
  15.4 0.1 pad_maximum_fusion.refs_0_
  15.5 4.0 %collective-permute-start.5 = (bf16[512,1024]{1,0:T(8,128)(2,1)S(1)}, bf16[512,1024]{1,0:T(8,128)(2,1)S(1)}, u32[]{:S(2)}, u32[]{:S(2)}) collective-permute-start(bf16[512,1024]{1,0:T(8,128)(2,1)S(1)} %pad_maximum_fusion.refs_0_), channel_id=1, source_target_pairs={{0,64},{1,17},{2,66},{3,19},{4,68},{5,21},{6,70},{7,23},{8,72},{9,... | collective-permute-start | bytes 3145736 | tf_op jit(solution)/shard_map/ppermute | solution.py:38
  19.5 0.1 pad_maximum_fusion.1
  19.5 1.1 %collective-permute-start.6 = (bf16[384,1024]{1,0:T(8,128)(2,1)S(1)}, bf16[384,1024]{1,0:T(8,128)(2,1)S(1)}, u32[]{:S(2)}, u32[]{:S(2)}) collective-permute-start(bf16[384,1024]{1,0:T(8,128)(2,1)S(1)} %pad_maximum_fusion.1), channel_id=1, source_target_pairs={{0,32},{1,9},{2,34},{3,11},{4,36},{5,13},{6,38},{7,15},{8,40},{9,1... | collective-permute-start | bytes 2359304 | tf_op jit(solution)/shard_map/ppermute | solution.py:38
  20.6 2.2 %collective-permute-start.7 = (bf16[384,1024]{1,0:T(8,128)(2,1)S(1)}, bf16[384,1024]{1,0:T(8,128)(2,1)S(1)}, u32[]{:S(2)}, u32[]{:S(2)}) collective-permute-start(bf16[384,1024]{1,0:T(8,128)(2,1)S(1)} %pad_maximum_fusion.1), channel_id=1, source_target_pairs={{0,96},{1,25},{2,98},{3,27},{4,100},{5,29},{6,102},{7,31},{8,104},... | collective-permute-start | bytes 2359304 | tf_op jit(solution)/shard_map/ppermute | solution.py:38
  22.8 0.0 collective-permute-start.3
  22.8 3.2 %collective-permute-start.4 = (bf16[128,1024]{1,0:T(8,128)(2,1)S(1)}, bf16[128,1024]{1,0:T(8,128)(2,1)S(1)}, u32[]{:S(2)}, u32[]{:S(2)}) collective-permute-start(bf16[128,1024]{1,0:T(8,128)(2,1)S(1)} %slice.24), channel_id=1, source_target_pairs={{0,96},{1,25},{2,98},{3,27},{4,100},{5,29},{6,102},{7,31},{8,104},... | collective-permute-start | bytes 786440 | tf_op jit(solution)/shard_map/ppermute | solution.py:38
  26.1 0.0 slice-done
  26.1 0.0 slice-done.1
  26.1 7.1 %base.3.refs_0_ = f32[512,512]{1,0:T(8,128)S(1)} custom-call(bf16[1024,8192]{1,0:T(8,128)(2,1)} %x_ref.7, bf16[8192,512]{1,0:T(8,128)(2,1)S(1)} %bitcast.6), custom_call_target="tpu_custom_call" | custom-call | flops 1048576 | bytes 1048576 | tf_op jit(solution)/shard_map/base/pallas_call | solution.py:120
  33.2 0.0 copy-done.2
  33.2 0.0 copy-done.3
  33.2 0.0 copy-done.4
  33.2 1.3 %shrink_own.1.refs_2_ = f32[1024,128]{1,0:T(8,128)S(1)} custom-call(s32[1024,128]{1,0:T(8,128)S(1)} %get-tuple-element.33.code_ref, bf16[1024,1024]{1,0:T(8,128)(2,1)S(1)} %get-tuple-element.34.x_ref, bf16[512,1024]{1,0:T(8,128)(2,1)S(1)} %pad_maximum_fusion.refs_0_), custom_call_target="tpu_custom_call" | custom-call | flops 1048576 | bytes 1048576 | tf_op jit(solution)/shard_map/shrink_own/pallas_call | solution.py:164
  34.5 6.1 %collective-permute-done.6.refs_0_ = bf16[384,1024]{1,0:T(8,128)(2,1)S(1)} collective-permute-done((bf16[384,1024]{1,0:T(8,128)(2,1)S(1)}, bf16[384,1024]{1,0:T(8,128)(2,1)S(1)}, u32[]{:S(2)}, u32[]{:S(2)}) %collective-permute-start.6) | collective-permute-done | bytes 786464 | tf_op jit(solution)/shard_map/ppermute | solution.py:38
  40.7 1.1 %collective-permute-done.7.refs_1_ = bf16[384,1024]{1,0:T(8,128)(2,1)S(1)} collective-permute-done((bf16[384,1024]{1,0:T(8,128)(2,1)S(1)}, bf16[384,1024]{1,0:T(8,128)(2,1)S(1)}, u32[]{:S(2)}, u32[]{:S(2)}) %collective-permute-start.7) | collective-permute-done | bytes 786464 | tf_op jit(solution)/shard_map/ppermute | solution.py:38
  41.7 2.4 %shrink_near.1.refs_3_ = f32[1024,128]{1,0:T(8,128)S(1)} custom-call(s32[1024,128]{1,0:T(8,128)S(1)} %get-tuple-element.33.code_ref, bf16[1024,1024]{1,0:T(8,128)(2,1)S(1)} %get-tuple-element.34.x_ref, bf16[384,1024]{1,0:T(8,128)(2,1)S(1)} %collective-permute-done.6.refs_0_, bf16[384,1024]{1,0:T(8,128)(2,1)S(1)} %collective-permute-done.7.refs_1_, ...), custom_call_target="tpu_custom_call" | custom-call | flops 1048576 | bytes 1048576 | tf_op jit(solution)/shard_map/shrink_near/pallas_call | solution.py:164
  44.1 0.0 slice-start.2
  44.1 0.0 slice-start.3
  44.1 0.0 slice-start.4
  44.1 0.0 copy-start.5
  44.1 0.0 collective-permute-done.3.refs_0_
  44.1 0.4 collective-permute-done.4.refs_1_
  44.5 0.0 collective-permute-done.5.refs_2_
  44.5 1.9 %shrink_far.1 = (f32[256,128]{1,0:T(8,128)S(1)}, f32[256,128]{1,0:T(8,128)S(1)}) custom-call(s32[1024,128]{1,0:T(8,128)S(1)} %get-tuple-element.33.code_ref, bf16[1024,1024]{1,0:T(8,128)(2,1)S(1)} %get-tuple-element.34.x_ref, bf16[128,1024]{1,0:T(8,128)(2,1)S(1)} %collective-permute-done.3.refs_0_, bf16[128,1024]{1,0:T(8,128)(2,1)S(1)} %collective-permute-done.4.refs_1_, ...), custom_call_target="tpu_custom_call" | custom-call | flops 1048576 | bytes 1048576 | tf_op jit(solution)/shard_map/shrink_far/pallas_call | solution.py:164
  46.5 0.1 collective-permute-start.8
  46.5 0.0 slice-done.2
  46.6 0.0 slice-done.3
  46.6 0.0 slice-done.4
  46.6 0.0 copy-done.5
  46.6 1.3 %collective-permute-start.11 = (bf16[512,512]{1,0:T(8,128)(2,1)S(1)}, bf16[512,512]{1,0:T(8,128)(2,1)S(1)}, u32[]{:S(2)}, u32[]{:S(2)}) collective-permute-start(bf16[512,512]{1,0:T(8,128)(2,1)S(1)} %pad_maximum_fusion.2.refs_3_), channel_id=1, source_target_pairs={{0,32},{1,9},{2,34},{3,11},{4,36},{5,13},{6,38},{7,15},{8,40},{9,1... | collective-permute-start | bytes 1572872 | tf_op jit(solution)/shard_map/ppermute | solution.py:38
  47.9 2.2 %collective-permute-start.12 = (bf16[512,512]{1,0:T(8,128)(2,1)S(1)}, bf16[512,512]{1,0:T(8,128)(2,1)S(1)}, u32[]{:S(2)}, u32[]{:S(2)}) collective-permute-start(bf16[512,512]{1,0:T(8,128)(2,1)S(1)} %pad_maximum_fusion.2.refs_3_), channel_id=1, source_target_pairs={{0,96},{1,25},{2,98},{3,27},{4,100},{5,29},{6,102},{7,31},{8,104},... | collective-permute-start | bytes 1572872 | tf_op jit(solution)/shard_map/ppermute | solution.py:38
  50.1 0.9 %collective-permute-start.13 = (bf16[512,512]{1,0:T(8,128)(2,1)S(1)}, bf16[512,512]{1,0:T(8,128)(2,1)S(1)}, u32[]{:S(2)}, u32[]{:S(2)}) collective-permute-start(bf16[512,512]{1,0:T(8,128)(2,1)S(1)} %pad_maximum_fusion.2.refs_3_), channel_id=1, source_target_pairs={{0,64},{1,17},{2,66},{3,19},{4,68},{5,21},{6,70},{7,23},{8,72},{9,... | collective-permute-start | bytes 1572872 | tf_op jit(solution)/shard_map/ppermute | solution.py:38
  51.1 0.0 collective-permute-done.8
  51.1 1.7 %collective-permute-start.9 = (f32[256,128]{1,0:T(8,128)S(1)}, f32[256,128]{1,0:T(8,128)S(1)}, u32[]{:S(2)}, u32[]{:S(2)}) collective-permute-start(f32[256,128]{1,0:T(8,128)S(1)} %add.9), channel_id=1, source_target_pairs={{0,2},{1,7},{2,0},{3,5},{4,6},{5,3},{6,4},{7,1},{8,10},{9,15},{10,... | collective-permute-start | bytes 393224 | tf_op jit(solution)/shard_map/ppermute | solution.py:51
  52.7 4.4 %base.4.refs_1_ = f32[256,512]{1,0:T(8,128)S(1)} custom-call(bf16[1024,8192]{1,0:T(8,128)(2,1)} %x_ref.7, bf16[8192,512]{1,0:T(8,128)(2,1)S(1)} %bitcast.6), custom_call_target="tpu_custom_call" | custom-call | flops 1048576 | bytes 1048576 | tf_op jit(solution)/shard_map/base/pallas_call | solution.py:120
  57.1 0.0 collective-permute-done.9
  57.1 2.3 %collective-permute-start.10 = (f32[256,128]{1,0:T(8,128)S(1)}, f32[256,128]{1,0:T(8,128)S(1)}, u32[]{:S(2)}, u32[]{:S(2)}) collective-permute-start(f32[256,128]{1,0:T(8,128)S(1)} %add.10), channel_id=1, source_target_pairs={{0,6},{1,3},{2,4},{3,1},{4,2},{5,7},{6,0},{7,5},{8,14},{9,11},{10,... | collective-permute-start | bytes 393224 | tf_op jit(solution)/shard_map/ppermute | solution.py:51
  59.4 4.4 %base.5.refs_2_ = f32[256,512]{1,0:T(8,128)S(1)} custom-call(bf16[1024,8192]{1,0:T(8,128)(2,1)} %x_ref.7, bf16[8192,512]{1,0:T(8,128)(2,1)S(1)} %bitcast.6), custom_call_target="tpu_custom_call" | custom-call | flops 1048576 | bytes 1048576 | tf_op jit(solution)/shard_map/base/pallas_call | solution.py:120
  63.8 0.0 collective-permute-done.10
  63.8 0.0 collective-permute-done.11.refs_4_
  63.8 0.0 collective-permute-done.12.refs_5_
  63.8 0.0 collective-permute-done.13.refs_6_
  63.9 0.1 collective-permute-start.14
  63.9 1.2 %collective-permute-done.14.other_ref = bf16[256,128]{1,0:T(8,128)(2,1)S(1)} collective-permute-done((bf16[256,128]{1,0:T(8,128)(2,1)S(1)}, bf16[256,128]{1,0:T(8,128)(2,1)S(1)}, u32[]{:S(2)}, u32[]{:S(2)}) %collective-permute-start.14) | collective-permute-done | bytes 65568 | tf_op jit(solution)/shard_map/ppermute | solution.py:44
  65.2 4.0 %expand.1 = bf16[1024,512]{1,0:T(8,128)(2,1)} custom-call(s32[1024,128]{1,0:T(8,128)S(1)} %get-tuple-element.33.code_ref, bf16[256,128]{1,0:T(8,128)(2,1)S(1)} %add_convert_fusion.mine_ref, bf16[256,128]{1,0:T(8,128)(2,1)S(1)} %collective-permute-done.14.other_ref, f32[512,512]{1,0:T(8,128)S(1)} %base.3.refs_0_, f32[256,512]{1,0:T(8,128)S(1)} %base.4.refs_1_, ...), custom_call_target="tpu_custom_call" | custom-call | flops 2147483648 | bytes 3145728 | tf_op jit(solution)/shard_map/expand/pallas_call | solution.py:212
  (8 shorter events, 0.1 us)
Async XLA Ops:
  1.1 9.1 %collective-permute-start = (bf16[128,1536]{1,0:T(8,128)(2,1)S(1)}, bf16[128,1536]{1,0:T(8,128)(2,1)S(1)}, u32[]{:S(2)}, u32[]{:S(2)}) collective-permute-start(bf16[128,1536]{1,0:T(8,128)(2,1)S(1)} %pad_maximum_fusion.3), channel_id=1, source_target_pairs={{0,8},{1,33},{2,10},{3,35},{4,12},{5,37},{6,14},{7,39},{8,16},{9,4... | collective-permute-start | bytes 1179656 | tf_op jit(solution)/shard_map/ppermute | solution.py:32
  2.7 7.8 %collective-permute-start.1 = (bf16[128,1536]{1,0:T(8,128)(2,1)S(1)}, bf16[128,1536]{1,0:T(8,128)(2,1)S(1)}, u32[]{:S(2)}, u32[]{:S(2)}) collective-permute-start(bf16[128,1536]{1,0:T(8,128)(2,1)S(1)} %pad_maximum_fusion.3), channel_id=1, source_target_pairs={{0,24},{1,97},{2,26},{3,99},{4,28},{5,101},{6,30},{7,103},{8,0},{9... | collective-permute-start | bytes 1179656 | tf_op jit(solution)/shard_map/ppermute | solution.py:32
  4.4 11.0 %collective-permute-start.2 = (bf16[128,1536]{1,0:T(8,128)(2,1)S(1)}, bf16[128,1536]{1,0:T(8,128)(2,1)S(1)}, u32[]{:S(2)}, u32[]{:S(2)}) collective-permute-start(bf16[128,1536]{1,0:T(8,128)(2,1)S(1)} %pad_maximum_fusion.3), channel_id=1, source_target_pairs={{0,16},{1,65},{2,18},{3,67},{4,20},{5,69},{6,22},{7,71},{8,24},{9,... | collective-permute-start | bytes 1179656 | tf_op jit(solution)/shard_map/ppermute | solution.py:32
  6.3 19.8 %slice-start = ((s8[8388608]{0:T(1024)(128)(4,1)}), s8[4194304]{0:T(1024)(128)(4,1)S(1)}, s32[]{:S(2)}) async-start(s8[8388608]{0:T(1024)(128)(4,1)} %bitcast.5), calls=%async_computation | async-start | bytes 8388608
  6.3 0.8 %copy-start = (s32[1024,1]{0,1:T(1,128)S(1)}, s32[1024,1]{0,1:T(1,128)}, u32[]{:S(2)}) copy-start(s32[1024,1]{0,1:T(1,128)} %param.6) | copy-start | bytes 12292
  7.1 8.3 %copy-start.1 = (bf16[2,1024,64]{1,2,0:T(8,128)(2,1)S(1)}, bf16[2,1024,64]{1,2,0:T(8,128)(2,1)}, u32[]{:S(2)}) copy-start(bf16[2,1024,64]{1,2,0:T(8,128)(2,1)} %param.8) | copy-start | bytes 786436
  7.1 19.0 %slice-start.1 = ((s8[8388608]{0:T(1024)(128)(4,1)}), s8[4194304]{0:T(1024)(128)(4,1)S(1)}, s32[]{:S(2)}) async-start(s8[8388608]{0:T(1024)(128)(4,1)} %bitcast.5), calls=%async_computation.1 | async-start | bytes 8388608
  10.1 23.1 %copy-start.3 = (bf16[128,1536]{1,0:T(8,128)(2,1)}, bf16[128,1536]{1,0:T(8,128)(2,1)S(1)}, u32[]{:S(2)}) copy-start(bf16[128,1536]{1,0:T(8,128)(2,1)S(1)} %collective-permute-done) | copy-start | bytes 1179652
  10.5 22.7 %copy-start.2 = (bf16[128,1536]{1,0:T(8,128)(2,1)}, bf16[128,1536]{1,0:T(8,128)(2,1)S(1)}, u32[]{:S(2)}) copy-start(bf16[128,1536]{1,0:T(8,128)(2,1)S(1)} %collective-permute-done.1) | copy-start | bytes 1179652
  15.4 17.8 %copy-start.4 = (bf16[128,1536]{1,0:T(8,128)(2,1)}, bf16[128,1536]{1,0:T(8,128)(2,1)S(1)}, u32[]{:S(2)}) copy-start(bf16[128,1536]{1,0:T(8,128)(2,1)S(1)} %collective-permute-done.2) | copy-start | bytes 1179652
  15.5 29.0 %collective-permute-start.5 = (bf16[512,1024]{1,0:T(8,128)(2,1)S(1)}, bf16[512,1024]{1,0:T(8,128)(2,1)S(1)}, u32[]{:S(2)}, u32[]{:S(2)}) collective-permute-start(bf16[512,1024]{1,0:T(8,128)(2,1)S(1)} %pad_maximum_fusion.refs_0_), channel_id=1, source_target_pairs={{0,64},{1,17},{2,66},{3,19},{4,68},{5,21},{6,70},{7,23},{8,72},{9,... | collective-permute-start | bytes 3145736 | tf_op jit(solution)/shard_map/ppermute | solution.py:38
  19.5 21.1 %collective-permute-start.6 = (bf16[384,1024]{1,0:T(8,128)(2,1)S(1)}, bf16[384,1024]{1,0:T(8,128)(2,1)S(1)}, u32[]{:S(2)}, u32[]{:S(2)}) collective-permute-start(bf16[384,1024]{1,0:T(8,128)(2,1)S(1)} %pad_maximum_fusion.1), channel_id=1, source_target_pairs={{0,32},{1,9},{2,34},{3,11},{4,36},{5,13},{6,38},{7,15},{8,40},{9,1... | collective-permute-start | bytes 2359304 | tf_op jit(solution)/shard_map/ppermute | solution.py:38
  20.6 21.1 %collective-permute-start.7 = (bf16[384,1024]{1,0:T(8,128)(2,1)S(1)}, bf16[384,1024]{1,0:T(8,128)(2,1)S(1)}, u32[]{:S(2)}, u32[]{:S(2)}) collective-permute-start(bf16[384,1024]{1,0:T(8,128)(2,1)S(1)} %pad_maximum_fusion.1), channel_id=1, source_target_pairs={{0,96},{1,25},{2,98},{3,27},{4,100},{5,29},{6,102},{7,31},{8,104},... | collective-permute-start | bytes 2359304 | tf_op jit(solution)/shard_map/ppermute | solution.py:38
  22.8 21.3 %collective-permute-start.3 = (bf16[128,1024]{1,0:T(8,128)(2,1)S(1)}, bf16[128,1024]{1,0:T(8,128)(2,1)S(1)}, u32[]{:S(2)}, u32[]{:S(2)}) collective-permute-start(bf16[128,1024]{1,0:T(8,128)(2,1)S(1)} %slice.24), channel_id=1, source_target_pairs={{0,32},{1,9},{2,34},{3,11},{4,36},{5,13},{6,38},{7,15},{8,40},{9,1... | collective-permute-start | bytes 786440 | tf_op jit(solution)/shard_map/ppermute | solution.py:38
  22.8 21.7 %collective-permute-start.4 = (bf16[128,1024]{1,0:T(8,128)(2,1)S(1)}, bf16[128,1024]{1,0:T(8,128)(2,1)S(1)}, u32[]{:S(2)}, u32[]{:S(2)}) collective-permute-start(bf16[128,1024]{1,0:T(8,128)(2,1)S(1)} %slice.24), channel_id=1, source_target_pairs={{0,96},{1,25},{2,98},{3,27},{4,100},{5,29},{6,102},{7,31},{8,104},... | collective-permute-start | bytes 786440 | tf_op jit(solution)/shard_map/ppermute | solution.py:38
  44.1 2.5 %slice-start.2 = ((bf16[128,1536]{1,0:T(8,128)(2,1)}), bf16[128,512]{1,0:T(8,128)(2,1)S(1)}, s32[]{:S(2)}) async-start(bf16[128,1536]{1,0:T(8,128)(2,1)} %copy-done.2), calls=%async_computation.2 | async-start | bytes 262144 | tf_op jit(solution)/shard_map/slice | solution.py:243
  44.1 2.5 %slice-start.3 = ((bf16[128,1536]{1,0:T(8,128)(2,1)}), bf16[128,512]{1,0:T(8,128)(2,1)S(1)}, s32[]{:S(2)}) async-start(bf16[128,1536]{1,0:T(8,128)(2,1)} %copy-done.3), calls=%async_computation.3 | async-start | bytes 262144 | tf_op jit(solution)/shard_map/slice | solution.py:243
  44.1 2.5 %slice-start.4 = ((bf16[128,1536]{1,0:T(8,128)(2,1)}), bf16[128,512]{1,0:T(8,128)(2,1)S(1)}, s32[]{:S(2)}) async-start(bf16[128,1536]{1,0:T(8,128)(2,1)} %copy-done.4), calls=%async_computation.4 | async-start | bytes 262144 | tf_op jit(solution)/shard_map/slice | solution.py:243
  44.1 2.5 %copy-start.5 = (bf16[2,64,512]{2,1,0:T(8,128)(2,1)S(1)}, bf16[2,64,512]{2,1,0:T(8,128)(2,1)}, u32[]{:S(2)}) copy-start(bf16[2,64,512]{2,1,0:T(8,128)(2,1)} %param.9) | copy-start | bytes 393220
  46.5 4.6 %collective-permute-start.8 = (f32[256,128]{1,0:T(8,128)S(1)}, f32[256,128]{1,0:T(8,128)S(1)}, u32[]{:S(2)}, u32[]{:S(2)}) collective-permute-start(f32[256,128]{1,0:T(8,128)S(1)} %get-tuple-element.45), channel_id=1, source_target_pairs={{0,1},{1,0},{2,3},{3,2},{4,5},{5,4},{6,7},{7,6},{8,9},{9,8},{10,11... | collective-permute-start | bytes 393224 | tf_op jit(solution)/shard_map/ppermute | solution.py:44
  46.6 17.2 %collective-permute-start.11 = (bf16[512,512]{1,0:T(8,128)(2,1)S(1)}, bf16[512,512]{1,0:T(8,128)(2,1)S(1)}, u32[]{:S(2)}, u32[]{:S(2)}) collective-permute-start(bf16[512,512]{1,0:T(8,128)(2,1)S(1)} %pad_maximum_fusion.2.refs_3_), channel_id=1, source_target_pairs={{0,32},{1,9},{2,34},{3,11},{4,36},{5,13},{6,38},{7,15},{8,40},{9,1... | collective-permute-start | bytes 1572872 | tf_op jit(solution)/shard_map/ppermute | solution.py:38
  47.9 15.9 %collective-permute-start.12 = (bf16[512,512]{1,0:T(8,128)(2,1)S(1)}, bf16[512,512]{1,0:T(8,128)(2,1)S(1)}, u32[]{:S(2)}, u32[]{:S(2)}) collective-permute-start(bf16[512,512]{1,0:T(8,128)(2,1)S(1)} %pad_maximum_fusion.2.refs_3_), channel_id=1, source_target_pairs={{0,96},{1,25},{2,98},{3,27},{4,100},{5,29},{6,102},{7,31},{8,104},... | collective-permute-start | bytes 1572872 | tf_op jit(solution)/shard_map/ppermute | solution.py:38
  50.1 13.7 %collective-permute-start.13 = (bf16[512,512]{1,0:T(8,128)(2,1)S(1)}, bf16[512,512]{1,0:T(8,128)(2,1)S(1)}, u32[]{:S(2)}, u32[]{:S(2)}) collective-permute-start(bf16[512,512]{1,0:T(8,128)(2,1)S(1)} %pad_maximum_fusion.2.refs_3_), channel_id=1, source_target_pairs={{0,64},{1,17},{2,66},{3,19},{4,68},{5,21},{6,70},{7,23},{8,72},{9,... | collective-permute-start | bytes 1572872 | tf_op jit(solution)/shard_map/ppermute | solution.py:38
  51.1 6.0 %collective-permute-start.9 = (f32[256,128]{1,0:T(8,128)S(1)}, f32[256,128]{1,0:T(8,128)S(1)}, u32[]{:S(2)}, u32[]{:S(2)}) collective-permute-start(f32[256,128]{1,0:T(8,128)S(1)} %add.9), channel_id=1, source_target_pairs={{0,2},{1,7},{2,0},{3,5},{4,6},{5,3},{6,4},{7,1},{8,10},{9,15},{10,... | collective-permute-start | bytes 393224 | tf_op jit(solution)/shard_map/ppermute | solution.py:51
  57.1 6.7 %collective-permute-start.10 = (f32[256,128]{1,0:T(8,128)S(1)}, f32[256,128]{1,0:T(8,128)S(1)}, u32[]{:S(2)}, u32[]{:S(2)}) collective-permute-start(f32[256,128]{1,0:T(8,128)S(1)} %add.10), channel_id=1, source_target_pairs={{0,6},{1,3},{2,4},{3,1},{4,2},{5,7},{6,0},{7,5},{8,14},{9,11},{10,... | collective-permute-start | bytes 393224 | tf_op jit(solution)/shard_map/ppermute | solution.py:51
  63.9 1.3 %collective-permute-start.14 = (bf16[256,128]{1,0:T(8,128)(2,1)S(1)}, bf16[256,128]{1,0:T(8,128)(2,1)S(1)}, u32[]{:S(2)}, u32[]{:S(2)}) collective-permute-start(bf16[256,128]{1,0:T(8,128)(2,1)S(1)} %add_convert_fusion.mine_ref), channel_id=1, source_target_pairs={{0,1},{1,0},{2,3},{3,2},{4,5},{5,4},{6,7},{7,6},{8,9},{9,8},{10,11... | collective-permute-start | bytes 196616 | tf_op jit(solution)/shard_map/ppermute | solution.py:44

commit v5 on v4

--- a/solution.py
+++ b/solution.py
@@ -115,7 +115,7 @@
         o_ref[rows, :] = jnp.dot(xb[rows, :], w_ref[...], preferred_element_type=F32)
 
 
-def base_rows(x, w, at, rows, block=128):
+def base_rows(x, w, at, rows, block=256):
     k, n = w.shape
     return pl.pallas_call(
         functools.partial(base_kernel, at),
@@ -156,7 +156,7 @@
     give_ref[...] = jnp.where(core == 0, high, low)
 
 
-def shrink(code, x, groups, total, last, name):
+def shrink(code, x, groups, total, last, name, weight=1 << 20):
     m = x.shape[0]
     args = [code, x] + [a for parts, _ in groups for a in parts] + ([] if total is None else [total])
     rows = m // 4 if last else m
@@ -169,7 +169,7 @@
         out_specs=[VMEM] * 2 if last else VMEM,
         out_shape=[shape] * 2 if last else shape,
         compiler_params=params(16),
-        cost_estimate=cost(1 << 20, 1 << 20),
+        cost_estimate=cost(weight, 1 << 20),
         name=name,
     )(*args)
 
@@ -179,10 +179,13 @@
     block = o_ref.shape[0]
     step = pl.program_id(0)
     code = code_ref[pl.ds(pl.multiple_of(step * block, block), block), :]
-    mine = step % 2 == lax.axis_index("tp") % 2
-    packed = jnp.where(mine, mine_ref[...].astype(F32), other_ref[...].astype(F32))
+    core = lax.axis_index("tp") % 2
+    mine, other = mine_ref[...].astype(F32), other_ref[...].astype(F32)
+    packed = jnp.concatenate(
+        [jnp.where(core == 0, mine, other), jnp.where(core == 0, other, mine)], axis=0
+    )
     lane = lax.broadcasted_iota(jnp.int32, packed.shape, 1)
-    left = (lane < 64) == (step < 2)
+    left = (lane < 64) == (step == 0)
     rows = jnp.where(left, packed, pltpu.roll(packed, 64, 1))
     delta = None
     for j, b_ref in zip(HOPS, b_refs):
@@ -195,10 +198,9 @@
     at = 0
     for size, base_ref in zip(pieces, base_refs):
 
-        @pl.when((step * block >= at) & (step * block < at + size))
-        def _(at=at, base_ref=base_ref):
-            row = pl.ds(pl.multiple_of(step * block - at, block), block)
-            o_ref[...] = (base_ref[row, :] + adapter_scale * delta).astype(BF)
+        @pl.when(step == at // block)
+        def _(row=pl.ds(at % block, size), base_ref=base_ref):
+            o_ref[row, :] = (base_ref[...] + adapter_scale * delta[row.start : row.start + size]).astype(BF)
 
         at += size
 
@@ -207,11 +209,11 @@
     n = bases[0].shape[1]
     pieces = [a.shape[0] for a in bases]
     m = sum(pieces)
-    block = m // 4
+    block = m // 2
     args = [code, mine, other, *bases, *parts]
     return pl.pallas_call(
         functools.partial(expand_kernel, pieces),
-        grid=(4,),
+        grid=(2,),
         in_specs=[VMEM] * len(args),
         out_specs=pl.BlockSpec((block, n), lambda i: (i, 0)),
         out_shape=jax.ShapeDtypeStruct((m, n), BF),
@@ -246,7 +248,7 @@
     total = shrink(code, here, [([d_own], [(0, i) for i in HOPS])], None, False, "shrink_own")
     a_before, a_after, total, base[0] = tie(a_before, a_after, total, base[0])
     groups = [([a], [(j, 0), (j, -1), (j, 1)]) for a, j in ((a_before, -1), (a_after, 1))]
-    total = shrink(code, here, groups, total, False, "shrink_near")
+    total = shrink(code, here, groups, total, False, "shrink_near", 5000000000)
     u_own = tie(u_own, base[0])[0]
     ups = [u_own] + [second(u_own, d) for d in (1, -1, 2)]
     b_before, b_after, d_opposite, total = tie(b_before, b_after, d_opposite, total)
@@ -258,7 +260,9 @@
         there, piece = tie(pair(keep, step), base_rows(activations, query_matrix, at, m // 4))
         keep = keep + there
         base.append(piece)
-    mine, *ups = tie(keep.astype(BF), *ups)
+        if step == 0:
+            keep, *ups = tie(keep, *ups)
+    mine = keep.astype(BF)
     return expand(code, mine, other_core(mine), base, ups)
 
 

time: 70.4 us -> 71 us (level)
  starting transfers between devices: 24.2 us -> 28.2 us
  waiting for transfers between devices: 15 us -> 11.4 us
    ppermute x3, waiting for transfers between devices: 6.14 us -> 1.28 us  [first(): lax.ppermute(a, AXES, every(lambda x, y, z, c: (x, y, z + d, c) if c else...]
    ppermute x8, starting transfers between devices: 14.9 us -> 18 us  [second(): lax.ppermute(a, AXES, every(lambda x, y, z, c: (x + d, y, z, c) if c else...]
    ppermute x2, waiting for transfers between devices: 1.24 us -> 2.58 us  [other_core(): return lax.ppermute(a, AXES, every(lambda x, y, z, c: (x, y, z, 1 - c)))]
    ppermute x2, starting transfers between devices: 3.92 us -> 4.85 us  [pair(): return lax.ppermute(a, AXES, every(to))]
  transfers between devices with their start and end apart: 15 -> 15, of which waited for: 7 -> 6; matrix products, arithmetic and copies ran while one was open for 0% -> 0% of each run, Pallas kernels for 31% -> 34%
where the time goes in v5:
time: 71 us; the launch traced here: 69.6 us
  starting transfers between devices  28.2 us (40%)
  Pallas kernels  27.5 us (39%)
  waiting for transfers between devices  11.4 us (16%)
  other arithmetic  1.26 us (2%)
  local copies, waits for them, and re-layouts  0.93 us (1%)
    ppermute x8, starting transfers between devices, second(): lax.ppermute(a, AXES, every(lambda x, y, z, c: (x + d, y, z, c) if c else...  18 us
    pallas_call x3, Pallas kernels, base_rows(): pl.pallas_call(functools.partial(base_kernel, at), in_specs=[HBM, VMEM],...  16.2 us
    ppermute x8, waiting for transfers between devices, second(): lax.ppermute(a, AXES, every(lambda x, y, z, c: (x + d, y, z, c) if c else...  7.58 us
    pallas_call x3, Pallas kernels, shrink(): pl.pallas_call(functools.partial(shrink_kernel, [(len(parts), places) for...  5.55 us
    ppermute x3, starting transfers between devices, first(): lax.ppermute(a, AXES, every(lambda x, y, z, c: (x, y, z + d, c) if c else...  5.2 us
    ppermute x2, starting transfers between devices, pair(): return lax.ppermute(a, AXES, every(to))  4.85 us
    pallas_call x1, Pallas kernels, expand(): pl.pallas_call(functools.partial(expand_kernel, pieces), grid=(2,), in_sp...  3.69 us
    ppermute x2, waiting for transfers between devices, other_core(): return lax.ppermute(a, AXES, every(lambda x, y, z, c: (x, y, z, 1 - c)))  2.58 us
  transfers between devices with their start and end apart: 15, of which 6 were waited for; matrix products, arithmetic and copies ran while one was open for 0% of the time, Pallas kernels for 34%

profile of v5, /device:TPU:0, one launch (start us, length us, event | category | flops | bytes accessed | tf_op | source)
XLA Modules:
  0.0 69.6 jit_solution(11729493055537949150)
XLA Ops:
  0.0 1.0 %pad_maximum_fusion.3 = bf16[128,1536]{1,0:T(8,128)(2,1)S(1)} fusion(bf16[128,512]{1,0:T(8,128)(2,1)} %bitcast.11, bf16[128,1024]{1,0:T(8,128)(2,1)} %bitcast.8), kind=kLoop, calls=%fused_computation.3 | loop fusion | flops 786432 | bytes 786432 | tf_op jit(solution)/shard_map/concatenate | solution.py:235
  1.1 1.6 %collective-permute-start = (bf16[128,1536]{1,0:T(8,128)(2,1)S(1)}, bf16[128,1536]{1,0:T(8,128)(2,1)S(1)}, u32[]{:S(2)}, u32[]{:S(2)}) collective-permute-start(bf16[128,1536]{1,0:T(8,128)(2,1)S(1)} %pad_maximum_fusion.3), channel_id=1, source_target_pairs={{0,8},{1,33},{2,10},{3,35},{4,12},{5,37},{6,14},{7,39},{8,16},{9,4... | collective-permute-start | bytes 1179656 | tf_op jit(solution)/shard_map/ppermute | solution.py:32
  2.7 1.7 %collective-permute-start.1 = (bf16[128,1536]{1,0:T(8,128)(2,1)S(1)}, bf16[128,1536]{1,0:T(8,128)(2,1)S(1)}, u32[]{:S(2)}, u32[]{:S(2)}) collective-permute-start(bf16[128,1536]{1,0:T(8,128)(2,1)S(1)} %pad_maximum_fusion.3), channel_id=1, source_target_pairs={{0,24},{1,97},{2,26},{3,99},{4,28},{5,101},{6,30},{7,103},{8,0},{9... | collective-permute-start | bytes 1179656 | tf_op jit(solution)/shard_map/ppermute | solution.py:32
  4.4 1.9 %collective-permute-start.2 = (bf16[128,1536]{1,0:T(8,128)(2,1)S(1)}, bf16[128,1536]{1,0:T(8,128)(2,1)S(1)}, u32[]{:S(2)}, u32[]{:S(2)}) collective-permute-start(bf16[128,1536]{1,0:T(8,128)(2,1)S(1)} %pad_maximum_fusion.3), channel_id=1, source_target_pairs={{0,16},{1,65},{2,18},{3,67},{4,20},{5,69},{6,22},{7,71},{8,24},{9,... | collective-permute-start | bytes 1179656 | tf_op jit(solution)/shard_map/ppermute | solution.py:32
  6.3 0.0 slice-start
  6.3 0.0 copy-start
  6.3 0.8 %copy-done = s32[1024,1]{0,1:T(1,128)S(1)} copy-done((s32[1024,1]{0,1:T(1,128)S(1)}, s32[1024,1]{0,1:T(1,128)}, u32[]{:S(2)}) %copy-start) | copy-done | bytes 4120
  7.1 0.0 copy-start.1
  7.1 0.0 slice-start.1
  7.1 2.1 %prepare.1 = (bf16[1024,1024]{1,0:T(8,128)(2,1)S(1)}, s32[1024,128]{1,0:T(8,128)S(1)}) custom-call(s32[8,128]{1,0:T(8,128)S(1)} %bitcast.7, bf16[1024,8192]{1,0:T(8,128)(2,1)} %x_ref.7), custom_call_target="tpu_custom_call" | custom-call | bytes 1048576 | tf_op jit(solution)/shard_map/prepare/pallas_call | solution.py:86
  9.2 0.9 %collective-permute-done = bf16[128,1536]{1,0:T(8,128)(2,1)S(1)} collective-permute-done((bf16[128,1536]{1,0:T(8,128)(2,1)S(1)}, bf16[128,1536]{1,0:T(8,128)(2,1)S(1)}, u32[]{:S(2)}, u32[]{:S(2)}) %collective-permute-start) | collective-permute-done | bytes 393248 | tf_op jit(solution)/shard_map/ppermute | solution.py:32
  10.1 0.0 copy-start.3
  10.1 0.4 collective-permute-done.1
  10.5 0.0 copy-start.2
  10.5 0.0 copy-done.1
  10.5 0.1 pad_maximum_fusion.1
  10.6 5.5 %collective-permute-start.6 = (bf16[384,1024]{1,0:T(8,128)(2,1)S(1)}, bf16[384,1024]{1,0:T(8,128)(2,1)S(1)}, u32[]{:S(2)}, u32[]{:S(2)}) collective-permute-start(bf16[384,1024]{1,0:T(8,128)(2,1)S(1)} %pad_maximum_fusion.1), channel_id=1, source_target_pairs={{0,32},{1,9},{2,34},{3,11},{4,36},{5,13},{6,38},{7,15},{8,40},{9,1... | collective-permute-start | bytes 2359304 | tf_op jit(solution)/shard_map/ppermute | solution.py:38
  16.1 2.2 %collective-permute-start.7 = (bf16[384,1024]{1,0:T(8,128)(2,1)S(1)}, bf16[384,1024]{1,0:T(8,128)(2,1)S(1)}, u32[]{:S(2)}, u32[]{:S(2)}) collective-permute-start(bf16[384,1024]{1,0:T(8,128)(2,1)S(1)} %pad_maximum_fusion.1), channel_id=1, source_target_pairs={{0,96},{1,25},{2,98},{3,27},{4,100},{5,29},{6,102},{7,31},{8,104},... | collective-permute-start | bytes 2359304 | tf_op jit(solution)/shard_map/ppermute | solution.py:38
  18.3 0.0 collective-permute-done.2
  18.3 0.0 copy-start.4
  18.3 0.1 pad_maximum_fusion.refs_0_
  18.4 1.9 %collective-permute-start.5 = (bf16[512,1024]{1,0:T(8,128)(2,1)S(1)}, bf16[512,1024]{1,0:T(8,128)(2,1)S(1)}, u32[]{:S(2)}, u32[]{:S(2)}) collective-permute-start(bf16[512,1024]{1,0:T(8,128)(2,1)S(1)} %pad_maximum_fusion.refs_0_), channel_id=1, source_target_pairs={{0,64},{1,17},{2,66},{3,19},{4,68},{5,21},{6,70},{7,23},{8,72},{9,... | collective-permute-start | bytes 3145736 | tf_op jit(solution)/shard_map/ppermute | solution.py:38
  20.3 1.0 %collective-permute-start.3 = (bf16[128,1024]{1,0:T(8,128)(2,1)S(1)}, bf16[128,1024]{1,0:T(8,128)(2,1)S(1)}, u32[]{:S(2)}, u32[]{:S(2)}) collective-permute-start(bf16[128,1024]{1,0:T(8,128)(2,1)S(1)} %slice.24), channel_id=1, source_target_pairs={{0,32},{1,9},{2,34},{3,11},{4,36},{5,13},{6,38},{7,15},{8,40},{9,1... | collective-permute-start | bytes 786440 | tf_op jit(solution)/shard_map/ppermute | solution.py:38
  21.3 0.0 slice-done
  21.3 0.0 slice-done.1
  21.3 7.0 %base.3.refs_0_ = f32[512,512]{1,0:T(8,128)S(1)} custom-call(bf16[1024,8192]{1,0:T(8,128)(2,1)} %x_ref.7, bf16[8192,512]{1,0:T(8,128)(2,1)S(1)} %bitcast.6), custom_call_target="tpu_custom_call" | custom-call | flops 1048576 | bytes 1048576 | tf_op jit(solution)/shard_map/base/pallas_call | solution.py:120
  28.3 2.3 %collective-permute-start.4 = (bf16[128,1024]{1,0:T(8,128)(2,1)S(1)}, bf16[128,1024]{1,0:T(8,128)(2,1)S(1)}, u32[]{:S(2)}, u32[]{:S(2)}) collective-permute-start(bf16[128,1024]{1,0:T(8,128)(2,1)S(1)} %slice.24), channel_id=1, source_target_pairs={{0,96},{1,25},{2,98},{3,27},{4,100},{5,29},{6,102},{7,31},{8,104},... | collective-permute-start | bytes 786440 | tf_op jit(solution)/shard_map/ppermute | solution.py:38
  30.6 0.0 copy-done.2
  30.6 0.0 copy-done.3
  30.6 0.0 copy-done.4
  30.6 0.0 slice-start.2
  30.6 0.0 slice-start.3
  30.6 0.0 slice-start.4
  30.6 0.0 copy-start.5
  30.6 1.3 %shrink_own.1.refs_2_ = f32[1024,128]{1,0:T(8,128)S(1)} custom-call(s32[1024,128]{1,0:T(8,128)S(1)} %get-tuple-element.33.code_ref, bf16[1024,1024]{1,0:T(8,128)(2,1)S(1)} %get-tuple-element.34.x_ref, bf16[512,1024]{1,0:T(8,128)(2,1)S(1)} %pad_maximum_fusion.refs_0_), custom_call_target="tpu_custom_call" | custom-call | flops 1048576 | bytes 1048576 | tf_op jit(solution)/shard_map/shrink_own/pallas_call | solution.py:164
  31.9 0.0 slice-done.2
  32.0 0.0 slice-done.3
  32.0 0.0 slice-done.4
  32.0 0.0 copy-done.5
  32.0 0.0 collective-permute-done.6.refs_0_
  32.0 7.0 %collective-permute-done.7.refs_1_ = bf16[384,1024]{1,0:T(8,128)(2,1)S(1)} collective-permute-done((bf16[384,1024]{1,0:T(8,128)(2,1)S(1)}, bf16[384,1024]{1,0:T(8,128)(2,1)S(1)}, u32[]{:S(2)}, u32[]{:S(2)}) %collective-permute-start.7) | collective-permute-done | bytes 786464 | tf_op jit(solution)/shard_map/ppermute | solution.py:38
  39.1 0.0 collective-permute-start.10
  39.1 3.7 %collective-permute-start.11 = (bf16[512,512]{1,0:T(8,128)(2,1)S(1)}, bf16[512,512]{1,0:T(8,128)(2,1)S(1)}, u32[]{:S(2)}, u32[]{:S(2)}) collective-permute-start(bf16[512,512]{1,0:T(8,128)(2,1)S(1)} %pad_maximum_fusion.2.refs_3_), channel_id=1, source_target_pairs={{0,96},{1,25},{2,98},{3,27},{4,100},{5,29},{6,102},{7,31},{8,104},... | collective-permute-start | bytes 1572872 | tf_op jit(solution)/shard_map/ppermute | solution.py:38
  42.7 0.0 collective-permute-done.3.refs_0_
  42.7 1.5 %collective-permute-start.12 = (bf16[512,512]{1,0:T(8,128)(2,1)S(1)}, bf16[512,512]{1,0:T(8,128)(2,1)S(1)}, u32[]{:S(2)}, u32[]{:S(2)}) collective-permute-start(bf16[512,512]{1,0:T(8,128)(2,1)S(1)} %pad_maximum_fusion.2.refs_3_), channel_id=1, source_target_pairs={{0,64},{1,17},{2,66},{3,19},{4,68},{5,21},{6,70},{7,23},{8,72},{9,... | collective-permute-start | bytes 1572872 | tf_op jit(solution)/shard_map/ppermute | solution.py:38
  44.2 2.4 %shrink_near.1.refs_3_ = f32[1024,128]{1,0:T(8,128)S(1)} custom-call(s32[1024,128]{1,0:T(8,128)S(1)} %get-tuple-element.33.code_ref, bf16[1024,1024]{1,0:T(8,128)(2,1)S(1)} %get-tuple-element.34.x_ref, bf16[384,1024]{1,0:T(8,128)(2,1)S(1)} %collective-permute-done.6.refs_0_, bf16[384,1024]{1,0:T(8,128)(2,1)S(1)} %collective-permute-done.7.refs_1_, ...), custom_call_target="tpu_custom_call" | custom-call | flops 5000000000 | bytes 1048576 | tf_op jit(solution)/shard_map/shrink_near/pallas_call | solution.py:164
  46.6 0.0 collective-permute-done.4.refs_1_
  46.6 0.0 collective-permute-done.5.refs_2_
  46.6 1.9 %shrink_far.1 = (f32[256,128]{1,0:T(8,128)S(1)}, f32[256,128]{1,0:T(8,128)S(1)}) custom-call(s32[1024,128]{1,0:T(8,128)S(1)} %get-tuple-element.33.code_ref, bf16[1024,1024]{1,0:T(8,128)(2,1)S(1)} %get-tuple-element.34.x_ref, bf16[128,1024]{1,0:T(8,128)(2,1)S(1)} %collective-permute-done.3.refs_0_, bf16[128,1024]{1,0:T(8,128)(2,1)S(1)} %collective-permute-done.4.refs_1_, ...), custom_call_target="tpu_custom_call" | custom-call | flops 1048576 | bytes 1048576 | tf_op jit(solution)/shard_map/shrink_far/pallas_call | solution.py:164
  48.5 0.1 collective-permute-start.8
  48.6 1.3 %collective-permute-done.8 = f32[256,128]{1,0:T(8,128)S(1)} collective-permute-done((f32[256,128]{1,0:T(8,128)S(1)}, f32[256,128]{1,0:T(8,128)S(1)}, u32[]{:S(2)}, u32[]{:S(2)}) %collective-permute-start.8) | collective-permute-done | bytes 131104 | tf_op jit(solution)/shard_map/ppermute | solution.py:44
  49.9 1.8 %collective-permute-start.9 = (f32[256,128]{1,0:T(8,128)S(1)}, f32[256,128]{1,0:T(8,128)S(1)}, u32[]{:S(2)}, u32[]{:S(2)}) collective-permute-start(f32[256,128]{1,0:T(8,128)S(1)} %add.9), channel_id=1, source_target_pairs={{0,2},{1,7},{2,0},{3,5},{4,6},{5,3},{6,4},{7,1},{8,10},{9,15},{10,... | collective-permute-start | bytes 393224 | tf_op jit(solution)/shard_map/ppermute | solution.py:51
  51.8 4.6 %base.4.refs_1_ = f32[256,512]{1,0:T(8,128)S(1)} custom-call(bf16[1024,8192]{1,0:T(8,128)(2,1)} %x_ref.7, bf16[8192,512]{1,0:T(8,128)(2,1)S(1)} %bitcast.6), custom_call_target="tpu_custom_call" | custom-call | flops 1048576 | bytes 1048576 | tf_op jit(solution)/shard_map/base/pallas_call | solution.py:120
  56.4 0.0 collective-permute-done.9
  56.4 0.0 collective-permute-done.10.refs_4_
  56.4 0.0 collective-permute-done.11.refs_5_
  56.4 0.5 collective-permute-done.12.refs_6_
  57.0 3.0 %collective-permute-start.13 = (f32[256,128]{1,0:T(8,128)S(1)}, f32[256,128]{1,0:T(8,128)S(1)}, u32[]{:S(2)}, u32[]{:S(2)}) collective-permute-start(f32[256,128]{1,0:T(8,128)S(1)} %add.10), channel_id=1, source_target_pairs={{0,6},{1,3},{2,4},{3,1},{4,2},{5,7},{6,0},{7,5},{8,14},{9,11},{10,... | collective-permute-start | bytes 393224 | tf_op jit(solution)/shard_map/ppermute | solution.py:51
  60.0 4.6 %base.5.refs_2_ = f32[256,512]{1,0:T(8,128)S(1)} custom-call(bf16[1024,8192]{1,0:T(8,128)(2,1)} %x_ref.7, bf16[8192,512]{1,0:T(8,128)(2,1)S(1)} %bitcast.6), custom_call_target="tpu_custom_call" | custom-call | flops 1048576 | bytes 1048576 | tf_op jit(solution)/shard_map/base/pallas_call | solution.py:120
  64.6 0.0 collective-permute-done.13
  64.6 0.1 collective-permute-start.14
  64.7 1.2 %collective-permute-done.14.other_ref = bf16[256,128]{1,0:T(8,128)(2,1)S(1)} collective-permute-done((bf16[256,128]{1,0:T(8,128)(2,1)S(1)}, bf16[256,128]{1,0:T(8,128)(2,1)S(1)}, u32[]{:S(2)}, u32[]{:S(2)}) %collective-permute-start.14) | collective-permute-done | bytes 65568 | tf_op jit(solution)/shard_map/ppermute | solution.py:44
  66.0 3.7 %expand.1 = bf16[1024,512]{1,0:T(8,128)(2,1)} custom-call(s32[1024,128]{1,0:T(8,128)S(1)} %get-tuple-element.33.code_ref, bf16[256,128]{1,0:T(8,128)(2,1)S(1)} %add_convert_fusion.mine_ref, bf16[256,128]{1,0:T(8,128)(2,1)S(1)} %collective-permute-done.14.other_ref, f32[512,512]{1,0:T(8,128)S(1)} %base.3.refs_0_, f32[256,512]{1,0:T(8,128)S(1)} %base.4.refs_1_, ...), custom_call_target="tpu_custom_call" | custom-call | flops 2147483648 | bytes 3145728 | tf_op jit(solution)/shard_map/expand/pallas_call | solution.py:214
  (8 shorter events, 0.1 us)
Async XLA Ops:
  1.1 9.1 %collective-permute-start = (bf16[128,1536]{1,0:T(8,128)(2,1)S(1)}, bf16[128,1536]{1,0:T(8,128)(2,1)S(1)}, u32[]{:S(2)}, u32[]{:S(2)}) collective-permute-start(bf16[128,1536]{1,0:T(8,128)(2,1)S(1)} %pad_maximum_fusion.3), channel_id=1, source_target_pairs={{0,8},{1,33},{2,10},{3,35},{4,12},{5,37},{6,14},{7,39},{8,16},{9,4... | collective-permute-start | bytes 1179656 | tf_op jit(solution)/shard_map/ppermute | solution.py:32
  2.7 7.8 %collective-permute-start.1 = (bf16[128,1536]{1,0:T(8,128)(2,1)S(1)}, bf16[128,1536]{1,0:T(8,128)(2,1)S(1)}, u32[]{:S(2)}, u32[]{:S(2)}) collective-permute-start(bf16[128,1536]{1,0:T(8,128)(2,1)S(1)} %pad_maximum_fusion.3), channel_id=1, source_target_pairs={{0,24},{1,97},{2,26},{3,99},{4,28},{5,101},{6,30},{7,103},{8,0},{9... | collective-permute-start | bytes 1179656 | tf_op jit(solution)/shard_map/ppermute | solution.py:32
  4.4 13.9 %collective-permute-start.2 = (bf16[128,1536]{1,0:T(8,128)(2,1)S(1)}, bf16[128,1536]{1,0:T(8,128)(2,1)S(1)}, u32[]{:S(2)}, u32[]{:S(2)}) collective-permute-start(bf16[128,1536]{1,0:T(8,128)(2,1)S(1)} %pad_maximum_fusion.3), channel_id=1, source_target_pairs={{0,16},{1,65},{2,18},{3,67},{4,20},{5,69},{6,22},{7,71},{8,24},{9,... | collective-permute-start | bytes 1179656 | tf_op jit(solution)/shard_map/ppermute | solution.py:32
  6.3 15.0 %slice-start = ((s8[8388608]{0:T(1024)(128)(4,1)}), s8[4194304]{0:T(1024)(128)(4,1)S(1)}, s32[]{:S(2)}) async-start(s8[8388608]{0:T(1024)(128)(4,1)} %bitcast.5), calls=%async_computation | async-start | bytes 8388608
  6.3 0.8 %copy-start = (s32[1024,1]{0,1:T(1,128)S(1)}, s32[1024,1]{0,1:T(1,128)}, u32[]{:S(2)}) copy-start(s32[1024,1]{0,1:T(1,128)} %param.6) | copy-start | bytes 12292
  7.1 3.4 %copy-start.1 = (bf16[2,1024,64]{1,2,0:T(8,128)(2,1)S(1)}, bf16[2,1024,64]{1,2,0:T(8,128)(2,1)}, u32[]{:S(2)}) copy-start(bf16[2,1024,64]{1,2,0:T(8,128)(2,1)} %param.8) | copy-start | bytes 786436
  7.1 14.2 %slice-start.1 = ((s8[8388608]{0:T(1024)(128)(4,1)}), s8[4194304]{0:T(1024)(128)(4,1)S(1)}, s32[]{:S(2)}) async-start(s8[8388608]{0:T(1024)(128)(4,1)} %bitcast.5), calls=%async_computation.1 | async-start | bytes 8388608
  10.1 20.5 %copy-start.3 = (bf16[128,1536]{1,0:T(8,128)(2,1)}, bf16[128,1536]{1,0:T(8,128)(2,1)S(1)}, u32[]{:S(2)}) copy-start(bf16[128,1536]{1,0:T(8,128)(2,1)S(1)} %collective-permute-done) | copy-start | bytes 1179652
  10.5 20.1 %copy-start.2 = (bf16[128,1536]{1,0:T(8,128)(2,1)}, bf16[128,1536]{1,0:T(8,128)(2,1)S(1)}, u32[]{:S(2)}) copy-start(bf16[128,1536]{1,0:T(8,128)(2,1)S(1)} %collective-permute-done.1) | copy-start | bytes 1179652
  10.6 21.4 %collective-permute-start.6 = (bf16[384,1024]{1,0:T(8,128)(2,1)S(1)}, bf16[384,1024]{1,0:T(8,128)(2,1)S(1)}, u32[]{:S(2)}, u32[]{:S(2)}) collective-permute-start(bf16[384,1024]{1,0:T(8,128)(2,1)S(1)} %pad_maximum_fusion.1), channel_id=1, source_target_pairs={{0,32},{1,9},{2,34},{3,11},{4,36},{5,13},{6,38},{7,15},{8,40},{9,1... | collective-permute-start | bytes 2359304 | tf_op jit(solution)/shard_map/ppermute | solution.py:38
  16.1 23.0 %collective-permute-start.7 = (bf16[384,1024]{1,0:T(8,128)(2,1)S(1)}, bf16[384,1024]{1,0:T(8,128)(2,1)S(1)}, u32[]{:S(2)}, u32[]{:S(2)}) collective-permute-start(bf16[384,1024]{1,0:T(8,128)(2,1)S(1)} %pad_maximum_fusion.1), channel_id=1, source_target_pairs={{0,96},{1,25},{2,98},{3,27},{4,100},{5,29},{6,102},{7,31},{8,104},... | collective-permute-start | bytes 2359304 | tf_op jit(solution)/shard_map/ppermute | solution.py:38
  18.3 12.3 %copy-start.4 = (bf16[128,1536]{1,0:T(8,128)(2,1)}, bf16[128,1536]{1,0:T(8,128)(2,1)S(1)}, u32[]{:S(2)}) copy-start(bf16[128,1536]{1,0:T(8,128)(2,1)S(1)} %collective-permute-done.2) | copy-start | bytes 1179652
  18.4 28.2 %collective-permute-start.5 = (bf16[512,1024]{1,0:T(8,128)(2,1)S(1)}, bf16[512,1024]{1,0:T(8,128)(2,1)S(1)}, u32[]{:S(2)}, u32[]{:S(2)}) collective-permute-start(bf16[512,1024]{1,0:T(8,128)(2,1)S(1)} %pad_maximum_fusion.refs_0_), channel_id=1, source_target_pairs={{0,64},{1,17},{2,66},{3,19},{4,68},{5,21},{6,70},{7,23},{8,72},{9,... | collective-permute-start | bytes 3145736 | tf_op jit(solution)/shard_map/ppermute | solution.py:38
  20.3 22.5 %collective-permute-start.3 = (bf16[128,1024]{1,0:T(8,128)(2,1)S(1)}, bf16[128,1024]{1,0:T(8,128)(2,1)S(1)}, u32[]{:S(2)}, u32[]{:S(2)}) collective-permute-start(bf16[128,1024]{1,0:T(8,128)(2,1)S(1)} %slice.24), channel_id=1, source_target_pairs={{0,32},{1,9},{2,34},{3,11},{4,36},{5,13},{6,38},{7,15},{8,40},{9,1... | collective-permute-start | bytes 786440 | tf_op jit(solution)/shard_map/ppermute | solution.py:38
  28.3 18.3 %collective-permute-start.4 = (bf16[128,1024]{1,0:T(8,128)(2,1)S(1)}, bf16[128,1024]{1,0:T(8,128)(2,1)S(1)}, u32[]{:S(2)}, u32[]{:S(2)}) collective-permute-start(bf16[128,1024]{1,0:T(8,128)(2,1)S(1)} %slice.24), channel_id=1, source_target_pairs={{0,96},{1,25},{2,98},{3,27},{4,100},{5,29},{6,102},{7,31},{8,104},... | collective-permute-start | bytes 786440 | tf_op jit(solution)/shard_map/ppermute | solution.py:38
  30.6 1.3 %slice-start.2 = ((bf16[128,1536]{1,0:T(8,128)(2,1)}), bf16[128,512]{1,0:T(8,128)(2,1)S(1)}, s32[]{:S(2)}) async-start(bf16[128,1536]{1,0:T(8,128)(2,1)} %copy-done.2), calls=%async_computation.2 | async-start | bytes 262144 | tf_op jit(solution)/shard_map/slice | solution.py:245
  30.6 1.4 %slice-start.3 = ((bf16[128,1536]{1,0:T(8,128)(2,1)}), bf16[128,512]{1,0:T(8,128)(2,1)S(1)}, s32[]{:S(2)}) async-start(bf16[128,1536]{1,0:T(8,128)(2,1)} %copy-done.3), calls=%async_computation.3 | async-start | bytes 262144 | tf_op jit(solution)/shard_map/slice | solution.py:245
  30.6 1.4 %slice-start.4 = ((bf16[128,1536]{1,0:T(8,128)(2,1)}), bf16[128,512]{1,0:T(8,128)(2,1)S(1)}, s32[]{:S(2)}) async-start(bf16[128,1536]{1,0:T(8,128)(2,1)} %copy-done.4), calls=%async_computation.4 | async-start | bytes 262144 | tf_op jit(solution)/shard_map/slice | solution.py:245
  30.6 1.4 %copy-start.5 = (bf16[2,64,512]{2,1,0:T(8,128)(2,1)S(1)}, bf16[2,64,512]{2,1,0:T(8,128)(2,1)}, u32[]{:S(2)}) copy-start(bf16[2,64,512]{2,1,0:T(8,128)(2,1)} %param.9) | copy-start | bytes 393220
  39.1 17.3 %collective-permute-start.10 = (bf16[512,512]{1,0:T(8,128)(2,1)S(1)}, bf16[512,512]{1,0:T(8,128)(2,1)S(1)}, u32[]{:S(2)}, u32[]{:S(2)}) collective-permute-start(bf16[512,512]{1,0:T(8,128)(2,1)S(1)} %pad_maximum_fusion.2.refs_3_), channel_id=1, source_target_pairs={{0,32},{1,9},{2,34},{3,11},{4,36},{5,13},{6,38},{7,15},{8,40},{9,1... | collective-permute-start | bytes 1572872 | tf_op jit(solution)/shard_map/ppermute | solution.py:38
  39.1 17.3 %collective-permute-start.11 = (bf16[512,512]{1,0:T(8,128)(2,1)S(1)}, bf16[512,512]{1,0:T(8,128)(2,1)S(1)}, u32[]{:S(2)}, u32[]{:S(2)}) collective-permute-start(bf16[512,512]{1,0:T(8,128)(2,1)S(1)} %pad_maximum_fusion.2.refs_3_), channel_id=1, source_target_pairs={{0,96},{1,25},{2,98},{3,27},{4,100},{5,29},{6,102},{7,31},{8,104},... | collective-permute-start | bytes 1572872 | tf_op jit(solution)/shard_map/ppermute | solution.py:38
  42.7 14.2 %collective-permute-start.12 = (bf16[512,512]{1,0:T(8,128)(2,1)S(1)}, bf16[512,512]{1,0:T(8,128)(2,1)S(1)}, u32[]{:S(2)}, u32[]{:S(2)}) collective-permute-start(bf16[512,512]{1,0:T(8,128)(2,1)S(1)} %pad_maximum_fusion.2.refs_3_), channel_id=1, source_target_pairs={{0,64},{1,17},{2,66},{3,19},{4,68},{5,21},{6,70},{7,23},{8,72},{9,... | collective-permute-start | bytes 1572872 | tf_op jit(solution)/shard_map/ppermute | solution.py:38
  48.5 1.4 %collective-permute-start.8 = (f32[256,128]{1,0:T(8,128)S(1)}, f32[256,128]{1,0:T(8,128)S(1)}, u32[]{:S(2)}, u32[]{:S(2)}) collective-permute-start(f32[256,128]{1,0:T(8,128)S(1)} %get-tuple-element.45), channel_id=1, source_target_pairs={{0,1},{1,0},{2,3},{3,2},{4,5},{5,4},{6,7},{7,6},{8,9},{9,8},{10,11... | collective-permute-start | bytes 393224 | tf_op jit(solution)/shard_map/ppermute | solution.py:44
  49.9 6.4 %collective-permute-start.9 = (f32[256,128]{1,0:T(8,128)S(1)}, f32[256,128]{1,0:T(8,128)S(1)}, u32[]{:S(2)}, u32[]{:S(2)}) collective-permute-start(f32[256,128]{1,0:T(8,128)S(1)} %add.9), channel_id=1, source_target_pairs={{0,2},{1,7},{2,0},{3,5},{4,6},{5,3},{6,4},{7,1},{8,10},{9,15},{10,... | collective-permute-start | bytes 393224 | tf_op jit(solution)/shard_map/ppermute | solution.py:51
  57.0 7.6 %collective-permute-start.13 = (f32[256,128]{1,0:T(8,128)S(1)}, f32[256,128]{1,0:T(8,128)S(1)}, u32[]{:S(2)}, u32[]{:S(2)}) collective-permute-start(f32[256,128]{1,0:T(8,128)S(1)} %add.10), channel_id=1, source_target_pairs={{0,6},{1,3},{2,4},{3,1},{4,2},{5,7},{6,0},{7,5},{8,14},{9,11},{10,... | collective-permute-start | bytes 393224 | tf_op jit(solution)/shard_map/ppermute | solution.py:51
  64.6 1.3 %collective-permute-start.14 = (bf16[256,128]{1,0:T(8,128)(2,1)S(1)}, bf16[256,128]{1,0:T(8,128)(2,1)S(1)}, u32[]{:S(2)}, u32[]{:S(2)}) collective-permute-start(bf16[256,128]{1,0:T(8,128)(2,1)S(1)} %add_convert_fusion.mine_ref), channel_id=1, source_target_pairs={{0,1},{1,0},{2,3},{3,2},{4,5},{5,4},{6,7},{7,6},{8,9},{9,8},{10,11... | collective-permute-start | bytes 196616 | tf_op jit(solution)/shard_map/ppermute | solution.py:44

commit v6 on v5

v6 whole, which is shorter than its diff:
```python
import functools

import jax
import jax.numpy as jnp
from jax import lax
from jax.experimental import pallas as pl
from jax.experimental.pallas import tpu as pltpu
from jax.sharding import PartitionSpec as P

BF, F32 = jnp.bfloat16, jnp.float32
AXES = ("rep", "tp")
RING = 4
HOPS = (0, -1, 1, 2)
adapter_scale = 0.5


def device_of(x, y, z, c):
    return (z % RING * RING + x % RING) * 2 * RING + y % RING * 2 + c


def every(f):
    return [
        (device_of(x, y, z, c), device_of(*f(x, y, z, c)))
        for z in range(RING)
        for x in range(RING)
        for y in range(RING)
        for c in range(2)
    ]


def first(a, d):
    return lax.ppermute(
        a, AXES, every(lambda x, y, z, c: (x, y, z + d, c) if c else (x + d, y, z, c))
    )


def second(a, d):
    return lax.ppermute(
        a, AXES, every(lambda x, y, z, c: (x + d, y, z, c) if c else (x, y, z + d, c))
    )


def other_core(a):
    return lax.ppermute(a, AXES, every(lambda x, y, z, c: (x, y, z, 1 - c)))


def pair(a, step):
    def to(x, y, z, c):
        return (x, (y ^ 1) if (c + step) % 2 == 0 else (3 - y), z, c)

    return lax.ppermute(a, AXES, every(to))


def params(mib):
    return pltpu.CompilerParams(vmem_limit_bytes=mib << 20)


def cost(flops, moved):
    return pl.CostEstimate(flops=flops, bytes_accessed=moved, transcendentals=0)


VMEM = pl.BlockSpec(memory_space=pltpu.VMEM)
HBM = pl.BlockSpec(memory_space=pltpu.HBM)


def owner(j, i):
    rep, core = lax.axis_index("rep"), lax.axis_index("tp") % 2
    dz, dx = jnp.where(core == 0, j, i), jnp.where(core == 0, i, j)
    return (rep // RING + dz + RING) % RING * RING + (rep % RING + dx + RING) % RING


def prep_kernel(ident_ref, x_ref, here_ref, half_ref, code_ref, sems):
    width, rows = here_ref.shape[1], half_ref.shape[0]
    at = pl.multiple_of(lax.axis_index("tp") * width, width)
    here = pltpu.make_async_copy(x_ref.at[:, pl.ds(at, width)], here_ref, sems.at[0])
    half = pltpu.make_async_copy(x_ref.at[pl.ds(0, rows)], half_ref, sems.at[1])
    here.start()
    half.start()
    side = lax.broadcasted_iota(jnp.int32, (128, 128), 1) // 64
    for r in range(ident_ref.shape[0]):
        ident = jnp.broadcast_to(ident_ref[r : r + 1, :], (128, 128)).T
        code_ref[128 * r : 128 * r + 128, :] = jnp.where((ident & 1) == side, ident >> 1, -1)
    here.wait()
    half.wait()


def prepare(ident, x, width):
    m, k = x.shape
    return pl.pallas_call(
        prep_kernel,
        in_specs=[VMEM, HBM],
        out_specs=[VMEM] * 3,
        out_shape=[
            jax.ShapeDtypeStruct((m, width), BF),
            jax.ShapeDtypeStruct((m // 2, k), BF),
            jax.ShapeDtypeStruct((m, 128), jnp.int32),
        ],
        scratch_shapes=[pltpu.SemaphoreType.DMA((2,))],
        compiler_params=params(28),
        cost_estimate=cost(0, 1 << 20),
        name="prepare",
    )(ident.reshape(m // 128, 128), x)


def base_kernel(half_ref, x_ref, w_ref, o_ref, xb, sems):
    half, block = xb.shape[0], 256
    count = half // block
    copies = [
        pltpu.make_async_copy(
            x_ref.at[pl.ds(half + i * block, block)], xb.at[pl.ds(i * block, block)], sems.at[i]
        )
        for i in range(count)
    ]
    for copy in copies:
        copy.start()

    def multiply(rows, at):
        o_ref[pl.ds(at, block), :] = jnp.dot(rows, w_ref[...], preferred_element_type=F32)

    def first_rows(i, _):
        at = pl.multiple_of(i * block, block)
        multiply(half_ref[pl.ds(at, block), :], at)
        return 0

    def other_rows(i, _):
        at = pl.multiple_of(i * block, block)
        multiply(xb[pl.ds(at, block), :], half + at)
        return 0

    lax.fori_loop(0, count, first_rows, 0)
    for copy in copies:
        copy.wait()
    lax.fori_loop(0, count, other_rows, 0)


def base_product(half, x, w):
    (m, k), n = x.shape, w.shape[1]
    return pl.pallas_call(
        base_kernel,
        in_specs=[VMEM, HBM, VMEM],
        out_specs=VMEM,
        out_shape=jax.ShapeDtypeStruct((m, n), F32),
        scratch_shapes=[pltpu.VMEM((m // 2, k), BF), pltpu.SemaphoreType.DMA((m // 512,))],
        compiler_params=params(22),
        cost_estimate=cost(1 << 20, 1 << 20),
        name="base",
    )(half, x, w)


def shrink_kernel(groups, has_sum, last, code_ref, x_ref, *refs):
    code = code_ref[...]
    refs = list(refs)
    total = None
    for count, places in groups:
        parts = [refs.pop(0)[...] for _ in range(count)]
        a = parts[0] if count == 1 else jnp.concatenate(parts, axis=0)
        p = lax.dot_general(x_ref[...], a, (((1,), (1,)), ((), ())), preferred_element_type=F32)
        for k, (j, i) in enumerate(places):
            term = jnp.where(code == owner(j, i), p[:, 128 * k : 128 * k + 128], 0.0)
            total = term if total is None else total + term
    if has_sum:
        total = total + refs.pop(0)[...]
    if not last:
        refs[0][...] = total
        return
    keep_ref, give_ref = refs
    half = total.shape[0] // 2
    folded = total + pltpu.roll(total, 64, 1)
    lane = lax.broadcasted_iota(jnp.int32, (half, 128), 1)
    packed = jnp.where(lane < 64, folded[:half], folded[half:])
    low, high = packed[: half // 2], packed[half // 2 :]
    core = lax.axis_index("tp") % 2
    keep_ref[...] = jnp.where(core == 0, low, high)
    give_ref[...] = jnp.where(core == 0, high, low)


def shrink(code, x, groups, total, last, name, weight=1 << 20):
    m = x.shape[0]
    args = [code, x] + [a for parts, _ in groups for a in parts] + ([] if total is None else [total])
    rows = m // 4 if last else m
    shape = jax.ShapeDtypeStruct((rows, 128), F32)
    return pl.pallas_call(
        functools.partial(
            shrink_kernel, [(len(parts), places) for parts, places in groups], total is not None, last
        ),
        in_specs=[VMEM] * len(args),
        out_specs=[VMEM] * 2 if last else VMEM,
        out_shape=[shape] * 2 if last else shape,
        compiler_params=params(16),
        cost_estimate=cost(weight, 1 << 20),
        name=name,
    )(*args)


def expand_kernel(groups, code_ref, mine_ref, other_ref, base_ref, *refs):
    b_refs, o_ref = refs[:-1], refs[-1]
    block = o_ref.shape[0]
    step = pl.program_id(0)
    here = pl.ds(pl.multiple_of(step * block, block), block)
    code = code_ref[here, :]
    core = lax.axis_index("tp") % 2
    mine, other = mine_ref[...].astype(F32), other_ref[...].astype(F32)
    packed = jnp.concatenate(
        [jnp.where(core == 0, mine, other), jnp.where(core == 0, other, mine)], axis=0
    )
    lane = lax.broadcasted_iota(jnp.int32, packed.shape, 1)
    left = (lane < 64) == (step == 0)
    rows = jnp.where(left, packed, pltpu.roll(packed, 64, 1))
    delta = None
    for places, b_ref in zip(groups, b_refs):
        spread = jnp.concatenate(
            [jnp.where(code == owner(j, i), rows, 0.0).astype(BF) for j, i in places], axis=1
        )
        d = jnp.dot(spread, b_ref[...], preferred_element_type=F32)
        delta = d if delta is None else delta + d
    delta = delta.astype(BF).astype(F32)
    o_ref[...] = (base_ref[here, :] + adapter_scale * delta).astype(BF)


def expand(code, mine, other, base, parts):
    m, n = base.shape
    block = m // 2
    args = [code, mine, other, base] + [a for a, _ in parts]
    return pl.pallas_call(
        functools.partial(expand_kernel, [places for _, places in parts]),
        grid=(2,),
        in_specs=[VMEM] * len(args),
        out_specs=pl.BlockSpec((block, n), lambda i: (i, 0)),
        out_shape=jax.ShapeDtypeStruct((m, n), BF),
        compiler_params=params(12),
        cost_estimate=cost(2 * m * n * 2048, 6 * m * n),
        name="expand",
    )(*args)


def tie(*arrays):
    return lax.optimization_barrier(arrays)


def forward(before, after):
    half = before.shape[0] // 2
    return second(before[:half], 1), second(after[half:], -1)


def per_device(activations, token_adapter_index, query_matrix, down, up):
    down = jnp.swapaxes(down, 1, 2).reshape(128, -1)
    up = up.reshape(128, -1)
    width = down.shape[1]
    row = lambda j, hops=HOPS: [(j, i) for i in hops]

    both = jnp.concatenate([down, up], axis=1)
    near = [first(both, d) for d in (1, -1, 2)]
    here, half, code = prepare(token_adapter_index, activations, width)
    near, here, half, code = tie(near, here, half, code)
    d_own = jnp.concatenate([down] + [a[:, :width] for a in near], axis=0)
    u_own = jnp.concatenate([up] + [a[:, width:] for a in near], axis=0)

    d_own, u_own = tie(d_own, u_own)
    d_before, d_after = second(d_own, 1), second(d_own, -1)
    base = base_product(half, activations, query_matrix)
    d_before, d_after, base = tie(d_before, d_after, base)
    d_far = forward(d_before, d_after)
    groups = [([d_own], row(0)), ([d_before], row(-1)), ([d_after], row(1))]
    total = shrink(code, here, groups, None, False, "shrink_near")
    u_before, u_after = second(u_own, 1), second(u_own, -1)
    *d_far, total = tie(*d_far, total)
    keep, give = shrink(code, here, [(d_far, row(2))], total, True, "shrink_far")
    keep = keep + other_core(give)
    keep, u_before, u_after = tie(keep, u_before, u_after)
    u_far = forward(u_before, u_after)
    keep = keep + pair(keep, 0)
    keep = keep + pair(keep, 1)
    mine = keep.astype(BF)
    parts = [(u_own, row(0)), (u_before, row(-1)), (u_after, row(1))]
    parts += [(a, row(2, hops)) for a, hops in zip(u_far, (HOPS[:2], HOPS[2:]))]
    return expand(code, mine, other_core(mine), base, parts)


def solution(mesh):
    in_specs = (
        P("rep", None),
        P("rep", None),
        P(None, "tp"),
        P("rep", "tp", None),
        P("rep", None, "tp"),
    )
    return jax.shard_map(
        per_device, mesh=mesh, in_specs=in_specs, out_specs=P("rep", "tp"), check_vma=False
    )
```

time: 71 us -> 71.1 us (level); the launches traced: 69.6 us -> 70.9 us
  waiting for transfers between devices: 11.4 us -> 26.4 us
  starting transfers between devices: 28.2 us -> 20.2 us
  Pallas kernels: 27.5 us -> 21.9 us
    ppermute x8, waiting for transfers between devices: 7.58 us -> 16.7 us  [second(): lax.ppermute(a, AXES, every(lambda x, y, z, c: (x + d, y, z, c) if c else...]
    ppermute x8, starting transfers between devices: 18 us -> 10.3 us  [second(): lax.ppermute(a, AXES, every(lambda x, y, z, c: (x + d, y, z, c) if c else...]
    pallas_call x5 -> x3, Pallas kernels: 22 us -> 17 us  [the longest x1 9.32 us: base_product(): pl.pallas_call(base_kernel, in_specs=[VMEM, HBM, VMEM], out_specs=VMEM, o...]
    ppermute x2, waiting for transfers between devices: 0.01 us -> 4.74 us  [pair(): return lax.ppermute(a, AXES, every(to))]
    ppermute x3, waiting for transfers between devices: 1.28 us -> 3.56 us  [first(): lax.ppermute(a, AXES, every(lambda x, y, z, c: (x, y, z + d, c) if c else...]
    ppermute x2, waiting for transfers between devices: 2.58 us -> 1.34 us  [other_core(): return lax.ppermute(a, AXES, every(lambda x, y, z, c: (x, y, z, 1 - c)))]
    pallas_call x3 -> x2, Pallas kernels: 5.55 us -> 4.87 us  [shrink(): pl.pallas_call(functools.partial(shrink_kernel, [(len(parts), places) for...]
  transfers between devices with their start and end apart: 15 -> 15, of which waited for: 6 -> 12; matrix products, arithmetic and copies ran while one was open for 0% -> 0% of each run, Pallas kernels for 34% -> 26%
where the time goes in v6:
time: 71.1 us; the launch traced here: 70.9 us
  waiting for transfers between devices  26.4 us (37%)
  Pallas kernels  21.9 us (31%)
  starting transfers between devices  20.2 us (28%)
  other arithmetic  1.34 us (2%)
  local copies, waits for them, and re-layouts  0.9 us (1%)
    ppermute x8, waiting for transfers between devices, second(): lax.ppermute(a, AXES, every(lambda x, y, z, c: (x + d, y, z, c) if c else...  16.7 us
    ppermute x8, starting transfers between devices, second(): lax.ppermute(a, AXES, every(lambda x, y, z, c: (x + d, y, z, c) if c else...  10.3 us
    pallas_call x1, Pallas kernels, base_product(): pl.pallas_call(base_kernel, in_specs=[VMEM, HBM, VMEM], out_specs=VMEM, o...  9.32 us
    ppermute x3, starting transfers between devices, first(): lax.ppermute(a, AXES, every(lambda x, y, z, c: (x, y, z + d, c) if c else...  5.21 us
    pallas_call x2, Pallas kernels, shrink(): pl.pallas_call(functools.partial(shrink_kernel, [(len(parts), places) for...  4.87 us
    ppermute x2, waiting for transfers between devices, pair(): return lax.ppermute(a, AXES, every(to))  4.74 us
    ppermute x2, starting transfers between devices, pair(): return lax.ppermute(a, AXES, every(to))  4.5 us
    pallas_call x1, Pallas kernels, prepare(): pl.pallas_call(prep_kernel, in_specs=[VMEM, HBM], out_specs=[VMEM] * 3, o...  4.28 us
  transfers between devices with their start and end apart: 15, of which 12 were waited for; matrix products, arithmetic and copies ran while one was open for 0% of the time, Pallas kernels for 26%

profile of v6, /device:TPU:0, one launch (start us, length us, event | category | flops | bytes accessed | tf_op | source)
XLA Modules:
  0.0 70.9 jit_solution(13036889500362826792)
XLA Ops:
  0.0 0.0 slice-start
  0.0 1.2 %pad_maximum_fusion.2 = bf16[128,1536]{1,0:T(8,128)(2,1)S(1)} fusion(bf16[128,512]{1,0:T(8,128)(2,1)} %bitcast.10, bf16[128,1024]{1,0:T(8,128)(2,1)} %bitcast.8), kind=kLoop, calls=%fused_computation.2 | loop fusion | flops 786432 | bytes 786432 | tf_op jit(solution)/shard_map/concatenate | solution.py:251
  1.2 3.2 %collective-permute-start.2 = (bf16[128,1536]{1,0:T(8,128)(2,1)S(1)}, bf16[128,1536]{1,0:T(8,128)(2,1)S(1)}, u32[]{:S(2)}, u32[]{:S(2)}) collective-permute-start(bf16[128,1536]{1,0:T(8,128)(2,1)S(1)} %pad_maximum_fusion.2), channel_id=1, source_target_pairs={{0,16},{1,65},{2,18},{3,67},{4,20},{5,69},{6,22},{7,71},{8,24},{9,... | collective-permute-start | bytes 1179656 | tf_op jit(solution)/shard_map/ppermute | solution.py:32
  4.4 1.1 %collective-permute-start.1 = (bf16[128,1536]{1,0:T(8,128)(2,1)S(1)}, bf16[128,1536]{1,0:T(8,128)(2,1)S(1)}, u32[]{:S(2)}, u32[]{:S(2)}) collective-permute-start(bf16[128,1536]{1,0:T(8,128)(2,1)S(1)} %pad_maximum_fusion.2), channel_id=1, source_target_pairs={{0,24},{1,97},{2,26},{3,99},{4,28},{5,101},{6,30},{7,103},{8,0},{9... | collective-permute-start | bytes 1179656 | tf_op jit(solution)/shard_map/ppermute | solution.py:32
  5.5 0.9 %collective-permute-start = (bf16[128,1536]{1,0:T(8,128)(2,1)S(1)}, bf16[128,1536]{1,0:T(8,128)(2,1)S(1)}, u32[]{:S(2)}, u32[]{:S(2)}) collective-permute-start(bf16[128,1536]{1,0:T(8,128)(2,1)S(1)} %pad_maximum_fusion.2), channel_id=1, source_target_pairs={{0,8},{1,33},{2,10},{3,35},{4,12},{5,37},{6,14},{7,39},{8,16},{9,4... | collective-permute-start | bytes 1179656 | tf_op jit(solution)/shard_map/ppermute | solution.py:32
  6.4 0.0 copy-start
  6.4 0.7 copy-done
  7.1 0.0 slice-start.1
  7.1 4.3 %prepare.1 = (bf16[1024,1024]{1,0:T(8,128)(2,1)S(1)}, bf16[512,8192]{1,0:T(8,128)(2,1)S(1)}, s32[1024,128]{1,0:T(8,128)S(1)}) custom-call(s32[8,128]{1,0:T(8,128)S(1)} %bitcast.7, bf16[1024,8192]{1,0:T(8,128)(2,1)} %x_ref.3), custom_call_target="tpu_custom_call" | custom-call | bytes 1048576 | tf_op jit(solution)/shard_map/prepare/pallas_call | solution.py:89
  11.4 0.0 copy-start.2
  11.4 0.0 copy-start.1
  11.4 0.0 collective-permute-done.2
  11.4 3.6 %collective-permute-done.1 = bf16[128,1536]{1,0:T(8,128)(2,1)S(1)} collective-permute-done((bf16[128,1536]{1,0:T(8,128)(2,1)S(1)}, bf16[128,1536]{1,0:T(8,128)(2,1)S(1)}, u32[]{:S(2)}, u32[]{:S(2)}) %collective-permute-start.1) | collective-permute-done | bytes 393248 | tf_op jit(solution)/shard_map/ppermute | solution.py:32
  15.0 0.0 collective-permute-done
  15.1 0.0 copy-done.2
  15.2 0.0 copy-done.1
  15.2 0.1 pad_maximum_fusion.refs_0_
  15.3 4.1 %collective-permute-start.4 = (bf16[512,1024]{1,0:T(8,128)(2,1)S(1)}, bf16[512,1024]{1,0:T(8,128)(2,1)S(1)}, u32[]{:S(2)}, u32[]{:S(2)}) collective-permute-start(bf16[512,1024]{1,0:T(8,128)(2,1)S(1)} %pad_maximum_fusion.refs_0_), channel_id=1, source_target_pairs={{0,96},{1,25},{2,98},{3,27},{4,100},{5,29},{6,102},{7,31},{8,104},... | collective-permute-start | bytes 3145736 | tf_op jit(solution)/shard_map/ppermute | solution.py:38
  19.4 0.0 collective-permute-start.3
  19.4 0.0 slice-done
  19.4 0.0 slice-done.1
  19.4 9.3 %base.1.base_ref = f32[1024,512]{1,0:T(8,128)S(1)} custom-call(bf16[512,8192]{1,0:T(8,128)(2,1)S(1)} %get-tuple-element.36.half_ref, bf16[1024,8192]{1,0:T(8,128)(2,1)} %x_ref.3, bf16[8192,512]{1,0:T(8,128)(2,1)S(1)} %bitcast.6), custom_call_target="tpu_custom_call" | custom-call | flops 1048576 | bytes 1048576 | tf_op jit(solution)/shard_map/base/pallas_call | solution.py:138
  28.7 3.0 %collective-permute-done.4.refs_2_ = bf16[512,1024]{1,0:T(8,128)(2,1)S(1)} collective-permute-done((bf16[512,1024]{1,0:T(8,128)(2,1)S(1)}, bf16[512,1024]{1,0:T(8,128)(2,1)S(1)}, u32[]{:S(2)}, u32[]{:S(2)}) %collective-permute-start.4) | collective-permute-done | bytes 1048608 | tf_op jit(solution)/shard_map/ppermute | solution.py:38
  31.7 3.7 %collective-permute-done.3.refs_1_ = bf16[512,1024]{1,0:T(8,128)(2,1)S(1)} collective-permute-done((bf16[512,1024]{1,0:T(8,128)(2,1)S(1)}, bf16[512,1024]{1,0:T(8,128)(2,1)S(1)}, u32[]{:S(2)}, u32[]{:S(2)}) %collective-permute-start.3) | collective-permute-done | bytes 1048608 | tf_op jit(solution)/shard_map/ppermute | solution.py:38
  35.5 0.1 collective-permute-start.6
  35.5 2.0 %collective-permute-start.5 = (bf16[256,1024]{1,0:T(8,128)(2,1)S(1)}, bf16[256,1024]{1,0:T(8,128)(2,1)S(1)}, u32[]{:S(2)}, u32[]{:S(2)}) collective-permute-start(bf16[256,1024]{1,0:T(8,128)(2,1)S(1)} %slice.36), channel_id=1, source_target_pairs={{0,32},{1,9},{2,34},{3,11},{4,36},{5,13},{6,38},{7,15},{8,40},{9,1... | collective-permute-start | bytes 1572872 | tf_op jit(solution)/shard_map/ppermute | solution.py:38
  37.6 1.3 %collective-permute-start.9 = (bf16[512,512]{1,0:T(8,128)(2,1)S(1)}, bf16[512,512]{1,0:T(8,128)(2,1)S(1)}, u32[]{:S(2)}, u32[]{:S(2)}) collective-permute-start(bf16[512,512]{1,0:T(8,128)(2,1)S(1)} %pad_maximum_fusion.1.refs_0_), channel_id=1, source_target_pairs={{0,96},{1,25},{2,98},{3,27},{4,100},{5,29},{6,102},{7,31},{8,104},... | collective-permute-start | bytes 1572872 | tf_op jit(solution)/shard_map/ppermute | solution.py:38
  38.8 0.7 %collective-permute-start.8 = (bf16[512,512]{1,0:T(8,128)(2,1)S(1)}, bf16[512,512]{1,0:T(8,128)(2,1)S(1)}, u32[]{:S(2)}, u32[]{:S(2)}) collective-permute-start(bf16[512,512]{1,0:T(8,128)(2,1)S(1)} %pad_maximum_fusion.1.refs_0_), channel_id=1, source_target_pairs={{0,32},{1,9},{2,34},{3,11},{4,36},{5,13},{6,38},{7,15},{8,40},{9,1... | collective-permute-start | bytes 1572872 | tf_op jit(solution)/shard_map/ppermute | solution.py:38
  39.6 3.5 %shrink_near.1.refs_2_ = f32[1024,128]{1,0:T(8,128)S(1)} custom-call(s32[1024,128]{1,0:T(8,128)S(1)} %get-tuple-element.30.code_ref, bf16[1024,1024]{1,0:T(8,128)(2,1)S(1)} %get-tuple-element.31.x_ref, bf16[512,1024]{1,0:T(8,128)(2,1)S(1)} %pad_maximum_fusion.refs_0_, bf16[512,1024]{1,0:T(8,128)(2,1)S(1)} %collective-permute-done.3.refs_1_, ...), custom_call_target="tpu_custom_call" | custom-call | flops 1048576 | bytes 1048576 | tf_op jit(solution)/shard_map/shrink_near/pallas_call | solution.py:182
  43.1 1.6 %collective-permute-done.6.refs_1_ = bf16[256,1024]{1,0:T(8,128)(2,1)S(1)} collective-permute-done((bf16[256,1024]{1,0:T(8,128)(2,1)S(1)}, bf16[256,1024]{1,0:T(8,128)(2,1)S(1)}, u32[]{:S(2)}, u32[]{:S(2)}) %collective-permute-start.6) | collective-permute-done | bytes 524320 | tf_op jit(solution)/shard_map/ppermute | solution.py:38
  44.7 1.3 %collective-permute-done.5.refs_0_ = bf16[256,1024]{1,0:T(8,128)(2,1)S(1)} collective-permute-done((bf16[256,1024]{1,0:T(8,128)(2,1)S(1)}, bf16[256,1024]{1,0:T(8,128)(2,1)S(1)}, u32[]{:S(2)}, u32[]{:S(2)}) %collective-permute-start.5) | collective-permute-done | bytes 524320 | tf_op jit(solution)/shard_map/ppermute | solution.py:38
  46.0 1.4 %shrink_far.1 = (f32[256,128]{1,0:T(8,128)S(1)}, f32[256,128]{1,0:T(8,128)S(1)}) custom-call(s32[1024,128]{1,0:T(8,128)S(1)} %get-tuple-element.30.code_ref, bf16[1024,1024]{1,0:T(8,128)(2,1)S(1)} %get-tuple-element.31.x_ref, bf16[256,1024]{1,0:T(8,128)(2,1)S(1)} %collective-permute-done.5.refs_0_, bf16[256,1024]{1,0:T(8,128)(2,1)S(1)} %collective-permute-done.6.refs_1_, ...), custom_call_target="tpu_custom_call" | custom-call | flops 1048576 | bytes 1048576 | tf_op jit(solution)/shard_map/shrink_far/pallas_call | solution.py:182
  47.4 0.1 collective-permute-start.7
  47.5 1.3 %collective-permute-done.7 = f32[256,128]{1,0:T(8,128)S(1)} collective-permute-done((f32[256,128]{1,0:T(8,128)S(1)}, f32[256,128]{1,0:T(8,128)S(1)}, u32[]{:S(2)}, u32[]{:S(2)}) %collective-permute-start.7) | collective-permute-done | bytes 131104 | tf_op jit(solution)/shard_map/ppermute | solution.py:44
  48.8 1.5 %collective-permute-done.9.refs_2_ = bf16[512,512]{1,0:T(8,128)(2,1)S(1)} collective-permute-done((bf16[512,512]{1,0:T(8,128)(2,1)S(1)}, bf16[512,512]{1,0:T(8,128)(2,1)S(1)}, u32[]{:S(2)}, u32[]{:S(2)}) %collective-permute-start.9) | collective-permute-done | bytes 524320 | tf_op jit(solution)/shard_map/ppermute | solution.py:38
  50.3 1.3 %collective-permute-done.8.refs_1_ = bf16[512,512]{1,0:T(8,128)(2,1)S(1)} collective-permute-done((bf16[512,512]{1,0:T(8,128)(2,1)S(1)}, bf16[512,512]{1,0:T(8,128)(2,1)S(1)}, u32[]{:S(2)}, u32[]{:S(2)}) %collective-permute-start.8) | collective-permute-done | bytes 524320 | tf_op jit(solution)/shard_map/ppermute | solution.py:38
  51.6 1.6 %collective-permute-start.10 = (f32[256,128]{1,0:T(8,128)S(1)}, f32[256,128]{1,0:T(8,128)S(1)}, u32[]{:S(2)}, u32[]{:S(2)}) collective-permute-start(f32[256,128]{1,0:T(8,128)S(1)} %add.9), channel_id=1, source_target_pairs={{0,2},{1,7},{2,0},{3,5},{4,6},{5,3},{6,4},{7,1},{8,10},{9,15},{10,... | collective-permute-start | bytes 393224 | tf_op jit(solution)/shard_map/ppermute | solution.py:51
  53.2 3.6 %collective-permute-done.10 = f32[256,128]{1,0:T(8,128)S(1)} collective-permute-done((f32[256,128]{1,0:T(8,128)S(1)}, f32[256,128]{1,0:T(8,128)S(1)}, u32[]{:S(2)}, u32[]{:S(2)}) %collective-permute-start.10) | collective-permute-done | bytes 131104 | tf_op jit(solution)/shard_map/ppermute | solution.py:51
  56.8 2.9 %collective-permute-start.11 = (f32[256,128]{1,0:T(8,128)S(1)}, f32[256,128]{1,0:T(8,128)S(1)}, u32[]{:S(2)}, u32[]{:S(2)}) collective-permute-start(f32[256,128]{1,0:T(8,128)S(1)} %add.10), channel_id=1, source_target_pairs={{0,6},{1,3},{2,4},{3,1},{4,2},{5,7},{6,0},{7,5},{8,14},{9,11},{10,... | collective-permute-start | bytes 393224 | tf_op jit(solution)/shard_map/ppermute | solution.py:51
  59.7 0.1 collective-permute-start.14
  59.8 2.0 %collective-permute-start.13 = (bf16[256,512]{1,0:T(8,128)(2,1)S(1)}, bf16[256,512]{1,0:T(8,128)(2,1)S(1)}, u32[]{:S(2)}, u32[]{:S(2)}) collective-permute-start(bf16[256,512]{1,0:T(8,128)(2,1)S(1)} %slice.38), channel_id=1, source_target_pairs={{0,32},{1,9},{2,34},{3,11},{4,36},{5,13},{6,38},{7,15},{8,40},{9,1... | collective-permute-start | bytes 786440 | tf_op jit(solution)/shard_map/ppermute | solution.py:38
  61.8 1.2 %collective-permute-done.11 = f32[256,128]{1,0:T(8,128)S(1)} collective-permute-done((f32[256,128]{1,0:T(8,128)S(1)}, f32[256,128]{1,0:T(8,128)S(1)}, u32[]{:S(2)}, u32[]{:S(2)}) %collective-permute-start.11) | collective-permute-done | bytes 131104 | tf_op jit(solution)/shard_map/ppermute | solution.py:51
  63.1 0.1 collective-permute-start.12
  63.1 3.0 %collective-permute-done.14.refs_4_ = bf16[256,512]{1,0:T(8,128)(2,1)S(1)} collective-permute-done((bf16[256,512]{1,0:T(8,128)(2,1)S(1)}, bf16[256,512]{1,0:T(8,128)(2,1)S(1)}, u32[]{:S(2)}, u32[]{:S(2)}) %collective-permute-start.14) | collective-permute-done | bytes 262176 | tf_op jit(solution)/shard_map/ppermute | solution.py:38
  66.2 1.3 %collective-permute-done.13.refs_3_ = bf16[256,512]{1,0:T(8,128)(2,1)S(1)} collective-permute-done((bf16[256,512]{1,0:T(8,128)(2,1)S(1)}, bf16[256,512]{1,0:T(8,128)(2,1)S(1)}, u32[]{:S(2)}, u32[]{:S(2)}) %collective-permute-start.13) | collective-permute-done | bytes 262176 | tf_op jit(solution)/shard_map/ppermute | solution.py:38
  67.5 0.0 collective-permute-done.12.other_ref
  67.5 3.4 %expand.1 = bf16[1024,512]{1,0:T(8,128)(2,1)} custom-call(s32[1024,128]{1,0:T(8,128)S(1)} %get-tuple-element.30.code_ref, bf16[256,128]{1,0:T(8,128)(2,1)S(1)} %add_convert_fusion.mine_ref, bf16[256,128]{1,0:T(8,128)(2,1)S(1)} %collective-permute-done.12.other_ref, f32[1024,512]{1,0:T(8,128)S(1)} %base.1.base_ref, ...), custom_call_target="tpu_custom_call" | custom-call | flops 2147483648 | bytes 3145728 | tf_op jit(solution)/shard_map/expand/pallas_call | solution.py:224
  (15 shorter events, 0.3 us)
Async XLA Ops:
  0.0 19.4 %slice-start = ((s8[8388608]{0:T(1024)(128)(4,1)}), s8[4194304]{0:T(1024)(128)(4,1)S(1)}, s32[]{:S(2)}) async-start(s8[8388608]{0:T(1024)(128)(4,1)} %bitcast.5), calls=%async_computation | async-start | bytes 8388608
  1.2 10.2 %collective-permute-start.2 = (bf16[128,1536]{1,0:T(8,128)(2,1)S(1)}, bf16[128,1536]{1,0:T(8,128)(2,1)S(1)}, u32[]{:S(2)}, u32[]{:S(2)}) collective-permute-start(bf16[128,1536]{1,0:T(8,128)(2,1)S(1)} %pad_maximum_fusion.2), channel_id=1, source_target_pairs={{0,16},{1,65},{2,18},{3,67},{4,20},{5,69},{6,22},{7,71},{8,24},{9,... | collective-permute-start | bytes 1179656 | tf_op jit(solution)/shard_map/ppermute | solution.py:32
  4.4 10.6 %collective-permute-start.1 = (bf16[128,1536]{1,0:T(8,128)(2,1)S(1)}, bf16[128,1536]{1,0:T(8,128)(2,1)S(1)}, u32[]{:S(2)}, u32[]{:S(2)}) collective-permute-start(bf16[128,1536]{1,0:T(8,128)(2,1)S(1)} %pad_maximum_fusion.2), channel_id=1, source_target_pairs={{0,24},{1,97},{2,26},{3,99},{4,28},{5,101},{6,30},{7,103},{8,0},{9... | collective-permute-start | bytes 1179656 | tf_op jit(solution)/shard_map/ppermute | solution.py:32
  5.5 9.5 %collective-permute-start = (bf16[128,1536]{1,0:T(8,128)(2,1)S(1)}, bf16[128,1536]{1,0:T(8,128)(2,1)S(1)}, u32[]{:S(2)}, u32[]{:S(2)}) collective-permute-start(bf16[128,1536]{1,0:T(8,128)(2,1)S(1)} %pad_maximum_fusion.2), channel_id=1, source_target_pairs={{0,8},{1,33},{2,10},{3,35},{4,12},{5,37},{6,14},{7,39},{8,16},{9,4... | collective-permute-start | bytes 1179656 | tf_op jit(solution)/shard_map/ppermute | solution.py:32
  6.4 0.7 copy-start
  7.1 12.3 %slice-start.1 = ((s8[8388608]{0:T(1024)(128)(4,1)}), s8[4194304]{0:T(1024)(128)(4,1)S(1)}, s32[]{:S(2)}) async-start(s8[8388608]{0:T(1024)(128)(4,1)} %bitcast.5), calls=%async_computation.1 | async-start | bytes 8388608
  11.4 3.7 %copy-start.2 = (bf16[2,64,512]{2,1,0:T(8,128)(2,1)S(1)}, bf16[2,64,512]{2,1,0:T(8,128)(2,1)}, u32[]{:S(2)}) copy-start(bf16[2,64,512]{2,1,0:T(8,128)(2,1)} %param.9) | copy-start | bytes 393220
  11.4 3.8 %copy-start.1 = (bf16[2,1024,64]{1,2,0:T(8,128)(2,1)S(1)}, bf16[2,1024,64]{1,2,0:T(8,128)(2,1)}, u32[]{:S(2)}) copy-start(bf16[2,1024,64]{1,2,0:T(8,128)(2,1)} %param.8) | copy-start | bytes 786436
  15.3 16.4 %collective-permute-start.4 = (bf16[512,1024]{1,0:T(8,128)(2,1)S(1)}, bf16[512,1024]{1,0:T(8,128)(2,1)S(1)}, u32[]{:S(2)}, u32[]{:S(2)}) collective-permute-start(bf16[512,1024]{1,0:T(8,128)(2,1)S(1)} %pad_maximum_fusion.refs_0_), channel_id=1, source_target_pairs={{0,96},{1,25},{2,98},{3,27},{4,100},{5,29},{6,102},{7,31},{8,104},... | collective-permute-start | bytes 3145736 | tf_op jit(solution)/shard_map/ppermute | solution.py:38
  19.4 16.0 %collective-permute-start.3 = (bf16[512,1024]{1,0:T(8,128)(2,1)S(1)}, bf16[512,1024]{1,0:T(8,128)(2,1)S(1)}, u32[]{:S(2)}, u32[]{:S(2)}) collective-permute-start(bf16[512,1024]{1,0:T(8,128)(2,1)S(1)} %pad_maximum_fusion.refs_0_), channel_id=1, source_target_pairs={{0,32},{1,9},{2,34},{3,11},{4,36},{5,13},{6,38},{7,15},{8,40},{9,1... | collective-permute-start | bytes 3145736 | tf_op jit(solution)/shard_map/ppermute | solution.py:38
  35.5 9.3 %collective-permute-start.6 = (bf16[256,1024]{1,0:T(8,128)(2,1)S(1)}, bf16[256,1024]{1,0:T(8,128)(2,1)S(1)}, u32[]{:S(2)}, u32[]{:S(2)}) collective-permute-start(bf16[256,1024]{1,0:T(8,128)(2,1)S(1)} %slice.37), channel_id=1, source_target_pairs={{0,96},{1,25},{2,98},{3,27},{4,100},{5,29},{6,102},{7,31},{8,104},... | collective-permute-start | bytes 1572872 | tf_op jit(solution)/shard_map/ppermute | solution.py:38
  35.5 10.5 %collective-permute-start.5 = (bf16[256,1024]{1,0:T(8,128)(2,1)S(1)}, bf16[256,1024]{1,0:T(8,128)(2,1)S(1)}, u32[]{:S(2)}, u32[]{:S(2)}) collective-permute-start(bf16[256,1024]{1,0:T(8,128)(2,1)S(1)} %slice.36), channel_id=1, source_target_pairs={{0,32},{1,9},{2,34},{3,11},{4,36},{5,13},{6,38},{7,15},{8,40},{9,1... | collective-permute-start | bytes 1572872 | tf_op jit(solution)/shard_map/ppermute | solution.py:38
  37.6 12.8 %collective-permute-start.9 = (bf16[512,512]{1,0:T(8,128)(2,1)S(1)}, bf16[512,512]{1,0:T(8,128)(2,1)S(1)}, u32[]{:S(2)}, u32[]{:S(2)}) collective-permute-start(bf16[512,512]{1,0:T(8,128)(2,1)S(1)} %pad_maximum_fusion.1.refs_0_), channel_id=1, source_target_pairs={{0,96},{1,25},{2,98},{3,27},{4,100},{5,29},{6,102},{7,31},{8,104},... | collective-permute-start | bytes 1572872 | tf_op jit(solution)/shard_map/ppermute | solution.py:38
  38.8 12.8 %collective-permute-start.8 = (bf16[512,512]{1,0:T(8,128)(2,1)S(1)}, bf16[512,512]{1,0:T(8,128)(2,1)S(1)}, u32[]{:S(2)}, u32[]{:S(2)}) collective-permute-start(bf16[512,512]{1,0:T(8,128)(2,1)S(1)} %pad_maximum_fusion.1.refs_0_), channel_id=1, source_target_pairs={{0,32},{1,9},{2,34},{3,11},{4,36},{5,13},{6,38},{7,15},{8,40},{9,1... | collective-permute-start | bytes 1572872 | tf_op jit(solution)/shard_map/ppermute | solution.py:38
  47.4 1.4 %collective-permute-start.7 = (f32[256,128]{1,0:T(8,128)S(1)}, f32[256,128]{1,0:T(8,128)S(1)}, u32[]{:S(2)}, u32[]{:S(2)}) collective-permute-start(f32[256,128]{1,0:T(8,128)S(1)} %get-tuple-element.43), channel_id=1, source_target_pairs={{0,1},{1,0},{2,3},{3,2},{4,5},{5,4},{6,7},{7,6},{8,9},{9,8},{10,11... | collective-permute-start | bytes 393224 | tf_op jit(solution)/shard_map/ppermute | solution.py:44
  51.6 5.1 %collective-permute-start.10 = (f32[256,128]{1,0:T(8,128)S(1)}, f32[256,128]{1,0:T(8,128)S(1)}, u32[]{:S(2)}, u32[]{:S(2)}) collective-permute-start(f32[256,128]{1,0:T(8,128)S(1)} %add.9), channel_id=1, source_target_pairs={{0,2},{1,7},{2,0},{3,5},{4,6},{5,3},{6,4},{7,1},{8,10},{9,15},{10,... | collective-permute-start | bytes 393224 | tf_op jit(solution)/shard_map/ppermute | solution.py:51
  56.8 6.3 %collective-permute-start.11 = (f32[256,128]{1,0:T(8,128)S(1)}, f32[256,128]{1,0:T(8,128)S(1)}, u32[]{:S(2)}, u32[]{:S(2)}) collective-permute-start(f32[256,128]{1,0:T(8,128)S(1)} %add.10), channel_id=1, source_target_pairs={{0,6},{1,3},{2,4},{3,1},{4,2},{5,7},{6,0},{7,5},{8,14},{9,11},{10,... | collective-permute-start | bytes 393224 | tf_op jit(solution)/shard_map/ppermute | solution.py:51
  59.7 6.4 %collective-permute-start.14 = (bf16[256,512]{1,0:T(8,128)(2,1)S(1)}, bf16[256,512]{1,0:T(8,128)(2,1)S(1)}, u32[]{:S(2)}, u32[]{:S(2)}) collective-permute-start(bf16[256,512]{1,0:T(8,128)(2,1)S(1)} %slice.39), channel_id=1, source_target_pairs={{0,96},{1,25},{2,98},{3,27},{4,100},{5,29},{6,102},{7,31},{8,104},... | collective-permute-start | bytes 786440 | tf_op jit(solution)/shard_map/ppermute | solution.py:38
  59.8 7.7 %collective-permute-start.13 = (bf16[256,512]{1,0:T(8,128)(2,1)S(1)}, bf16[256,512]{1,0:T(8,128)(2,1)S(1)}, u32[]{:S(2)}, u32[]{:S(2)}) collective-permute-start(bf16[256,512]{1,0:T(8,128)(2,1)S(1)} %slice.38), channel_id=1, source_target_pairs={{0,32},{1,9},{2,34},{3,11},{4,36},{5,13},{6,38},{7,15},{8,40},{9,1... | collective-permute-start | bytes 786440 | tf_op jit(solution)/shard_map/ppermute | solution.py:38
  63.1 4.4 %collective-permute-start.12 = (bf16[256,128]{1,0:T(8,128)(2,1)S(1)}, bf16[256,128]{1,0:T(8,128)(2,1)S(1)}, u32[]{:S(2)}, u32[]{:S(2)}) collective-permute-start(bf16[256,128]{1,0:T(8,128)(2,1)S(1)} %add_convert_fusion.mine_ref), channel_id=1, source_target_pairs={{0,1},{1,0},{2,3},{3,2},{4,5},{5,4},{6,7},{7,6},{8,9},{9,8},{10,11... | collective-permute-start | bytes 196616 | tf_op jit(solution)/shard_map/ppermute | solution.py:44

commit v7 on v6

--- a/solution.py
+++ b/solution.py
@@ -102,49 +102,47 @@
     )(ident.reshape(m // 128, 128), x)
 
 
-def base_kernel(half_ref, x_ref, w_ref, o_ref, xb, sems):
-    half, block = xb.shape[0], 256
-    count = half // block
-    copies = [
-        pltpu.make_async_copy(
-            x_ref.at[pl.ds(half + i * block, block)], xb.at[pl.ds(i * block, block)], sems.at[i]
-        )
-        for i in range(count)
-    ]
-    for copy in copies:
-        copy.start()
-
-    def multiply(rows, at):
-        o_ref[pl.ds(at, block), :] = jnp.dot(rows, w_ref[...], preferred_element_type=F32)
-
-    def first_rows(i, _):
-        at = pl.multiple_of(i * block, block)
-        multiply(half_ref[pl.ds(at, block), :], at)
+def multiply(x_ref, w_ref, o_ref, block=256):
+    def rows(i, _):
+        at = pl.ds(pl.multiple_of(i * block, block), block)
+        o_ref[at, :] = jnp.dot(x_ref[at, :], w_ref[...], preferred_element_type=F32)
         return 0
 
-    def other_rows(i, _):
-        at = pl.multiple_of(i * block, block)
-        multiply(xb[pl.ds(at, block), :], half + at)
-        return 0
-
-    lax.fori_loop(0, count, first_rows, 0)
-    for copy in copies:
-        copy.wait()
-    lax.fori_loop(0, count, other_rows, 0)
-
-
-def base_product(half, x, w):
-    (m, k), n = x.shape, w.shape[1]
+    lax.fori_loop(0, x_ref.shape[0] // block, rows, 0)
+
+
+def base_kernel(half_ref, w_ref, x_ref, o_ref, rest_ref, sem):
+    rows = rest_ref.shape[0]
+    copy = pltpu.make_async_copy(x_ref.at[pl.ds(rows, rows)], rest_ref, sem)
+    copy.start()
+    multiply(half_ref, w_ref, o_ref)
+    copy.wait()
+
+
+def base_first(half, w, x):
+    rows, n = half.shape[0], w.shape[1]
     return pl.pallas_call(
         base_kernel,
-        in_specs=[VMEM, HBM, VMEM],
+        in_specs=[VMEM, VMEM, HBM],
+        out_specs=[VMEM, VMEM],
+        out_shape=[jax.ShapeDtypeStruct((rows, n), F32), jax.ShapeDtypeStruct(half.shape, BF)],
+        scratch_shapes=[pltpu.SemaphoreType.DMA],
+        compiler_params=params(28),
+        cost_estimate=cost(5000000000, 1 << 20),
+        name="base_first",
+    )(half, w, x)
+
+
+def base_second(rest, w):
+    return pl.pallas_call(
+        multiply,
+        in_specs=[VMEM, VMEM],
         out_specs=VMEM,
-        out_shape=jax.ShapeDtypeStruct((m, n), F32),
-        scratch_shapes=[pltpu.VMEM((m // 2, k), BF), pltpu.SemaphoreType.DMA((m // 512,))],
-        compiler_params=params(22),
-        cost_estimate=cost(1 << 20, 1 << 20),
-        name="base",
-    )(half, x, w)
+        out_shape=jax.ShapeDtypeStruct((rest.shape[0], w.shape[1]), F32),
+        compiler_params=params(12),
+        cost_estimate=cost(5000000000, 1 << 20),
+        name="base_second",
+    )(rest, w)
 
 
 def shrink_kernel(groups, has_sum, last, code_ref, x_ref, *refs):
@@ -192,7 +190,7 @@
     )(*args)
 
 
-def expand_kernel(groups, code_ref, mine_ref, other_ref, base_ref, *refs):
+def expand_kernel(groups, code_ref, mine_ref, other_ref, top_ref, bottom_ref, *refs):
     b_refs, o_ref = refs[:-1], refs[-1]
     block = o_ref.shape[0]
     step = pl.program_id(0)
@@ -214,13 +212,17 @@
         d = jnp.dot(spread, b_ref[...], preferred_element_type=F32)
         delta = d if delta is None else delta + d
     delta = delta.astype(BF).astype(F32)
-    o_ref[...] = (base_ref[here, :] + adapter_scale * delta).astype(BF)
+    for i, base_ref in enumerate((top_ref, bottom_ref)):
+
+        @pl.when(step == i)
+        def _(base_ref=base_ref):
+            o_ref[...] = (base_ref[...] + adapter_scale * delta).astype(BF)
 
 
 def expand(code, mine, other, base, parts):
-    m, n = base.shape
-    block = m // 2
-    args = [code, mine, other, base] + [a for a, _ in parts]
+    block, n = base[0].shape
+    m = 2 * block
+    args = [code, mine, other, *base] + [a for a, _ in parts]
     return pl.pallas_call(
         functools.partial(expand_kernel, [places for _, places in parts]),
         grid=(2,),
@@ -237,11 +239,6 @@
     return lax.optimization_barrier(arrays)
 
 
-def forward(before, after):
-    half = before.shape[0] // 2
-    return second(before[:half], 1), second(after[half:], -1)
-
-
 def per_device(activations, token_adapter_index, query_matrix, down, up):
     down = jnp.swapaxes(down, 1, 2).reshape(128, -1)
     up = up.reshape(128, -1)
@@ -249,30 +246,36 @@
     row = lambda j, hops=HOPS: [(j, i) for i in hops]
 
     both = jnp.concatenate([down, up], axis=1)
-    near = [first(both, d) for d in (1, -1, 2)]
+    before, after = first(both, 1), first(both, -1)
     here, half, code = prepare(token_adapter_index, activations, width)
-    near, here, half, code = tie(near, here, half, code)
-    d_own = jnp.concatenate([down] + [a[:, :width] for a in near], axis=0)
-    u_own = jnp.concatenate([up] + [a[:, width:] for a in near], axis=0)
-
-    d_own, u_own = tie(d_own, u_own)
-    d_before, d_after = second(d_own, 1), second(d_own, -1)
-    base = base_product(half, activations, query_matrix)
-    d_before, d_after, base = tie(d_before, d_after, base)
-    d_far = forward(d_before, d_after)
-    groups = [([d_own], row(0)), ([d_before], row(-1)), ([d_after], row(1))]
+    both, here, half, code = tie(both, here, half, code)
+    far = first(both, 2)
+    close = jnp.concatenate([down, before[:, :width], after[:, :width]], axis=0)
+    a_before, a_after = second(close, 1), second(close, -1)
+    base, rest = base_first(half, query_matrix, activations)
+    far, base, rest = tie(far, base, rest)
+    d_far = far[:, :width]
+    u_own = jnp.concatenate([up] + [a[:, width:] for a in (before, after, far)], axis=0)
+    b_before, b_after = second(d_far, 1), second(d_far, -1)
+    d_own = jnp.concatenate([close, d_far], axis=0)
+    base = [base, base_second(rest, query_matrix)]
+    a_before, a_after, b_before, b_after, base[1] = tie(a_before, a_after, b_before, b_after, base[1])
+
+    d_two = [second(a_before[:256], 1), second(jnp.concatenate([a_after[256:], b_after]), -1)]
+    groups = [([d_own], row(0)), ([a_before, b_before], row(-1)), ([a_after, b_after], row(1))]
     total = shrink(code, here, groups, None, False, "shrink_near")
+    total, u_own = tie(total, u_own)
     u_before, u_after = second(u_own, 1), second(u_own, -1)
-    *d_far, total = tie(*d_far, total)
-    keep, give = shrink(code, here, [(d_far, row(2))], total, True, "shrink_far")
+    *d_two, total = tie(*d_two, total)
+    keep, give = shrink(code, here, [(d_two, row(2))], total, True, "shrink_far")
     keep = keep + other_core(give)
     keep, u_before, u_after = tie(keep, u_before, u_after)
-    u_far = forward(u_before, u_after)
+    u_two = [second(u_before[:256], 1), second(u_after[256:], -1)]
     keep = keep + pair(keep, 0)
     keep = keep + pair(keep, 1)
-    mine = keep.astype(BF)
+    mine, *u_two = tie(keep.astype(BF), *u_two)
     parts = [(u_own, row(0)), (u_before, row(-1)), (u_after, row(1))]
-    parts += [(a, row(2, hops)) for a, hops in zip(u_far, (HOPS[:2], HOPS[2:]))]
+    parts += [(a, row(2, hops)) for a, hops in zip(u_two, (HOPS[:2], HOPS[2:]))]
     return expand(code, mine, other_core(mine), base, parts)
 
 

time: 71.1 us -> 73.3 us (1.031); the launches traced: 70.9 us -> 72.1 us
  starting transfers between devices: 20.2 us -> 29.8 us
  waiting for transfers between devices: 26.4 us -> 17.2 us
    ppermute x8 -> x10, starting transfers between devices: 10.3 us -> 19.9 us  [second(): lax.ppermute(a, AXES, every(lambda x, y, z, c: (x + d, y, z, c) if c else...]
    ppermute x8 -> x10, waiting for transfers between devices: 16.7 us -> 10.4 us  [second(): lax.ppermute(a, AXES, every(lambda x, y, z, c: (x + d, y, z, c) if c else...]
    ppermute x3, waiting for transfers between devices: 3.56 us -> 0.71 us  [first(): lax.ppermute(a, AXES, every(lambda x, y, z, c: (x, y, z + d, c) if c else...]
    ppermute x2, waiting for transfers between devices: 1.34 us -> 2.59 us  [other_core(): return lax.ppermute(a, AXES, every(lambda x, y, z, c: (x, y, z, 1 - c)))]
    ppermute x2, waiting for transfers between devices: 4.74 us -> 3.58 us  [pair(): return lax.ppermute(a, AXES, every(to))]
    pallas_call x1 -> x2, Pallas kernels: 9.32 us -> 9.45 us  [the longest x1 4.81 us: base_first(): pl.pallas_call(base_kernel, in_specs=[VMEM, VMEM, HBM], out_specs=[VMEM,...]
  transfers between devices with their start and end apart: 15 -> 17, of which waited for: 12 -> 7; matrix products, arithmetic and copies ran while one was open for 0% -> 0% of each run, Pallas kernels for 26% -> 26%
where the time goes in v7:
time: 73.3 us; the launch traced here: 72.1 us
  starting transfers between devices  29.8 us (41%)
  Pallas kernels  22.5 us (31%)
  waiting for transfers between devices  17.2 us (23%)
  other arithmetic  1.3 us (2%)
  local copies, waits for them, and re-layouts  1.03 us (1%)
    ppermute x10, starting transfers between devices, second(): lax.ppermute(a, AXES, every(lambda x, y, z, c: (x + d, y, z, c) if c else...  19.9 us
    ppermute x10, waiting for transfers between devices, second(): lax.ppermute(a, AXES, every(lambda x, y, z, c: (x + d, y, z, c) if c else...  10.4 us
    ppermute x3, starting transfers between devices, first(): lax.ppermute(a, AXES, every(lambda x, y, z, c: (x, y, z + d, c) if c else...  5.28 us
    pallas_call x2, Pallas kernels, shrink(): pl.pallas_call(functools.partial(shrink_kernel, [(len(parts), places) for...  4.86 us
    pallas_call x1, Pallas kernels, base_first(): pl.pallas_call(base_kernel, in_specs=[VMEM, VMEM, HBM], out_specs=[VMEM,...  4.81 us
    pallas_call x1, Pallas kernels, base_second(): pl.pallas_call(multiply, in_specs=[VMEM, VMEM], out_specs=VMEM, out_shape...  4.64 us
    pallas_call x1, Pallas kernels, prepare(): pl.pallas_call(prep_kernel, in_specs=[VMEM, HBM], out_specs=[VMEM] * 3, o...  4.52 us
    ppermute x2, starting transfers between devices, pair(): return lax.ppermute(a, AXES, every(to))  4.48 us
  transfers between devices with their start and end apart: 17, of which 7 were waited for; matrix products, arithmetic and copies ran while one was open for 0% of the time, Pallas kernels for 26%

profile of v7, /device:TPU:0, one launch (start us, length us, event | category | flops | bytes accessed | tf_op | source)
XLA Modules:
  0.0 72.1 jit_solution(5141230792711789254)
XLA Ops:
  0.0 1.0 %pad_maximum_fusion.4 = bf16[128,1536]{1,0:T(8,128)(2,1)S(1)} fusion(bf16[128,512]{1,0:T(8,128)(2,1)} %bitcast.11, bf16[128,1024]{1,0:T(8,128)(2,1)} %bitcast.8), kind=kLoop, calls=%fused_computation.4 | loop fusion | flops 786432 | bytes 786432 | tf_op jit(solution)/shard_map/concatenate | solution.py:248
  1.1 1.6 %collective-permute-start = (bf16[128,1536]{1,0:T(8,128)(2,1)S(1)}, bf16[128,1536]{1,0:T(8,128)(2,1)S(1)}, u32[]{:S(2)}, u32[]{:S(2)}) collective-permute-start(bf16[128,1536]{1,0:T(8,128)(2,1)S(1)} %pad_maximum_fusion.4), channel_id=1, source_target_pairs={{0,8},{1,33},{2,10},{3,35},{4,12},{5,37},{6,14},{7,39},{8,16},{9,4... | collective-permute-start | bytes 1179656 | tf_op jit(solution)/shard_map/ppermute | solution.py:32
  2.7 1.7 %collective-permute-start.1 = (bf16[128,1536]{1,0:T(8,128)(2,1)S(1)}, bf16[128,1536]{1,0:T(8,128)(2,1)S(1)}, u32[]{:S(2)}, u32[]{:S(2)}) collective-permute-start(bf16[128,1536]{1,0:T(8,128)(2,1)S(1)} %pad_maximum_fusion.4), channel_id=1, source_target_pairs={{0,24},{1,97},{2,26},{3,99},{4,28},{5,101},{6,30},{7,103},{8,0},{9... | collective-permute-start | bytes 1179656 | tf_op jit(solution)/shard_map/ppermute | solution.py:32
  4.4 0.0 slice-start
  4.4 0.0 copy-start
  4.4 0.8 %copy-done = s32[1024,1]{0,1:T(1,128)S(1)} copy-done((s32[1024,1]{0,1:T(1,128)S(1)}, s32[1024,1]{0,1:T(1,128)}, u32[]{:S(2)}) %copy-start) | copy-done | bytes 4120
  5.2 0.0 copy-start.1
  5.2 0.0 slice-start.1
  5.2 4.5 %prepare.1 = (bf16[1024,1024]{1,0:T(8,128)(2,1)S(1)}, bf16[512,8192]{1,0:T(8,128)(2,1)S(1)}, s32[1024,128]{1,0:T(8,128)S(1)}) custom-call(s32[8,128]{1,0:T(8,128)S(1)} %bitcast.7, bf16[1024,8192]{1,0:T(8,128)(2,1)} %x_ref.3), custom_call_target="tpu_custom_call" | custom-call | bytes 1048576 | tf_op jit(solution)/shard_map/prepare/pallas_call | solution.py:89
  9.7 2.0 %collective-permute-start.4 = (bf16[128,1536]{1,0:T(8,128)(2,1)S(1)}, bf16[128,1536]{1,0:T(8,128)(2,1)S(1)}, u32[]{:S(2)}, u32[]{:S(2)}) collective-permute-start(bf16[128,1536]{1,0:T(8,128)(2,1)S(1)} %pad_maximum_fusion.4), channel_id=1, source_target_pairs={{0,16},{1,65},{2,18},{3,67},{4,20},{5,69},{6,22},{7,71},{8,24},{9,... | collective-permute-start | bytes 1179656 | tf_op jit(solution)/shard_map/ppermute | solution.py:32
  11.7 0.0 collective-permute-done
  11.7 0.0 collective-permute-done.1
  11.8 0.0 copy-done.1
  11.8 0.1 pad_maximum_fusion.1
  11.8 2.0 %collective-permute-start.2 = (bf16[384,1024]{1,0:T(8,128)(2,1)S(1)}, bf16[384,1024]{1,0:T(8,128)(2,1)S(1)}, u32[]{:S(2)}, u32[]{:S(2)}) collective-permute-start(bf16[384,1024]{1,0:T(8,128)(2,1)S(1)} %pad_maximum_fusion.1), channel_id=1, source_target_pairs={{0,32},{1,9},{2,34},{3,11},{4,36},{5,13},{6,38},{7,15},{8,40},{9,1... | collective-permute-start | bytes 2359304 | tf_op jit(solution)/shard_map/ppermute | solution.py:38
  13.8 2.2 %collective-permute-start.3 = (bf16[384,1024]{1,0:T(8,128)(2,1)S(1)}, bf16[384,1024]{1,0:T(8,128)(2,1)S(1)}, u32[]{:S(2)}, u32[]{:S(2)}) collective-permute-start(bf16[384,1024]{1,0:T(8,128)(2,1)S(1)} %pad_maximum_fusion.1), channel_id=1, source_target_pairs={{0,96},{1,25},{2,98},{3,27},{4,100},{5,29},{6,102},{7,31},{8,104},... | collective-permute-start | bytes 2359304 | tf_op jit(solution)/shard_map/ppermute | solution.py:38
  16.0 0.0 slice-done
  16.0 0.0 slice-done.1
  16.0 4.8 %base_first.1 = (f32[512,512]{1,0:T(8,128)S(1)}, bf16[512,8192]{1,0:T(8,128)(2,1)S(1)}) custom-call(bf16[512,8192]{1,0:T(8,128)(2,1)S(1)} %get-tuple-element.41.half_ref, bf16[8192,512]{1,0:T(8,128)(2,1)S(1)} %bitcast.6, bf16[1024,8192]{1,0:T(8,128)(2,1)} %x_ref.3), custom_call_target="tpu_custom_call" | custom-call | flops 5000000000 | bytes 1048576 | tf_op jit(solution)/shard_map/base_first/pallas_call | solution.py:124
  20.9 0.7 collective-permute-done.4
  21.6 3.2 %collective-permute-start.5 = (bf16[128,1024]{1,0:T(8,128)(2,1)S(1)}, bf16[128,1024]{1,0:T(8,128)(2,1)S(1)}, u32[]{:S(2)}, u32[]{:S(2)}) collective-permute-start(bf16[128,1024]{1,0:T(8,128)(2,1)S(1)} %slice.32), channel_id=1, source_target_pairs={{0,32},{1,9},{2,34},{3,11},{4,36},{5,13},{6,38},{7,15},{8,40},{9,1... | collective-permute-start | bytes 786440 | tf_op jit(solution)/shard_map/ppermute | solution.py:38
  24.8 2.8 %collective-permute-start.6 = (bf16[128,1024]{1,0:T(8,128)(2,1)S(1)}, bf16[128,1024]{1,0:T(8,128)(2,1)S(1)}, u32[]{:S(2)}, u32[]{:S(2)}) collective-permute-start(bf16[128,1024]{1,0:T(8,128)(2,1)S(1)} %slice.32), channel_id=1, source_target_pairs={{0,96},{1,25},{2,98},{3,27},{4,100},{5,29},{6,102},{7,31},{8,104},... | collective-permute-start | bytes 786440 | tf_op jit(solution)/shard_map/ppermute | solution.py:38
  27.6 4.6 %base_second.1.bottom_ref = f32[512,512]{1,0:T(8,128)S(1)} custom-call(bf16[512,8192]{1,0:T(8,128)(2,1)S(1)} %get-tuple-element.45.x_ref, bf16[8192,512]{1,0:T(8,128)(2,1)S(1)} %bitcast.6), custom_call_target="tpu_custom_call" | custom-call | flops 5000000000 | bytes 1048576 | tf_op jit(solution)/shard_map/base_second/pallas_call | solution.py:137
  32.2 0.0 collective-permute-done.5.refs_2_
  32.2 0.0 collective-permute-done.6.refs_4_
  32.2 0.0 collective-permute-done.2.refs_1_
  32.2 0.0 collective-permute-done.3.refs_3_
  32.3 0.0 copy-start.2
  32.3 3.0 %collective-permute-start.8 = (bf16[256,1024]{1,0:T(8,128)(2,1)S(1)}, bf16[256,1024]{1,0:T(8,128)(2,1)S(1)}, u32[]{:S(2)}, u32[]{:S(2)}) collective-permute-start(bf16[256,1024]{1,0:T(8,128)(2,1)S(1)} %pad_maximum_fusion.2), channel_id=1, source_target_pairs={{0,96},{1,25},{2,98},{3,27},{4,100},{5,29},{6,102},{7,31},{8,104},... | collective-permute-start | bytes 1572872 | tf_op jit(solution)/shard_map/ppermute | solution.py:38
  35.3 0.1 collective-permute-start.7
  35.4 0.1 pad_maximum_fusion.refs_0_
  35.6 0.0 copy-done.2
  35.6 3.5 %shrink_near.1.refs_2_ = f32[1024,128]{1,0:T(8,128)S(1)} custom-call(s32[1024,128]{1,0:T(8,128)S(1)} %get-tuple-element.38.code_ref, bf16[1024,1024]{1,0:T(8,128)(2,1)S(1)} %get-tuple-element.39.x_ref, bf16[512,1024]{1,0:T(8,128)(2,1)S(1)} %pad_maximum_fusion.refs_0_, bf16[384,1024]{1,0:T(8,128)(2,1)S(1)} %collective-permute-done.2.refs_1_, ...), custom_call_target="tpu_custom_call" | custom-call | flops 1048576 | bytes 1048576 | tf_op jit(solution)/shard_map/shrink_near/pallas_call | solution.py:180
  39.1 0.6 collective-permute-start.10
  39.7 2.7 %collective-permute-start.11 = (bf16[512,512]{1,0:T(8,128)(2,1)S(1)}, bf16[512,512]{1,0:T(8,128)(2,1)S(1)}, u32[]{:S(2)}, u32[]{:S(2)}) collective-permute-start(bf16[512,512]{1,0:T(8,128)(2,1)S(1)} %pad_maximum_fusion.3.refs_0_), channel_id=1, source_target_pairs={{0,96},{1,25},{2,98},{3,27},{4,100},{5,29},{6,102},{7,31},{8,104},... | collective-permute-start | bytes 1572872 | tf_op jit(solution)/shard_map/ppermute | solution.py:38
  42.5 0.0 collective-permute-done.8.refs_1_
  42.5 3.3 %collective-permute-done.7.refs_0_ = bf16[256,1024]{1,0:T(8,128)(2,1)S(1)} collective-permute-done((bf16[256,1024]{1,0:T(8,128)(2,1)S(1)}, bf16[256,1024]{1,0:T(8,128)(2,1)S(1)}, u32[]{:S(2)}, u32[]{:S(2)}) %collective-permute-start.7) | collective-permute-done | bytes 524320 | tf_op jit(solution)/shard_map/ppermute | solution.py:38
  45.8 1.4 %shrink_far.1 = (f32[256,128]{1,0:T(8,128)S(1)}, f32[256,128]{1,0:T(8,128)S(1)}) custom-call(s32[1024,128]{1,0:T(8,128)S(1)} %get-tuple-element.38.code_ref, bf16[1024,1024]{1,0:T(8,128)(2,1)S(1)} %get-tuple-element.39.x_ref, bf16[256,1024]{1,0:T(8,128)(2,1)S(1)} %collective-permute-done.7.refs_0_, bf16[256,1024]{1,0:T(8,128)(2,1)S(1)} %collective-permute-done.8.refs_1_, ...), custom_call_target="tpu_custom_call" | custom-call | flops 1048576 | bytes 1048576 | tf_op jit(solution)/shard_map/shrink_far/pallas_call | solution.py:180
  47.2 0.1 collective-permute-start.9
  47.3 1.3 %collective-permute-done.9 = f32[256,128]{1,0:T(8,128)S(1)} collective-permute-done((f32[256,128]{1,0:T(8,128)S(1)}, f32[256,128]{1,0:T(8,128)S(1)}, u32[]{:S(2)}, u32[]{:S(2)}) %collective-permute-start.9) | collective-permute-done | bytes 131104 | tf_op jit(solution)/shard_map/ppermute | solution.py:44
  48.6 2.8 %collective-permute-done.10.refs_1_ = bf16[512,512]{1,0:T(8,128)(2,1)S(1)} collective-permute-done((bf16[512,512]{1,0:T(8,128)(2,1)S(1)}, bf16[512,512]{1,0:T(8,128)(2,1)S(1)}, u32[]{:S(2)}, u32[]{:S(2)}) %collective-permute-start.10) | collective-permute-done | bytes 524320 | tf_op jit(solution)/shard_map/ppermute | solution.py:38
  51.4 0.0 collective-permute-done.11.refs_2_
  51.4 1.6 %collective-permute-start.12 = (f32[256,128]{1,0:T(8,128)S(1)}, f32[256,128]{1,0:T(8,128)S(1)}, u32[]{:S(2)}, u32[]{:S(2)}) collective-permute-start(f32[256,128]{1,0:T(8,128)S(1)} %add.9), channel_id=1, source_target_pairs={{0,2},{1,7},{2,0},{3,5},{4,6},{5,3},{6,4},{7,1},{8,10},{9,15},{10,... | collective-permute-start | bytes 393224 | tf_op jit(solution)/shard_map/ppermute | solution.py:51
  53.0 3.6 %collective-permute-done.12 = f32[256,128]{1,0:T(8,128)S(1)} collective-permute-done((f32[256,128]{1,0:T(8,128)S(1)}, f32[256,128]{1,0:T(8,128)S(1)}, u32[]{:S(2)}, u32[]{:S(2)}) %collective-permute-start.12) | collective-permute-done | bytes 131104 | tf_op jit(solution)/shard_map/ppermute | solution.py:51
  56.6 2.9 %collective-permute-start.13 = (f32[256,128]{1,0:T(8,128)S(1)}, f32[256,128]{1,0:T(8,128)S(1)}, u32[]{:S(2)}, u32[]{:S(2)}) collective-permute-start(f32[256,128]{1,0:T(8,128)S(1)} %add.10), channel_id=1, source_target_pairs={{0,6},{1,3},{2,4},{3,1},{4,2},{5,7},{6,0},{7,5},{8,14},{9,11},{10,... | collective-permute-start | bytes 393224 | tf_op jit(solution)/shard_map/ppermute | solution.py:51
  59.5 0.1 collective-permute-start.14
  59.6 3.3 %collective-permute-start.15 = (bf16[256,512]{1,0:T(8,128)(2,1)S(1)}, bf16[256,512]{1,0:T(8,128)(2,1)S(1)}, u32[]{:S(2)}, u32[]{:S(2)}) collective-permute-start(bf16[256,512]{1,0:T(8,128)(2,1)S(1)} %slice.39), channel_id=1, source_target_pairs={{0,96},{1,25},{2,98},{3,27},{4,100},{5,29},{6,102},{7,31},{8,104},... | collective-permute-start | bytes 786440 | tf_op jit(solution)/shard_map/ppermute | solution.py:38
  62.9 0.0 collective-permute-done.13
  62.9 4.2 %collective-permute-done.14.refs_3_ = bf16[256,512]{1,0:T(8,128)(2,1)S(1)} collective-permute-done((bf16[256,512]{1,0:T(8,128)(2,1)S(1)}, bf16[256,512]{1,0:T(8,128)(2,1)S(1)}, u32[]{:S(2)}, u32[]{:S(2)}) %collective-permute-start.14) | collective-permute-done | bytes 262176 | tf_op jit(solution)/shard_map/ppermute | solution.py:38
  67.2 0.0 collective-permute-done.15.refs_4_
  67.2 0.0 collective-permute-start.16
  67.2 1.3 %collective-permute-done.16.other_ref = bf16[256,128]{1,0:T(8,128)(2,1)S(1)} collective-permute-done((bf16[256,128]{1,0:T(8,128)(2,1)S(1)}, bf16[256,128]{1,0:T(8,128)(2,1)S(1)}, u32[]{:S(2)}, u32[]{:S(2)}) %collective-permute-start.16) | collective-permute-done | bytes 65568 | tf_op jit(solution)/shard_map/ppermute | solution.py:44
  68.4 3.7 %expand.1 = bf16[1024,512]{1,0:T(8,128)(2,1)} custom-call(s32[1024,128]{1,0:T(8,128)S(1)} %get-tuple-element.38.code_ref, bf16[256,128]{1,0:T(8,128)(2,1)S(1)} %add_convert_fusion.mine_ref, bf16[256,128]{1,0:T(8,128)(2,1)S(1)} %collective-permute-done.16.other_ref, f32[512,512]{1,0:T(8,128)S(1)} %get-tuple-element.61.top_ref, ...), custom_call_target="tpu_custom_call" | custom-call | flops 2147483648 | bytes 3145728 | tf_op jit(solution)/shard_map/expand/pallas_call | solution.py:226
  (16 shorter events, 0.3 us)
Async XLA Ops:
  1.1 10.7 %collective-permute-start = (bf16[128,1536]{1,0:T(8,128)(2,1)S(1)}, bf16[128,1536]{1,0:T(8,128)(2,1)S(1)}, u32[]{:S(2)}, u32[]{:S(2)}) collective-permute-start(bf16[128,1536]{1,0:T(8,128)(2,1)S(1)} %pad_maximum_fusion.4), channel_id=1, source_target_pairs={{0,8},{1,33},{2,10},{3,35},{4,12},{5,37},{6,14},{7,39},{8,16},{9,4... | collective-permute-start | bytes 1179656 | tf_op jit(solution)/shard_map/ppermute | solution.py:32
  2.7 9.0 %collective-permute-start.1 = (bf16[128,1536]{1,0:T(8,128)(2,1)S(1)}, bf16[128,1536]{1,0:T(8,128)(2,1)S(1)}, u32[]{:S(2)}, u32[]{:S(2)}) collective-permute-start(bf16[128,1536]{1,0:T(8,128)(2,1)S(1)} %pad_maximum_fusion.4), channel_id=1, source_target_pairs={{0,24},{1,97},{2,26},{3,99},{4,28},{5,101},{6,30},{7,103},{8,0},{9... | collective-permute-start | bytes 1179656 | tf_op jit(solution)/shard_map/ppermute | solution.py:32
  4.4 11.7 %slice-start = ((s8[8388608]{0:T(1024)(128)(4,1)}), s8[4194304]{0:T(1024)(128)(4,1)S(1)}, s32[]{:S(2)}) async-start(s8[8388608]{0:T(1024)(128)(4,1)} %bitcast.5), calls=%async_computation | async-start | bytes 8388608
  4.4 0.8 %copy-start = (s32[1024,1]{0,1:T(1,128)S(1)}, s32[1024,1]{0,1:T(1,128)}, u32[]{:S(2)}) copy-start(s32[1024,1]{0,1:T(1,128)} %param.6) | copy-start | bytes 12292
  5.2 6.6 %copy-start.1 = (bf16[2,1024,64]{1,2,0:T(8,128)(2,1)S(1)}, bf16[2,1024,64]{1,2,0:T(8,128)(2,1)}, u32[]{:S(2)}) copy-start(bf16[2,1024,64]{1,2,0:T(8,128)(2,1)} %param.8) | copy-start | bytes 786436
  5.2 10.8 %slice-start.1 = ((s8[8388608]{0:T(1024)(128)(4,1)}), s8[4194304]{0:T(1024)(128)(4,1)S(1)}, s32[]{:S(2)}) async-start(s8[8388608]{0:T(1024)(128)(4,1)} %bitcast.5), calls=%async_computation.1 | async-start | bytes 8388608
  9.7 11.8 %collective-permute-start.4 = (bf16[128,1536]{1,0:T(8,128)(2,1)S(1)}, bf16[128,1536]{1,0:T(8,128)(2,1)S(1)}, u32[]{:S(2)}, u32[]{:S(2)}) collective-permute-start(bf16[128,1536]{1,0:T(8,128)(2,1)S(1)} %pad_maximum_fusion.4), channel_id=1, source_target_pairs={{0,16},{1,65},{2,18},{3,67},{4,20},{5,69},{6,22},{7,71},{8,24},{9,... | collective-permute-start | bytes 1179656 | tf_op jit(solution)/shard_map/ppermute | solution.py:32
  11.8 20.4 %collective-permute-start.2 = (bf16[384,1024]{1,0:T(8,128)(2,1)S(1)}, bf16[384,1024]{1,0:T(8,128)(2,1)S(1)}, u32[]{:S(2)}, u32[]{:S(2)}) collective-permute-start(bf16[384,1024]{1,0:T(8,128)(2,1)S(1)} %pad_maximum_fusion.1), channel_id=1, source_target_pairs={{0,32},{1,9},{2,34},{3,11},{4,36},{5,13},{6,38},{7,15},{8,40},{9,1... | collective-permute-start | bytes 2359304 | tf_op jit(solution)/shard_map/ppermute | solution.py:38
  13.8 18.4 %collective-permute-start.3 = (bf16[384,1024]{1,0:T(8,128)(2,1)S(1)}, bf16[384,1024]{1,0:T(8,128)(2,1)S(1)}, u32[]{:S(2)}, u32[]{:S(2)}) collective-permute-start(bf16[384,1024]{1,0:T(8,128)(2,1)S(1)} %pad_maximum_fusion.1), channel_id=1, source_target_pairs={{0,96},{1,25},{2,98},{3,27},{4,100},{5,29},{6,102},{7,31},{8,104},... | collective-permute-start | bytes 2359304 | tf_op jit(solution)/shard_map/ppermute | solution.py:38
  21.6 10.6 %collective-permute-start.5 = (bf16[128,1024]{1,0:T(8,128)(2,1)S(1)}, bf16[128,1024]{1,0:T(8,128)(2,1)S(1)}, u32[]{:S(2)}, u32[]{:S(2)}) collective-permute-start(bf16[128,1024]{1,0:T(8,128)(2,1)S(1)} %slice.32), channel_id=1, source_target_pairs={{0,32},{1,9},{2,34},{3,11},{4,36},{5,13},{6,38},{7,15},{8,40},{9,1... | collective-permute-start | bytes 786440 | tf_op jit(solution)/shard_map/ppermute | solution.py:38
  24.8 7.5 %collective-permute-start.6 = (bf16[128,1024]{1,0:T(8,128)(2,1)S(1)}, bf16[128,1024]{1,0:T(8,128)(2,1)S(1)}, u32[]{:S(2)}, u32[]{:S(2)}) collective-permute-start(bf16[128,1024]{1,0:T(8,128)(2,1)S(1)} %slice.32), channel_id=1, source_target_pairs={{0,96},{1,25},{2,98},{3,27},{4,100},{5,29},{6,102},{7,31},{8,104},... | collective-permute-start | bytes 786440 | tf_op jit(solution)/shard_map/ppermute | solution.py:38
  32.3 3.2 %copy-start.2 = (bf16[2,64,512]{2,1,0:T(8,128)(2,1)S(1)}, bf16[2,64,512]{2,1,0:T(8,128)(2,1)}, u32[]{:S(2)}) copy-start(bf16[2,64,512]{2,1,0:T(8,128)(2,1)} %param.9) | copy-start | bytes 393220
  32.3 10.1 %collective-permute-start.8 = (bf16[256,1024]{1,0:T(8,128)(2,1)S(1)}, bf16[256,1024]{1,0:T(8,128)(2,1)S(1)}, u32[]{:S(2)}, u32[]{:S(2)}) collective-permute-start(bf16[256,1024]{1,0:T(8,128)(2,1)S(1)} %pad_maximum_fusion.2), channel_id=1, source_target_pairs={{0,96},{1,25},{2,98},{3,27},{4,100},{5,29},{6,102},{7,31},{8,104},... | collective-permute-start | bytes 1572872 | tf_op jit(solution)/shard_map/ppermute | solution.py:38
  35.3 10.5 %collective-permute-start.7 = (bf16[256,1024]{1,0:T(8,128)(2,1)S(1)}, bf16[256,1024]{1,0:T(8,128)(2,1)S(1)}, u32[]{:S(2)}, u32[]{:S(2)}) collective-permute-start(bf16[256,1024]{1,0:T(8,128)(2,1)S(1)} %slice.33), channel_id=1, source_target_pairs={{0,32},{1,9},{2,34},{3,11},{4,36},{5,13},{6,38},{7,15},{8,40},{9,1... | collective-permute-start | bytes 1572872 | tf_op jit(solution)/shard_map/ppermute | solution.py:38
  39.1 12.3 %collective-permute-start.10 = (bf16[512,512]{1,0:T(8,128)(2,1)S(1)}, bf16[512,512]{1,0:T(8,128)(2,1)S(1)}, u32[]{:S(2)}, u32[]{:S(2)}) collective-permute-start(bf16[512,512]{1,0:T(8,128)(2,1)S(1)} %pad_maximum_fusion.3.refs_0_), channel_id=1, source_target_pairs={{0,32},{1,9},{2,34},{3,11},{4,36},{5,13},{6,38},{7,15},{8,40},{9,1... | collective-permute-start | bytes 1572872 | tf_op jit(solution)/shard_map/ppermute | solution.py:38
  39.7 11.7 %collective-permute-start.11 = (bf16[512,512]{1,0:T(8,128)(2,1)S(1)}, bf16[512,512]{1,0:T(8,128)(2,1)S(1)}, u32[]{:S(2)}, u32[]{:S(2)}) collective-permute-start(bf16[512,512]{1,0:T(8,128)(2,1)S(1)} %pad_maximum_fusion.3.refs_0_), channel_id=1, source_target_pairs={{0,96},{1,25},{2,98},{3,27},{4,100},{5,29},{6,102},{7,31},{8,104},... | collective-permute-start | bytes 1572872 | tf_op jit(solution)/shard_map/ppermute | solution.py:38
  47.2 1.4 %collective-permute-start.9 = (f32[256,128]{1,0:T(8,128)S(1)}, f32[256,128]{1,0:T(8,128)S(1)}, u32[]{:S(2)}, u32[]{:S(2)}) collective-permute-start(f32[256,128]{1,0:T(8,128)S(1)} %get-tuple-element.55), channel_id=1, source_target_pairs={{0,1},{1,0},{2,3},{3,2},{4,5},{5,4},{6,7},{7,6},{8,9},{9,8},{10,11... | collective-permute-start | bytes 393224 | tf_op jit(solution)/shard_map/ppermute | solution.py:44
  51.4 5.2 %collective-permute-start.12 = (f32[256,128]{1,0:T(8,128)S(1)}, f32[256,128]{1,0:T(8,128)S(1)}, u32[]{:S(2)}, u32[]{:S(2)}) collective-permute-start(f32[256,128]{1,0:T(8,128)S(1)} %add.9), channel_id=1, source_target_pairs={{0,2},{1,7},{2,0},{3,5},{4,6},{5,3},{6,4},{7,1},{8,10},{9,15},{10,... | collective-permute-start | bytes 393224 | tf_op jit(solution)/shard_map/ppermute | solution.py:51
  56.6 6.3 %collective-permute-start.13 = (f32[256,128]{1,0:T(8,128)S(1)}, f32[256,128]{1,0:T(8,128)S(1)}, u32[]{:S(2)}, u32[]{:S(2)}) collective-permute-start(f32[256,128]{1,0:T(8,128)S(1)} %add.10), channel_id=1, source_target_pairs={{0,6},{1,3},{2,4},{3,1},{4,2},{5,7},{6,0},{7,5},{8,14},{9,11},{10,... | collective-permute-start | bytes 393224 | tf_op jit(solution)/shard_map/ppermute | solution.py:51
  59.5 7.7 %collective-permute-start.14 = (bf16[256,512]{1,0:T(8,128)(2,1)S(1)}, bf16[256,512]{1,0:T(8,128)(2,1)S(1)}, u32[]{:S(2)}, u32[]{:S(2)}) collective-permute-start(bf16[256,512]{1,0:T(8,128)(2,1)S(1)} %slice.38), channel_id=1, source_target_pairs={{0,32},{1,9},{2,34},{3,11},{4,36},{5,13},{6,38},{7,15},{8,40},{9,1... | collective-permute-start | bytes 786440 | tf_op jit(solution)/shard_map/ppermute | solution.py:38
  59.6 7.5 %collective-permute-start.15 = (bf16[256,512]{1,0:T(8,128)(2,1)S(1)}, bf16[256,512]{1,0:T(8,128)(2,1)S(1)}, u32[]{:S(2)}, u32[]{:S(2)}) collective-permute-start(bf16[256,512]{1,0:T(8,128)(2,1)S(1)} %slice.39), channel_id=1, source_target_pairs={{0,96},{1,25},{2,98},{3,27},{4,100},{5,29},{6,102},{7,31},{8,104},... | collective-permute-start | bytes 786440 | tf_op jit(solution)/shard_map/ppermute | solution.py:38
  67.2 1.3 %collective-permute-start.16 = (bf16[256,128]{1,0:T(8,128)(2,1)S(1)}, bf16[256,128]{1,0:T(8,128)(2,1)S(1)}, u32[]{:S(2)}, u32[]{:S(2)}) collective-permute-start(bf16[256,128]{1,0:T(8,128)(2,1)S(1)} %add_convert_fusion.mine_ref), channel_id=1, source_target_pairs={{0,1},{1,0},{2,3},{3,2},{4,5},{5,4},{6,7},{7,6},{8,9},{9,8},{10,11... | collective-permute-start | bytes 196616 | tf_op jit(solution)/shard_map/ppermute | solution.py:44

commit v8 on v7

--- a/solution.py
+++ b/solution.py
@@ -69,37 +69,49 @@
     return (rep // RING + dz + RING) % RING * RING + (rep % RING + dx + RING) % RING
 
 
-def prep_kernel(ident_ref, x_ref, here_ref, half_ref, code_ref, sems):
+def code_kernel(ident_ref, code_ref):
+    side = lax.broadcasted_iota(jnp.int32, (128, 128), 1) // 64
+    for r in range(ident_ref.shape[0]):
+        ident = jnp.broadcast_to(ident_ref[r : r + 1, :], (128, 128)).T
+        code_ref[128 * r : 128 * r + 128, :] = jnp.where((ident & 1) == side, ident >> 1, -1)
+
+
+def mask_code(ident):
+    m = ident.shape[0]
+    return pl.pallas_call(
+        code_kernel,
+        in_specs=[VMEM],
+        out_specs=VMEM,
+        out_shape=jax.ShapeDtypeStruct((m, 128), jnp.int32),
+        compiler_params=params(2),
+        cost_estimate=cost(1 << 20, 1 << 20),
+        name="mask_code",
+    )(ident.reshape(m // 128, 128))
+
+
+def fetch_kernel(x_ref, here_ref, half_ref, sems):
     width, rows = here_ref.shape[1], half_ref.shape[0]
     at = pl.multiple_of(lax.axis_index("tp") * width, width)
     here = pltpu.make_async_copy(x_ref.at[:, pl.ds(at, width)], here_ref, sems.at[0])
     half = pltpu.make_async_copy(x_ref.at[pl.ds(0, rows)], half_ref, sems.at[1])
     here.start()
     half.start()
-    side = lax.broadcasted_iota(jnp.int32, (128, 128), 1) // 64
-    for r in range(ident_ref.shape[0]):
-        ident = jnp.broadcast_to(ident_ref[r : r + 1, :], (128, 128)).T
-        code_ref[128 * r : 128 * r + 128, :] = jnp.where((ident & 1) == side, ident >> 1, -1)
     here.wait()
     half.wait()
 
 
-def prepare(ident, x, width):
+def fetch(x, width):
     m, k = x.shape
     return pl.pallas_call(
-        prep_kernel,
-        in_specs=[VMEM, HBM],
-        out_specs=[VMEM] * 3,
-        out_shape=[
-            jax.ShapeDtypeStruct((m, width), BF),
-            jax.ShapeDtypeStruct((m // 2, k), BF),
-            jax.ShapeDtypeStruct((m, 128), jnp.int32),
-        ],
+        fetch_kernel,
+        in_specs=[HBM],
+        out_specs=[VMEM] * 2,
+        out_shape=[jax.ShapeDtypeStruct((m, width), BF), jax.ShapeDtypeStruct((m // 2, k), BF)],
         scratch_shapes=[pltpu.SemaphoreType.DMA((2,))],
         compiler_params=params(28),
-        cost_estimate=cost(0, 1 << 20),
-        name="prepare",
-    )(ident.reshape(m // 128, 128), x)
+        cost_estimate=cost(1000000, 1 << 20),
+        name="fetch",
+    )(x)
 
 
 def multiply(x_ref, w_ref, o_ref, block=256):
@@ -128,7 +140,7 @@
         out_shape=[jax.ShapeDtypeStruct((rows, n), F32), jax.ShapeDtypeStruct(half.shape, BF)],
         scratch_shapes=[pltpu.SemaphoreType.DMA],
         compiler_params=params(28),
-        cost_estimate=cost(5000000000, 1 << 20),
+        cost_estimate=cost(1000000, 1 << 20),
         name="base_first",
     )(half, w, x)
 
@@ -140,7 +152,7 @@
         out_specs=VMEM,
         out_shape=jax.ShapeDtypeStruct((rest.shape[0], w.shape[1]), F32),
         compiler_params=params(12),
-        cost_estimate=cost(5000000000, 1 << 20),
+        cost_estimate=cost(1000000, 1 << 20),
         name="base_second",
     )(rest, w)
 
@@ -205,11 +217,11 @@
     left = (lane < 64) == (step == 0)
     rows = jnp.where(left, packed, pltpu.roll(packed, 64, 1))
     delta = None
-    for places, b_ref in zip(groups, b_refs):
+    for (places, ref_at, lanes), b_ref in zip(groups, b_refs):
         spread = jnp.concatenate(
             [jnp.where(code == owner(j, i), rows, 0.0).astype(BF) for j, i in places], axis=1
         )
-        d = jnp.dot(spread, b_ref[...], preferred_element_type=F32)
+        d = jnp.dot(spread, b_ref[ref_at:, lanes : lanes + o_ref.shape[1]], preferred_element_type=F32)
         delta = d if delta is None else delta + d
     delta = delta.astype(BF).astype(F32)
     for i, base_ref in enumerate((top_ref, bottom_ref)):
@@ -222,9 +234,9 @@
 def expand(code, mine, other, base, parts):
     block, n = base[0].shape
     m = 2 * block
-    args = [code, mine, other, *base] + [a for a, _ in parts]
-    return pl.pallas_call(
-        functools.partial(expand_kernel, [places for _, places in parts]),
+    args = [code, mine, other, *base] + [part[0] for part in parts]
+    return pl.pallas_call(
+        functools.partial(expand_kernel, [part[1:] for part in parts]),
         grid=(2,),
         in_specs=[VMEM] * len(args),
         out_specs=pl.BlockSpec((block, n), lambda i: (i, 0)),
@@ -242,40 +254,45 @@
 def per_device(activations, token_adapter_index, query_matrix, down, up):
     down = jnp.swapaxes(down, 1, 2).reshape(128, -1)
     up = up.reshape(128, -1)
-    width = down.shape[1]
+    width, columns = down.shape[1], up.shape[1]
     row = lambda j, hops=HOPS: [(j, i) for i in hops]
 
-    both = jnp.concatenate([down, up], axis=1)
-    before, after = first(both, 1), first(both, -1)
-    here, half, code = prepare(token_adapter_index, activations, width)
-    both, here, half, code = tie(both, here, half, code)
+    before, after = first(down, 1), first(down, -1)
+    code = mask_code(token_adapter_index)
+    both, code = tie(jnp.concatenate([down, up], axis=1), code)
     far = first(both, 2)
-    close = jnp.concatenate([down, before[:, :width], after[:, :width]], axis=0)
+    close = jnp.concatenate([both[:, :width], before, after], axis=0)
     a_before, a_after = second(close, 1), second(close, -1)
-    base, rest = base_first(half, query_matrix, activations)
-    far, base, rest = tie(far, base, rest)
+    here, half = fetch(tie(activations, before, after)[0], width)
+    late_up = tie(up, code)[0]
+    u_near = [first(late_up, d) for d in (1, -1)]
+
+    far, half, *u_near = tie(far, half, *u_near)
     d_far = far[:, :width]
-    u_own = jnp.concatenate([up] + [a[:, width:] for a in (before, after, far)], axis=0)
-    b_before, b_after = second(d_far, 1), second(d_far, -1)
-    d_own = jnp.concatenate([close, d_far], axis=0)
-    base = [base, base_second(rest, query_matrix)]
-    a_before, a_after, b_before, b_after, base[1] = tie(a_before, a_after, b_before, b_after, base[1])
-
-    d_two = [second(a_before[:256], 1), second(jnp.concatenate([a_after[256:], b_after]), -1)]
-    groups = [([d_own], row(0)), ([a_before, b_before], row(-1)), ([a_after, b_after], row(1))]
-    total = shrink(code, here, groups, None, False, "shrink_near")
-    total, u_own = tie(total, u_own)
-    u_before, u_after = second(u_own, 1), second(u_own, -1)
+    u_own = [jnp.concatenate([up, u_near[0]], axis=0), jnp.concatenate([u_near[1], far[:, width:]], axis=0)]
+    load = jnp.concatenate([d_far, jnp.concatenate(u_own, axis=1)], axis=0)
+    b_before, b_after = second(load, 1), second(load, -1)
+    top, rest = base_first(half, query_matrix, activations)
+    base = [top, base_second(rest, query_matrix)]
+    a_before, a_after, base[1] = tie(a_before, a_after, base[1])
+    groups = [([close, d_far], row(0)), ([a_before], row(-1, HOPS[:3])), ([a_after], row(1, HOPS[:3]))]
+    total = shrink(code, here, groups, None, False, "shrink_near", 20000000000)
+    d_two = [second(a_before[:256], 1), second(jnp.concatenate([a_after[256:], b_after[:128]]), -1)]
+    total, u_before, u_after = tie(total, b_before[128:, :columns], b_after[128:, columns:])
+    u_two = [second(u_before, 1), second(u_after, -1)]
+    groups = [([b_before[:128], b_after[:128]], [(-1, 2), (1, 2)])]
+    total = shrink(code, here, groups, total, False, "shrink_side")
     *d_two, total = tie(*d_two, total)
     keep, give = shrink(code, here, [(d_two, row(2))], total, True, "shrink_far")
+    keep, give, *u_two = tie(keep, give, *u_two)
     keep = keep + other_core(give)
-    keep, u_before, u_after = tie(keep, u_before, u_after)
-    u_two = [second(u_before[:256], 1), second(u_after[256:], -1)]
     keep = keep + pair(keep, 0)
     keep = keep + pair(keep, 1)
-    mine, *u_two = tie(keep.astype(BF), *u_two)
-    parts = [(u_own, row(0)), (u_before, row(-1)), (u_after, row(1))]
-    parts += [(a, row(2, hops)) for a, hops in zip(u_two, (HOPS[:2], HOPS[2:]))]
+    mine = keep.astype(BF)
+    parts = []
+    for j, a, at in ((0, load, 128), (-1, b_before, 128), (1, b_after, 128)):
+        parts += [(a, row(j, HOPS[:2]), at, 0), (a, row(j, HOPS[2:]), at, columns)]
+    parts += [(a, row(2, hops), 0, 0) for a, hops in zip(u_two, (HOPS[:2], HOPS[2:]))]
     return expand(code, mine, other_core(mine), base, parts)
 
 

time: 73.3 us -> 67.3 us (0.918)
  waiting for transfers between devices: 17.2 us -> 11.4 us
    ppermute x10 -> x8, waiting for transfers between devices: 10.4 us -> 2.21 us  [second(): lax.ppermute(a, AXES, every(lambda x, y, z, c: (x + d, y, z, c) if c else...]
    ppermute x10 -> x8, starting transfers between devices: 19.9 us -> 16.1 us  [second(): lax.ppermute(a, AXES, every(lambda x, y, z, c: (x + d, y, z, c) if c else...]
    ppermute x3 -> x5, starting transfers between devices: 5.28 us -> 8.45 us  [first(): lax.ppermute(a, AXES, every(lambda x, y, z, c: (x, y, z + d, c) if c else...]
    ppermute x2, waiting for transfers between devices: 3.58 us -> 6.57 us  [pair(): return lax.ppermute(a, AXES, every(to))]
    pallas_call x2 -> x3, Pallas kernels: 4.86 us -> 5.55 us  [shrink(): pl.pallas_call(functools.partial(shrink_kernel, [(len(parts), places) for...]
    pallas_call x2 -> x3, Pallas kernels: 8.21 us -> 7.91 us  [the longest x1 4.05 us: fetch(): pl.pallas_call(fetch_kernel, in_specs=[HBM], out_specs=[VMEM] * 2, out_sh...]
  transfers between devices with their start and end apart: 17 -> 17, of which waited for: 7 -> 5; matrix products, arithmetic and copies ran while one was open for 0% -> 2% of each run, Pallas kernels for 26% -> 29%
where the time goes in v8:
time: 67.3 us; the launch traced here: 66 us
  starting transfers between devices  29.4 us (44%)
  Pallas kernels  22.8 us (34%)
  waiting for transfers between devices  11.4 us (17%)
  other arithmetic  1.28 us (2%)
  local copies, waits for them, and re-layouts  0.88 us (1%)
    ppermute x8, starting transfers between devices, second(): lax.ppermute(a, AXES, every(lambda x, y, z, c: (x + d, y, z, c) if c else...  16.1 us
    ppermute x5, starting transfers between devices, first(): lax.ppermute(a, AXES, every(lambda x, y, z, c: (x, y, z + d, c) if c else...  8.45 us
    ppermute x2, waiting for transfers between devices, pair(): return lax.ppermute(a, AXES, every(to))  6.57 us
    pallas_call x3, Pallas kernels, shrink(): pl.pallas_call(functools.partial(shrink_kernel, [(len(parts), places) for...  5.55 us
    ppermute x2, starting transfers between devices, pair(): return lax.ppermute(a, AXES, every(to))  4.74 us
    pallas_call x1, Pallas kernels, base_first(): pl.pallas_call(base_kernel, in_specs=[VMEM, VMEM, HBM], out_specs=[VMEM,...  4.66 us
    pallas_call x1, Pallas kernels, base_second(): pl.pallas_call(multiply, in_specs=[VMEM, VMEM], out_specs=VMEM, out_shape...  4.64 us
    pallas_call x1, Pallas kernels, fetch(): pl.pallas_call(fetch_kernel, in_specs=[HBM], out_specs=[VMEM] * 2, out_sh...  4.05 us
  transfers between devices with their start and end apart: 17, of which 5 were waited for; matrix products, arithmetic and copies ran while one was open for 2% of the time, Pallas kernels for 29%

profile of v8, /device:TPU:0, one launch (start us, length us, event | category | flops | bytes accessed | tf_op | source)
XLA Modules:
  0.0 66.0 jit_solution(3787602020411266663)
XLA Ops:
  0.0 1.6 %collective-permute-start = (bf16[128,1024]{1,0:T(8,128)(2,1)}, bf16[128,1024]{1,0:T(8,128)(2,1)S(1)}, u32[]{:S(2)}, u32[]{:S(2)}) collective-permute-start(bf16[128,1024]{1,0:T(8,128)(2,1)} %bitcast.12), channel_id=1, source_target_pairs={{0,8},{1,33},{2,10},{3,35},{4,12},{5,37},{6,14},{7,39},{8,16},{9,4... | collective-permute-start | bytes 786440 | tf_op jit(solution)/shard_map/ppermute | solution.py:32
  1.6 1.7 %collective-permute-start.1 = (bf16[128,1024]{1,0:T(8,128)(2,1)}, bf16[128,1024]{1,0:T(8,128)(2,1)S(1)}, u32[]{:S(2)}, u32[]{:S(2)}) collective-permute-start(bf16[128,1024]{1,0:T(8,128)(2,1)} %bitcast.13), channel_id=1, source_target_pairs={{0,24},{1,97},{2,26},{3,99},{4,28},{5,101},{6,30},{7,103},{8,0},{9... | collective-permute-start | bytes 786440 | tf_op jit(solution)/shard_map/ppermute | solution.py:32
  3.2 1.1 %pad_maximum_fusion.2 = bf16[128,1536]{1,0:T(8,128)(2,1)S(1)} fusion(bf16[128,512]{1,0:T(8,128)(2,1)} %bitcast.8, bf16[128,1024]{1,0:T(8,128)(2,1)} %bitcast.14), kind=kLoop, calls=%fused_computation.3 | loop fusion | flops 786432 | bytes 786432 | tf_op jit(solution)/shard_map/concatenate | solution.py:262
  4.3 0.0 copy-start
  4.3 0.7 %copy-done = s32[1024,1]{0,1:T(1,128)S(1)} copy-done((s32[1024,1]{0,1:T(1,128)S(1)}, s32[1024,1]{0,1:T(1,128)}, u32[]{:S(2)}) %copy-start) | copy-done | bytes 4120
  5.0 0.2 mask_code.1.code_ref
  5.2 2.0 %collective-permute-start.4 = (bf16[128,1536]{1,0:T(8,128)(2,1)S(1)}, bf16[128,1536]{1,0:T(8,128)(2,1)S(1)}, u32[]{:S(2)}, u32[]{:S(2)}) collective-permute-start(bf16[128,1536]{1,0:T(8,128)(2,1)S(1)} %pad_maximum_fusion.2), channel_id=1, source_target_pairs={{0,16},{1,65},{2,18},{3,67},{4,20},{5,69},{6,22},{7,71},{8,24},{9,... | collective-permute-start | bytes 1179656 | tf_op jit(solution)/shard_map/ppermute | solution.py:32
  7.2 0.6 collective-permute-start.5
  7.8 2.6 %collective-permute-start.6 = (bf16[128,512]{1,0:T(8,128)(2,1)}, bf16[128,512]{1,0:T(8,128)(2,1)S(1)}, u32[]{:S(2)}, u32[]{:S(2)}) collective-permute-start(bf16[128,512]{1,0:T(8,128)(2,1)} %bitcast.10), channel_id=1, source_target_pairs={{0,24},{1,97},{2,26},{3,99},{4,28},{5,101},{6,30},{7,103},{8,0},{9... | collective-permute-start | bytes 393224 | tf_op jit(solution)/shard_map/ppermute | solution.py:32
  10.4 0.0 collective-permute-done
  10.4 0.0 collective-permute-done.1
  10.5 0.0 slice-start
  10.5 0.1 pad_maximum_fusion.refs_0_
  10.5 0.0 copy-start.1
  10.5 0.0 slice-start.1
  10.6 2.0 %collective-permute-start.2 = (bf16[384,1024]{1,0:T(8,128)(2,1)S(1)}, bf16[384,1024]{1,0:T(8,128)(2,1)S(1)}, u32[]{:S(2)}, u32[]{:S(2)}) collective-permute-start(bf16[384,1024]{1,0:T(8,128)(2,1)S(1)} %pad_maximum_fusion.refs_0_), channel_id=1, source_target_pairs={{0,32},{1,9},{2,34},{3,11},{4,36},{5,13},{6,38},{7,15},{8,40},{9,1... | collective-permute-start | bytes 2359304 | tf_op jit(solution)/shard_map/ppermute | solution.py:38
  12.5 2.2 %collective-permute-start.3 = (bf16[384,1024]{1,0:T(8,128)(2,1)S(1)}, bf16[384,1024]{1,0:T(8,128)(2,1)S(1)}, u32[]{:S(2)}, u32[]{:S(2)}) collective-permute-start(bf16[384,1024]{1,0:T(8,128)(2,1)S(1)} %pad_maximum_fusion.refs_0_), channel_id=1, source_target_pairs={{0,96},{1,25},{2,98},{3,27},{4,100},{5,29},{6,102},{7,31},{8,104},... | collective-permute-start | bytes 2359304 | tf_op jit(solution)/shard_map/ppermute | solution.py:38
  14.7 4.0 %fetch.1 = (bf16[1024,1024]{1,0:T(8,128)(2,1)S(1)}, bf16[512,8192]{1,0:T(8,128)(2,1)S(1)}) custom-call(bf16[1024,8192]{1,0:T(8,128)(2,1)} %x_ref.2), custom_call_target="tpu_custom_call" | custom-call | flops 1000000 | bytes 1048576 | tf_op jit(solution)/shard_map/fetch/pallas_call | solution.py:105
  18.8 0.0 collective-permute-done.5
  18.8 0.0 collective-permute-done.6
  18.8 0.0 collective-permute-done.4
  18.9 0.0 copy-done.1
  18.9 0.1 maximum_maximum_fusion.refs_0_.refs_1_
  19.0 4.8 %collective-permute-start.8 = (bf16[384,1024]{1,0:T(8,128)(2,1)S(1)}, bf16[384,1024]{1,0:T(8,128)(2,1)S(1)}, u32[]{:S(2)}, u32[]{:S(2)}) collective-permute-start(bf16[384,1024]{1,0:T(8,128)(2,1)S(1)} %maximum_maximum_fusion.refs_0_.refs_1_), channel_id=1, source_target_pairs={{0,96},{1,25},{2,98},{3,27},{4,100},{5,29},{6,102},{7,31},{8,104},... | collective-permute-start | bytes 2359304 | tf_op jit(solution)/shard_map/ppermute | solution.py:38
  23.8 0.0 collective-permute-start.10
  23.8 0.0 slice-done
  23.8 0.0 slice-done.1
  23.8 4.7 %base_first.1 = (f32[512,512]{1,0:T(8,128)S(1)}, bf16[512,8192]{1,0:T(8,128)(2,1)S(1)}) custom-call(bf16[512,8192]{1,0:T(8,128)(2,1)S(1)} %get-tuple-element.38.half_ref, bf16[8192,512]{1,0:T(8,128)(2,1)S(1)} %bitcast.6, bf16[1024,8192]{1,0:T(8,128)(2,1)} %x_ref.2), custom_call_target="tpu_custom_call" | custom-call | flops 1000000 | bytes 1048576 | tf_op jit(solution)/shard_map/base_first/pallas_call | solution.py:136
  28.5 4.6 %base_second.1.bottom_ref = f32[512,512]{1,0:T(8,128)S(1)} custom-call(bf16[512,8192]{1,0:T(8,128)(2,1)S(1)} %get-tuple-element.39.x_ref, bf16[8192,512]{1,0:T(8,128)(2,1)S(1)} %bitcast.6), custom_call_target="tpu_custom_call" | custom-call | flops 1000000 | bytes 1048576 | tf_op jit(solution)/shard_map/base_second/pallas_call | solution.py:149
  33.1 0.0 collective-permute-done.2.refs_2_
  33.1 0.0 collective-permute-done.3.refs_3_
  33.2 0.1 collective-permute-start.7
  33.3 0.0 collective-permute-done.8.refs_4_.refs_5_
  33.4 3.7 %collective-permute-start.9 = (bf16[256,1024]{1,0:T(8,128)(2,1)S(1)}, bf16[256,1024]{1,0:T(8,128)(2,1)S(1)}, u32[]{:S(2)}, u32[]{:S(2)}) collective-permute-start(bf16[256,1024]{1,0:T(8,128)(2,1)S(1)} %pad_maximum_fusion.1), channel_id=1, source_target_pairs={{0,96},{1,25},{2,98},{3,27},{4,100},{5,29},{6,102},{7,31},{8,104},... | collective-permute-start | bytes 1572872 | tf_op jit(solution)/shard_map/ppermute | solution.py:38
  37.1 3.5 %shrink_near.1.refs_2_ = f32[1024,128]{1,0:T(8,128)S(1)} custom-call(s32[1024,128]{1,0:T(8,128)S(1)} %mask_code.1.code_ref, bf16[1024,1024]{1,0:T(8,128)(2,1)S(1)} %get-tuple-element.34.x_ref, bf16[384,1024]{1,0:T(8,128)(2,1)S(1)} %pad_maximum_fusion.refs_0_, bf16[128,1024]{1,0:T(8,128)(2,1)S(1)} %slice.31.refs_1_, ...), custom_call_target="tpu_custom_call" | custom-call | flops 20000000000 | bytes 1048576 | tf_op jit(solution)/shard_map/shrink_near/pallas_call | solution.py:192
  40.6 0.0 collective-permute-done.10.refs_2_.refs_3_
  40.6 0.1 collective-permute-start.11
  40.7 3.2 %collective-permute-start.12 = (bf16[256,512]{1,0:T(8,128)(2,1)S(1)}, bf16[256,512]{1,0:T(8,128)(2,1)S(1)}, u32[]{:S(2)}, u32[]{:S(2)}) collective-permute-start(bf16[256,512]{1,0:T(8,128)(2,1)S(1)} %slice.40), channel_id=1, source_target_pairs={{0,96},{1,25},{2,98},{3,27},{4,100},{5,29},{6,102},{7,31},{8,104},... | collective-permute-start | bytes 786440 | tf_op jit(solution)/shard_map/ppermute | solution.py:38
  44.0 0.7 %shrink_side.1.refs_2_ = f32[1024,128]{1,0:T(8,128)S(1)} custom-call(s32[1024,128]{1,0:T(8,128)S(1)} %mask_code.1.code_ref, bf16[1024,1024]{1,0:T(8,128)(2,1)S(1)} %get-tuple-element.34.x_ref, bf16[128,1024]{1,0:T(8,128)(2,1)S(1)} %slice.38.refs_0_, bf16[128,1024]{1,0:T(8,128)(2,1)S(1)} %slice.37.refs_1_, f32[1024,128]{1,0:T(8,128)S(1)} %shrink_near.1.refs_2_), custom_call_target="tpu_custom_call" | custom-call | flops 1048576 | bytes 1048576 | tf_op jit(solution)/shard_map/shrink_side/pallas_call | solution.py:192
  44.7 0.0 collective-permute-done.7.refs_0_
  44.7 0.0 collective-permute-done.9.refs_1_
  44.7 1.4 %shrink_far.1 = (f32[256,128]{1,0:T(8,128)S(1)}, f32[256,128]{1,0:T(8,128)S(1)}) custom-call(s32[1024,128]{1,0:T(8,128)S(1)} %mask_code.1.code_ref, bf16[1024,1024]{1,0:T(8,128)(2,1)S(1)} %get-tuple-element.34.x_ref, bf16[256,1024]{1,0:T(8,128)(2,1)S(1)} %collective-permute-done.7.refs_0_, bf16[256,1024]{1,0:T(8,128)(2,1)S(1)} %collective-permute-done.9.refs_1_, ...), custom_call_target="tpu_custom_call" | custom-call | flops 1048576 | bytes 1048576 | tf_op jit(solution)/shard_map/shrink_far/pallas_call | solution.py:192
  46.1 2.2 %collective-permute-done.11.refs_6_ = bf16[256,512]{1,0:T(8,128)(2,1)S(1)} collective-permute-done((bf16[256,512]{1,0:T(8,128)(2,1)S(1)}, bf16[256,512]{1,0:T(8,128)(2,1)S(1)}, u32[]{:S(2)}, u32[]{:S(2)}) %collective-permute-start.11) | collective-permute-done | bytes 262176 | tf_op jit(solution)/shard_map/ppermute | solution.py:38
  48.3 0.0 collective-permute-done.12.refs_7_
  48.3 0.0 collective-permute-start.13
  48.3 1.3 %collective-permute-done.13 = f32[256,128]{1,0:T(8,128)S(1)} collective-permute-done((f32[256,128]{1,0:T(8,128)S(1)}, f32[256,128]{1,0:T(8,128)S(1)}, u32[]{:S(2)}, u32[]{:S(2)}) %collective-permute-start.13) | collective-permute-done | bytes 131104 | tf_op jit(solution)/shard_map/ppermute | solution.py:44
  49.7 1.6 %collective-permute-start.14 = (f32[256,128]{1,0:T(8,128)S(1)}, f32[256,128]{1,0:T(8,128)S(1)}, u32[]{:S(2)}, u32[]{:S(2)}) collective-permute-start(f32[256,128]{1,0:T(8,128)S(1)} %add.9), channel_id=1, source_target_pairs={{0,2},{1,7},{2,0},{3,5},{4,6},{5,3},{6,4},{7,1},{8,10},{9,15},{10,... | collective-permute-start | bytes 393224 | tf_op jit(solution)/shard_map/ppermute | solution.py:51
  51.3 3.4 %collective-permute-done.14 = f32[256,128]{1,0:T(8,128)S(1)} collective-permute-done((f32[256,128]{1,0:T(8,128)S(1)}, f32[256,128]{1,0:T(8,128)S(1)}, u32[]{:S(2)}, u32[]{:S(2)}) %collective-permute-start.14) | collective-permute-done | bytes 131104 | tf_op jit(solution)/shard_map/ppermute | solution.py:51
  54.7 3.1 %collective-permute-start.15 = (f32[256,128]{1,0:T(8,128)S(1)}, f32[256,128]{1,0:T(8,128)S(1)}, u32[]{:S(2)}, u32[]{:S(2)}) collective-permute-start(f32[256,128]{1,0:T(8,128)S(1)} %add.10), channel_id=1, source_target_pairs={{0,6},{1,3},{2,4},{3,1},{4,2},{5,7},{6,0},{7,5},{8,14},{9,11},{10,... | collective-permute-start | bytes 393224 | tf_op jit(solution)/shard_map/ppermute | solution.py:51
  57.8 3.2 %collective-permute-done.15 = f32[256,128]{1,0:T(8,128)S(1)} collective-permute-done((f32[256,128]{1,0:T(8,128)S(1)}, f32[256,128]{1,0:T(8,128)S(1)}, u32[]{:S(2)}, u32[]{:S(2)}) %collective-permute-start.15) | collective-permute-done | bytes 131104 | tf_op jit(solution)/shard_map/ppermute | solution.py:51
  61.0 0.1 collective-permute-start.16
  61.1 1.2 %collective-permute-done.16.other_ref = bf16[256,128]{1,0:T(8,128)(2,1)S(1)} collective-permute-done((bf16[256,128]{1,0:T(8,128)(2,1)S(1)}, bf16[256,128]{1,0:T(8,128)(2,1)S(1)}, u32[]{:S(2)}, u32[]{:S(2)}) %collective-permute-start.16) | collective-permute-done | bytes 65568 | tf_op jit(solution)/shard_map/ppermute | solution.py:44
  62.3 3.7 %expand.1 = bf16[1024,512]{1,0:T(8,128)(2,1)} custom-call(s32[1024,128]{1,0:T(8,128)S(1)} %mask_code.1.code_ref, bf16[256,128]{1,0:T(8,128)(2,1)S(1)} %add_convert_fusion.mine_ref, bf16[256,128]{1,0:T(8,128)(2,1)S(1)} %collective-permute-done.16.other_ref, f32[512,512]{1,0:T(8,128)S(1)} %get-tuple-element.55.top_ref, f32[512,512]{1,0:T(8,128)S(1)} %base_second.1.bottom_ref, ...), custom_call_target="tpu_custom_call" | custom-call | flops 2147483648 | bytes 3145728 | tf_op jit(solution)/shard_map/expand/pallas_call | solution.py:238
  (14 shorter events, 0.3 us)
Async XLA Ops:
  0.0 10.4 %collective-permute-start = (bf16[128,1024]{1,0:T(8,128)(2,1)}, bf16[128,1024]{1,0:T(8,128)(2,1)S(1)}, u32[]{:S(2)}, u32[]{:S(2)}) collective-permute-start(bf16[128,1024]{1,0:T(8,128)(2,1)} %bitcast.12), channel_id=1, source_target_pairs={{0,8},{1,33},{2,10},{3,35},{4,12},{5,37},{6,14},{7,39},{8,16},{9,4... | collective-permute-start | bytes 786440 | tf_op jit(solution)/shard_map/ppermute | solution.py:32
  1.6 8.9 %collective-permute-start.1 = (bf16[128,1024]{1,0:T(8,128)(2,1)}, bf16[128,1024]{1,0:T(8,128)(2,1)S(1)}, u32[]{:S(2)}, u32[]{:S(2)}) collective-permute-start(bf16[128,1024]{1,0:T(8,128)(2,1)} %bitcast.13), channel_id=1, source_target_pairs={{0,24},{1,97},{2,26},{3,99},{4,28},{5,101},{6,30},{7,103},{8,0},{9... | collective-permute-start | bytes 786440 | tf_op jit(solution)/shard_map/ppermute | solution.py:32
  4.3 0.7 %copy-start = (s32[1024,1]{0,1:T(1,128)S(1)}, s32[1024,1]{0,1:T(1,128)}, u32[]{:S(2)}) copy-start(s32[1024,1]{0,1:T(1,128)} %param.6) | copy-start | bytes 12292
  5.2 13.6 %collective-permute-start.4 = (bf16[128,1536]{1,0:T(8,128)(2,1)S(1)}, bf16[128,1536]{1,0:T(8,128)(2,1)S(1)}, u32[]{:S(2)}, u32[]{:S(2)}) collective-permute-start(bf16[128,1536]{1,0:T(8,128)(2,1)S(1)} %pad_maximum_fusion.2), channel_id=1, source_target_pairs={{0,16},{1,65},{2,18},{3,67},{4,20},{5,69},{6,22},{7,71},{8,24},{9,... | collective-permute-start | bytes 1179656 | tf_op jit(solution)/shard_map/ppermute | solution.py:32
  7.2 11.6 %collective-permute-start.5 = (bf16[128,512]{1,0:T(8,128)(2,1)}, bf16[128,512]{1,0:T(8,128)(2,1)S(1)}, u32[]{:S(2)}, u32[]{:S(2)}) collective-permute-start(bf16[128,512]{1,0:T(8,128)(2,1)} %bitcast.9), channel_id=1, source_target_pairs={{0,8},{1,33},{2,10},{3,35},{4,12},{5,37},{6,14},{7,39},{8,16},{9,4... | collective-permute-start | bytes 393224 | tf_op jit(solution)/shard_map/ppermute | solution.py:32
  7.8 11.0 %collective-permute-start.6 = (bf16[128,512]{1,0:T(8,128)(2,1)}, bf16[128,512]{1,0:T(8,128)(2,1)S(1)}, u32[]{:S(2)}, u32[]{:S(2)}) collective-permute-start(bf16[128,512]{1,0:T(8,128)(2,1)} %bitcast.10), channel_id=1, source_target_pairs={{0,24},{1,97},{2,26},{3,99},{4,28},{5,101},{6,30},{7,103},{8,0},{9... | collective-permute-start | bytes 393224 | tf_op jit(solution)/shard_map/ppermute | solution.py:32
  10.5 13.3 %slice-start = ((s8[8388608]{0:T(1024)(128)(4,1)}), s8[4194304]{0:T(1024)(128)(4,1)S(1)}, s32[]{:S(2)}) async-start(s8[8388608]{0:T(1024)(128)(4,1)} %bitcast.5), calls=%async_computation | async-start | bytes 8388608
  10.5 8.3 %copy-start.1 = (bf16[2,64,512]{2,1,0:T(8,128)(2,1)S(1)}, bf16[2,64,512]{2,1,0:T(8,128)(2,1)}, u32[]{:S(2)}) copy-start(bf16[2,64,512]{2,1,0:T(8,128)(2,1)} %param.9) | copy-start | bytes 393220
  10.5 13.3 %slice-start.1 = ((s8[8388608]{0:T(1024)(128)(4,1)}), s8[4194304]{0:T(1024)(128)(4,1)S(1)}, s32[]{:S(2)}) async-start(s8[8388608]{0:T(1024)(128)(4,1)} %bitcast.5), calls=%async_computation.1 | async-start | bytes 8388608
  10.6 22.6 %collective-permute-start.2 = (bf16[384,1024]{1,0:T(8,128)(2,1)S(1)}, bf16[384,1024]{1,0:T(8,128)(2,1)S(1)}, u32[]{:S(2)}, u32[]{:S(2)}) collective-permute-start(bf16[384,1024]{1,0:T(8,128)(2,1)S(1)} %pad_maximum_fusion.refs_0_), channel_id=1, source_target_pairs={{0,32},{1,9},{2,34},{3,11},{4,36},{5,13},{6,38},{7,15},{8,40},{9,1... | collective-permute-start | bytes 2359304 | tf_op jit(solution)/shard_map/ppermute | solution.py:38
  12.5 20.6 %collective-permute-start.3 = (bf16[384,1024]{1,0:T(8,128)(2,1)S(1)}, bf16[384,1024]{1,0:T(8,128)(2,1)S(1)}, u32[]{:S(2)}, u32[]{:S(2)}) collective-permute-start(bf16[384,1024]{1,0:T(8,128)(2,1)S(1)} %pad_maximum_fusion.refs_0_), channel_id=1, source_target_pairs={{0,96},{1,25},{2,98},{3,27},{4,100},{5,29},{6,102},{7,31},{8,104},... | collective-permute-start | bytes 2359304 | tf_op jit(solution)/shard_map/ppermute | solution.py:38
  19.0 14.3 %collective-permute-start.8 = (bf16[384,1024]{1,0:T(8,128)(2,1)S(1)}, bf16[384,1024]{1,0:T(8,128)(2,1)S(1)}, u32[]{:S(2)}, u32[]{:S(2)}) collective-permute-start(bf16[384,1024]{1,0:T(8,128)(2,1)S(1)} %maximum_maximum_fusion.refs_0_.refs_1_), channel_id=1, source_target_pairs={{0,96},{1,25},{2,98},{3,27},{4,100},{5,29},{6,102},{7,31},{8,104},... | collective-permute-start | bytes 2359304 | tf_op jit(solution)/shard_map/ppermute | solution.py:38
  23.8 16.8 %collective-permute-start.10 = (bf16[384,1024]{1,0:T(8,128)(2,1)S(1)}, bf16[384,1024]{1,0:T(8,128)(2,1)S(1)}, u32[]{:S(2)}, u32[]{:S(2)}) collective-permute-start(bf16[384,1024]{1,0:T(8,128)(2,1)S(1)} %maximum_maximum_fusion.refs_0_.refs_1_), channel_id=1, source_target_pairs={{0,32},{1,9},{2,34},{3,11},{4,36},{5,13},{6,38},{7,15},{8,40},{9,1... | collective-permute-start | bytes 2359304 | tf_op jit(solution)/shard_map/ppermute | solution.py:38
  33.2 11.5 %collective-permute-start.7 = (bf16[256,1024]{1,0:T(8,128)(2,1)S(1)}, bf16[256,1024]{1,0:T(8,128)(2,1)S(1)}, u32[]{:S(2)}, u32[]{:S(2)}) collective-permute-start(bf16[256,1024]{1,0:T(8,128)(2,1)S(1)} %slice.29), channel_id=1, source_target_pairs={{0,32},{1,9},{2,34},{3,11},{4,36},{5,13},{6,38},{7,15},{8,40},{9,1... | collective-permute-start | bytes 1572872 | tf_op jit(solution)/shard_map/ppermute | solution.py:38
  33.4 11.4 %collective-permute-start.9 = (bf16[256,1024]{1,0:T(8,128)(2,1)S(1)}, bf16[256,1024]{1,0:T(8,128)(2,1)S(1)}, u32[]{:S(2)}, u32[]{:S(2)}) collective-permute-start(bf16[256,1024]{1,0:T(8,128)(2,1)S(1)} %pad_maximum_fusion.1), channel_id=1, source_target_pairs={{0,96},{1,25},{2,98},{3,27},{4,100},{5,29},{6,102},{7,31},{8,104},... | collective-permute-start | bytes 1572872 | tf_op jit(solution)/shard_map/ppermute | solution.py:38
  40.6 7.7 %collective-permute-start.11 = (bf16[256,512]{1,0:T(8,128)(2,1)S(1)}, bf16[256,512]{1,0:T(8,128)(2,1)S(1)}, u32[]{:S(2)}, u32[]{:S(2)}) collective-permute-start(bf16[256,512]{1,0:T(8,128)(2,1)S(1)} %slice.39), channel_id=1, source_target_pairs={{0,32},{1,9},{2,34},{3,11},{4,36},{5,13},{6,38},{7,15},{8,40},{9,1... | collective-permute-start | bytes 786440 | tf_op jit(solution)/shard_map/ppermute | solution.py:38
  40.7 7.6 %collective-permute-start.12 = (bf16[256,512]{1,0:T(8,128)(2,1)S(1)}, bf16[256,512]{1,0:T(8,128)(2,1)S(1)}, u32[]{:S(2)}, u32[]{:S(2)}) collective-permute-start(bf16[256,512]{1,0:T(8,128)(2,1)S(1)} %slice.40), channel_id=1, source_target_pairs={{0,96},{1,25},{2,98},{3,27},{4,100},{5,29},{6,102},{7,31},{8,104},... | collective-permute-start | bytes 786440 | tf_op jit(solution)/shard_map/ppermute | solution.py:38
  48.3 1.3 %collective-permute-start.13 = (f32[256,128]{1,0:T(8,128)S(1)}, f32[256,128]{1,0:T(8,128)S(1)}, u32[]{:S(2)}, u32[]{:S(2)}) collective-permute-start(f32[256,128]{1,0:T(8,128)S(1)} %get-tuple-element.54), channel_id=1, source_target_pairs={{0,1},{1,0},{2,3},{3,2},{4,5},{5,4},{6,7},{7,6},{8,9},{9,8},{10,11... | collective-permute-start | bytes 393224 | tf_op jit(solution)/shard_map/ppermute | solution.py:44
  49.7 5.0 %collective-permute-start.14 = (f32[256,128]{1,0:T(8,128)S(1)}, f32[256,128]{1,0:T(8,128)S(1)}, u32[]{:S(2)}, u32[]{:S(2)}) collective-permute-start(f32[256,128]{1,0:T(8,128)S(1)} %add.9), channel_id=1, source_target_pairs={{0,2},{1,7},{2,0},{3,5},{4,6},{5,3},{6,4},{7,1},{8,10},{9,15},{10,... | collective-permute-start | bytes 393224 | tf_op jit(solution)/shard_map/ppermute | solution.py:51
  54.7 6.3 %collective-permute-start.15 = (f32[256,128]{1,0:T(8,128)S(1)}, f32[256,128]{1,0:T(8,128)S(1)}, u32[]{:S(2)}, u32[]{:S(2)}) collective-permute-start(f32[256,128]{1,0:T(8,128)S(1)} %add.10), channel_id=1, source_target_pairs={{0,6},{1,3},{2,4},{3,1},{4,2},{5,7},{6,0},{7,5},{8,14},{9,11},{10,... | collective-permute-start | bytes 393224 | tf_op jit(solution)/shard_map/ppermute | solution.py:51
  61.0 1.3 %collective-permute-start.16 = (bf16[256,128]{1,0:T(8,128)(2,1)S(1)}, bf16[256,128]{1,0:T(8,128)(2,1)S(1)}, u32[]{:S(2)}, u32[]{:S(2)}) collective-permute-start(bf16[256,128]{1,0:T(8,128)(2,1)S(1)} %add_convert_fusion.mine_ref), channel_id=1, source_target_pairs={{0,1},{1,0},{2,3},{3,2},{4,5},{5,4},{6,7},{7,6},{8,9},{9,8},{10,11... | collective-permute-start | bytes 196616 | tf_op jit(solution)/shard_map/ppermute | solution.py:44

commit v9 on v8

--- a/solution.py
+++ b/solution.py
@@ -140,7 +140,7 @@
         out_shape=[jax.ShapeDtypeStruct((rows, n), F32), jax.ShapeDtypeStruct(half.shape, BF)],
         scratch_shapes=[pltpu.SemaphoreType.DMA],
         compiler_params=params(28),
-        cost_estimate=cost(1000000, 1 << 20),
+        cost_estimate=cost(5000000000, 1 << 20),
         name="base_first",
     )(half, w, x)
 
@@ -152,7 +152,7 @@
         out_specs=VMEM,
         out_shape=jax.ShapeDtypeStruct((rest.shape[0], w.shape[1]), F32),
         compiler_params=params(12),
-        cost_estimate=cost(1000000, 1 << 20),
+        cost_estimate=cost(5000000000, 1 << 20),
         name="base_second",
     )(rest, w)
 
@@ -254,46 +254,35 @@
 def per_device(activations, token_adapter_index, query_matrix, down, up):
     down = jnp.swapaxes(down, 1, 2).reshape(128, -1)
     up = up.reshape(128, -1)
-    width, columns = down.shape[1], up.shape[1]
+    width = down.shape[1]
     row = lambda j, hops=HOPS: [(j, i) for i in hops]
 
-    before, after = first(down, 1), first(down, -1)
+    near = [first(down, d) for d in (1, -1, 2)]
     code = mask_code(token_adapter_index)
-    both, code = tie(jnp.concatenate([down, up], axis=1), code)
-    far = first(both, 2)
-    close = jnp.concatenate([both[:, :width], before, after], axis=0)
-    a_before, a_after = second(close, 1), second(close, -1)
-    here, half = fetch(tie(activations, before, after)[0], width)
-    late_up = tie(up, code)[0]
-    u_near = [first(late_up, d) for d in (1, -1)]
-
-    far, half, *u_near = tie(far, half, *u_near)
-    d_far = far[:, :width]
-    u_own = [jnp.concatenate([up, u_near[0]], axis=0), jnp.concatenate([u_near[1], far[:, width:]], axis=0)]
-    load = jnp.concatenate([d_far, jnp.concatenate(u_own, axis=1)], axis=0)
-    b_before, b_after = second(load, 1), second(load, -1)
+    here, half = fetch(tie(activations, code)[0], width)
+    near, here, half, up = tie(near, here, half, up)
+    d_own = jnp.concatenate([down, *near], axis=0)
+    d_before, d_after = second(d_own, 1), second(d_own, -1)
+    u_own = jnp.concatenate([up] + [first(up, d) for d in (1, -1, 2)], axis=0)
     top, rest = base_first(half, query_matrix, activations)
-    base = [top, base_second(rest, query_matrix)]
-    a_before, a_after, base[1] = tie(a_before, a_after, base[1])
-    groups = [([close, d_far], row(0)), ([a_before], row(-1, HOPS[:3])), ([a_after], row(1, HOPS[:3]))]
-    total = shrink(code, here, groups, None, False, "shrink_near", 20000000000)
-    d_two = [second(a_before[:256], 1), second(jnp.concatenate([a_after[256:], b_after[:128]]), -1)]
-    total, u_before, u_after = tie(total, b_before[128:, :columns], b_after[128:, columns:])
-    u_two = [second(u_before, 1), second(u_after, -1)]
-    groups = [([b_before[:128], b_after[:128]], [(-1, 2), (1, 2)])]
-    total = shrink(code, here, groups, total, False, "shrink_side")
+    d_before, d_after, top = tie(d_before, d_after, top)
+
+    d_two = [second(d_before[:256], 1), second(d_after[256:], -1)]
+    groups = [([d_own], row(0)), ([d_before], row(-1)), ([d_after], row(1))]
+    total = shrink(code, here, groups, None, False, "shrink_near", 5000000000)
+    total, u_own = tie(total, u_own)
+    u_before, u_after = second(u_own, 1), second(u_own, -1)
     *d_two, total = tie(*d_two, total)
     keep, give = shrink(code, here, [(d_two, row(2))], total, True, "shrink_far")
-    keep, give, *u_two = tie(keep, give, *u_two)
     keep = keep + other_core(give)
+    u_two = [second(u_before[:256], 1), second(u_after[256:], -1)]
     keep = keep + pair(keep, 0)
-    keep = keep + pair(keep, 1)
+    there, bottom, *u_two = tie(pair(keep, 1), base_second(rest, query_matrix), *u_two)
+    keep = keep + there
     mine = keep.astype(BF)
-    parts = []
-    for j, a, at in ((0, load, 128), (-1, b_before, 128), (1, b_after, 128)):
-        parts += [(a, row(j, HOPS[:2]), at, 0), (a, row(j, HOPS[2:]), at, columns)]
+    parts = [(u_own, row(0), 0, 0), (u_before, row(-1), 0, 0), (u_after, row(1), 0, 0)]
     parts += [(a, row(2, hops), 0, 0) for a, hops in zip(u_two, (HOPS[:2], HOPS[2:]))]
-    return expand(code, mine, other_core(mine), base, parts)
+    return expand(code, mine, other_core(mine), [top, bottom], parts)
 
 
 def solution(mesh):

time: 67.3 us -> 66.5 us (0.988)
  waiting for transfers between devices: 11.4 us -> 13.3 us
  other arithmetic: 1.28 us -> 0.15 us
  starting transfers between devices: 29.4 us -> 28.6 us
    ppermute x2, waiting for transfers between devices: 6.57 us -> 0.01 us  [pair(): return lax.ppermute(a, AXES, every(to))]
    ppermute x5 -> x6, waiting for transfers between devices: 0.01 us -> 4.31 us  [first(): lax.ppermute(a, AXES, every(lambda x, y, z, c: (x, y, z + d, c) if c else...]
    ppermute x8, waiting for transfers between devices: 2.21 us -> 6.42 us  [second(): lax.ppermute(a, AXES, every(lambda x, y, z, c: (x + d, y, z, c) if c else...]
    ppermute x8, starting transfers between devices: 16.1 us -> 14.2 us  [second(): lax.ppermute(a, AXES, every(lambda x, y, z, c: (x + d, y, z, c) if c else...]
    concatenate x4 -> x2, other arithmetic: 1.23 us -> 0.1 us  [the longest x1 0.07 us: per_device(): d_own = jnp.concatenate([down, *near], axis=0)]
    ppermute x5 -> x6, starting transfers between devices: 8.45 us -> 9.23 us  [first(): lax.ppermute(a, AXES, every(lambda x, y, z, c: (x, y, z + d, c) if c else...]
    pallas_call x3 -> x2, Pallas kernels: 5.55 us -> 4.81 us  [shrink(): pl.pallas_call(functools.partial(shrink_kernel, [(len(parts), places) for...]
  transfers between devices with their start and end apart: 17 -> 18, of which waited for: 5 -> 9; matrix products, arithmetic and copies ran while one was open for 2% -> 0% of each run, Pallas kernels for 29% -> 28%
where the time goes in v9:
time: 66.5 us; the launch traced here: 65.3 us
  starting transfers between devices  28.6 us (43%)
  Pallas kernels  22.2 us (33%)
  waiting for transfers between devices  13.3 us (20%)
  local copies, waits for them, and re-layouts  0.82 us (1%)
    ppermute x8, starting transfers between devices, second(): lax.ppermute(a, AXES, every(lambda x, y, z, c: (x + d, y, z, c) if c else...  14.2 us
    ppermute x6, starting transfers between devices, first(): lax.ppermute(a, AXES, every(lambda x, y, z, c: (x, y, z + d, c) if c else...  9.23 us
    ppermute x8, waiting for transfers between devices, second(): lax.ppermute(a, AXES, every(lambda x, y, z, c: (x + d, y, z, c) if c else...  6.42 us
    ppermute x2, starting transfers between devices, pair(): return lax.ppermute(a, AXES, every(to))  4.92 us
    pallas_call x2, Pallas kernels, shrink(): pl.pallas_call(functools.partial(shrink_kernel, [(len(parts), places) for...  4.81 us
    pallas_call x1, Pallas kernels, base_first(): pl.pallas_call(base_kernel, in_specs=[VMEM, VMEM, HBM], out_specs=[VMEM,...  4.66 us
    pallas_call x1, Pallas kernels, base_second(): pl.pallas_call(multiply, in_specs=[VMEM, VMEM], out_specs=VMEM, out_shape...  4.64 us
    ppermute x6, waiting for transfers between devices, first(): lax.ppermute(a, AXES, every(lambda x, y, z, c: (x, y, z + d, c) if c else...  4.31 us
  transfers between devices with their start and end apart: 18, of which 9 were waited for; matrix products, arithmetic and copies ran while one was open for 0% of the time, Pallas kernels for 28%

profile of v9, /device:TPU:0, one launch (start us, length us, event | category | flops | bytes accessed | tf_op | source)
XLA Modules:
  0.0 65.3 jit_solution(12822700112838495493)
XLA Ops:
  0.0 1.6 %collective-permute-start = (bf16[128,1024]{1,0:T(8,128)(2,1)}, bf16[128,1024]{1,0:T(8,128)(2,1)S(1)}, u32[]{:S(2)}, u32[]{:S(2)}) collective-permute-start(bf16[128,1024]{1,0:T(8,128)(2,1)} %bitcast.8), channel_id=1, source_target_pairs={{0,8},{1,33},{2,10},{3,35},{4,12},{5,37},{6,14},{7,39},{8,16},{9,4... | collective-permute-start | bytes 786440 | tf_op jit(solution)/shard_map/ppermute | solution.py:32
  1.6 1.7 %collective-permute-start.1 = (bf16[128,1024]{1,0:T(8,128)(2,1)}, bf16[128,1024]{1,0:T(8,128)(2,1)S(1)}, u32[]{:S(2)}, u32[]{:S(2)}) collective-permute-start(bf16[128,1024]{1,0:T(8,128)(2,1)} %bitcast.9), channel_id=1, source_target_pairs={{0,24},{1,97},{2,26},{3,99},{4,28},{5,101},{6,30},{7,103},{8,0},{9... | collective-permute-start | bytes 786440 | tf_op jit(solution)/shard_map/ppermute | solution.py:32
  3.2 1.9 %collective-permute-start.2 = (bf16[128,1024]{1,0:T(8,128)(2,1)}, bf16[128,1024]{1,0:T(8,128)(2,1)S(1)}, u32[]{:S(2)}, u32[]{:S(2)}) collective-permute-start(bf16[128,1024]{1,0:T(8,128)(2,1)} %bitcast.10), channel_id=1, source_target_pairs={{0,16},{1,65},{2,18},{3,67},{4,20},{5,69},{6,22},{7,71},{8,24},{9,... | collective-permute-start | bytes 786440 | tf_op jit(solution)/shard_map/ppermute | solution.py:32
  5.1 0.0 copy-start
  5.1 0.7 %copy-done = s32[1024,1]{0,1:T(1,128)S(1)} copy-done((s32[1024,1]{0,1:T(1,128)S(1)}, s32[1024,1]{0,1:T(1,128)}, u32[]{:S(2)}) %copy-start) | copy-done | bytes 4120
  5.8 0.0 slice-start
  5.8 0.2 mask_code.1.code_ref
  6.0 0.0 copy-start.1
  6.0 0.0 slice-start.1
  6.1 4.2 %fetch.1 = (bf16[1024,1024]{1,0:T(8,128)(2,1)S(1)}, bf16[512,8192]{1,0:T(8,128)(2,1)S(1)}) custom-call(bf16[1024,8192]{1,0:T(8,128)(2,1)} %x_ref.2), custom_call_target="tpu_custom_call" | custom-call | flops 1000000 | bytes 1048576 | tf_op jit(solution)/shard_map/fetch/pallas_call | solution.py:105
  10.3 0.0 copy-start.2
  10.3 0.0 collective-permute-done
  10.3 0.0 collective-permute-done.1
  10.3 1.4 %collective-permute-done.2 = bf16[128,1024]{1,0:T(8,128)(2,1)S(1)} collective-permute-done((bf16[128,1024]{1,0:T(8,128)(2,1)}, bf16[128,1024]{1,0:T(8,128)(2,1)S(1)}, u32[]{:S(2)}, u32[]{:S(2)}) %collective-permute-start.2) | collective-permute-done | bytes 262176 | tf_op jit(solution)/shard_map/ppermute | solution.py:32
  11.7 0.0 copy-done.1
  11.7 0.1 pad_maximum_fusion.refs_0_
  11.7 2.0 %collective-permute-start.3 = (bf16[512,1024]{1,0:T(8,128)(2,1)S(1)}, bf16[512,1024]{1,0:T(8,128)(2,1)S(1)}, u32[]{:S(2)}, u32[]{:S(2)}) collective-permute-start(bf16[512,1024]{1,0:T(8,128)(2,1)S(1)} %pad_maximum_fusion.refs_0_), channel_id=1, source_target_pairs={{0,32},{1,9},{2,34},{3,11},{4,36},{5,13},{6,38},{7,15},{8,40},{9,1... | collective-permute-start | bytes 3145736 | tf_op jit(solution)/shard_map/ppermute | solution.py:38
  13.7 2.2 %collective-permute-start.4 = (bf16[512,1024]{1,0:T(8,128)(2,1)S(1)}, bf16[512,1024]{1,0:T(8,128)(2,1)S(1)}, u32[]{:S(2)}, u32[]{:S(2)}) collective-permute-start(bf16[512,1024]{1,0:T(8,128)(2,1)S(1)} %pad_maximum_fusion.refs_0_), channel_id=1, source_target_pairs={{0,96},{1,25},{2,98},{3,27},{4,100},{5,29},{6,102},{7,31},{8,104},... | collective-permute-start | bytes 3145736 | tf_op jit(solution)/shard_map/ppermute | solution.py:38
  15.9 0.0 copy-done.2
  15.9 1.6 %collective-permute-start.9 = (bf16[128,512]{1,0:T(8,128)(2,1)S(1)}, bf16[128,512]{1,0:T(8,128)(2,1)S(1)}, u32[]{:S(2)}, u32[]{:S(2)}) collective-permute-start(bf16[128,512]{1,0:T(8,128)(2,1)S(1)} %bitcast.12), channel_id=1, source_target_pairs={{0,16},{1,65},{2,18},{3,67},{4,20},{5,69},{6,22},{7,71},{8,24},{9,... | collective-permute-start | bytes 393224 | tf_op jit(solution)/shard_map/ppermute | solution.py:32
  17.5 2.5 %collective-permute-start.8 = (bf16[128,512]{1,0:T(8,128)(2,1)S(1)}, bf16[128,512]{1,0:T(8,128)(2,1)S(1)}, u32[]{:S(2)}, u32[]{:S(2)}) collective-permute-start(bf16[128,512]{1,0:T(8,128)(2,1)S(1)} %bitcast.13), channel_id=1, source_target_pairs={{0,24},{1,97},{2,26},{3,99},{4,28},{5,101},{6,30},{7,103},{8,0},{9... | collective-permute-start | bytes 393224 | tf_op jit(solution)/shard_map/ppermute | solution.py:32
  20.0 0.0 collective-permute-start.7
  20.0 0.0 slice-done
  20.0 0.0 slice-done.1
  20.1 4.7 %base_first.1 = (f32[512,512]{1,0:T(8,128)S(1)}, bf16[512,8192]{1,0:T(8,128)(2,1)S(1)}) custom-call(bf16[512,8192]{1,0:T(8,128)(2,1)S(1)} %get-tuple-element.37.half_ref, bf16[8192,512]{1,0:T(8,128)(2,1)S(1)} %bitcast.6, bf16[1024,8192]{1,0:T(8,128)(2,1)} %x_ref.2), custom_call_target="tpu_custom_call" | custom-call | flops 5000000000 | bytes 1048576 | tf_op jit(solution)/shard_map/base_first/pallas_call | solution.py:136
  24.7 0.0 collective-permute-done.9
  24.7 1.5 %collective-permute-done.8 = bf16[128,512]{1,0:T(8,128)(2,1)S(1)} collective-permute-done((bf16[128,512]{1,0:T(8,128)(2,1)S(1)}, bf16[128,512]{1,0:T(8,128)(2,1)S(1)}, u32[]{:S(2)}, u32[]{:S(2)}) %collective-permute-start.8) | collective-permute-done | bytes 131104 | tf_op jit(solution)/shard_map/ppermute | solution.py:32
  26.3 1.4 %collective-permute-done.7 = bf16[128,512]{1,0:T(8,128)(2,1)S(1)} collective-permute-done((bf16[128,512]{1,0:T(8,128)(2,1)S(1)}, bf16[128,512]{1,0:T(8,128)(2,1)S(1)}, u32[]{:S(2)}, u32[]{:S(2)}) %collective-permute-start.7) | collective-permute-done | bytes 131104 | tf_op jit(solution)/shard_map/ppermute | solution.py:32
  27.7 3.7 %collective-permute-done.3.refs_1_ = bf16[512,1024]{1,0:T(8,128)(2,1)S(1)} collective-permute-done((bf16[512,1024]{1,0:T(8,128)(2,1)S(1)}, bf16[512,1024]{1,0:T(8,128)(2,1)S(1)}, u32[]{:S(2)}, u32[]{:S(2)}) %collective-permute-start.3) | collective-permute-done | bytes 1048608 | tf_op jit(solution)/shard_map/ppermute | solution.py:38
  31.4 0.0 collective-permute-done.4.refs_2_
  31.5 1.9 %collective-permute-start.5 = (bf16[256,1024]{1,0:T(8,128)(2,1)S(1)}, bf16[256,1024]{1,0:T(8,128)(2,1)S(1)}, u32[]{:S(2)}, u32[]{:S(2)}) collective-permute-start(bf16[256,1024]{1,0:T(8,128)(2,1)S(1)} %slice.12), channel_id=1, source_target_pairs={{0,32},{1,9},{2,34},{3,11},{4,36},{5,13},{6,38},{7,15},{8,40},{9,1... | collective-permute-start | bytes 1572872 | tf_op jit(solution)/shard_map/ppermute | solution.py:38
  33.4 1.5 %collective-permute-start.6 = (bf16[256,1024]{1,0:T(8,128)(2,1)S(1)}, bf16[256,1024]{1,0:T(8,128)(2,1)S(1)}, u32[]{:S(2)}, u32[]{:S(2)}) collective-permute-start(bf16[256,1024]{1,0:T(8,128)(2,1)S(1)} %slice.13), channel_id=1, source_target_pairs={{0,96},{1,25},{2,98},{3,27},{4,100},{5,29},{6,102},{7,31},{8,104},... | collective-permute-start | bytes 1572872 | tf_op jit(solution)/shard_map/ppermute | solution.py:38
  34.9 3.5 %shrink_near.1.refs_2_ = f32[1024,128]{1,0:T(8,128)S(1)} custom-call(s32[1024,128]{1,0:T(8,128)S(1)} %mask_code.1.code_ref, bf16[1024,1024]{1,0:T(8,128)(2,1)S(1)} %get-tuple-element.33.x_ref, bf16[512,1024]{1,0:T(8,128)(2,1)S(1)} %pad_maximum_fusion.refs_0_, bf16[512,1024]{1,0:T(8,128)(2,1)S(1)} %collective-permute-done.3.refs_1_, ...), custom_call_target="tpu_custom_call" | custom-call | flops 5000000000 | bytes 1048576 | tf_op jit(solution)/shard_map/shrink_near/pallas_call | solution.py:192
  38.4 0.6 collective-permute-start.13
  39.0 2.7 %collective-permute-start.15 = (bf16[512,512]{1,0:T(8,128)(2,1)S(1)}, bf16[512,512]{1,0:T(8,128)(2,1)S(1)}, u32[]{:S(2)}, u32[]{:S(2)}) collective-permute-start(bf16[512,512]{1,0:T(8,128)(2,1)S(1)} %pad_maximum_fusion.1.refs_0_), channel_id=1, source_target_pairs={{0,96},{1,25},{2,98},{3,27},{4,100},{5,29},{6,102},{7,31},{8,104},... | collective-permute-start | bytes 1572872 | tf_op jit(solution)/shard_map/ppermute | solution.py:38
  41.7 0.3 collective-permute-done.5.refs_0_
  42.0 0.7 %collective-permute-done.6.refs_1_ = bf16[256,1024]{1,0:T(8,128)(2,1)S(1)} collective-permute-done((bf16[256,1024]{1,0:T(8,128)(2,1)S(1)}, bf16[256,1024]{1,0:T(8,128)(2,1)S(1)}, u32[]{:S(2)}, u32[]{:S(2)}) %collective-permute-start.6) | collective-permute-done | bytes 524320 | tf_op jit(solution)/shard_map/ppermute | solution.py:38
  42.7 1.4 %shrink_far.1 = (f32[256,128]{1,0:T(8,128)S(1)}, f32[256,128]{1,0:T(8,128)S(1)}) custom-call(s32[1024,128]{1,0:T(8,128)S(1)} %mask_code.1.code_ref, bf16[1024,1024]{1,0:T(8,128)(2,1)S(1)} %get-tuple-element.33.x_ref, bf16[256,1024]{1,0:T(8,128)(2,1)S(1)} %collective-permute-done.5.refs_0_, bf16[256,1024]{1,0:T(8,128)(2,1)S(1)} %collective-permute-done.6.refs_1_, ...), custom_call_target="tpu_custom_call" | custom-call | flops 1048576 | bytes 1048576 | tf_op jit(solution)/shard_map/shrink_far/pallas_call | solution.py:192
  44.0 0.1 collective-permute-start.10
  44.1 1.3 %collective-permute-done.10 = f32[256,128]{1,0:T(8,128)S(1)} collective-permute-done((f32[256,128]{1,0:T(8,128)S(1)}, f32[256,128]{1,0:T(8,128)S(1)}, u32[]{:S(2)}, u32[]{:S(2)}) %collective-permute-start.10) | collective-permute-done | bytes 131104 | tf_op jit(solution)/shard_map/ppermute | solution.py:44
  45.5 1.7 %collective-permute-start.11 = (f32[256,128]{1,0:T(8,128)S(1)}, f32[256,128]{1,0:T(8,128)S(1)}, u32[]{:S(2)}, u32[]{:S(2)}) collective-permute-start(f32[256,128]{1,0:T(8,128)S(1)} %add.9), channel_id=1, source_target_pairs={{0,2},{1,7},{2,0},{3,5},{4,6},{5,3},{6,4},{7,1},{8,10},{9,15},{10,... | collective-permute-start | bytes 393224 | tf_op jit(solution)/shard_map/ppermute | solution.py:51
  47.1 1.7 %collective-permute-done.13.refs_1_ = bf16[512,512]{1,0:T(8,128)(2,1)S(1)} collective-permute-done((bf16[512,512]{1,0:T(8,128)(2,1)S(1)}, bf16[512,512]{1,0:T(8,128)(2,1)S(1)}, u32[]{:S(2)}, u32[]{:S(2)}) %collective-permute-start.13) | collective-permute-done | bytes 524320 | tf_op jit(solution)/shard_map/ppermute | solution.py:38
  48.9 0.1 collective-permute-start.14
  48.9 0.0 collective-permute-done.15.refs_2_
  49.0 3.3 %collective-permute-start.16 = (bf16[256,512]{1,0:T(8,128)(2,1)S(1)}, bf16[256,512]{1,0:T(8,128)(2,1)S(1)}, u32[]{:S(2)}, u32[]{:S(2)}) collective-permute-start(bf16[256,512]{1,0:T(8,128)(2,1)S(1)} %slice.17), channel_id=1, source_target_pairs={{0,96},{1,25},{2,98},{3,27},{4,100},{5,29},{6,102},{7,31},{8,104},... | collective-permute-start | bytes 786440 | tf_op jit(solution)/shard_map/ppermute | solution.py:38
  52.3 0.0 collective-permute-done.11
  52.3 3.3 %collective-permute-start.12 = (f32[256,128]{1,0:T(8,128)S(1)}, f32[256,128]{1,0:T(8,128)S(1)}, u32[]{:S(2)}, u32[]{:S(2)}) collective-permute-start(f32[256,128]{1,0:T(8,128)S(1)} %add.10), channel_id=1, source_target_pairs={{0,6},{1,3},{2,4},{3,1},{4,2},{5,7},{6,0},{7,5},{8,14},{9,11},{10,... | collective-permute-start | bytes 393224 | tf_op jit(solution)/shard_map/ppermute | solution.py:51
  55.6 4.6 %base_second.1.bottom_ref = f32[512,512]{1,0:T(8,128)S(1)} custom-call(bf16[512,8192]{1,0:T(8,128)(2,1)S(1)} %get-tuple-element.48.x_ref, bf16[8192,512]{1,0:T(8,128)(2,1)S(1)} %bitcast.6), custom_call_target="tpu_custom_call" | custom-call | flops 5000000000 | bytes 1048576 | tf_op jit(solution)/shard_map/base_second/pallas_call | solution.py:149
  60.2 0.0 collective-permute-done.14.refs_3_
  60.2 0.0 collective-permute-done.16.refs_4_
  60.2 0.0 collective-permute-done.12
  60.3 0.1 collective-permute-start.17
  60.4 1.2 %collective-permute-done.17.other_ref = bf16[256,128]{1,0:T(8,128)(2,1)S(1)} collective-permute-done((bf16[256,128]{1,0:T(8,128)(2,1)S(1)}, bf16[256,128]{1,0:T(8,128)(2,1)S(1)}, u32[]{:S(2)}, u32[]{:S(2)}) %collective-permute-start.17) | collective-permute-done | bytes 65568 | tf_op jit(solution)/shard_map/ppermute | solution.py:44
  61.6 3.7 %expand.1 = bf16[1024,512]{1,0:T(8,128)(2,1)} custom-call(s32[1024,128]{1,0:T(8,128)S(1)} %mask_code.1.code_ref, bf16[256,128]{1,0:T(8,128)(2,1)S(1)} %add_convert_fusion.mine_ref, bf16[256,128]{1,0:T(8,128)(2,1)S(1)} %collective-permute-done.17.other_ref, f32[512,512]{1,0:T(8,128)S(1)} %get-tuple-element.51.top_ref, f32[512,512]{1,0:T(8,128)S(1)} %base_second.1.bottom_ref, ...), custom_call_target="tpu_custom_call" | custom-call | flops 2147483648 | bytes 3145728 | tf_op jit(solution)/shard_map/expand/pallas_call | solution.py:238
  (9 shorter events, 0.2 us)
Async XLA Ops:
  0.0 10.3 %collective-permute-start = (bf16[128,1024]{1,0:T(8,128)(2,1)}, bf16[128,1024]{1,0:T(8,128)(2,1)S(1)}, u32[]{:S(2)}, u32[]{:S(2)}) collective-permute-start(bf16[128,1024]{1,0:T(8,128)(2,1)} %bitcast.8), channel_id=1, source_target_pairs={{0,8},{1,33},{2,10},{3,35},{4,12},{5,37},{6,14},{7,39},{8,16},{9,4... | collective-permute-start | bytes 786440 | tf_op jit(solution)/shard_map/ppermute | solution.py:32
  1.6 8.7 %collective-permute-start.1 = (bf16[128,1024]{1,0:T(8,128)(2,1)}, bf16[128,1024]{1,0:T(8,128)(2,1)S(1)}, u32[]{:S(2)}, u32[]{:S(2)}) collective-permute-start(bf16[128,1024]{1,0:T(8,128)(2,1)} %bitcast.9), channel_id=1, source_target_pairs={{0,24},{1,97},{2,26},{3,99},{4,28},{5,101},{6,30},{7,103},{8,0},{9... | collective-permute-start | bytes 786440 | tf_op jit(solution)/shard_map/ppermute | solution.py:32
  3.2 8.4 %collective-permute-start.2 = (bf16[128,1024]{1,0:T(8,128)(2,1)}, bf16[128,1024]{1,0:T(8,128)(2,1)S(1)}, u32[]{:S(2)}, u32[]{:S(2)}) collective-permute-start(bf16[128,1024]{1,0:T(8,128)(2,1)} %bitcast.10), channel_id=1, source_target_pairs={{0,16},{1,65},{2,18},{3,67},{4,20},{5,69},{6,22},{7,71},{8,24},{9,... | collective-permute-start | bytes 786440 | tf_op jit(solution)/shard_map/ppermute | solution.py:32
  5.1 0.7 %copy-start = (s32[1024,1]{0,1:T(1,128)S(1)}, s32[1024,1]{0,1:T(1,128)}, u32[]{:S(2)}) copy-start(s32[1024,1]{0,1:T(1,128)} %param.6) | copy-start | bytes 12292
  5.8 14.2 %slice-start = ((s8[8388608]{0:T(1024)(128)(4,1)}), s8[4194304]{0:T(1024)(128)(4,1)S(1)}, s32[]{:S(2)}) async-start(s8[8388608]{0:T(1024)(128)(4,1)} %bitcast.5), calls=%async_computation | async-start | bytes 8388608
  6.0 5.6 %copy-start.1 = (bf16[2,1024,64]{1,2,0:T(8,128)(2,1)S(1)}, bf16[2,1024,64]{1,2,0:T(8,128)(2,1)}, u32[]{:S(2)}) copy-start(bf16[2,1024,64]{1,2,0:T(8,128)(2,1)} %param.8) | copy-start | bytes 786436
  6.0 14.0 %slice-start.1 = ((s8[8388608]{0:T(1024)(128)(4,1)}), s8[4194304]{0:T(1024)(128)(4,1)S(1)}, s32[]{:S(2)}) async-start(s8[8388608]{0:T(1024)(128)(4,1)} %bitcast.5), calls=%async_computation.1 | async-start | bytes 8388608
  10.3 5.7 %copy-start.2 = (bf16[2,64,512]{2,1,0:T(8,128)(2,1)S(1)}, bf16[2,64,512]{2,1,0:T(8,128)(2,1)}, u32[]{:S(2)}) copy-start(bf16[2,64,512]{2,1,0:T(8,128)(2,1)} %param.9) | copy-start | bytes 393220
  11.7 19.7 %collective-permute-start.3 = (bf16[512,1024]{1,0:T(8,128)(2,1)S(1)}, bf16[512,1024]{1,0:T(8,128)(2,1)S(1)}, u32[]{:S(2)}, u32[]{:S(2)}) collective-permute-start(bf16[512,1024]{1,0:T(8,128)(2,1)S(1)} %pad_maximum_fusion.refs_0_), channel_id=1, source_target_pairs={{0,32},{1,9},{2,34},{3,11},{4,36},{5,13},{6,38},{7,15},{8,40},{9,1... | collective-permute-start | bytes 3145736 | tf_op jit(solution)/shard_map/ppermute | solution.py:38
  13.7 17.7 %collective-permute-start.4 = (bf16[512,1024]{1,0:T(8,128)(2,1)S(1)}, bf16[512,1024]{1,0:T(8,128)(2,1)S(1)}, u32[]{:S(2)}, u32[]{:S(2)}) collective-permute-start(bf16[512,1024]{1,0:T(8,128)(2,1)S(1)} %pad_maximum_fusion.refs_0_), channel_id=1, source_target_pairs={{0,96},{1,25},{2,98},{3,27},{4,100},{5,29},{6,102},{7,31},{8,104},... | collective-permute-start | bytes 3145736 | tf_op jit(solution)/shard_map/ppermute | solution.py:38
  15.9 8.8 %collective-permute-start.9 = (bf16[128,512]{1,0:T(8,128)(2,1)S(1)}, bf16[128,512]{1,0:T(8,128)(2,1)S(1)}, u32[]{:S(2)}, u32[]{:S(2)}) collective-permute-start(bf16[128,512]{1,0:T(8,128)(2,1)S(1)} %bitcast.12), channel_id=1, source_target_pairs={{0,16},{1,65},{2,18},{3,67},{4,20},{5,69},{6,22},{7,71},{8,24},{9,... | collective-permute-start | bytes 393224 | tf_op jit(solution)/shard_map/ppermute | solution.py:32
  17.5 8.8 %collective-permute-start.8 = (bf16[128,512]{1,0:T(8,128)(2,1)S(1)}, bf16[128,512]{1,0:T(8,128)(2,1)S(1)}, u32[]{:S(2)}, u32[]{:S(2)}) collective-permute-start(bf16[128,512]{1,0:T(8,128)(2,1)S(1)} %bitcast.13), channel_id=1, source_target_pairs={{0,24},{1,97},{2,26},{3,99},{4,28},{5,101},{6,30},{7,103},{8,0},{9... | collective-permute-start | bytes 393224 | tf_op jit(solution)/shard_map/ppermute | solution.py:32
  20.0 7.6 %collective-permute-start.7 = (bf16[128,512]{1,0:T(8,128)(2,1)S(1)}, bf16[128,512]{1,0:T(8,128)(2,1)S(1)}, u32[]{:S(2)}, u32[]{:S(2)}) collective-permute-start(bf16[128,512]{1,0:T(8,128)(2,1)S(1)} %bitcast.14), channel_id=1, source_target_pairs={{0,8},{1,33},{2,10},{3,35},{4,12},{5,37},{6,14},{7,39},{8,16},{9,4... | collective-permute-start | bytes 393224 | tf_op jit(solution)/shard_map/ppermute | solution.py:32
  31.5 10.5 %collective-permute-start.5 = (bf16[256,1024]{1,0:T(8,128)(2,1)S(1)}, bf16[256,1024]{1,0:T(8,128)(2,1)S(1)}, u32[]{:S(2)}, u32[]{:S(2)}) collective-permute-start(bf16[256,1024]{1,0:T(8,128)(2,1)S(1)} %slice.12), channel_id=1, source_target_pairs={{0,32},{1,9},{2,34},{3,11},{4,36},{5,13},{6,38},{7,15},{8,40},{9,1... | collective-permute-start | bytes 1572872 | tf_op jit(solution)/shard_map/ppermute | solution.py:38
  33.4 9.3 %collective-permute-start.6 = (bf16[256,1024]{1,0:T(8,128)(2,1)S(1)}, bf16[256,1024]{1,0:T(8,128)(2,1)S(1)}, u32[]{:S(2)}, u32[]{:S(2)}) collective-permute-start(bf16[256,1024]{1,0:T(8,128)(2,1)S(1)} %slice.13), channel_id=1, source_target_pairs={{0,96},{1,25},{2,98},{3,27},{4,100},{5,29},{6,102},{7,31},{8,104},... | collective-permute-start | bytes 1572872 | tf_op jit(solution)/shard_map/ppermute | solution.py:38
  38.4 10.5 %collective-permute-start.13 = (bf16[512,512]{1,0:T(8,128)(2,1)S(1)}, bf16[512,512]{1,0:T(8,128)(2,1)S(1)}, u32[]{:S(2)}, u32[]{:S(2)}) collective-permute-start(bf16[512,512]{1,0:T(8,128)(2,1)S(1)} %pad_maximum_fusion.1.refs_0_), channel_id=1, source_target_pairs={{0,32},{1,9},{2,34},{3,11},{4,36},{5,13},{6,38},{7,15},{8,40},{9,1... | collective-permute-start | bytes 1572872 | tf_op jit(solution)/shard_map/ppermute | solution.py:38
  39.0 9.9 %collective-permute-start.15 = (bf16[512,512]{1,0:T(8,128)(2,1)S(1)}, bf16[512,512]{1,0:T(8,128)(2,1)S(1)}, u32[]{:S(2)}, u32[]{:S(2)}) collective-permute-start(bf16[512,512]{1,0:T(8,128)(2,1)S(1)} %pad_maximum_fusion.1.refs_0_), channel_id=1, source_target_pairs={{0,96},{1,25},{2,98},{3,27},{4,100},{5,29},{6,102},{7,31},{8,104},... | collective-permute-start | bytes 1572872 | tf_op jit(solution)/shard_map/ppermute | solution.py:38
  44.0 1.4 %collective-permute-start.10 = (f32[256,128]{1,0:T(8,128)S(1)}, f32[256,128]{1,0:T(8,128)S(1)}, u32[]{:S(2)}, u32[]{:S(2)}) collective-permute-start(f32[256,128]{1,0:T(8,128)S(1)} %get-tuple-element.47), channel_id=1, source_target_pairs={{0,1},{1,0},{2,3},{3,2},{4,5},{5,4},{6,7},{7,6},{8,9},{9,8},{10,11... | collective-permute-start | bytes 393224 | tf_op jit(solution)/shard_map/ppermute | solution.py:44
  45.5 6.8 %collective-permute-start.11 = (f32[256,128]{1,0:T(8,128)S(1)}, f32[256,128]{1,0:T(8,128)S(1)}, u32[]{:S(2)}, u32[]{:S(2)}) collective-permute-start(f32[256,128]{1,0:T(8,128)S(1)} %add.9), channel_id=1, source_target_pairs={{0,2},{1,7},{2,0},{3,5},{4,6},{5,3},{6,4},{7,1},{8,10},{9,15},{10,... | collective-permute-start | bytes 393224 | tf_op jit(solution)/shard_map/ppermute | solution.py:51
  48.9 11.3 %collective-permute-start.14 = (bf16[256,512]{1,0:T(8,128)(2,1)S(1)}, bf16[256,512]{1,0:T(8,128)(2,1)S(1)}, u32[]{:S(2)}, u32[]{:S(2)}) collective-permute-start(bf16[256,512]{1,0:T(8,128)(2,1)S(1)} %slice.16), channel_id=1, source_target_pairs={{0,32},{1,9},{2,34},{3,11},{4,36},{5,13},{6,38},{7,15},{8,40},{9,1... | collective-permute-start | bytes 786440 | tf_op jit(solution)/shard_map/ppermute | solution.py:38
  49.0 11.2 %collective-permute-start.16 = (bf16[256,512]{1,0:T(8,128)(2,1)S(1)}, bf16[256,512]{1,0:T(8,128)(2,1)S(1)}, u32[]{:S(2)}, u32[]{:S(2)}) collective-permute-start(bf16[256,512]{1,0:T(8,128)(2,1)S(1)} %slice.17), channel_id=1, source_target_pairs={{0,96},{1,25},{2,98},{3,27},{4,100},{5,29},{6,102},{7,31},{8,104},... | collective-permute-start | bytes 786440 | tf_op jit(solution)/shard_map/ppermute | solution.py:38
  52.3 7.9 %collective-permute-start.12 = (f32[256,128]{1,0:T(8,128)S(1)}, f32[256,128]{1,0:T(8,128)S(1)}, u32[]{:S(2)}, u32[]{:S(2)}) collective-permute-start(f32[256,128]{1,0:T(8,128)S(1)} %add.10), channel_id=1, source_target_pairs={{0,6},{1,3},{2,4},{3,1},{4,2},{5,7},{6,0},{7,5},{8,14},{9,11},{10,... | collective-permute-start | bytes 393224 | tf_op jit(solution)/shard_map/ppermute | solution.py:51
  60.3 1.3 %collective-permute-start.17 = (bf16[256,128]{1,0:T(8,128)(2,1)S(1)}, bf16[256,128]{1,0:T(8,128)(2,1)S(1)}, u32[]{:S(2)}, u32[]{:S(2)}) collective-permute-start(bf16[256,128]{1,0:T(8,128)(2,1)S(1)} %add_convert_fusion.mine_ref), channel_id=1, source_target_pairs={{0,1},{1,0},{2,3},{3,2},{4,5},{5,4},{6,7},{7,6},{8,9},{9,8},{10,11... | collective-permute-start | bytes 196616 | tf_op jit(solution)/shard_map/ppermute | solution.py:44

commit v10 on v9

--- a/solution.py
+++ b/solution.py
@@ -114,40 +114,51 @@
     )(x)
 
 
-def multiply(x_ref, w_ref, o_ref, block=256):
-    def rows(i, _):
-        at = pl.ds(pl.multiple_of(i * block, block), block)
-        o_ref[at, :] = jnp.dot(x_ref[at, :], w_ref[...], preferred_element_type=F32)
+def multiply(x_ref, w_ref, o_ref, rows, at=0, block=256):
+    def step(i, _):
+        here = pl.ds(pl.multiple_of(i * block, block), block)
+        there = pl.ds(pl.multiple_of(at + i * block, block), block)
+        o_ref[there, :] = jnp.dot(x_ref[here, :], w_ref[...], preferred_element_type=F32)
         return 0
 
-    lax.fori_loop(0, x_ref.shape[0] // block, rows, 0)
-
-
-def base_kernel(half_ref, w_ref, x_ref, o_ref, rest_ref, sem):
-    rows = rest_ref.shape[0]
-    copy = pltpu.make_async_copy(x_ref.at[pl.ds(rows, rows)], rest_ref, sem)
-    copy.start()
-    multiply(half_ref, w_ref, o_ref)
-    copy.wait()
+    lax.fori_loop(0, rows // block, step, 0)
+
+
+def base_kernel(half_ref, w_ref, x_ref, o_ref, rest_ref, xb, sems):
+    half, most, last = half_ref.shape[0], o_ref.shape[0], rest_ref.shape[0]
+    copies = [
+        pltpu.make_async_copy(x_ref.at[pl.ds(half, most - half)], xb, sems.at[0]),
+        pltpu.make_async_copy(x_ref.at[pl.ds(most, last)], rest_ref, sems.at[1]),
+    ]
+    for copy in copies:
+        copy.start()
+    multiply(half_ref, w_ref, o_ref, half)
+    copies[0].wait()
+    multiply(xb, w_ref, o_ref, most - half, half)
+    copies[1].wait()
 
 
 def base_first(half, w, x):
-    rows, n = half.shape[0], w.shape[1]
+    (m, k), n = x.shape, w.shape[1]
     return pl.pallas_call(
         base_kernel,
         in_specs=[VMEM, VMEM, HBM],
         out_specs=[VMEM, VMEM],
-        out_shape=[jax.ShapeDtypeStruct((rows, n), F32), jax.ShapeDtypeStruct(half.shape, BF)],
-        scratch_shapes=[pltpu.SemaphoreType.DMA],
+        out_shape=[jax.ShapeDtypeStruct((m * 3 // 4, n), F32), jax.ShapeDtypeStruct((m // 4, k), BF)],
+        scratch_shapes=[pltpu.VMEM((m // 4, k), BF), pltpu.SemaphoreType.DMA((2,))],
         compiler_params=params(28),
         cost_estimate=cost(5000000000, 1 << 20),
         name="base_first",
     )(half, w, x)
 
 
+def base_second_kernel(x_ref, w_ref, o_ref):
+    multiply(x_ref, w_ref, o_ref, x_ref.shape[0])
+
+
 def base_second(rest, w):
     return pl.pallas_call(
-        multiply,
+        base_second_kernel,
         in_specs=[VMEM, VMEM],
         out_specs=VMEM,
         out_shape=jax.ShapeDtypeStruct((rest.shape[0], w.shape[1]), F32),
@@ -224,16 +235,21 @@
         d = jnp.dot(spread, b_ref[ref_at:, lanes : lanes + o_ref.shape[1]], preferred_element_type=F32)
         delta = d if delta is None else delta + d
     delta = delta.astype(BF).astype(F32)
-    for i, base_ref in enumerate((top_ref, bottom_ref)):
-
-        @pl.when(step == i)
-        def _(base_ref=base_ref):
-            o_ref[...] = (base_ref[...] + adapter_scale * delta).astype(BF)
+    quarter = block // 2
+
+    @pl.when(step == 0)
+    def _():
+        o_ref[...] = (top_ref[:block, :] + adapter_scale * delta).astype(BF)
+
+    @pl.when(step == 1)
+    def _():
+        o_ref[:quarter, :] = (top_ref[block:, :] + adapter_scale * delta[:quarter]).astype(BF)
+        o_ref[quarter:, :] = (bottom_ref[...] + adapter_scale * delta[quarter:]).astype(BF)
 
 
 def expand(code, mine, other, base, parts):
-    block, n = base[0].shape
-    m = 2 * block
+    m, n = code.shape[0], base[0].shape[1]
+    block = m // 2
     args = [code, mine, other, *base] + [part[0] for part in parts]
     return pl.pallas_call(
         functools.partial(expand_kernel, [part[1:] for part in parts]),

time: 66.5 us -> 65 us (0.977)
  waiting for transfers between devices: 13.3 us -> 11.8 us
    ppermute x6, waiting for transfers between devices: 4.31 us -> 1.97 us  [first(): lax.ppermute(a, AXES, every(lambda x, y, z, c: (x, y, z + d, c) if c else...]
    pallas_call x1, Pallas kernels: 4.66 us -> 6.99 us  [base_first(): pl.pallas_call(base_kernel, in_specs=[VMEM, VMEM, HBM], out_specs=[VMEM,...]
    pallas_call x1, Pallas kernels: 4.64 us -> 2.31 us  [base_second(): pl.pallas_call(base_second_kernel, in_specs=[VMEM, VMEM], out_specs=VMEM,...]
    ppermute x2, waiting for transfers between devices: 0.01 us -> 0.83 us  [pair(): return lax.ppermute(a, AXES, every(to))]
  transfers between devices with their start and end apart: 18 -> 18, of which waited for: 9 -> 9; matrix products, arithmetic and copies ran while one was open for 0% -> 0% of each run, Pallas kernels for 28% -> 29%
where the time goes in v10:
time: 65 us; the launch traced here: 63.8 us
  starting transfers between devices  28.6 us (44%)
  Pallas kernels  22.2 us (34%)
  waiting for transfers between devices  11.8 us (18%)
  local copies, waits for them, and re-layouts  0.82 us (1%)
    ppermute x8, starting transfers between devices, second(): lax.ppermute(a, AXES, every(lambda x, y, z, c: (x + d, y, z, c) if c else...  14.4 us
    ppermute x6, starting transfers between devices, first(): lax.ppermute(a, AXES, every(lambda x, y, z, c: (x, y, z + d, c) if c else...  9.23 us
    pallas_call x1, Pallas kernels, base_first(): pl.pallas_call(base_kernel, in_specs=[VMEM, VMEM, HBM], out_specs=[VMEM,...  6.99 us
    ppermute x8, waiting for transfers between devices, second(): lax.ppermute(a, AXES, every(lambda x, y, z, c: (x + d, y, z, c) if c else...  6.42 us
    pallas_call x2, Pallas kernels, shrink(): pl.pallas_call(functools.partial(shrink_kernel, [(len(parts), places) for...  4.81 us
    ppermute x2, starting transfers between devices, pair(): return lax.ppermute(a, AXES, every(to))  4.74 us
    pallas_call x1, Pallas kernels, fetch(): pl.pallas_call(fetch_kernel, in_specs=[HBM], out_specs=[VMEM] * 2, out_sh...  4.22 us
    pallas_call x1, Pallas kernels, expand(): pl.pallas_call(functools.partial(expand_kernel, [part[1:] for part in par...  3.67 us
  transfers between devices with their start and end apart: 18, of which 9 were waited for; matrix products, arithmetic and copies ran while one was open for 0% of the time, Pallas kernels for 29%

profile of v10, /device:TPU:0, one launch (start us, length us, event | category | flops | bytes accessed | tf_op | source)
XLA Modules:
  0.0 63.8 jit_solution(733294792062189520)
XLA Ops:
  0.0 1.6 %collective-permute-start = (bf16[128,1024]{1,0:T(8,128)(2,1)}, bf16[128,1024]{1,0:T(8,128)(2,1)S(1)}, u32[]{:S(2)}, u32[]{:S(2)}) collective-permute-start(bf16[128,1024]{1,0:T(8,128)(2,1)} %bitcast.8), channel_id=1, source_target_pairs={{0,8},{1,33},{2,10},{3,35},{4,12},{5,37},{6,14},{7,39},{8,16},{9,4... | collective-permute-start | bytes 786440 | tf_op jit(solution)/shard_map/ppermute | solution.py:32
  1.6 1.7 %collective-permute-start.1 = (bf16[128,1024]{1,0:T(8,128)(2,1)}, bf16[128,1024]{1,0:T(8,128)(2,1)S(1)}, u32[]{:S(2)}, u32[]{:S(2)}) collective-permute-start(bf16[128,1024]{1,0:T(8,128)(2,1)} %bitcast.9), channel_id=1, source_target_pairs={{0,24},{1,97},{2,26},{3,99},{4,28},{5,101},{6,30},{7,103},{8,0},{9... | collective-permute-start | bytes 786440 | tf_op jit(solution)/shard_map/ppermute | solution.py:32
  3.2 1.9 %collective-permute-start.2 = (bf16[128,1024]{1,0:T(8,128)(2,1)}, bf16[128,1024]{1,0:T(8,128)(2,1)S(1)}, u32[]{:S(2)}, u32[]{:S(2)}) collective-permute-start(bf16[128,1024]{1,0:T(8,128)(2,1)} %bitcast.10), channel_id=1, source_target_pairs={{0,16},{1,65},{2,18},{3,67},{4,20},{5,69},{6,22},{7,71},{8,24},{9,... | collective-permute-start | bytes 786440 | tf_op jit(solution)/shard_map/ppermute | solution.py:32
  5.1 0.0 copy-start
  5.1 0.7 %copy-done = s32[1024,1]{0,1:T(1,128)S(1)} copy-done((s32[1024,1]{0,1:T(1,128)S(1)}, s32[1024,1]{0,1:T(1,128)}, u32[]{:S(2)}) %copy-start) | copy-done | bytes 4120
  5.8 0.0 slice-start
  5.8 0.2 mask_code.1.code_ref
  6.0 0.0 copy-start.1
  6.0 0.0 slice-start.1
  6.1 4.2 %fetch.1 = (bf16[1024,1024]{1,0:T(8,128)(2,1)S(1)}, bf16[512,8192]{1,0:T(8,128)(2,1)S(1)}) custom-call(bf16[1024,8192]{1,0:T(8,128)(2,1)} %x_ref.2), custom_call_target="tpu_custom_call" | custom-call | flops 1000000 | bytes 1048576 | tf_op jit(solution)/shard_map/fetch/pallas_call | solution.py:105
  10.3 0.0 copy-start.2
  10.3 0.0 collective-permute-done
  10.3 0.0 collective-permute-done.1
  10.3 1.4 %collective-permute-done.2 = bf16[128,1024]{1,0:T(8,128)(2,1)S(1)} collective-permute-done((bf16[128,1024]{1,0:T(8,128)(2,1)}, bf16[128,1024]{1,0:T(8,128)(2,1)S(1)}, u32[]{:S(2)}, u32[]{:S(2)}) %collective-permute-start.2) | collective-permute-done | bytes 262176 | tf_op jit(solution)/shard_map/ppermute | solution.py:32
  11.7 0.0 copy-done.1
  11.7 0.1 pad_maximum_fusion.refs_0_
  11.7 2.0 %collective-permute-start.3 = (bf16[512,1024]{1,0:T(8,128)(2,1)S(1)}, bf16[512,1024]{1,0:T(8,128)(2,1)S(1)}, u32[]{:S(2)}, u32[]{:S(2)}) collective-permute-start(bf16[512,1024]{1,0:T(8,128)(2,1)S(1)} %pad_maximum_fusion.refs_0_), channel_id=1, source_target_pairs={{0,32},{1,9},{2,34},{3,11},{4,36},{5,13},{6,38},{7,15},{8,40},{9,1... | collective-permute-start | bytes 3145736 | tf_op jit(solution)/shard_map/ppermute | solution.py:38
  13.7 2.2 %collective-permute-start.4 = (bf16[512,1024]{1,0:T(8,128)(2,1)S(1)}, bf16[512,1024]{1,0:T(8,128)(2,1)S(1)}, u32[]{:S(2)}, u32[]{:S(2)}) collective-permute-start(bf16[512,1024]{1,0:T(8,128)(2,1)S(1)} %pad_maximum_fusion.refs_0_), channel_id=1, source_target_pairs={{0,96},{1,25},{2,98},{3,27},{4,100},{5,29},{6,102},{7,31},{8,104},... | collective-permute-start | bytes 3145736 | tf_op jit(solution)/shard_map/ppermute | solution.py:38
  15.9 0.0 copy-done.2
  15.9 1.6 %collective-permute-start.9 = (bf16[128,512]{1,0:T(8,128)(2,1)S(1)}, bf16[128,512]{1,0:T(8,128)(2,1)S(1)}, u32[]{:S(2)}, u32[]{:S(2)}) collective-permute-start(bf16[128,512]{1,0:T(8,128)(2,1)S(1)} %bitcast.12), channel_id=1, source_target_pairs={{0,16},{1,65},{2,18},{3,67},{4,20},{5,69},{6,22},{7,71},{8,24},{9,... | collective-permute-start | bytes 393224 | tf_op jit(solution)/shard_map/ppermute | solution.py:32
  17.5 2.5 %collective-permute-start.8 = (bf16[128,512]{1,0:T(8,128)(2,1)S(1)}, bf16[128,512]{1,0:T(8,128)(2,1)S(1)}, u32[]{:S(2)}, u32[]{:S(2)}) collective-permute-start(bf16[128,512]{1,0:T(8,128)(2,1)S(1)} %bitcast.13), channel_id=1, source_target_pairs={{0,24},{1,97},{2,26},{3,99},{4,28},{5,101},{6,30},{7,103},{8,0},{9... | collective-permute-start | bytes 393224 | tf_op jit(solution)/shard_map/ppermute | solution.py:32
  20.0 0.0 collective-permute-start.7
  20.0 0.0 slice-done
  20.0 0.0 slice-done.1
  20.1 7.0 %base_first.1 = (f32[768,512]{1,0:T(8,128)S(1)}, bf16[256,8192]{1,0:T(8,128)(2,1)S(1)}) custom-call(bf16[512,8192]{1,0:T(8,128)(2,1)S(1)} %get-tuple-element.37.half_ref, bf16[8192,512]{1,0:T(8,128)(2,1)S(1)} %bitcast.6, bf16[1024,8192]{1,0:T(8,128)(2,1)} %x_ref.2), custom_call_target="tpu_custom_call" | custom-call | flops 5000000000 | bytes 1048576 | tf_op jit(solution)/shard_map/base_first/pallas_call | solution.py:143
  27.1 0.0 collective-permute-done.9
  27.1 0.0 collective-permute-done.8
  27.1 0.6 collective-permute-done.7
  27.7 3.7 %collective-permute-done.3.refs_1_ = bf16[512,1024]{1,0:T(8,128)(2,1)S(1)} collective-permute-done((bf16[512,1024]{1,0:T(8,128)(2,1)S(1)}, bf16[512,1024]{1,0:T(8,128)(2,1)S(1)}, u32[]{:S(2)}, u32[]{:S(2)}) %collective-permute-start.3) | collective-permute-done | bytes 1048608 | tf_op jit(solution)/shard_map/ppermute | solution.py:38
  31.4 0.0 collective-permute-done.4.refs_2_
  31.5 1.9 %collective-permute-start.5 = (bf16[256,1024]{1,0:T(8,128)(2,1)S(1)}, bf16[256,1024]{1,0:T(8,128)(2,1)S(1)}, u32[]{:S(2)}, u32[]{:S(2)}) collective-permute-start(bf16[256,1024]{1,0:T(8,128)(2,1)S(1)} %slice.12), channel_id=1, source_target_pairs={{0,32},{1,9},{2,34},{3,11},{4,36},{5,13},{6,38},{7,15},{8,40},{9,1... | collective-permute-start | bytes 1572872 | tf_op jit(solution)/shard_map/ppermute | solution.py:38
  33.4 1.5 %collective-permute-start.6 = (bf16[256,1024]{1,0:T(8,128)(2,1)S(1)}, bf16[256,1024]{1,0:T(8,128)(2,1)S(1)}, u32[]{:S(2)}, u32[]{:S(2)}) collective-permute-start(bf16[256,1024]{1,0:T(8,128)(2,1)S(1)} %slice.13), channel_id=1, source_target_pairs={{0,96},{1,25},{2,98},{3,27},{4,100},{5,29},{6,102},{7,31},{8,104},... | collective-permute-start | bytes 1572872 | tf_op jit(solution)/shard_map/ppermute | solution.py:38
  34.9 3.5 %shrink_near.1.refs_2_ = f32[1024,128]{1,0:T(8,128)S(1)} custom-call(s32[1024,128]{1,0:T(8,128)S(1)} %mask_code.1.code_ref, bf16[1024,1024]{1,0:T(8,128)(2,1)S(1)} %get-tuple-element.33.x_ref, bf16[512,1024]{1,0:T(8,128)(2,1)S(1)} %pad_maximum_fusion.refs_0_, bf16[512,1024]{1,0:T(8,128)(2,1)S(1)} %collective-permute-done.3.refs_1_, ...), custom_call_target="tpu_custom_call" | custom-call | flops 5000000000 | bytes 1048576 | tf_op jit(solution)/shard_map/shrink_near/pallas_call | solution.py:203
  38.4 0.6 %collective-permute-start.13 = (bf16[512,512]{1,0:T(8,128)(2,1)S(1)}, bf16[512,512]{1,0:T(8,128)(2,1)S(1)}, u32[]{:S(2)}, u32[]{:S(2)}) collective-permute-start(bf16[512,512]{1,0:T(8,128)(2,1)S(1)} %pad_maximum_fusion.1.refs_0_), channel_id=1, source_target_pairs={{0,32},{1,9},{2,34},{3,11},{4,36},{5,13},{6,38},{7,15},{8,40},{9,1... | collective-permute-start | bytes 1572872 | tf_op jit(solution)/shard_map/ppermute | solution.py:38
  39.0 2.7 %collective-permute-start.15 = (bf16[512,512]{1,0:T(8,128)(2,1)S(1)}, bf16[512,512]{1,0:T(8,128)(2,1)S(1)}, u32[]{:S(2)}, u32[]{:S(2)}) collective-permute-start(bf16[512,512]{1,0:T(8,128)(2,1)S(1)} %pad_maximum_fusion.1.refs_0_), channel_id=1, source_target_pairs={{0,96},{1,25},{2,98},{3,27},{4,100},{5,29},{6,102},{7,31},{8,104},... | collective-permute-start | bytes 1572872 | tf_op jit(solution)/shard_map/ppermute | solution.py:38
  41.7 0.3 collective-permute-done.5.refs_0_
  42.0 0.7 %collective-permute-done.6.refs_1_ = bf16[256,1024]{1,0:T(8,128)(2,1)S(1)} collective-permute-done((bf16[256,1024]{1,0:T(8,128)(2,1)S(1)}, bf16[256,1024]{1,0:T(8,128)(2,1)S(1)}, u32[]{:S(2)}, u32[]{:S(2)}) %collective-permute-start.6) | collective-permute-done | bytes 524320 | tf_op jit(solution)/shard_map/ppermute | solution.py:38
  42.7 1.4 %shrink_far.1 = (f32[256,128]{1,0:T(8,128)S(1)}, f32[256,128]{1,0:T(8,128)S(1)}) custom-call(s32[1024,128]{1,0:T(8,128)S(1)} %mask_code.1.code_ref, bf16[1024,1024]{1,0:T(8,128)(2,1)S(1)} %get-tuple-element.33.x_ref, bf16[256,1024]{1,0:T(8,128)(2,1)S(1)} %collective-permute-done.5.refs_0_, bf16[256,1024]{1,0:T(8,128)(2,1)S(1)} %collective-permute-done.6.refs_1_, ...), custom_call_target="tpu_custom_call" | custom-call | flops 1048576 | bytes 1048576 | tf_op jit(solution)/shard_map/shrink_far/pallas_call | solution.py:203
  44.0 0.1 collective-permute-start.10
  44.1 1.3 %collective-permute-done.10 = f32[256,128]{1,0:T(8,128)S(1)} collective-permute-done((f32[256,128]{1,0:T(8,128)S(1)}, f32[256,128]{1,0:T(8,128)S(1)}, u32[]{:S(2)}, u32[]{:S(2)}) %collective-permute-start.10) | collective-permute-done | bytes 131104 | tf_op jit(solution)/shard_map/ppermute | solution.py:44
  45.5 1.7 %collective-permute-start.11 = (f32[256,128]{1,0:T(8,128)S(1)}, f32[256,128]{1,0:T(8,128)S(1)}, u32[]{:S(2)}, u32[]{:S(2)}) collective-permute-start(f32[256,128]{1,0:T(8,128)S(1)} %add.9), channel_id=1, source_target_pairs={{0,2},{1,7},{2,0},{3,5},{4,6},{5,3},{6,4},{7,1},{8,10},{9,15},{10,... | collective-permute-start | bytes 393224 | tf_op jit(solution)/shard_map/ppermute | solution.py:51
  47.1 1.7 %collective-permute-done.13.refs_1_ = bf16[512,512]{1,0:T(8,128)(2,1)S(1)} collective-permute-done((bf16[512,512]{1,0:T(8,128)(2,1)S(1)}, bf16[512,512]{1,0:T(8,128)(2,1)S(1)}, u32[]{:S(2)}, u32[]{:S(2)}) %collective-permute-start.13) | collective-permute-done | bytes 524320 | tf_op jit(solution)/shard_map/ppermute | solution.py:38
  48.9 0.3 collective-permute-start.14
  49.1 0.0 collective-permute-done.15.refs_2_
  49.2 3.3 %collective-permute-start.16 = (bf16[256,512]{1,0:T(8,128)(2,1)S(1)}, bf16[256,512]{1,0:T(8,128)(2,1)S(1)}, u32[]{:S(2)}, u32[]{:S(2)}) collective-permute-start(bf16[256,512]{1,0:T(8,128)(2,1)S(1)} %slice.17), channel_id=1, source_target_pairs={{0,96},{1,25},{2,98},{3,27},{4,100},{5,29},{6,102},{7,31},{8,104},... | collective-permute-start | bytes 786440 | tf_op jit(solution)/shard_map/ppermute | solution.py:38
  52.4 0.0 collective-permute-done.11
  52.5 3.1 %collective-permute-start.12 = (f32[256,128]{1,0:T(8,128)S(1)}, f32[256,128]{1,0:T(8,128)S(1)}, u32[]{:S(2)}, u32[]{:S(2)}) collective-permute-start(f32[256,128]{1,0:T(8,128)S(1)} %add.10), channel_id=1, source_target_pairs={{0,6},{1,3},{2,4},{3,1},{4,2},{5,7},{6,0},{7,5},{8,14},{9,11},{10,... | collective-permute-start | bytes 393224 | tf_op jit(solution)/shard_map/ppermute | solution.py:51
  55.6 2.3 %base_second.1.bottom_ref = f32[256,512]{1,0:T(8,128)S(1)} custom-call(bf16[256,8192]{1,0:T(8,128)(2,1)S(1)} %get-tuple-element.48.x_ref, bf16[8192,512]{1,0:T(8,128)(2,1)S(1)} %bitcast.6), custom_call_target="tpu_custom_call" | custom-call | flops 5000000000 | bytes 1048576 | tf_op jit(solution)/shard_map/base_second/pallas_call | solution.py:160
  57.9 0.0 collective-permute-done.14.refs_3_
  57.9 0.0 collective-permute-done.16.refs_4_
  57.9 0.8 %collective-permute-done.12 = f32[256,128]{1,0:T(8,128)S(1)} collective-permute-done((f32[256,128]{1,0:T(8,128)S(1)}, f32[256,128]{1,0:T(8,128)S(1)}, u32[]{:S(2)}, u32[]{:S(2)}) %collective-permute-start.12) | collective-permute-done | bytes 131104 | tf_op jit(solution)/shard_map/ppermute | solution.py:51
  58.7 0.1 collective-permute-start.17
  58.8 1.2 %collective-permute-done.17.other_ref = bf16[256,128]{1,0:T(8,128)(2,1)S(1)} collective-permute-done((bf16[256,128]{1,0:T(8,128)(2,1)S(1)}, bf16[256,128]{1,0:T(8,128)(2,1)S(1)}, u32[]{:S(2)}, u32[]{:S(2)}) %collective-permute-start.17) | collective-permute-done | bytes 65568 | tf_op jit(solution)/shard_map/ppermute | solution.py:44
  60.1 3.7 %expand.1 = bf16[1024,512]{1,0:T(8,128)(2,1)} custom-call(s32[1024,128]{1,0:T(8,128)S(1)} %mask_code.1.code_ref, bf16[256,128]{1,0:T(8,128)(2,1)S(1)} %add_convert_fusion.mine_ref, bf16[256,128]{1,0:T(8,128)(2,1)S(1)} %collective-permute-done.17.other_ref, f32[768,512]{1,0:T(8,128)S(1)} %get-tuple-element.51.top_ref, f32[256,512]{1,0:T(8,128)S(1)} %base_second.1.bottom_ref, ...), custom_call_target="tpu_custom_call" | custom-call | flops 2147483648 | bytes 3145728 | tf_op jit(solution)/shard_map/expand/pallas_call | solution.py:254
  (9 shorter events, 0.2 us)
Async XLA Ops:
  0.0 10.3 %collective-permute-start = (bf16[128,1024]{1,0:T(8,128)(2,1)}, bf16[128,1024]{1,0:T(8,128)(2,1)S(1)}, u32[]{:S(2)}, u32[]{:S(2)}) collective-permute-start(bf16[128,1024]{1,0:T(8,128)(2,1)} %bitcast.8), channel_id=1, source_target_pairs={{0,8},{1,33},{2,10},{3,35},{4,12},{5,37},{6,14},{7,39},{8,16},{9,4... | collective-permute-start | bytes 786440 | tf_op jit(solution)/shard_map/ppermute | solution.py:32
  1.6 8.7 %collective-permute-start.1 = (bf16[128,1024]{1,0:T(8,128)(2,1)}, bf16[128,1024]{1,0:T(8,128)(2,1)S(1)}, u32[]{:S(2)}, u32[]{:S(2)}) collective-permute-start(bf16[128,1024]{1,0:T(8,128)(2,1)} %bitcast.9), channel_id=1, source_target_pairs={{0,24},{1,97},{2,26},{3,99},{4,28},{5,101},{6,30},{7,103},{8,0},{9... | collective-permute-start | bytes 786440 | tf_op jit(solution)/shard_map/ppermute | solution.py:32
  3.2 8.4 %collective-permute-start.2 = (bf16[128,1024]{1,0:T(8,128)(2,1)}, bf16[128,1024]{1,0:T(8,128)(2,1)S(1)}, u32[]{:S(2)}, u32[]{:S(2)}) collective-permute-start(bf16[128,1024]{1,0:T(8,128)(2,1)} %bitcast.10), channel_id=1, source_target_pairs={{0,16},{1,65},{2,18},{3,67},{4,20},{5,69},{6,22},{7,71},{8,24},{9,... | collective-permute-start | bytes 786440 | tf_op jit(solution)/shard_map/ppermute | solution.py:32
  5.1 0.7 %copy-start = (s32[1024,1]{0,1:T(1,128)S(1)}, s32[1024,1]{0,1:T(1,128)}, u32[]{:S(2)}) copy-start(s32[1024,1]{0,1:T(1,128)} %param.6) | copy-start | bytes 12292
  5.8 14.2 %slice-start = ((s8[8388608]{0:T(1024)(128)(4,1)}), s8[4194304]{0:T(1024)(128)(4,1)S(1)}, s32[]{:S(2)}) async-start(s8[8388608]{0:T(1024)(128)(4,1)} %bitcast.5), calls=%async_computation | async-start | bytes 8388608
  6.0 5.6 %copy-start.1 = (bf16[2,1024,64]{1,2,0:T(8,128)(2,1)S(1)}, bf16[2,1024,64]{1,2,0:T(8,128)(2,1)}, u32[]{:S(2)}) copy-start(bf16[2,1024,64]{1,2,0:T(8,128)(2,1)} %param.8) | copy-start | bytes 786436
  6.0 14.0 %slice-start.1 = ((s8[8388608]{0:T(1024)(128)(4,1)}), s8[4194304]{0:T(1024)(128)(4,1)S(1)}, s32[]{:S(2)}) async-start(s8[8388608]{0:T(1024)(128)(4,1)} %bitcast.5), calls=%async_computation.1 | async-start | bytes 8388608
  10.3 5.7 %copy-start.2 = (bf16[2,64,512]{2,1,0:T(8,128)(2,1)S(1)}, bf16[2,64,512]{2,1,0:T(8,128)(2,1)}, u32[]{:S(2)}) copy-start(bf16[2,64,512]{2,1,0:T(8,128)(2,1)} %param.9) | copy-start | bytes 393220
  11.7 19.7 %collective-permute-start.3 = (bf16[512,1024]{1,0:T(8,128)(2,1)S(1)}, bf16[512,1024]{1,0:T(8,128)(2,1)S(1)}, u32[]{:S(2)}, u32[]{:S(2)}) collective-permute-start(bf16[512,1024]{1,0:T(8,128)(2,1)S(1)} %pad_maximum_fusion.refs_0_), channel_id=1, source_target_pairs={{0,32},{1,9},{2,34},{3,11},{4,36},{5,13},{6,38},{7,15},{8,40},{9,1... | collective-permute-start | bytes 3145736 | tf_op jit(solution)/shard_map/ppermute | solution.py:38
  13.7 17.7 %collective-permute-start.4 = (bf16[512,1024]{1,0:T(8,128)(2,1)S(1)}, bf16[512,1024]{1,0:T(8,128)(2,1)S(1)}, u32[]{:S(2)}, u32[]{:S(2)}) collective-permute-start(bf16[512,1024]{1,0:T(8,128)(2,1)S(1)} %pad_maximum_fusion.refs_0_), channel_id=1, source_target_pairs={{0,96},{1,25},{2,98},{3,27},{4,100},{5,29},{6,102},{7,31},{8,104},... | collective-permute-start | bytes 3145736 | tf_op jit(solution)/shard_map/ppermute | solution.py:38
  15.9 11.1 %collective-permute-start.9 = (bf16[128,512]{1,0:T(8,128)(2,1)S(1)}, bf16[128,512]{1,0:T(8,128)(2,1)S(1)}, u32[]{:S(2)}, u32[]{:S(2)}) collective-permute-start(bf16[128,512]{1,0:T(8,128)(2,1)S(1)} %bitcast.12), channel_id=1, source_target_pairs={{0,16},{1,65},{2,18},{3,67},{4,20},{5,69},{6,22},{7,71},{8,24},{9,... | collective-permute-start | bytes 393224 | tf_op jit(solution)/shard_map/ppermute | solution.py:32
  17.5 9.6 %collective-permute-start.8 = (bf16[128,512]{1,0:T(8,128)(2,1)S(1)}, bf16[128,512]{1,0:T(8,128)(2,1)S(1)}, u32[]{:S(2)}, u32[]{:S(2)}) collective-permute-start(bf16[128,512]{1,0:T(8,128)(2,1)S(1)} %bitcast.13), channel_id=1, source_target_pairs={{0,24},{1,97},{2,26},{3,99},{4,28},{5,101},{6,30},{7,103},{8,0},{9... | collective-permute-start | bytes 393224 | tf_op jit(solution)/shard_map/ppermute | solution.py:32
  20.0 7.6 %collective-permute-start.7 = (bf16[128,512]{1,0:T(8,128)(2,1)S(1)}, bf16[128,512]{1,0:T(8,128)(2,1)S(1)}, u32[]{:S(2)}, u32[]{:S(2)}) collective-permute-start(bf16[128,512]{1,0:T(8,128)(2,1)S(1)} %bitcast.14), channel_id=1, source_target_pairs={{0,8},{1,33},{2,10},{3,35},{4,12},{5,37},{6,14},{7,39},{8,16},{9,4... | collective-permute-start | bytes 393224 | tf_op jit(solution)/shard_map/ppermute | solution.py:32
  31.5 10.5 %collective-permute-start.5 = (bf16[256,1024]{1,0:T(8,128)(2,1)S(1)}, bf16[256,1024]{1,0:T(8,128)(2,1)S(1)}, u32[]{:S(2)}, u32[]{:S(2)}) collective-permute-start(bf16[256,1024]{1,0:T(8,128)(2,1)S(1)} %slice.12), channel_id=1, source_target_pairs={{0,32},{1,9},{2,34},{3,11},{4,36},{5,13},{6,38},{7,15},{8,40},{9,1... | collective-permute-start | bytes 1572872 | tf_op jit(solution)/shard_map/ppermute | solution.py:38
  33.4 9.3 %collective-permute-start.6 = (bf16[256,1024]{1,0:T(8,128)(2,1)S(1)}, bf16[256,1024]{1,0:T(8,128)(2,1)S(1)}, u32[]{:S(2)}, u32[]{:S(2)}) collective-permute-start(bf16[256,1024]{1,0:T(8,128)(2,1)S(1)} %slice.13), channel_id=1, source_target_pairs={{0,96},{1,25},{2,98},{3,27},{4,100},{5,29},{6,102},{7,31},{8,104},... | collective-permute-start | bytes 1572872 | tf_op jit(solution)/shard_map/ppermute | solution.py:38
  38.4 10.5 %collective-permute-start.13 = (bf16[512,512]{1,0:T(8,128)(2,1)S(1)}, bf16[512,512]{1,0:T(8,128)(2,1)S(1)}, u32[]{:S(2)}, u32[]{:S(2)}) collective-permute-start(bf16[512,512]{1,0:T(8,128)(2,1)S(1)} %pad_maximum_fusion.1.refs_0_), channel_id=1, source_target_pairs={{0,32},{1,9},{2,34},{3,11},{4,36},{5,13},{6,38},{7,15},{8,40},{9,1... | collective-permute-start | bytes 1572872 | tf_op jit(solution)/shard_map/ppermute | solution.py:38
  39.0 10.1 %collective-permute-start.15 = (bf16[512,512]{1,0:T(8,128)(2,1)S(1)}, bf16[512,512]{1,0:T(8,128)(2,1)S(1)}, u32[]{:S(2)}, u32[]{:S(2)}) collective-permute-start(bf16[512,512]{1,0:T(8,128)(2,1)S(1)} %pad_maximum_fusion.1.refs_0_), channel_id=1, source_target_pairs={{0,96},{1,25},{2,98},{3,27},{4,100},{5,29},{6,102},{7,31},{8,104},... | collective-permute-start | bytes 1572872 | tf_op jit(solution)/shard_map/ppermute | solution.py:38
  44.0 1.4 %collective-permute-start.10 = (f32[256,128]{1,0:T(8,128)S(1)}, f32[256,128]{1,0:T(8,128)S(1)}, u32[]{:S(2)}, u32[]{:S(2)}) collective-permute-start(f32[256,128]{1,0:T(8,128)S(1)} %get-tuple-element.47), channel_id=1, source_target_pairs={{0,1},{1,0},{2,3},{3,2},{4,5},{5,4},{6,7},{7,6},{8,9},{9,8},{10,11... | collective-permute-start | bytes 393224 | tf_op jit(solution)/shard_map/ppermute | solution.py:44
  45.5 7.0 %collective-permute-start.11 = (f32[256,128]{1,0:T(8,128)S(1)}, f32[256,128]{1,0:T(8,128)S(1)}, u32[]{:S(2)}, u32[]{:S(2)}) collective-permute-start(f32[256,128]{1,0:T(8,128)S(1)} %add.9), channel_id=1, source_target_pairs={{0,2},{1,7},{2,0},{3,5},{4,6},{5,3},{6,4},{7,1},{8,10},{9,15},{10,... | collective-permute-start | bytes 393224 | tf_op jit(solution)/shard_map/ppermute | solution.py:51
  48.9 9.0 %collective-permute-start.14 = (bf16[256,512]{1,0:T(8,128)(2,1)S(1)}, bf16[256,512]{1,0:T(8,128)(2,1)S(1)}, u32[]{:S(2)}, u32[]{:S(2)}) collective-permute-start(bf16[256,512]{1,0:T(8,128)(2,1)S(1)} %slice.16), channel_id=1, source_target_pairs={{0,32},{1,9},{2,34},{3,11},{4,36},{5,13},{6,38},{7,15},{8,40},{9,1... | collective-permute-start | bytes 786440 | tf_op jit(solution)/shard_map/ppermute | solution.py:38
  49.2 8.7 %collective-permute-start.16 = (bf16[256,512]{1,0:T(8,128)(2,1)S(1)}, bf16[256,512]{1,0:T(8,128)(2,1)S(1)}, u32[]{:S(2)}, u32[]{:S(2)}) collective-permute-start(bf16[256,512]{1,0:T(8,128)(2,1)S(1)} %slice.17), channel_id=1, source_target_pairs={{0,96},{1,25},{2,98},{3,27},{4,100},{5,29},{6,102},{7,31},{8,104},... | collective-permute-start | bytes 786440 | tf_op jit(solution)/shard_map/ppermute | solution.py:38
  52.5 6.3 %collective-permute-start.12 = (f32[256,128]{1,0:T(8,128)S(1)}, f32[256,128]{1,0:T(8,128)S(1)}, u32[]{:S(2)}, u32[]{:S(2)}) collective-permute-start(f32[256,128]{1,0:T(8,128)S(1)} %add.10), channel_id=1, source_target_pairs={{0,6},{1,3},{2,4},{3,1},{4,2},{5,7},{6,0},{7,5},{8,14},{9,11},{10,... | collective-permute-start | bytes 393224 | tf_op jit(solution)/shard_map/ppermute | solution.py:51
  58.7 1.3 %collective-permute-start.17 = (bf16[256,128]{1,0:T(8,128)(2,1)S(1)}, bf16[256,128]{1,0:T(8,128)(2,1)S(1)}, u32[]{:S(2)}, u32[]{:S(2)}) collective-permute-start(bf16[256,128]{1,0:T(8,128)(2,1)S(1)} %add_convert_fusion.mine_ref), channel_id=1, source_target_pairs={{0,1},{1,0},{2,3},{3,2},{4,5},{5,4},{6,7},{7,6},{8,9},{9,8},{10,11... | collective-permute-start | bytes 196616 | tf_op jit(solution)/shard_map/ppermute | solution.py:44

commit v11 on v10

--- a/solution.py
+++ b/solution.py
@@ -213,8 +213,8 @@
     )(*args)
 
 
-def expand_kernel(groups, code_ref, mine_ref, other_ref, top_ref, bottom_ref, *refs):
-    b_refs, o_ref = refs[:-1], refs[-1]
+def expand_kernel(code_ref, mine_ref, other_ref, top_ref, bottom_ref, *refs):
+    *b_refs, o_ref, b_all = refs
     block = o_ref.shape[0]
     step = pl.program_id(0)
     here = pl.ds(pl.multiple_of(step * block, block), block)
@@ -227,13 +227,19 @@
     lane = lax.broadcasted_iota(jnp.int32, packed.shape, 1)
     left = (lane < 64) == (step == 0)
     rows = jnp.where(left, packed, pltpu.roll(packed, 64, 1))
-    delta = None
-    for (places, ref_at, lanes), b_ref in zip(groups, b_refs):
-        spread = jnp.concatenate(
-            [jnp.where(code == owner(j, i), rows, 0.0).astype(BF) for j, i in places], axis=1
-        )
-        d = jnp.dot(spread, b_ref[ref_at:, lanes : lanes + o_ref.shape[1]], preferred_element_type=F32)
-        delta = d if delta is None else delta + d
+    n = o_ref.shape[1]
+
+    @pl.when(step == 0)
+    def _():
+        for k in range(16):
+            part, at = b_refs[k // 4], 64 * (k % 4)
+            for side in range(2):
+                b_all[pl.ds(128 * k + 64 * side, 64), :] = part[pl.ds(at, 64), n * side : n * side + n]
+
+    spread = jnp.concatenate(
+        [jnp.where(code == owner(j, i), rows, 0.0).astype(BF) for i in HOPS for j in HOPS], axis=1
+    )
+    delta = jnp.dot(spread, b_all[...], preferred_element_type=F32)
     delta = delta.astype(BF).astype(F32)
     quarter = block // 2
 
@@ -247,17 +253,18 @@
         o_ref[quarter:, :] = (bottom_ref[...] + adapter_scale * delta[quarter:]).astype(BF)
 
 
-def expand(code, mine, other, base, parts):
+def expand(code, mine, other, base, ups):
     m, n = code.shape[0], base[0].shape[1]
     block = m // 2
-    args = [code, mine, other, *base] + [part[0] for part in parts]
-    return pl.pallas_call(
-        functools.partial(expand_kernel, [part[1:] for part in parts]),
+    args = [code, mine, other, *base, *ups]
+    return pl.pallas_call(
+        expand_kernel,
         grid=(2,),
         in_specs=[VMEM] * len(args),
         out_specs=pl.BlockSpec((block, n), lambda i: (i, 0)),
         out_shape=jax.ShapeDtypeStruct((m, n), BF),
-        compiler_params=params(12),
+        scratch_shapes=[pltpu.VMEM((2048, n), BF)],
+        compiler_params=params(14),
         cost_estimate=cost(2 * m * n * 2048, 6 * m * n),
         name="expand",
     )(*args)
@@ -276,29 +283,32 @@
     near = [first(down, d) for d in (1, -1, 2)]
     code = mask_code(token_adapter_index)
     here, half = fetch(tie(activations, code)[0], width)
-    near, here, half, up = tie(near, here, half, up)
-    d_own = jnp.concatenate([down, *near], axis=0)
-    d_before, d_after = second(d_own, 1), second(d_own, -1)
-    u_own = jnp.concatenate([up] + [first(up, d) for d in (1, -1, 2)], axis=0)
-    top, rest = base_first(half, query_matrix, activations)
-    d_before, d_after, top = tie(d_before, d_after, top)
-
-    d_two = [second(d_before[:256], 1), second(d_after[256:], -1)]
-    groups = [([d_own], row(0)), ([d_before], row(-1)), ([d_after], row(1))]
+    before, after, far, here, half = tie(*near, here, half)
+    own_up = jnp.concatenate([up[:64], up[64:]], axis=1)
+    top = jnp.concatenate([down, before, own_up], axis=0)
+    bottom = jnp.concatenate([after, far, own_up], axis=0)
+    top_before, bottom_after = second(top, 1), second(bottom, -1)
+    bottom_before, top_after = second(bottom[:256], 1), second(top[:256], -1)
+    base, rest = base_first(half, query_matrix, activations)
+    top_before, bottom_after, base = tie(top_before, bottom_after, base)
+
+    top_two, bottom_two = second(top_before, 1), second(bottom_after[:256], -1)
+    groups = [
+        ([top[:256], bottom[:256]], row(0)),
+        ([top_before[:256], bottom_before], row(-1)),
+        ([top_after, bottom_after[:256]], row(1)),
+    ]
     total = shrink(code, here, groups, None, False, "shrink_near", 5000000000)
-    total, u_own = tie(total, u_own)
-    u_before, u_after = second(u_own, 1), second(u_own, -1)
-    *d_two, total = tie(*d_two, total)
+    top_two, bottom_two, total = tie(top_two, bottom_two, total)
+    d_two = [top_two[:256], bottom_two]
     keep, give = shrink(code, here, [(d_two, row(2))], total, True, "shrink_far")
     keep = keep + other_core(give)
-    u_two = [second(u_before[:256], 1), second(u_after[256:], -1)]
+    column = jnp.concatenate([own_up] + [a[256:] for a in (top_before, bottom_after, top_two)], axis=0)
+    ups = [column] + [first(column, d) for d in (1, -1, 2)]
     keep = keep + pair(keep, 0)
-    there, bottom, *u_two = tie(pair(keep, 1), base_second(rest, query_matrix), *u_two)
-    keep = keep + there
-    mine = keep.astype(BF)
-    parts = [(u_own, row(0), 0, 0), (u_before, row(-1), 0, 0), (u_after, row(1), 0, 0)]
-    parts += [(a, row(2, hops), 0, 0) for a, hops in zip(u_two, (HOPS[:2], HOPS[2:]))]
-    return expand(code, mine, other_core(mine), [top, bottom], parts)
+    there, last = tie(pair(keep, 1), base_second(rest, query_matrix))
+    mine, *ups = tie((keep + there).astype(BF), *ups)
+    return expand(code, mine, other_core(mine), [base, last], ups)
 
 
 def solution(mesh):

time: 65 us -> 68.1 us (1.048)
  waiting for transfers between devices: 11.8 us -> 18.9 us
  starting transfers between devices: 28.6 us -> 24.2 us
    ppermute x6, waiting for transfers between devices: 1.97 us -> 7.75 us  [first(): lax.ppermute(a, AXES, every(lambda x, y, z, c: (x, y, z + d, c) if c else...]
    ppermute x8 -> x6, starting transfers between devices: 14.4 us -> 10.8 us  [second(): lax.ppermute(a, AXES, every(lambda x, y, z, c: (x + d, y, z, c) if c else...]
    ppermute x2, waiting for transfers between devices: 0.83 us -> 1.62 us  [pair(): return lax.ppermute(a, AXES, every(to))]
    ppermute x2, starting transfers between devices: 4.74 us -> 3.97 us  [pair(): return lax.ppermute(a, AXES, every(to))]
    ppermute x8 -> x6, waiting for transfers between devices: 6.42 us -> 7.13 us  [second(): lax.ppermute(a, AXES, every(lambda x, y, z, c: (x + d, y, z, c) if c else...]
  transfers between devices with their start and end apart: 18 -> 16, of which waited for: 9 -> 12; matrix products, arithmetic and copies ran while one was open for 0% -> 0% of each run, Pallas kernels for 29% -> 26%
where the time goes in v11:
time: 68.1 us; the launch traced here: 66.9 us
  starting transfers between devices  24.2 us (36%)
  Pallas kernels  22.4 us (33%)
  waiting for transfers between devices  18.9 us (28%)
  local copies, waits for them, and re-layouts  0.89 us (1%)
    ppermute x6, starting transfers between devices, second(): lax.ppermute(a, AXES, every(lambda x, y, z, c: (x + d, y, z, c) if c else...  10.8 us
    ppermute x6, starting transfers between devices, first(): lax.ppermute(a, AXES, every(lambda x, y, z, c: (x, y, z + d, c) if c else...  9.2 us
    ppermute x6, waiting for transfers between devices, first(): lax.ppermute(a, AXES, every(lambda x, y, z, c: (x, y, z + d, c) if c else...  7.75 us
    ppermute x6, waiting for transfers between devices, second(): lax.ppermute(a, AXES, every(lambda x, y, z, c: (x + d, y, z, c) if c else...  7.13 us
    pallas_call x1, Pallas kernels, base_first(): pl.pallas_call(base_kernel, in_specs=[VMEM, VMEM, HBM], out_specs=[VMEM,...  6.99 us
    pallas_call x2, Pallas kernels, shrink(): pl.pallas_call(functools.partial(shrink_kernel, [(len(parts), places) for...  4.81 us
    pallas_call x1, Pallas kernels, fetch(): pl.pallas_call(fetch_kernel, in_specs=[HBM], out_specs=[VMEM] * 2, out_sh...  4.2 us
    ppermute x2, starting transfers between devices, pair(): return lax.ppermute(a, AXES, every(to))  3.97 us
  transfers between devices with their start and end apart: 16, of which 12 were waited for; matrix products, arithmetic and copies ran while one was open for 0% of the time, Pallas kernels for 26%

profile of v11, /device:TPU:0, one launch (start us, length us, event | category | flops | bytes accessed | tf_op | source)
XLA Modules:
  0.0 66.9 jit_solution(6399439188706580590)
XLA Ops:
  0.0 3.1 %collective-permute-start.2 = (bf16[128,1024]{1,0:T(8,128)(2,1)}, bf16[128,1024]{1,0:T(8,128)(2,1)S(1)}, u32[]{:S(2)}, u32[]{:S(2)}) collective-permute-start(bf16[128,1024]{1,0:T(8,128)(2,1)} %bitcast.11), channel_id=1, source_target_pairs={{0,16},{1,65},{2,18},{3,67},{4,20},{5,69},{6,22},{7,71},{8,24},{9,... | collective-permute-start | bytes 786440 | tf_op jit(solution)/shard_map/ppermute | solution.py:32
  3.1 1.1 %collective-permute-start.1 = (bf16[128,1024]{1,0:T(8,128)(2,1)}, bf16[128,1024]{1,0:T(8,128)(2,1)S(1)}, u32[]{:S(2)}, u32[]{:S(2)}) collective-permute-start(bf16[128,1024]{1,0:T(8,128)(2,1)} %bitcast.12), channel_id=1, source_target_pairs={{0,24},{1,97},{2,26},{3,99},{4,28},{5,101},{6,30},{7,103},{8,0},{9... | collective-permute-start | bytes 786440 | tf_op jit(solution)/shard_map/ppermute | solution.py:32
  4.2 0.9 %collective-permute-start = (bf16[128,1024]{1,0:T(8,128)(2,1)}, bf16[128,1024]{1,0:T(8,128)(2,1)S(1)}, u32[]{:S(2)}, u32[]{:S(2)}) collective-permute-start(bf16[128,1024]{1,0:T(8,128)(2,1)} %bitcast.13), channel_id=1, source_target_pairs={{0,8},{1,33},{2,10},{3,35},{4,12},{5,37},{6,14},{7,39},{8,16},{9,4... | collective-permute-start | bytes 786440 | tf_op jit(solution)/shard_map/ppermute | solution.py:32
  5.1 0.0 copy-start
  5.1 0.7 %copy-done = s32[1024,1]{0,1:T(1,128)S(1)} copy-done((s32[1024,1]{0,1:T(1,128)S(1)}, s32[1024,1]{0,1:T(1,128)}, u32[]{:S(2)}) %copy-start) | copy-done | bytes 4120
  5.8 0.0 slice-start
  5.8 0.2 mask_code.1.code_ref
  6.0 0.0 copy-start.2
  6.0 0.0 copy-start.1
  6.1 0.0 slice-start.1
  6.1 4.2 %fetch.1 = (bf16[1024,1024]{1,0:T(8,128)(2,1)S(1)}, bf16[512,8192]{1,0:T(8,128)(2,1)S(1)}) custom-call(bf16[1024,8192]{1,0:T(8,128)(2,1)} %x_ref.2), custom_call_target="tpu_custom_call" | custom-call | flops 1000000 | bytes 1048576 | tf_op jit(solution)/shard_map/fetch/pallas_call | solution.py:105
  10.3 0.0 copy-done.2
  10.3 0.0 collective-permute-done.2
  10.3 0.8 %collective-permute-done.1 = bf16[128,1024]{1,0:T(8,128)(2,1)S(1)} collective-permute-done((bf16[128,1024]{1,0:T(8,128)(2,1)}, bf16[128,1024]{1,0:T(8,128)(2,1)S(1)}, u32[]{:S(2)}, u32[]{:S(2)}) %collective-permute-start.1) | collective-permute-done | bytes 262176 | tf_op jit(solution)/shard_map/ppermute | solution.py:32
  11.1 1.0 %collective-permute-done = bf16[128,1024]{1,0:T(8,128)(2,1)S(1)} collective-permute-done((bf16[128,1024]{1,0:T(8,128)(2,1)}, bf16[128,1024]{1,0:T(8,128)(2,1)S(1)}, u32[]{:S(2)}, u32[]{:S(2)}) %collective-permute-start) | collective-permute-done | bytes 262176 | tf_op jit(solution)/shard_map/ppermute | solution.py:32
  12.1 0.0 copy-done.1
  12.1 0.1 fusion
  12.2 4.1 %collective-permute-start.4 = (bf16[320,1024]{1,0:T(8,128)(2,1)S(1)}, bf16[320,1024]{1,0:T(8,128)(2,1)S(1)}, u32[]{:S(2)}, u32[]{:S(2)}) collective-permute-start(bf16[320,1024]{1,0:T(8,128)(2,1)S(1)} %get-tuple-element.55), channel_id=1, source_target_pairs={{0,96},{1,25},{2,98},{3,27},{4,100},{5,29},{6,102},{7,31},{8,104},... | collective-permute-start | bytes 1966088 | tf_op jit(solution)/shard_map/ppermute | solution.py:38
  16.3 0.0 collective-permute-start.3
  16.3 0.1 collective-permute-start.7
  16.5 3.3 %collective-permute-start.8 = (bf16[256,1024]{1,0:T(8,128)(2,1)S(1)}, bf16[256,1024]{1,0:T(8,128)(2,1)S(1)}, u32[]{:S(2)}, u32[]{:S(2)}) collective-permute-start(bf16[256,1024]{1,0:T(8,128)(2,1)S(1)} %pad_maximum_fusion.1.refs_0_), channel_id=1, source_target_pairs={{0,96},{1,25},{2,98},{3,27},{4,100},{5,29},{6,102},{7,31},{8,104},... | collective-permute-start | bytes 1572872 | tf_op jit(solution)/shard_map/ppermute | solution.py:38
  19.8 0.0 slice-done
  19.8 0.0 slice-done.1
  19.8 7.0 %base_first.1 = (f32[768,512]{1,0:T(8,128)S(1)}, bf16[256,8192]{1,0:T(8,128)(2,1)S(1)}) custom-call(bf16[512,8192]{1,0:T(8,128)(2,1)S(1)} %get-tuple-element.37.half_ref, bf16[8192,512]{1,0:T(8,128)(2,1)S(1)} %bitcast.9, bf16[1024,8192]{1,0:T(8,128)(2,1)} %x_ref.2), custom_call_target="tpu_custom_call" | custom-call | flops 5000000000 | bytes 1048576 | tf_op jit(solution)/shard_map/base_first/pallas_call | solution.py:143
  26.8 0.0 collective-permute-done.4
  26.8 1.3 %collective-permute-done.3 = bf16[320,1024]{1,0:T(8,128)(2,1)S(1)} collective-permute-done((bf16[320,1024]{1,0:T(8,128)(2,1)S(1)}, bf16[320,1024]{1,0:T(8,128)(2,1)S(1)}, u32[]{:S(2)}, u32[]{:S(2)}) %collective-permute-start.3) | collective-permute-done | bytes 655392 | tf_op jit(solution)/shard_map/ppermute | solution.py:38
  28.1 0.0 collective-permute-start.5
  28.1 3.3 %collective-permute-start.6 = (bf16[256,1024]{1,0:T(8,128)(2,1)S(1)}, bf16[256,1024]{1,0:T(8,128)(2,1)S(1)}, u32[]{:S(2)}, u32[]{:S(2)}) collective-permute-start(bf16[256,1024]{1,0:T(8,128)(2,1)S(1)} %slice.41.refs_5_), channel_id=1, source_target_pairs={{0,96},{1,25},{2,98},{3,27},{4,100},{5,29},{6,102},{7,31},{8,104},... | collective-permute-start | bytes 1572872 | tf_op jit(solution)/shard_map/ppermute | solution.py:38
  31.5 2.2 %collective-permute-done.7.refs_3_ = bf16[256,1024]{1,0:T(8,128)(2,1)S(1)} collective-permute-done((bf16[256,1024]{1,0:T(8,128)(2,1)S(1)}, bf16[256,1024]{1,0:T(8,128)(2,1)S(1)}, u32[]{:S(2)}, u32[]{:S(2)}) %collective-permute-start.7) | collective-permute-done | bytes 524320 | tf_op jit(solution)/shard_map/ppermute | solution.py:38
  33.7 0.0 collective-permute-done.8.refs_4_
  33.7 3.4 %shrink_near.1.refs_2_ = f32[1024,128]{1,0:T(8,128)S(1)} custom-call(s32[1024,128]{1,0:T(8,128)S(1)} %mask_code.1.code_ref, bf16[1024,1024]{1,0:T(8,128)(2,1)S(1)} %get-tuple-element.33.x_ref, bf16[256,1024]{1,0:T(8,128)(2,1)S(1)} %pad_maximum_fusion.1.refs_0_, bf16[256,1024]{1,0:T(8,128)(2,1)S(1)} %constant_dynamic-update-slice_fusion.refs_1_, ...), custom_call_target="tpu_custom_call" | custom-call | flops 5000000000 | bytes 1048576 | tf_op jit(solution)/shard_map/shrink_near/pallas_call | solution.py:203
  37.2 1.0 %collective-permute-done.6.refs_1_ = bf16[256,1024]{1,0:T(8,128)(2,1)S(1)} collective-permute-done((bf16[256,1024]{1,0:T(8,128)(2,1)S(1)}, bf16[256,1024]{1,0:T(8,128)(2,1)S(1)}, u32[]{:S(2)}, u32[]{:S(2)}) %collective-permute-start.6) | collective-permute-done | bytes 524320 | tf_op jit(solution)/shard_map/ppermute | solution.py:38
  38.2 2.6 %collective-permute-done.5 = bf16[320,1024]{1,0:T(8,128)(2,1)S(1)} collective-permute-done((bf16[320,1024]{1,0:T(8,128)(2,1)S(1)}, bf16[320,1024]{1,0:T(8,128)(2,1)S(1)}, u32[]{:S(2)}, u32[]{:S(2)}) %collective-permute-start.5) | collective-permute-done | bytes 655392 | tf_op jit(solution)/shard_map/ppermute | solution.py:38
  40.8 1.4 %shrink_far.1 = (f32[256,128]{1,0:T(8,128)S(1)}, f32[256,128]{1,0:T(8,128)S(1)}) custom-call(s32[1024,128]{1,0:T(8,128)S(1)} %mask_code.1.code_ref, bf16[1024,1024]{1,0:T(8,128)(2,1)S(1)} %get-tuple-element.33.x_ref, bf16[256,1024]{1,0:T(8,128)(2,1)S(1)} %slice.43.refs_0_, bf16[256,1024]{1,0:T(8,128)(2,1)S(1)} %collective-permute-done.6.refs_1_, ...), custom_call_target="tpu_custom_call" | custom-call | flops 1048576 | bytes 1048576 | tf_op jit(solution)/shard_map/shrink_far/pallas_call | solution.py:203
  42.2 0.1 collective-permute-start.9
  42.2 1.3 %collective-permute-done.9 = f32[256,128]{1,0:T(8,128)S(1)} collective-permute-done((f32[256,128]{1,0:T(8,128)S(1)}, f32[256,128]{1,0:T(8,128)S(1)}, u32[]{:S(2)}, u32[]{:S(2)}) %collective-permute-start.9) | collective-permute-done | bytes 131104 | tf_op jit(solution)/shard_map/ppermute | solution.py:44
  43.6 1.7 %collective-permute-start.10 = (f32[256,128]{1,0:T(8,128)S(1)}, f32[256,128]{1,0:T(8,128)S(1)}, u32[]{:S(2)}, u32[]{:S(2)}) collective-permute-start(f32[256,128]{1,0:T(8,128)S(1)} %add.9), channel_id=1, source_target_pairs={{0,2},{1,7},{2,0},{3,5},{4,6},{5,3},{6,4},{7,1},{8,10},{9,15},{10,... | collective-permute-start | bytes 393224 | tf_op jit(solution)/shard_map/ppermute | solution.py:51
  45.4 2.0 %collective-permute-start.14 = (bf16[256,1024]{1,0:T(8,128)(2,1)S(1)}, bf16[256,1024]{1,0:T(8,128)(2,1)S(1)}, u32[]{:S(2)}, u32[]{:S(2)}) collective-permute-start(bf16[256,1024]{1,0:T(8,128)(2,1)S(1)} %pad_maximum_fusion.2.refs_0_), channel_id=1, source_target_pairs={{0,16},{1,65},{2,18},{3,67},{4,20},{5,69},{6,22},{7,71},{8,24},{9,... | collective-permute-start | bytes 1572872 | tf_op jit(solution)/shard_map/ppermute | solution.py:32
  47.4 1.2 %collective-permute-start.13 = (bf16[256,1024]{1,0:T(8,128)(2,1)S(1)}, bf16[256,1024]{1,0:T(8,128)(2,1)S(1)}, u32[]{:S(2)}, u32[]{:S(2)}) collective-permute-start(bf16[256,1024]{1,0:T(8,128)(2,1)S(1)} %pad_maximum_fusion.2.refs_0_), channel_id=1, source_target_pairs={{0,24},{1,97},{2,26},{3,99},{4,28},{5,101},{6,30},{7,103},{8,0},{9... | collective-permute-start | bytes 1572872 | tf_op jit(solution)/shard_map/ppermute | solution.py:32
  48.6 0.8 %collective-permute-start.12 = (bf16[256,1024]{1,0:T(8,128)(2,1)S(1)}, bf16[256,1024]{1,0:T(8,128)(2,1)S(1)}, u32[]{:S(2)}, u32[]{:S(2)}) collective-permute-start(bf16[256,1024]{1,0:T(8,128)(2,1)S(1)} %pad_maximum_fusion.2.refs_0_), channel_id=1, source_target_pairs={{0,8},{1,33},{2,10},{3,35},{4,12},{5,37},{6,14},{7,39},{8,16},{9,4... | collective-permute-start | bytes 1572872 | tf_op jit(solution)/shard_map/ppermute | solution.py:32
  49.4 0.0 collective-permute-done.10
  49.4 2.3 %collective-permute-start.11 = (f32[256,128]{1,0:T(8,128)S(1)}, f32[256,128]{1,0:T(8,128)S(1)}, u32[]{:S(2)}, u32[]{:S(2)}) collective-permute-start(f32[256,128]{1,0:T(8,128)S(1)} %add.10), channel_id=1, source_target_pairs={{0,6},{1,3},{2,4},{3,1},{4,2},{5,7},{6,0},{7,5},{8,14},{9,11},{10,... | collective-permute-start | bytes 393224 | tf_op jit(solution)/shard_map/ppermute | solution.py:51
  51.8 2.3 %base_second.1.bottom_ref = f32[256,512]{1,0:T(8,128)S(1)} custom-call(bf16[256,8192]{1,0:T(8,128)(2,1)S(1)} %get-tuple-element.46.x_ref, bf16[8192,512]{1,0:T(8,128)(2,1)S(1)} %bitcast.9), custom_call_target="tpu_custom_call" | custom-call | flops 5000000000 | bytes 1048576 | tf_op jit(solution)/shard_map/base_second/pallas_call | solution.py:160
  54.1 1.6 %collective-permute-done.11 = f32[256,128]{1,0:T(8,128)S(1)} collective-permute-done((f32[256,128]{1,0:T(8,128)S(1)}, f32[256,128]{1,0:T(8,128)S(1)}, u32[]{:S(2)}, u32[]{:S(2)}) %collective-permute-start.11) | collective-permute-done | bytes 131104 | tf_op jit(solution)/shard_map/ppermute | solution.py:51
  55.7 0.5 collective-permute-done.14.refs_3_
  56.2 4.6 %collective-permute-done.13.refs_2_ = bf16[256,1024]{1,0:T(8,128)(2,1)S(1)} collective-permute-done((bf16[256,1024]{1,0:T(8,128)(2,1)S(1)}, bf16[256,1024]{1,0:T(8,128)(2,1)S(1)}, u32[]{:S(2)}, u32[]{:S(2)}) %collective-permute-start.13) | collective-permute-done | bytes 524320 | tf_op jit(solution)/shard_map/ppermute | solution.py:32
  60.8 0.9 %collective-permute-done.12.refs_1_ = bf16[256,1024]{1,0:T(8,128)(2,1)S(1)} collective-permute-done((bf16[256,1024]{1,0:T(8,128)(2,1)S(1)}, bf16[256,1024]{1,0:T(8,128)(2,1)S(1)}, u32[]{:S(2)}, u32[]{:S(2)}) %collective-permute-start.12) | collective-permute-done | bytes 524320 | tf_op jit(solution)/shard_map/ppermute | solution.py:32
  61.7 0.2 collective-permute-start.15
  61.9 1.1 %collective-permute-done.15.other_ref = bf16[256,128]{1,0:T(8,128)(2,1)S(1)} collective-permute-done((bf16[256,128]{1,0:T(8,128)(2,1)S(1)}, bf16[256,128]{1,0:T(8,128)(2,1)S(1)}, u32[]{:S(2)}, u32[]{:S(2)}) %collective-permute-start.15) | collective-permute-done | bytes 65568 | tf_op jit(solution)/shard_map/ppermute | solution.py:44
  63.0 3.9 %expand.1 = bf16[1024,512]{1,0:T(8,128)(2,1)} custom-call(s32[1024,128]{1,0:T(8,128)S(1)} %mask_code.1.code_ref, bf16[256,128]{1,0:T(8,128)(2,1)S(1)} %add_convert_fusion.mine_ref, bf16[256,128]{1,0:T(8,128)(2,1)S(1)} %collective-permute-done.15.other_ref, f32[768,512]{1,0:T(8,128)S(1)} %get-tuple-element.49.top_ref, f32[256,512]{1,0:T(8,128)S(1)} %base_second.1.bottom_ref, ...), custom_call_target="tpu_custom_call" | custom-call | flops 2147483648 | bytes 3145728 | tf_op jit(solution)/shard_map/expand/pallas_call | solution.py:260
  (15 shorter events, 0.3 us)
Async XLA Ops:
  0.0 10.3 %collective-permute-start.2 = (bf16[128,1024]{1,0:T(8,128)(2,1)}, bf16[128,1024]{1,0:T(8,128)(2,1)S(1)}, u32[]{:S(2)}, u32[]{:S(2)}) collective-permute-start(bf16[128,1024]{1,0:T(8,128)(2,1)} %bitcast.11), channel_id=1, source_target_pairs={{0,16},{1,65},{2,18},{3,67},{4,20},{5,69},{6,22},{7,71},{8,24},{9,... | collective-permute-start | bytes 786440 | tf_op jit(solution)/shard_map/ppermute | solution.py:32
  3.1 8.0 %collective-permute-start.1 = (bf16[128,1024]{1,0:T(8,128)(2,1)}, bf16[128,1024]{1,0:T(8,128)(2,1)S(1)}, u32[]{:S(2)}, u32[]{:S(2)}) collective-permute-start(bf16[128,1024]{1,0:T(8,128)(2,1)} %bitcast.12), channel_id=1, source_target_pairs={{0,24},{1,97},{2,26},{3,99},{4,28},{5,101},{6,30},{7,103},{8,0},{9... | collective-permute-start | bytes 786440 | tf_op jit(solution)/shard_map/ppermute | solution.py:32
  4.2 7.8 %collective-permute-start = (bf16[128,1024]{1,0:T(8,128)(2,1)}, bf16[128,1024]{1,0:T(8,128)(2,1)S(1)}, u32[]{:S(2)}, u32[]{:S(2)}) collective-permute-start(bf16[128,1024]{1,0:T(8,128)(2,1)} %bitcast.13), channel_id=1, source_target_pairs={{0,8},{1,33},{2,10},{3,35},{4,12},{5,37},{6,14},{7,39},{8,16},{9,4... | collective-permute-start | bytes 786440 | tf_op jit(solution)/shard_map/ppermute | solution.py:32
  5.1 0.7 %copy-start = (s32[1024,1]{0,1:T(1,128)S(1)}, s32[1024,1]{0,1:T(1,128)}, u32[]{:S(2)}) copy-start(s32[1024,1]{0,1:T(1,128)} %param.6) | copy-start | bytes 12292
  5.8 13.9 %slice-start = ((s8[8388608]{0:T(1024)(128)(4,1)}), s8[4194304]{0:T(1024)(128)(4,1)S(1)}, s32[]{:S(2)}) async-start(s8[8388608]{0:T(1024)(128)(4,1)} %bitcast.8), calls=%async_computation | async-start | bytes 8388608
  6.0 4.2 %copy-start.2 = (bf16[2,64,512]{2,1,0:T(8,128)(2,1)S(1)}, bf16[2,64,512]{2,1,0:T(8,128)(2,1)}, u32[]{:S(2)}) copy-start(bf16[2,64,512]{2,1,0:T(8,128)(2,1)} %param.9) | copy-start | bytes 393220
  6.0 6.0 %copy-start.1 = (bf16[2,1024,64]{1,2,0:T(8,128)(2,1)S(1)}, bf16[2,1024,64]{1,2,0:T(8,128)(2,1)}, u32[]{:S(2)}) copy-start(bf16[2,1024,64]{1,2,0:T(8,128)(2,1)} %param.8) | copy-start | bytes 786436
  6.1 13.7 %slice-start.1 = ((s8[8388608]{0:T(1024)(128)(4,1)}), s8[4194304]{0:T(1024)(128)(4,1)S(1)}, s32[]{:S(2)}) async-start(s8[8388608]{0:T(1024)(128)(4,1)} %bitcast.8), calls=%async_computation.1 | async-start | bytes 8388608
  12.2 14.6 %collective-permute-start.4 = (bf16[320,1024]{1,0:T(8,128)(2,1)S(1)}, bf16[320,1024]{1,0:T(8,128)(2,1)S(1)}, u32[]{:S(2)}, u32[]{:S(2)}) collective-permute-start(bf16[320,1024]{1,0:T(8,128)(2,1)S(1)} %get-tuple-element.55), channel_id=1, source_target_pairs={{0,96},{1,25},{2,98},{3,27},{4,100},{5,29},{6,102},{7,31},{8,104},... | collective-permute-start | bytes 1966088 | tf_op jit(solution)/shard_map/ppermute | solution.py:38
  16.3 11.8 %collective-permute-start.3 = (bf16[320,1024]{1,0:T(8,128)(2,1)S(1)}, bf16[320,1024]{1,0:T(8,128)(2,1)S(1)}, u32[]{:S(2)}, u32[]{:S(2)}) collective-permute-start(bf16[320,1024]{1,0:T(8,128)(2,1)S(1)} %get-tuple-element.56), channel_id=1, source_target_pairs={{0,32},{1,9},{2,34},{3,11},{4,36},{5,13},{6,38},{7,15},{8,40},{9,1... | collective-permute-start | bytes 1966088 | tf_op jit(solution)/shard_map/ppermute | solution.py:38
  16.3 17.4 %collective-permute-start.7 = (bf16[256,1024]{1,0:T(8,128)(2,1)S(1)}, bf16[256,1024]{1,0:T(8,128)(2,1)S(1)}, u32[]{:S(2)}, u32[]{:S(2)}) collective-permute-start(bf16[256,1024]{1,0:T(8,128)(2,1)S(1)} %constant_dynamic-update-slice_fusion.refs_1_), channel_id=1, source_target_pairs={{0,32},{1,9},{2,34},{3,11},{4,36},{5,13},{6,38},{7,15},{8,40},{9,1... | collective-permute-start | bytes 1572872 | tf_op jit(solution)/shard_map/ppermute | solution.py:38
  16.5 17.3 %collective-permute-start.8 = (bf16[256,1024]{1,0:T(8,128)(2,1)S(1)}, bf16[256,1024]{1,0:T(8,128)(2,1)S(1)}, u32[]{:S(2)}, u32[]{:S(2)}) collective-permute-start(bf16[256,1024]{1,0:T(8,128)(2,1)S(1)} %pad_maximum_fusion.1.refs_0_), channel_id=1, source_target_pairs={{0,96},{1,25},{2,98},{3,27},{4,100},{5,29},{6,102},{7,31},{8,104},... | collective-permute-start | bytes 1572872 | tf_op jit(solution)/shard_map/ppermute | solution.py:38
  28.1 12.6 %collective-permute-start.5 = (bf16[320,1024]{1,0:T(8,128)(2,1)S(1)}, bf16[320,1024]{1,0:T(8,128)(2,1)S(1)}, u32[]{:S(2)}, u32[]{:S(2)}) collective-permute-start(bf16[320,1024]{1,0:T(8,128)(2,1)S(1)} %collective-permute-done.3), channel_id=1, source_target_pairs={{0,32},{1,9},{2,34},{3,11},{4,36},{5,13},{6,38},{7,15},{8,40},{9,1... | collective-permute-start | bytes 1966088 | tf_op jit(solution)/shard_map/ppermute | solution.py:38
  28.1 10.0 %collective-permute-start.6 = (bf16[256,1024]{1,0:T(8,128)(2,1)S(1)}, bf16[256,1024]{1,0:T(8,128)(2,1)S(1)}, u32[]{:S(2)}, u32[]{:S(2)}) collective-permute-start(bf16[256,1024]{1,0:T(8,128)(2,1)S(1)} %slice.41.refs_5_), channel_id=1, source_target_pairs={{0,96},{1,25},{2,98},{3,27},{4,100},{5,29},{6,102},{7,31},{8,104},... | collective-permute-start | bytes 1572872 | tf_op jit(solution)/shard_map/ppermute | solution.py:38
  42.2 1.4 %collective-permute-start.9 = (f32[256,128]{1,0:T(8,128)S(1)}, f32[256,128]{1,0:T(8,128)S(1)}, u32[]{:S(2)}, u32[]{:S(2)}) collective-permute-start(f32[256,128]{1,0:T(8,128)S(1)} %get-tuple-element.45), channel_id=1, source_target_pairs={{0,1},{1,0},{2,3},{3,2},{4,5},{5,4},{6,7},{7,6},{8,9},{9,8},{10,11... | collective-permute-start | bytes 393224 | tf_op jit(solution)/shard_map/ppermute | solution.py:44
  43.6 5.8 %collective-permute-start.10 = (f32[256,128]{1,0:T(8,128)S(1)}, f32[256,128]{1,0:T(8,128)S(1)}, u32[]{:S(2)}, u32[]{:S(2)}) collective-permute-start(f32[256,128]{1,0:T(8,128)S(1)} %add.9), channel_id=1, source_target_pairs={{0,2},{1,7},{2,0},{3,5},{4,6},{5,3},{6,4},{7,1},{8,10},{9,15},{10,... | collective-permute-start | bytes 393224 | tf_op jit(solution)/shard_map/ppermute | solution.py:51
  45.4 10.9 %collective-permute-start.14 = (bf16[256,1024]{1,0:T(8,128)(2,1)S(1)}, bf16[256,1024]{1,0:T(8,128)(2,1)S(1)}, u32[]{:S(2)}, u32[]{:S(2)}) collective-permute-start(bf16[256,1024]{1,0:T(8,128)(2,1)S(1)} %pad_maximum_fusion.2.refs_0_), channel_id=1, source_target_pairs={{0,16},{1,65},{2,18},{3,67},{4,20},{5,69},{6,22},{7,71},{8,24},{9,... | collective-permute-start | bytes 1572872 | tf_op jit(solution)/shard_map/ppermute | solution.py:32
  47.4 13.4 %collective-permute-start.13 = (bf16[256,1024]{1,0:T(8,128)(2,1)S(1)}, bf16[256,1024]{1,0:T(8,128)(2,1)S(1)}, u32[]{:S(2)}, u32[]{:S(2)}) collective-permute-start(bf16[256,1024]{1,0:T(8,128)(2,1)S(1)} %pad_maximum_fusion.2.refs_0_), channel_id=1, source_target_pairs={{0,24},{1,97},{2,26},{3,99},{4,28},{5,101},{6,30},{7,103},{8,0},{9... | collective-permute-start | bytes 1572872 | tf_op jit(solution)/shard_map/ppermute | solution.py:32
  48.6 13.2 %collective-permute-start.12 = (bf16[256,1024]{1,0:T(8,128)(2,1)S(1)}, bf16[256,1024]{1,0:T(8,128)(2,1)S(1)}, u32[]{:S(2)}, u32[]{:S(2)}) collective-permute-start(bf16[256,1024]{1,0:T(8,128)(2,1)S(1)} %pad_maximum_fusion.2.refs_0_), channel_id=1, source_target_pairs={{0,8},{1,33},{2,10},{3,35},{4,12},{5,37},{6,14},{7,39},{8,16},{9,4... | collective-permute-start | bytes 1572872 | tf_op jit(solution)/shard_map/ppermute | solution.py:32
  49.4 6.3 %collective-permute-start.11 = (f32[256,128]{1,0:T(8,128)S(1)}, f32[256,128]{1,0:T(8,128)S(1)}, u32[]{:S(2)}, u32[]{:S(2)}) collective-permute-start(f32[256,128]{1,0:T(8,128)S(1)} %add.10), channel_id=1, source_target_pairs={{0,6},{1,3},{2,4},{3,1},{4,2},{5,7},{6,0},{7,5},{8,14},{9,11},{10,... | collective-permute-start | bytes 393224 | tf_op jit(solution)/shard_map/ppermute | solution.py:51
  61.7 1.3 %collective-permute-start.15 = (bf16[256,128]{1,0:T(8,128)(2,1)S(1)}, bf16[256,128]{1,0:T(8,128)(2,1)S(1)}, u32[]{:S(2)}, u32[]{:S(2)}) collective-permute-start(bf16[256,128]{1,0:T(8,128)(2,1)S(1)} %add_convert_fusion.mine_ref), channel_id=1, source_target_pairs={{0,1},{1,0},{2,3},{3,2},{4,5},{5,4},{6,7},{7,6},{8,9},{9,8},{10,11... | collective-permute-start | bytes 196616 | tf_op jit(solution)/shard_map/ppermute | solution.py:44

commit v12 on v11

--- a/solution.py
+++ b/solution.py
@@ -232,7 +232,8 @@
     @pl.when(step == 0)
     def _():
         for k in range(16):
-            part, at = b_refs[k // 4], 64 * (k % 4)
+            i, j = k // 4, k % 4
+            part, at = (b_refs[i], 64 * j) if j < 3 else (b_refs[4 + i // 2], 64 * (i % 2))
             for side in range(2):
                 b_all[pl.ds(128 * k + 64 * side, 64), :] = part[pl.ds(at, 64), n * side : n * side + n]
 
@@ -292,23 +293,29 @@
     base, rest = base_first(half, query_matrix, activations)
     top_before, bottom_after, base = tie(top_before, bottom_after, base)
 
-    top_two, bottom_two = second(top_before, 1), second(bottom_after[:256], -1)
+    d_two = [second(top_before[:256], 1), second(bottom_after[:256], -1)]
     groups = [
         ([top[:256], bottom[:256]], row(0)),
         ([top_before[:256], bottom_before], row(-1)),
         ([top_after, bottom_after[:256]], row(1)),
     ]
     total = shrink(code, here, groups, None, False, "shrink_near", 5000000000)
-    top_two, bottom_two, total = tie(top_two, bottom_two, total)
-    d_two = [top_two[:256], bottom_two]
+    column = jnp.concatenate([own_up, top_before[256:], bottom_after[256:]], axis=0)
+    column, total = tie(column, total)
+    ups = [first(column, d) for d in (1, -1, 2)]
+    *d_two, total = tie(*d_two, total)
     keep, give = shrink(code, here, [(d_two, row(2))], total, True, "shrink_far")
     keep = keep + other_core(give)
-    column = jnp.concatenate([own_up] + [a[256:] for a in (top_before, bottom_after, top_two)], axis=0)
-    ups = [column] + [first(column, d) for d in (1, -1, 2)]
-    keep = keep + pair(keep, 0)
+    there, *ups = tie(pair(keep, 0), *ups)
+    keep = keep + there
+    ups = [column, *ups]
+    up_two = [
+        second(jnp.concatenate([a[64:128] for a in ups[:2]], axis=0), 1),
+        second(jnp.concatenate([a[128:] for a in ups[2:]], axis=0), -1),
+    ]
     there, last = tie(pair(keep, 1), base_second(rest, query_matrix))
-    mine, *ups = tie((keep + there).astype(BF), *ups)
-    return expand(code, mine, other_core(mine), [base, last], ups)
+    mine, *up_two = tie((keep + there).astype(BF), *up_two)
+    return expand(code, mine, other_core(mine), [base, last], [*ups, *up_two])
 
 
 def solution(mesh):

time: 68.1 us -> 70.1 us (1.029)
  starting transfers between devices: 24.2 us -> 25.9 us
    ppermute x6, waiting for transfers between devices: 7.75 us -> 3.02 us  [first(): lax.ppermute(a, AXES, every(lambda x, y, z, c: (x, y, z + d, c) if c else...]
    ppermute x6 -> x8, waiting for transfers between devices: 7.13 us -> 11.5 us  [second(): lax.ppermute(a, AXES, every(lambda x, y, z, c: (x + d, y, z, c) if c else...]
    ppermute x6 -> x8, starting transfers between devices: 10.8 us -> 11.7 us  [second(): lax.ppermute(a, AXES, every(lambda x, y, z, c: (x + d, y, z, c) if c else...]
    ppermute x2, starting transfers between devices: 3.97 us -> 4.91 us  [pair(): return lax.ppermute(a, AXES, every(to))]
  transfers between devices with their start and end apart: 16 -> 18, of which waited for: 12 -> 12; matrix products, arithmetic and copies ran while one was open for 0% -> 0% of each run, Pallas kernels for 26% -> 27%
where the time goes in v12:
time: 70.1 us; the launch traced here: 68.9 us
  starting transfers between devices  25.9 us (37%)
  Pallas kernels  22.4 us (32%)
  waiting for transfers between devices  19.2 us (27%)
  local copies, waits for them, and re-layouts  0.89 us (1%)
    ppermute x8, starting transfers between devices, second(): lax.ppermute(a, AXES, every(lambda x, y, z, c: (x + d, y, z, c) if c else...  11.7 us
    ppermute x8, waiting for transfers between devices, second(): lax.ppermute(a, AXES, every(lambda x, y, z, c: (x + d, y, z, c) if c else...  11.5 us
    ppermute x6, starting transfers between devices, first(): lax.ppermute(a, AXES, every(lambda x, y, z, c: (x, y, z + d, c) if c else...  9.21 us
    pallas_call x1, Pallas kernels, base_first(): pl.pallas_call(base_kernel, in_specs=[VMEM, VMEM, HBM], out_specs=[VMEM,...  6.99 us
    ppermute x2, starting transfers between devices, pair(): return lax.ppermute(a, AXES, every(to))  4.91 us
    pallas_call x2, Pallas kernels, shrink(): pl.pallas_call(functools.partial(shrink_kernel, [(len(parts), places) for...  4.8 us
    pallas_call x1, Pallas kernels, fetch(): pl.pallas_call(fetch_kernel, in_specs=[HBM], out_specs=[VMEM] * 2, out_sh...  4.2 us
    pallas_call x1, Pallas kernels, expand(): pl.pallas_call(expand_kernel, grid=(2,), in_specs=[VMEM] * len(args), out...  3.9 us
  transfers between devices with their start and end apart: 18, of which 12 were waited for; matrix products, arithmetic and copies ran while one was open for 0% of the time, Pallas kernels for 27%

profile of v12, /device:TPU:0, one launch (start us, length us, event | category | flops | bytes accessed | tf_op | source)
XLA Modules:
  0.0 68.9 jit_solution(2443710509502506183)
XLA Ops:
  0.0 3.1 %collective-permute-start.2 = (bf16[128,1024]{1,0:T(8,128)(2,1)}, bf16[128,1024]{1,0:T(8,128)(2,1)S(1)}, u32[]{:S(2)}, u32[]{:S(2)}) collective-permute-start(bf16[128,1024]{1,0:T(8,128)(2,1)} %bitcast.11), channel_id=1, source_target_pairs={{0,16},{1,65},{2,18},{3,67},{4,20},{5,69},{6,22},{7,71},{8,24},{9,... | collective-permute-start | bytes 786440 | tf_op jit(solution)/shard_map/ppermute | solution.py:32
  3.1 1.1 %collective-permute-start.1 = (bf16[128,1024]{1,0:T(8,128)(2,1)}, bf16[128,1024]{1,0:T(8,128)(2,1)S(1)}, u32[]{:S(2)}, u32[]{:S(2)}) collective-permute-start(bf16[128,1024]{1,0:T(8,128)(2,1)} %bitcast.12), channel_id=1, source_target_pairs={{0,24},{1,97},{2,26},{3,99},{4,28},{5,101},{6,30},{7,103},{8,0},{9... | collective-permute-start | bytes 786440 | tf_op jit(solution)/shard_map/ppermute | solution.py:32
  4.2 0.9 %collective-permute-start = (bf16[128,1024]{1,0:T(8,128)(2,1)}, bf16[128,1024]{1,0:T(8,128)(2,1)S(1)}, u32[]{:S(2)}, u32[]{:S(2)}) collective-permute-start(bf16[128,1024]{1,0:T(8,128)(2,1)} %bitcast.13), channel_id=1, source_target_pairs={{0,8},{1,33},{2,10},{3,35},{4,12},{5,37},{6,14},{7,39},{8,16},{9,4... | collective-permute-start | bytes 786440 | tf_op jit(solution)/shard_map/ppermute | solution.py:32
  5.1 0.0 copy-start
  5.1 0.7 copy-done
  5.8 0.0 slice-start
  5.8 0.2 mask_code.1.code_ref
  6.0 0.0 copy-start.2
  6.0 0.0 copy-start.1
  6.1 0.0 slice-start.1
  6.1 4.2 %fetch.1 = (bf16[1024,1024]{1,0:T(8,128)(2,1)S(1)}, bf16[512,8192]{1,0:T(8,128)(2,1)S(1)}) custom-call(bf16[1024,8192]{1,0:T(8,128)(2,1)} %x_ref.2), custom_call_target="tpu_custom_call" | custom-call | flops 1000000 | bytes 1048576 | tf_op jit(solution)/shard_map/fetch/pallas_call | solution.py:105
  10.3 0.0 copy-done.2
  10.3 0.0 collective-permute-done.2
  10.3 0.8 %collective-permute-done.1 = bf16[128,1024]{1,0:T(8,128)(2,1)S(1)} collective-permute-done((bf16[128,1024]{1,0:T(8,128)(2,1)}, bf16[128,1024]{1,0:T(8,128)(2,1)S(1)}, u32[]{:S(2)}, u32[]{:S(2)}) %collective-permute-start.1) | collective-permute-done | bytes 262176 | tf_op jit(solution)/shard_map/ppermute | solution.py:32
  11.1 1.0 %collective-permute-done = bf16[128,1024]{1,0:T(8,128)(2,1)S(1)} collective-permute-done((bf16[128,1024]{1,0:T(8,128)(2,1)}, bf16[128,1024]{1,0:T(8,128)(2,1)S(1)}, u32[]{:S(2)}, u32[]{:S(2)}) %collective-permute-start) | collective-permute-done | bytes 262176 | tf_op jit(solution)/shard_map/ppermute | solution.py:32
  12.1 0.0 copy-done.1
  12.1 0.1 fusion
  12.2 4.1 %collective-permute-start.4 = (bf16[320,1024]{1,0:T(8,128)(2,1)S(1)}, bf16[320,1024]{1,0:T(8,128)(2,1)S(1)}, u32[]{:S(2)}, u32[]{:S(2)}) collective-permute-start(bf16[320,1024]{1,0:T(8,128)(2,1)S(1)} %get-tuple-element.63), channel_id=1, source_target_pairs={{0,96},{1,25},{2,98},{3,27},{4,100},{5,29},{6,102},{7,31},{8,104},... | collective-permute-start | bytes 1966088 | tf_op jit(solution)/shard_map/ppermute | solution.py:38
  16.3 0.0 collective-permute-start.3
  16.3 0.1 collective-permute-start.7
  16.5 3.3 %collective-permute-start.8 = (bf16[256,1024]{1,0:T(8,128)(2,1)S(1)}, bf16[256,1024]{1,0:T(8,128)(2,1)S(1)}, u32[]{:S(2)}, u32[]{:S(2)}) collective-permute-start(bf16[256,1024]{1,0:T(8,128)(2,1)S(1)} %pad_maximum_fusion.1.refs_0_), channel_id=1, source_target_pairs={{0,96},{1,25},{2,98},{3,27},{4,100},{5,29},{6,102},{7,31},{8,104},... | collective-permute-start | bytes 1572872 | tf_op jit(solution)/shard_map/ppermute | solution.py:38
  19.8 0.0 slice-done
  19.8 0.0 slice-done.1
  19.8 7.0 %base_first.1 = (f32[768,512]{1,0:T(8,128)S(1)}, bf16[256,8192]{1,0:T(8,128)(2,1)S(1)}) custom-call(bf16[512,8192]{1,0:T(8,128)(2,1)S(1)} %get-tuple-element.41.half_ref, bf16[8192,512]{1,0:T(8,128)(2,1)S(1)} %bitcast.9, bf16[1024,8192]{1,0:T(8,128)(2,1)} %x_ref.2), custom_call_target="tpu_custom_call" | custom-call | flops 5000000000 | bytes 1048576 | tf_op jit(solution)/shard_map/base_first/pallas_call | solution.py:143
  26.8 0.0 collective-permute-done.4
  26.8 1.3 %collective-permute-done.3 = bf16[320,1024]{1,0:T(8,128)(2,1)S(1)} collective-permute-done((bf16[320,1024]{1,0:T(8,128)(2,1)S(1)}, bf16[320,1024]{1,0:T(8,128)(2,1)S(1)}, u32[]{:S(2)}, u32[]{:S(2)}) %collective-permute-start.3) | collective-permute-done | bytes 655392 | tf_op jit(solution)/shard_map/ppermute | solution.py:38
  28.2 0.8 %collective-permute-start.6 = (bf16[256,1024]{1,0:T(8,128)(2,1)S(1)}, bf16[256,1024]{1,0:T(8,128)(2,1)S(1)}, u32[]{:S(2)}, u32[]{:S(2)}) collective-permute-start(bf16[256,1024]{1,0:T(8,128)(2,1)S(1)} %slice.49.refs_5_), channel_id=1, source_target_pairs={{0,96},{1,25},{2,98},{3,27},{4,100},{5,29},{6,102},{7,31},{8,104},... | collective-permute-start | bytes 1572872 | tf_op jit(solution)/shard_map/ppermute | solution.py:38
  29.0 1.3 %collective-permute-start.5 = (bf16[256,1024]{1,0:T(8,128)(2,1)S(1)}, bf16[256,1024]{1,0:T(8,128)(2,1)S(1)}, u32[]{:S(2)}, u32[]{:S(2)}) collective-permute-start(bf16[256,1024]{1,0:T(8,128)(2,1)S(1)} %slice.48.refs_2_), channel_id=1, source_target_pairs={{0,32},{1,9},{2,34},{3,11},{4,36},{5,13},{6,38},{7,15},{8,40},{9,1... | collective-permute-start | bytes 1572872 | tf_op jit(solution)/shard_map/ppermute | solution.py:38
  30.4 3.4 %collective-permute-done.7.refs_3_ = bf16[256,1024]{1,0:T(8,128)(2,1)S(1)} collective-permute-done((bf16[256,1024]{1,0:T(8,128)(2,1)S(1)}, bf16[256,1024]{1,0:T(8,128)(2,1)S(1)}, u32[]{:S(2)}, u32[]{:S(2)}) %collective-permute-start.7) | collective-permute-done | bytes 524320 | tf_op jit(solution)/shard_map/ppermute | solution.py:38
  33.7 0.0 collective-permute-done.8.refs_4_
  33.7 3.4 %shrink_near.1.refs_2_ = f32[1024,128]{1,0:T(8,128)S(1)} custom-call(s32[1024,128]{1,0:T(8,128)S(1)} %mask_code.1.code_ref, bf16[1024,1024]{1,0:T(8,128)(2,1)S(1)} %get-tuple-element.37.x_ref, bf16[256,1024]{1,0:T(8,128)(2,1)S(1)} %pad_maximum_fusion.1.refs_0_, bf16[256,1024]{1,0:T(8,128)(2,1)S(1)} %constant_dynamic-update-slice_fusion.refs_1_, ...), custom_call_target="tpu_custom_call" | custom-call | flops 5000000000 | bytes 1048576 | tf_op jit(solution)/shard_map/shrink_near/pallas_call | solution.py:203
  37.2 2.0 %collective-permute-start.13 = (bf16[192,1024]{1,0:T(8,128)(2,1)S(1)}, bf16[192,1024]{1,0:T(8,128)(2,1)S(1)}, u32[]{:S(2)}, u32[]{:S(2)}) collective-permute-start(bf16[192,1024]{1,0:T(8,128)(2,1)S(1)} %pad_maximum_fusion.2.refs_0_), channel_id=1, source_target_pairs={{0,16},{1,65},{2,18},{3,67},{4,20},{5,69},{6,22},{7,71},{8,24},{9,... | collective-permute-start | bytes 1179656 | tf_op jit(solution)/shard_map/ppermute | solution.py:32
  39.2 1.2 %collective-permute-start.12 = (bf16[192,1024]{1,0:T(8,128)(2,1)S(1)}, bf16[192,1024]{1,0:T(8,128)(2,1)S(1)}, u32[]{:S(2)}, u32[]{:S(2)}) collective-permute-start(bf16[192,1024]{1,0:T(8,128)(2,1)S(1)} %pad_maximum_fusion.2.refs_0_), channel_id=1, source_target_pairs={{0,24},{1,97},{2,26},{3,99},{4,28},{5,101},{6,30},{7,103},{8,0},{9... | collective-permute-start | bytes 1179656 | tf_op jit(solution)/shard_map/ppermute | solution.py:32
  40.4 0.8 %collective-permute-start.11 = (bf16[192,1024]{1,0:T(8,128)(2,1)S(1)}, bf16[192,1024]{1,0:T(8,128)(2,1)S(1)}, u32[]{:S(2)}, u32[]{:S(2)}) collective-permute-start(bf16[192,1024]{1,0:T(8,128)(2,1)S(1)} %pad_maximum_fusion.2.refs_0_), channel_id=1, source_target_pairs={{0,8},{1,33},{2,10},{3,35},{4,12},{5,37},{6,14},{7,39},{8,16},{9,4... | collective-permute-start | bytes 1179656 | tf_op jit(solution)/shard_map/ppermute | solution.py:32
  41.3 0.0 collective-permute-done.6.refs_1_
  41.3 3.5 %collective-permute-done.5.refs_0_ = bf16[256,1024]{1,0:T(8,128)(2,1)S(1)} collective-permute-done((bf16[256,1024]{1,0:T(8,128)(2,1)S(1)}, bf16[256,1024]{1,0:T(8,128)(2,1)S(1)}, u32[]{:S(2)}, u32[]{:S(2)}) %collective-permute-start.5) | collective-permute-done | bytes 524320 | tf_op jit(solution)/shard_map/ppermute | solution.py:38
  44.8 1.4 %shrink_far.1 = (f32[256,128]{1,0:T(8,128)S(1)}, f32[256,128]{1,0:T(8,128)S(1)}) custom-call(s32[1024,128]{1,0:T(8,128)S(1)} %mask_code.1.code_ref, bf16[1024,1024]{1,0:T(8,128)(2,1)S(1)} %get-tuple-element.37.x_ref, bf16[256,1024]{1,0:T(8,128)(2,1)S(1)} %collective-permute-done.5.refs_0_, bf16[256,1024]{1,0:T(8,128)(2,1)S(1)} %collective-permute-done.6.refs_1_, ...), custom_call_target="tpu_custom_call" | custom-call | flops 1048576 | bytes 1048576 | tf_op jit(solution)/shard_map/shrink_far/pallas_call | solution.py:203
  46.2 0.1 collective-permute-start.9
  46.3 1.3 %collective-permute-done.9 = f32[256,128]{1,0:T(8,128)S(1)} collective-permute-done((f32[256,128]{1,0:T(8,128)S(1)}, f32[256,128]{1,0:T(8,128)S(1)}, u32[]{:S(2)}, u32[]{:S(2)}) %collective-permute-start.9) | collective-permute-done | bytes 131104 | tf_op jit(solution)/shard_map/ppermute | solution.py:44
  47.6 1.8 %collective-permute-start.10 = (f32[256,128]{1,0:T(8,128)S(1)}, f32[256,128]{1,0:T(8,128)S(1)}, u32[]{:S(2)}, u32[]{:S(2)}) collective-permute-start(f32[256,128]{1,0:T(8,128)S(1)} %add.9), channel_id=1, source_target_pairs={{0,2},{1,7},{2,0},{3,5},{4,6},{5,3},{6,4},{7,1},{8,10},{9,15},{10,... | collective-permute-start | bytes 393224 | tf_op jit(solution)/shard_map/ppermute | solution.py:51
  49.5 0.0 collective-permute-done.13.refs_3_
  49.5 0.4 collective-permute-done.12.refs_2_
  49.8 0.9 %collective-permute-done.11.refs_1_ = bf16[192,1024]{1,0:T(8,128)(2,1)S(1)} collective-permute-done((bf16[192,1024]{1,0:T(8,128)(2,1)S(1)}, bf16[192,1024]{1,0:T(8,128)(2,1)S(1)}, u32[]{:S(2)}, u32[]{:S(2)}) %collective-permute-start.11) | collective-permute-done | bytes 393248 | tf_op jit(solution)/shard_map/ppermute | solution.py:32
  50.8 2.1 %collective-permute-done.10 = f32[256,128]{1,0:T(8,128)S(1)} collective-permute-done((f32[256,128]{1,0:T(8,128)S(1)}, f32[256,128]{1,0:T(8,128)S(1)}, u32[]{:S(2)}, u32[]{:S(2)}) %collective-permute-start.10) | collective-permute-done | bytes 131104 | tf_op jit(solution)/shard_map/ppermute | solution.py:51
  52.9 3.1 %collective-permute-start.14 = (f32[256,128]{1,0:T(8,128)S(1)}, f32[256,128]{1,0:T(8,128)S(1)}, u32[]{:S(2)}, u32[]{:S(2)}) collective-permute-start(f32[256,128]{1,0:T(8,128)S(1)} %add.10), channel_id=1, source_target_pairs={{0,6},{1,3},{2,4},{3,1},{4,2},{5,7},{6,0},{7,5},{8,14},{9,11},{10,... | collective-permute-start | bytes 393224 | tf_op jit(solution)/shard_map/ppermute | solution.py:51
  56.0 0.1 collective-permute-start.16
  56.1 2.1 %collective-permute-start.15 = (bf16[128,1024]{1,0:T(8,128)(2,1)S(1)}, bf16[128,1024]{1,0:T(8,128)(2,1)S(1)}, u32[]{:S(2)}, u32[]{:S(2)}) collective-permute-start(bf16[128,1024]{1,0:T(8,128)(2,1)S(1)} %pad_maximum_fusion.3), channel_id=1, source_target_pairs={{0,32},{1,9},{2,34},{3,11},{4,36},{5,13},{6,38},{7,15},{8,40},{9,1... | collective-permute-start | bytes 786440 | tf_op jit(solution)/shard_map/ppermute | solution.py:38
  58.2 2.3 %base_second.1.bottom_ref = f32[256,512]{1,0:T(8,128)S(1)} custom-call(bf16[256,8192]{1,0:T(8,128)(2,1)S(1)} %get-tuple-element.53.x_ref, bf16[8192,512]{1,0:T(8,128)(2,1)S(1)} %bitcast.9), custom_call_target="tpu_custom_call" | custom-call | flops 5000000000 | bytes 1048576 | tf_op jit(solution)/shard_map/base_second/pallas_call | solution.py:160
  60.5 0.0 collective-permute-done.14
  60.6 1.9 %collective-permute-done.16.refs_5_ = bf16[128,1024]{1,0:T(8,128)(2,1)S(1)} collective-permute-done((bf16[128,1024]{1,0:T(8,128)(2,1)S(1)}, bf16[128,1024]{1,0:T(8,128)(2,1)S(1)}, u32[]{:S(2)}, u32[]{:S(2)}) %collective-permute-start.16) | collective-permute-done | bytes 262176 | tf_op jit(solution)/shard_map/ppermute | solution.py:38
  62.5 1.3 %collective-permute-done.15.refs_4_ = bf16[128,1024]{1,0:T(8,128)(2,1)S(1)} collective-permute-done((bf16[128,1024]{1,0:T(8,128)(2,1)S(1)}, bf16[128,1024]{1,0:T(8,128)(2,1)S(1)}, u32[]{:S(2)}, u32[]{:S(2)}) %collective-permute-start.15) | collective-permute-done | bytes 262176 | tf_op jit(solution)/shard_map/ppermute | solution.py:38
  63.8 0.0 collective-permute-start.17
  63.8 1.3 %collective-permute-done.17.other_ref = bf16[256,128]{1,0:T(8,128)(2,1)S(1)} collective-permute-done((bf16[256,128]{1,0:T(8,128)(2,1)S(1)}, bf16[256,128]{1,0:T(8,128)(2,1)S(1)}, u32[]{:S(2)}, u32[]{:S(2)}) %collective-permute-start.17) | collective-permute-done | bytes 65568 | tf_op jit(solution)/shard_map/ppermute | solution.py:44
  65.0 3.9 %expand.1 = bf16[1024,512]{1,0:T(8,128)(2,1)} custom-call(s32[1024,128]{1,0:T(8,128)S(1)} %mask_code.1.code_ref, bf16[256,128]{1,0:T(8,128)(2,1)S(1)} %add_convert_fusion.mine_ref, bf16[256,128]{1,0:T(8,128)(2,1)S(1)} %collective-permute-done.17.other_ref, f32[768,512]{1,0:T(8,128)S(1)} %get-tuple-element.59.top_ref, f32[256,512]{1,0:T(8,128)S(1)} %base_second.1.bottom_ref, ...), custom_call_target="tpu_custom_call" | custom-call | flops 2147483648 | bytes 3145728 | tf_op jit(solution)/shard_map/expand/pallas_call | solution.py:261
  (19 shorter events, 0.3 us)
Async XLA Ops:
  0.0 10.3 %collective-permute-start.2 = (bf16[128,1024]{1,0:T(8,128)(2,1)}, bf16[128,1024]{1,0:T(8,128)(2,1)S(1)}, u32[]{:S(2)}, u32[]{:S(2)}) collective-permute-start(bf16[128,1024]{1,0:T(8,128)(2,1)} %bitcast.11), channel_id=1, source_target_pairs={{0,16},{1,65},{2,18},{3,67},{4,20},{5,69},{6,22},{7,71},{8,24},{9,... | collective-permute-start | bytes 786440 | tf_op jit(solution)/shard_map/ppermute | solution.py:32
  3.1 8.0 %collective-permute-start.1 = (bf16[128,1024]{1,0:T(8,128)(2,1)}, bf16[128,1024]{1,0:T(8,128)(2,1)S(1)}, u32[]{:S(2)}, u32[]{:S(2)}) collective-permute-start(bf16[128,1024]{1,0:T(8,128)(2,1)} %bitcast.12), channel_id=1, source_target_pairs={{0,24},{1,97},{2,26},{3,99},{4,28},{5,101},{6,30},{7,103},{8,0},{9... | collective-permute-start | bytes 786440 | tf_op jit(solution)/shard_map/ppermute | solution.py:32
  4.2 7.8 %collective-permute-start = (bf16[128,1024]{1,0:T(8,128)(2,1)}, bf16[128,1024]{1,0:T(8,128)(2,1)S(1)}, u32[]{:S(2)}, u32[]{:S(2)}) collective-permute-start(bf16[128,1024]{1,0:T(8,128)(2,1)} %bitcast.13), channel_id=1, source_target_pairs={{0,8},{1,33},{2,10},{3,35},{4,12},{5,37},{6,14},{7,39},{8,16},{9,4... | collective-permute-start | bytes 786440 | tf_op jit(solution)/shard_map/ppermute | solution.py:32
  5.1 0.7 copy-start
  5.8 13.9 %slice-start = ((s8[8388608]{0:T(1024)(128)(4,1)}), s8[4194304]{0:T(1024)(128)(4,1)S(1)}, s32[]{:S(2)}) async-start(s8[8388608]{0:T(1024)(128)(4,1)} %bitcast.8), calls=%async_computation | async-start | bytes 8388608
  6.0 4.2 %copy-start.2 = (bf16[2,64,512]{2,1,0:T(8,128)(2,1)S(1)}, bf16[2,64,512]{2,1,0:T(8,128)(2,1)}, u32[]{:S(2)}) copy-start(bf16[2,64,512]{2,1,0:T(8,128)(2,1)} %param.9) | copy-start | bytes 393220
  6.0 6.0 %copy-start.1 = (bf16[2,1024,64]{1,2,0:T(8,128)(2,1)S(1)}, bf16[2,1024,64]{1,2,0:T(8,128)(2,1)}, u32[]{:S(2)}) copy-start(bf16[2,1024,64]{1,2,0:T(8,128)(2,1)} %param.8) | copy-start | bytes 786436
  6.1 13.7 %slice-start.1 = ((s8[8388608]{0:T(1024)(128)(4,1)}), s8[4194304]{0:T(1024)(128)(4,1)S(1)}, s32[]{:S(2)}) async-start(s8[8388608]{0:T(1024)(128)(4,1)} %bitcast.8), calls=%async_computation.1 | async-start | bytes 8388608
  12.2 14.6 %collective-permute-start.4 = (bf16[320,1024]{1,0:T(8,128)(2,1)S(1)}, bf16[320,1024]{1,0:T(8,128)(2,1)S(1)}, u32[]{:S(2)}, u32[]{:S(2)}) collective-permute-start(bf16[320,1024]{1,0:T(8,128)(2,1)S(1)} %get-tuple-element.63), channel_id=1, source_target_pairs={{0,96},{1,25},{2,98},{3,27},{4,100},{5,29},{6,102},{7,31},{8,104},... | collective-permute-start | bytes 1966088 | tf_op jit(solution)/shard_map/ppermute | solution.py:38
  16.3 11.8 %collective-permute-start.3 = (bf16[320,1024]{1,0:T(8,128)(2,1)S(1)}, bf16[320,1024]{1,0:T(8,128)(2,1)S(1)}, u32[]{:S(2)}, u32[]{:S(2)}) collective-permute-start(bf16[320,1024]{1,0:T(8,128)(2,1)S(1)} %get-tuple-element.64), channel_id=1, source_target_pairs={{0,32},{1,9},{2,34},{3,11},{4,36},{5,13},{6,38},{7,15},{8,40},{9,1... | collective-permute-start | bytes 1966088 | tf_op jit(solution)/shard_map/ppermute | solution.py:38
  16.3 17.4 %collective-permute-start.7 = (bf16[256,1024]{1,0:T(8,128)(2,1)S(1)}, bf16[256,1024]{1,0:T(8,128)(2,1)S(1)}, u32[]{:S(2)}, u32[]{:S(2)}) collective-permute-start(bf16[256,1024]{1,0:T(8,128)(2,1)S(1)} %constant_dynamic-update-slice_fusion.refs_1_), channel_id=1, source_target_pairs={{0,32},{1,9},{2,34},{3,11},{4,36},{5,13},{6,38},{7,15},{8,40},{9,1... | collective-permute-start | bytes 1572872 | tf_op jit(solution)/shard_map/ppermute | solution.py:38
  16.5 17.3 %collective-permute-start.8 = (bf16[256,1024]{1,0:T(8,128)(2,1)S(1)}, bf16[256,1024]{1,0:T(8,128)(2,1)S(1)}, u32[]{:S(2)}, u32[]{:S(2)}) collective-permute-start(bf16[256,1024]{1,0:T(8,128)(2,1)S(1)} %pad_maximum_fusion.1.refs_0_), channel_id=1, source_target_pairs={{0,96},{1,25},{2,98},{3,27},{4,100},{5,29},{6,102},{7,31},{8,104},... | collective-permute-start | bytes 1572872 | tf_op jit(solution)/shard_map/ppermute | solution.py:38
  28.2 13.0 %collective-permute-start.6 = (bf16[256,1024]{1,0:T(8,128)(2,1)S(1)}, bf16[256,1024]{1,0:T(8,128)(2,1)S(1)}, u32[]{:S(2)}, u32[]{:S(2)}) collective-permute-start(bf16[256,1024]{1,0:T(8,128)(2,1)S(1)} %slice.49.refs_5_), channel_id=1, source_target_pairs={{0,96},{1,25},{2,98},{3,27},{4,100},{5,29},{6,102},{7,31},{8,104},... | collective-permute-start | bytes 1572872 | tf_op jit(solution)/shard_map/ppermute | solution.py:38
  29.0 15.8 %collective-permute-start.5 = (bf16[256,1024]{1,0:T(8,128)(2,1)S(1)}, bf16[256,1024]{1,0:T(8,128)(2,1)S(1)}, u32[]{:S(2)}, u32[]{:S(2)}) collective-permute-start(bf16[256,1024]{1,0:T(8,128)(2,1)S(1)} %slice.48.refs_2_), channel_id=1, source_target_pairs={{0,32},{1,9},{2,34},{3,11},{4,36},{5,13},{6,38},{7,15},{8,40},{9,1... | collective-permute-start | bytes 1572872 | tf_op jit(solution)/shard_map/ppermute | solution.py:38
  37.2 12.3 %collective-permute-start.13 = (bf16[192,1024]{1,0:T(8,128)(2,1)S(1)}, bf16[192,1024]{1,0:T(8,128)(2,1)S(1)}, u32[]{:S(2)}, u32[]{:S(2)}) collective-permute-start(bf16[192,1024]{1,0:T(8,128)(2,1)S(1)} %pad_maximum_fusion.2.refs_0_), channel_id=1, source_target_pairs={{0,16},{1,65},{2,18},{3,67},{4,20},{5,69},{6,22},{7,71},{8,24},{9,... | collective-permute-start | bytes 1179656 | tf_op jit(solution)/shard_map/ppermute | solution.py:32
  39.2 10.6 %collective-permute-start.12 = (bf16[192,1024]{1,0:T(8,128)(2,1)S(1)}, bf16[192,1024]{1,0:T(8,128)(2,1)S(1)}, u32[]{:S(2)}, u32[]{:S(2)}) collective-permute-start(bf16[192,1024]{1,0:T(8,128)(2,1)S(1)} %pad_maximum_fusion.2.refs_0_), channel_id=1, source_target_pairs={{0,24},{1,97},{2,26},{3,99},{4,28},{5,101},{6,30},{7,103},{8,0},{9... | collective-permute-start | bytes 1179656 | tf_op jit(solution)/shard_map/ppermute | solution.py:32
  40.4 10.3 %collective-permute-start.11 = (bf16[192,1024]{1,0:T(8,128)(2,1)S(1)}, bf16[192,1024]{1,0:T(8,128)(2,1)S(1)}, u32[]{:S(2)}, u32[]{:S(2)}) collective-permute-start(bf16[192,1024]{1,0:T(8,128)(2,1)S(1)} %pad_maximum_fusion.2.refs_0_), channel_id=1, source_target_pairs={{0,8},{1,33},{2,10},{3,35},{4,12},{5,37},{6,14},{7,39},{8,16},{9,4... | collective-permute-start | bytes 1179656 | tf_op jit(solution)/shard_map/ppermute | solution.py:32
  46.2 1.4 %collective-permute-start.9 = (f32[256,128]{1,0:T(8,128)S(1)}, f32[256,128]{1,0:T(8,128)S(1)}, u32[]{:S(2)}, u32[]{:S(2)}) collective-permute-start(f32[256,128]{1,0:T(8,128)S(1)} %get-tuple-element.50), channel_id=1, source_target_pairs={{0,1},{1,0},{2,3},{3,2},{4,5},{5,4},{6,7},{7,6},{8,9},{9,8},{10,11... | collective-permute-start | bytes 393224 | tf_op jit(solution)/shard_map/ppermute | solution.py:44
  47.6 5.2 %collective-permute-start.10 = (f32[256,128]{1,0:T(8,128)S(1)}, f32[256,128]{1,0:T(8,128)S(1)}, u32[]{:S(2)}, u32[]{:S(2)}) collective-permute-start(f32[256,128]{1,0:T(8,128)S(1)} %add.9), channel_id=1, source_target_pairs={{0,2},{1,7},{2,0},{3,5},{4,6},{5,3},{6,4},{7,1},{8,10},{9,15},{10,... | collective-permute-start | bytes 393224 | tf_op jit(solution)/shard_map/ppermute | solution.py:51
  52.9 7.6 %collective-permute-start.14 = (f32[256,128]{1,0:T(8,128)S(1)}, f32[256,128]{1,0:T(8,128)S(1)}, u32[]{:S(2)}, u32[]{:S(2)}) collective-permute-start(f32[256,128]{1,0:T(8,128)S(1)} %add.10), channel_id=1, source_target_pairs={{0,6},{1,3},{2,4},{3,1},{4,2},{5,7},{6,0},{7,5},{8,14},{9,11},{10,... | collective-permute-start | bytes 393224 | tf_op jit(solution)/shard_map/ppermute | solution.py:51
  56.0 6.4 %collective-permute-start.16 = (bf16[128,1024]{1,0:T(8,128)(2,1)S(1)}, bf16[128,1024]{1,0:T(8,128)(2,1)S(1)}, u32[]{:S(2)}, u32[]{:S(2)}) collective-permute-start(bf16[128,1024]{1,0:T(8,128)(2,1)S(1)} %pad_maximum_fusion.4), channel_id=1, source_target_pairs={{0,96},{1,25},{2,98},{3,27},{4,100},{5,29},{6,102},{7,31},{8,104},... | collective-permute-start | bytes 786440 | tf_op jit(solution)/shard_map/ppermute | solution.py:38
  56.1 7.7 %collective-permute-start.15 = (bf16[128,1024]{1,0:T(8,128)(2,1)S(1)}, bf16[128,1024]{1,0:T(8,128)(2,1)S(1)}, u32[]{:S(2)}, u32[]{:S(2)}) collective-permute-start(bf16[128,1024]{1,0:T(8,128)(2,1)S(1)} %pad_maximum_fusion.3), channel_id=1, source_target_pairs={{0,32},{1,9},{2,34},{3,11},{4,36},{5,13},{6,38},{7,15},{8,40},{9,1... | collective-permute-start | bytes 786440 | tf_op jit(solution)/shard_map/ppermute | solution.py:38
  63.8 1.3 %collective-permute-start.17 = (bf16[256,128]{1,0:T(8,128)(2,1)S(1)}, bf16[256,128]{1,0:T(8,128)(2,1)S(1)}, u32[]{:S(2)}, u32[]{:S(2)}) collective-permute-start(bf16[256,128]{1,0:T(8,128)(2,1)S(1)} %add_convert_fusion.mine_ref), channel_id=1, source_target_pairs={{0,1},{1,0},{2,3},{3,2},{4,5},{5,4},{6,7},{7,6},{8,9},{9,8},{10,11... | collective-permute-start | bytes 196616 | tf_op jit(solution)/shard_map/ppermute | solution.py:44

commit v13 on v11

--- a/solution.py
+++ b/solution.py
@@ -213,6 +213,13 @@
     )(*args)
 
 
+UP_PLACES = [[(i, 64 * j, 64)] for i in range(3) for j in range(3)]
+UP_PLACES.insert(3, [(5, 0, 64)])
+UP_PLACES.insert(7, [(3, 96, 64)])
+UP_PLACES.insert(11, [(4, 96, 64)])
+UP_PLACES += [[(3, 0, 64)], [(3, 64, 32), (4, 0, 32)], [(4, 32, 64)], [(6, 0, 64)]]
+
+
 def expand_kernel(code_ref, mine_ref, other_ref, top_ref, bottom_ref, *refs):
     *b_refs, o_ref, b_all = refs
     block = o_ref.shape[0]
@@ -231,10 +238,12 @@
 
     @pl.when(step == 0)
     def _():
-        for k in range(16):
-            part, at = b_refs[k // 4], 64 * (k % 4)
+        for k, pieces in enumerate(UP_PLACES):
+            to = 128 * k
             for side in range(2):
-                b_all[pl.ds(128 * k + 64 * side, 64), :] = part[pl.ds(at, 64), n * side : n * side + n]
+                for part, at, count in pieces:
+                    b_all[pl.ds(to, count), :] = b_refs[part][pl.ds(at, count), n * side : n * side + n]
+                    to += count
 
     spread = jnp.concatenate(
         [jnp.where(code == owner(j, i), rows, 0.0).astype(BF) for i in HOPS for j in HOPS], axis=1
@@ -299,16 +308,21 @@
         ([top_after, bottom_after[:256]], row(1)),
     ]
     total = shrink(code, here, groups, None, False, "shrink_near", 5000000000)
+    column = jnp.concatenate([own_up, top_before[256:], bottom_after[256:]], axis=0)
+    column, total = tie(column, total)
+    c_before, c_after = first(column, 1), first(column, -1)
     top_two, bottom_two, total = tie(top_two, bottom_two, total)
     d_two = [top_two[:256], bottom_two]
     keep, give = shrink(code, here, [(d_two, row(2))], total, True, "shrink_far")
     keep = keep + other_core(give)
-    column = jnp.concatenate([own_up] + [a[256:] for a in (top_before, bottom_after, top_two)], axis=0)
-    ups = [column] + [first(column, d) for d in (1, -1, 2)]
+    up_two = top_two[256:]
+    w_before = first(jnp.concatenate([c_before[:96], up_two], axis=0), 1)
+    w_after = first(jnp.concatenate([c_after[96:], up_two], axis=0), -1)
+    w_two = first(up_two, 2)
     keep = keep + pair(keep, 0)
     there, last = tie(pair(keep, 1), base_second(rest, query_matrix))
-    mine, *ups = tie((keep + there).astype(BF), *ups)
-    return expand(code, mine, other_core(mine), [base, last], ups)
+    mine, *far_ups = tie((keep + there).astype(BF), w_before, w_after, up_two, w_two)
+    return expand(code, mine, other_core(mine), [base, last], [column, c_before, c_after, *far_ups])
 
 
 def solution(mesh):

time: 68.1 us -> 68.7 us (level)
  starting transfers between devices: 24.2 us -> 28.4 us
  waiting for transfers between devices: 18.9 us -> 15.2 us
    ppermute x6 -> x8, starting transfers between devices: 9.2 us -> 12.8 us  [first(): lax.ppermute(a, AXES, every(lambda x, y, z, c: (x, y, z + d, c) if c else...]
    ppermute x6, waiting for transfers between devices: 7.13 us -> 5.19 us  [second(): lax.ppermute(a, AXES, every(lambda x, y, z, c: (x + d, y, z, c) if c else...]
    ppermute x2, waiting for transfers between devices: 1.62 us -> 0.01 us  [pair(): return lax.ppermute(a, AXES, every(to))]
    ppermute x2, starting transfers between devices: 3.97 us -> 4.74 us  [pair(): return lax.ppermute(a, AXES, every(to))]
    ppermute x6 -> x8, waiting for transfers between devices: 7.75 us -> 7.47 us  [first(): lax.ppermute(a, AXES, every(lambda x, y, z, c: (x, y, z + d, c) if c else...]
  transfers between devices with their start and end apart: 16 -> 18, of which waited for: 12 -> 10; matrix products, arithmetic and copies ran while one was open for 0% -> 1% of each run, Pallas kernels for 26% -> 27%
where the time goes in v13:
time: 68.7 us; the launch traced here: 67.6 us
  starting transfers between devices  28.4 us (41%)
  Pallas kernels  22.4 us (33%)
  waiting for transfers between devices  15.2 us (22%)
  local copies, waits for them, and re-layouts  0.92 us (1%)
    ppermute x8, starting transfers between devices, first(): lax.ppermute(a, AXES, every(lambda x, y, z, c: (x, y, z + d, c) if c else...  12.8 us
    ppermute x6, starting transfers between devices, second(): lax.ppermute(a, AXES, every(lambda x, y, z, c: (x + d, y, z, c) if c else...  10.8 us
    ppermute x8, waiting for transfers between devices, first(): lax.ppermute(a, AXES, every(lambda x, y, z, c: (x, y, z + d, c) if c else...  7.47 us
    pallas_call x1, Pallas kernels, base_first(): pl.pallas_call(base_kernel, in_specs=[VMEM, VMEM, HBM], out_specs=[VMEM,...  6.99 us
    ppermute x6, waiting for transfers between devices, second(): lax.ppermute(a, AXES, every(lambda x, y, z, c: (x + d, y, z, c) if c else...  5.19 us
    pallas_call x2, Pallas kernels, shrink(): pl.pallas_call(functools.partial(shrink_kernel, [(len(parts), places) for...  4.8 us
    ppermute x2, starting transfers between devices, pair(): return lax.ppermute(a, AXES, every(to))  4.74 us
    pallas_call x1, Pallas kernels, fetch(): pl.pallas_call(fetch_kernel, in_specs=[HBM], out_specs=[VMEM] * 2, out_sh...  4.2 us
  transfers between devices with their start and end apart: 18, of which 10 were waited for; matrix products, arithmetic and copies ran while one was open for 1% of the time, Pallas kernels for 27%

profile of v13, /device:TPU:0, one launch (start us, length us, event | category | flops | bytes accessed | tf_op | source)
XLA Modules:
  0.0 67.6 jit_solution(16495519412504408384)
XLA Ops:
  0.0 3.1 %collective-permute-start.2 = (bf16[128,1024]{1,0:T(8,128)(2,1)}, bf16[128,1024]{1,0:T(8,128)(2,1)S(1)}, u32[]{:S(2)}, u32[]{:S(2)}) collective-permute-start(bf16[128,1024]{1,0:T(8,128)(2,1)} %bitcast.11), channel_id=1, source_target_pairs={{0,16},{1,65},{2,18},{3,67},{4,20},{5,69},{6,22},{7,71},{8,24},{9,... | collective-permute-start | bytes 786440 | tf_op jit(solution)/shard_map/ppermute | solution.py:32
  3.1 1.1 %collective-permute-start.1 = (bf16[128,1024]{1,0:T(8,128)(2,1)}, bf16[128,1024]{1,0:T(8,128)(2,1)S(1)}, u32[]{:S(2)}, u32[]{:S(2)}) collective-permute-start(bf16[128,1024]{1,0:T(8,128)(2,1)} %bitcast.12), channel_id=1, source_target_pairs={{0,24},{1,97},{2,26},{3,99},{4,28},{5,101},{6,30},{7,103},{8,0},{9... | collective-permute-start | bytes 786440 | tf_op jit(solution)/shard_map/ppermute | solution.py:32
  4.2 0.9 %collective-permute-start = (bf16[128,1024]{1,0:T(8,128)(2,1)}, bf16[128,1024]{1,0:T(8,128)(2,1)S(1)}, u32[]{:S(2)}, u32[]{:S(2)}) collective-permute-start(bf16[128,1024]{1,0:T(8,128)(2,1)} %bitcast.13), channel_id=1, source_target_pairs={{0,8},{1,33},{2,10},{3,35},{4,12},{5,37},{6,14},{7,39},{8,16},{9,4... | collective-permute-start | bytes 786440 | tf_op jit(solution)/shard_map/ppermute | solution.py:32
  5.1 0.0 copy-start
  5.1 0.7 %copy-done = s32[1024,1]{0,1:T(1,128)S(1)} copy-done((s32[1024,1]{0,1:T(1,128)S(1)}, s32[1024,1]{0,1:T(1,128)}, u32[]{:S(2)}) %copy-start) | copy-done | bytes 4120
  5.8 0.0 slice-start
  5.8 0.2 mask_code.1.code_ref
  6.0 0.0 copy-start.2
  6.0 0.0 copy-start.1
  6.1 0.0 slice-start.1
  6.1 4.2 %fetch.1 = (bf16[1024,1024]{1,0:T(8,128)(2,1)S(1)}, bf16[512,8192]{1,0:T(8,128)(2,1)S(1)}) custom-call(bf16[1024,8192]{1,0:T(8,128)(2,1)} %x_ref.2), custom_call_target="tpu_custom_call" | custom-call | flops 1000000 | bytes 1048576 | tf_op jit(solution)/shard_map/fetch/pallas_call | solution.py:105
  10.3 0.0 copy-done.2
  10.3 0.0 collective-permute-done.2
  10.3 0.8 %collective-permute-done.1 = bf16[128,1024]{1,0:T(8,128)(2,1)S(1)} collective-permute-done((bf16[128,1024]{1,0:T(8,128)(2,1)}, bf16[128,1024]{1,0:T(8,128)(2,1)S(1)}, u32[]{:S(2)}, u32[]{:S(2)}) %collective-permute-start.1) | collective-permute-done | bytes 262176 | tf_op jit(solution)/shard_map/ppermute | solution.py:32
  11.1 1.0 %collective-permute-done = bf16[128,1024]{1,0:T(8,128)(2,1)S(1)} collective-permute-done((bf16[128,1024]{1,0:T(8,128)(2,1)}, bf16[128,1024]{1,0:T(8,128)(2,1)S(1)}, u32[]{:S(2)}, u32[]{:S(2)}) %collective-permute-start) | collective-permute-done | bytes 262176 | tf_op jit(solution)/shard_map/ppermute | solution.py:32
  12.1 0.0 copy-done.1
  12.1 0.1 fusion
  12.2 4.1 %collective-permute-start.4 = (bf16[320,1024]{1,0:T(8,128)(2,1)S(1)}, bf16[320,1024]{1,0:T(8,128)(2,1)S(1)}, u32[]{:S(2)}, u32[]{:S(2)}) collective-permute-start(bf16[320,1024]{1,0:T(8,128)(2,1)S(1)} %get-tuple-element.61), channel_id=1, source_target_pairs={{0,96},{1,25},{2,98},{3,27},{4,100},{5,29},{6,102},{7,31},{8,104},... | collective-permute-start | bytes 1966088 | tf_op jit(solution)/shard_map/ppermute | solution.py:38
  16.3 0.0 collective-permute-start.3
  16.4 0.1 collective-permute-start.7
  16.5 3.3 %collective-permute-start.8 = (bf16[256,1024]{1,0:T(8,128)(2,1)S(1)}, bf16[256,1024]{1,0:T(8,128)(2,1)S(1)}, u32[]{:S(2)}, u32[]{:S(2)}) collective-permute-start(bf16[256,1024]{1,0:T(8,128)(2,1)S(1)} %pad_maximum_fusion.1.refs_0_), channel_id=1, source_target_pairs={{0,96},{1,25},{2,98},{3,27},{4,100},{5,29},{6,102},{7,31},{8,104},... | collective-permute-start | bytes 1572872 | tf_op jit(solution)/shard_map/ppermute | solution.py:38
  19.8 0.0 slice-done
  19.8 0.0 slice-done.1
  19.8 7.0 %base_first.1 = (f32[768,512]{1,0:T(8,128)S(1)}, bf16[256,8192]{1,0:T(8,128)(2,1)S(1)}) custom-call(bf16[512,8192]{1,0:T(8,128)(2,1)S(1)} %get-tuple-element.39.half_ref, bf16[8192,512]{1,0:T(8,128)(2,1)S(1)} %bitcast.9, bf16[1024,8192]{1,0:T(8,128)(2,1)} %x_ref.2), custom_call_target="tpu_custom_call" | custom-call | flops 5000000000 | bytes 1048576 | tf_op jit(solution)/shard_map/base_first/pallas_call | solution.py:143
  26.8 0.0 collective-permute-done.4
  26.8 1.3 %collective-permute-done.3 = bf16[320,1024]{1,0:T(8,128)(2,1)S(1)} collective-permute-done((bf16[320,1024]{1,0:T(8,128)(2,1)S(1)}, bf16[320,1024]{1,0:T(8,128)(2,1)S(1)}, u32[]{:S(2)}, u32[]{:S(2)}) %collective-permute-start.3) | collective-permute-done | bytes 655392 | tf_op jit(solution)/shard_map/ppermute | solution.py:38
  28.1 0.1 collective-permute-start.5
  28.3 3.3 %collective-permute-start.6 = (bf16[256,1024]{1,0:T(8,128)(2,1)S(1)}, bf16[256,1024]{1,0:T(8,128)(2,1)S(1)}, u32[]{:S(2)}, u32[]{:S(2)}) collective-permute-start(bf16[256,1024]{1,0:T(8,128)(2,1)S(1)} %slice.47.refs_5_), channel_id=1, source_target_pairs={{0,96},{1,25},{2,98},{3,27},{4,100},{5,29},{6,102},{7,31},{8,104},... | collective-permute-start | bytes 1572872 | tf_op jit(solution)/shard_map/ppermute | solution.py:38
  31.6 2.2 %collective-permute-done.7.refs_3_ = bf16[256,1024]{1,0:T(8,128)(2,1)S(1)} collective-permute-done((bf16[256,1024]{1,0:T(8,128)(2,1)S(1)}, bf16[256,1024]{1,0:T(8,128)(2,1)S(1)}, u32[]{:S(2)}, u32[]{:S(2)}) %collective-permute-start.7) | collective-permute-done | bytes 524320 | tf_op jit(solution)/shard_map/ppermute | solution.py:38
  33.7 0.0 collective-permute-done.8.refs_4_
  33.7 3.4 %shrink_near.1.refs_2_ = f32[1024,128]{1,0:T(8,128)S(1)} custom-call(s32[1024,128]{1,0:T(8,128)S(1)} %mask_code.1.code_ref, bf16[1024,1024]{1,0:T(8,128)(2,1)S(1)} %get-tuple-element.35.x_ref, bf16[256,1024]{1,0:T(8,128)(2,1)S(1)} %pad_maximum_fusion.1.refs_0_, bf16[256,1024]{1,0:T(8,128)(2,1)S(1)} %constant_dynamic-update-slice_fusion.refs_1_, ...), custom_call_target="tpu_custom_call" | custom-call | flops 5000000000 | bytes 1048576 | tf_op jit(solution)/shard_map/shrink_near/pallas_call | solution.py:203
  37.3 1.8 %collective-permute-start.14 = (bf16[192,1024]{1,0:T(8,128)(2,1)S(1)}, bf16[192,1024]{1,0:T(8,128)(2,1)S(1)}, u32[]{:S(2)}, u32[]{:S(2)}) collective-permute-start(bf16[192,1024]{1,0:T(8,128)(2,1)S(1)} %pad_maximum_fusion.2.refs_0_), channel_id=1, source_target_pairs={{0,24},{1,97},{2,26},{3,99},{4,28},{5,101},{6,30},{7,103},{8,0},{9... | collective-permute-start | bytes 1179656 | tf_op jit(solution)/shard_map/ppermute | solution.py:32
  39.0 0.3 collective-permute-start.12
  39.4 0.1 collective-permute-done.6.refs_1_
  39.5 1.6 %collective-permute-done.5 = bf16[320,1024]{1,0:T(8,128)(2,1)S(1)} collective-permute-done((bf16[320,1024]{1,0:T(8,128)(2,1)S(1)}, bf16[320,1024]{1,0:T(8,128)(2,1)S(1)}, u32[]{:S(2)}, u32[]{:S(2)}) %collective-permute-start.5) | collective-permute-done | bytes 655392 | tf_op jit(solution)/shard_map/ppermute | solution.py:38
  41.1 1.4 %shrink_far.1 = (f32[256,128]{1,0:T(8,128)S(1)}, f32[256,128]{1,0:T(8,128)S(1)}) custom-call(s32[1024,128]{1,0:T(8,128)S(1)} %mask_code.1.code_ref, bf16[1024,1024]{1,0:T(8,128)(2,1)S(1)} %get-tuple-element.35.x_ref, bf16[256,1024]{1,0:T(8,128)(2,1)S(1)} %slice.51.refs_0_, bf16[256,1024]{1,0:T(8,128)(2,1)S(1)} %collective-permute-done.6.refs_1_, ...), custom_call_target="tpu_custom_call" | custom-call | flops 1048576 | bytes 1048576 | tf_op jit(solution)/shard_map/shrink_far/pallas_call | solution.py:203
  42.4 0.1 collective-permute-start.9
  42.5 1.3 %collective-permute-done.9 = f32[256,128]{1,0:T(8,128)S(1)} collective-permute-done((f32[256,128]{1,0:T(8,128)S(1)}, f32[256,128]{1,0:T(8,128)S(1)}, u32[]{:S(2)}, u32[]{:S(2)}) %collective-permute-start.9) | collective-permute-done | bytes 131104 | tf_op jit(solution)/shard_map/ppermute | solution.py:44
  43.9 1.7 %collective-permute-start.10 = (f32[256,128]{1,0:T(8,128)S(1)}, f32[256,128]{1,0:T(8,128)S(1)}, u32[]{:S(2)}, u32[]{:S(2)}) collective-permute-start(f32[256,128]{1,0:T(8,128)S(1)} %add.9), channel_id=1, source_target_pairs={{0,2},{1,7},{2,0},{3,5},{4,6},{5,3},{6,4},{7,1},{8,10},{9,15},{10,... | collective-permute-start | bytes 393224 | tf_op jit(solution)/shard_map/ppermute | solution.py:51
  45.5 0.0 collective-permute-done.14.refs_2_
  45.6 2.5 %collective-permute-done.12.refs_1_ = bf16[192,1024]{1,0:T(8,128)(2,1)S(1)} collective-permute-done((bf16[192,1024]{1,0:T(8,128)(2,1)S(1)}, bf16[192,1024]{1,0:T(8,128)(2,1)S(1)}, u32[]{:S(2)}, u32[]{:S(2)}) %collective-permute-start.12) | collective-permute-done | bytes 393248 | tf_op jit(solution)/shard_map/ppermute | solution.py:32
  48.1 0.1 pad_maximum_fusion.3
  48.1 0.9 %collective-permute-start.15 = (bf16[160,1024]{1,0:T(8,128)(2,1)S(1)}, bf16[160,1024]{1,0:T(8,128)(2,1)S(1)}, u32[]{:S(2)}, u32[]{:S(2)}) collective-permute-start(bf16[160,1024]{1,0:T(8,128)(2,1)S(1)} %get-tuple-element.59), channel_id=1, source_target_pairs={{0,24},{1,97},{2,26},{3,99},{4,28},{5,101},{6,30},{7,103},{8,0},{9... | collective-permute-start | bytes 983048 | tf_op jit(solution)/shard_map/ppermute | solution.py:32
  49.1 1.3 %collective-permute-start.13 = (bf16[160,1024]{1,0:T(8,128)(2,1)S(1)}, bf16[160,1024]{1,0:T(8,128)(2,1)S(1)}, u32[]{:S(2)}, u32[]{:S(2)}) collective-permute-start(bf16[160,1024]{1,0:T(8,128)(2,1)S(1)} %get-tuple-element.60), channel_id=1, source_target_pairs={{0,8},{1,33},{2,10},{3,35},{4,12},{5,37},{6,14},{7,39},{8,16},{9,4... | collective-permute-start | bytes 983048 | tf_op jit(solution)/shard_map/ppermute | solution.py:32
  50.4 0.0 collective-permute-done.10
  50.4 3.1 %collective-permute-start.11 = (f32[256,128]{1,0:T(8,128)S(1)}, f32[256,128]{1,0:T(8,128)S(1)}, u32[]{:S(2)}, u32[]{:S(2)}) collective-permute-start(f32[256,128]{1,0:T(8,128)S(1)} %add.10), channel_id=1, source_target_pairs={{0,6},{1,3},{2,4},{3,1},{4,2},{5,7},{6,0},{7,5},{8,14},{9,11},{10,... | collective-permute-start | bytes 393224 | tf_op jit(solution)/shard_map/ppermute | solution.py:51
  53.5 2.3 %base_second.1.bottom_ref = f32[256,512]{1,0:T(8,128)S(1)} custom-call(bf16[256,8192]{1,0:T(8,128)(2,1)S(1)} %get-tuple-element.49.x_ref, bf16[8192,512]{1,0:T(8,128)(2,1)S(1)} %bitcast.9), custom_call_target="tpu_custom_call" | custom-call | flops 5000000000 | bytes 1048576 | tf_op jit(solution)/shard_map/base_second/pallas_call | solution.py:160
  55.8 3.3 %collective-permute-start.16 = (bf16[64,1024]{1,0:T(8,128)(2,1)S(1)}, bf16[64,1024]{1,0:T(8,128)(2,1)S(1)}, u32[]{:S(2)}, u32[]{:S(2)}) collective-permute-start(bf16[64,1024]{1,0:T(8,128)(2,1)S(1)} %slice.53.refs_5_), channel_id=1, source_target_pairs={{0,16},{1,65},{2,18},{3,67},{4,20},{5,69},{6,22},{7,71},{8,24},{9,... | collective-permute-start | bytes 393224 | tf_op jit(solution)/shard_map/ppermute | solution.py:32
  59.1 0.0 collective-permute-done.11
  59.1 3.3 %collective-permute-done.16.refs_6_ = bf16[64,1024]{1,0:T(8,128)(2,1)S(1)} collective-permute-done((bf16[64,1024]{1,0:T(8,128)(2,1)S(1)}, bf16[64,1024]{1,0:T(8,128)(2,1)S(1)}, u32[]{:S(2)}, u32[]{:S(2)}) %collective-permute-start.16) | collective-permute-done | bytes 131104 | tf_op jit(solution)/shard_map/ppermute | solution.py:32
  62.4 0.0 collective-permute-done.15.refs_4_
  62.4 0.0 collective-permute-done.13.refs_3_
  62.4 0.0 collective-permute-start.17
  62.4 1.2 %collective-permute-done.17.other_ref = bf16[256,128]{1,0:T(8,128)(2,1)S(1)} collective-permute-done((bf16[256,128]{1,0:T(8,128)(2,1)S(1)}, bf16[256,128]{1,0:T(8,128)(2,1)S(1)}, u32[]{:S(2)}, u32[]{:S(2)}) %collective-permute-start.17) | collective-permute-done | bytes 65568 | tf_op jit(solution)/shard_map/ppermute | solution.py:44
  63.6 3.9 %expand.1 = bf16[1024,512]{1,0:T(8,128)(2,1)} custom-call(s32[1024,128]{1,0:T(8,128)S(1)} %mask_code.1.code_ref, bf16[256,128]{1,0:T(8,128)(2,1)S(1)} %add_convert_fusion.mine_ref, bf16[256,128]{1,0:T(8,128)(2,1)S(1)} %collective-permute-done.17.other_ref, f32[768,512]{1,0:T(8,128)S(1)} %get-tuple-element.53.top_ref, f32[256,512]{1,0:T(8,128)S(1)} %base_second.1.bottom_ref, ...), custom_call_target="tpu_custom_call" | custom-call | flops 2147483648 | bytes 3145728 | tf_op jit(solution)/shard_map/expand/pallas_call | solution.py:269
  (17 shorter events, 0.3 us)
Async XLA Ops:
  0.0 10.3 %collective-permute-start.2 = (bf16[128,1024]{1,0:T(8,128)(2,1)}, bf16[128,1024]{1,0:T(8,128)(2,1)S(1)}, u32[]{:S(2)}, u32[]{:S(2)}) collective-permute-start(bf16[128,1024]{1,0:T(8,128)(2,1)} %bitcast.11), channel_id=1, source_target_pairs={{0,16},{1,65},{2,18},{3,67},{4,20},{5,69},{6,22},{7,71},{8,24},{9,... | collective-permute-start | bytes 786440 | tf_op jit(solution)/shard_map/ppermute | solution.py:32
  3.1 8.0 %collective-permute-start.1 = (bf16[128,1024]{1,0:T(8,128)(2,1)}, bf16[128,1024]{1,0:T(8,128)(2,1)S(1)}, u32[]{:S(2)}, u32[]{:S(2)}) collective-permute-start(bf16[128,1024]{1,0:T(8,128)(2,1)} %bitcast.12), channel_id=1, source_target_pairs={{0,24},{1,97},{2,26},{3,99},{4,28},{5,101},{6,30},{7,103},{8,0},{9... | collective-permute-start | bytes 786440 | tf_op jit(solution)/shard_map/ppermute | solution.py:32
  4.2 7.8 %collective-permute-start = (bf16[128,1024]{1,0:T(8,128)(2,1)}, bf16[128,1024]{1,0:T(8,128)(2,1)S(1)}, u32[]{:S(2)}, u32[]{:S(2)}) collective-permute-start(bf16[128,1024]{1,0:T(8,128)(2,1)} %bitcast.13), channel_id=1, source_target_pairs={{0,8},{1,33},{2,10},{3,35},{4,12},{5,37},{6,14},{7,39},{8,16},{9,4... | collective-permute-start | bytes 786440 | tf_op jit(solution)/shard_map/ppermute | solution.py:32
  5.1 0.7 %copy-start = (s32[1024,1]{0,1:T(1,128)S(1)}, s32[1024,1]{0,1:T(1,128)}, u32[]{:S(2)}) copy-start(s32[1024,1]{0,1:T(1,128)} %param.6) | copy-start | bytes 12292
  5.8 13.9 %slice-start = ((s8[8388608]{0:T(1024)(128)(4,1)}), s8[4194304]{0:T(1024)(128)(4,1)S(1)}, s32[]{:S(2)}) async-start(s8[8388608]{0:T(1024)(128)(4,1)} %bitcast.8), calls=%async_computation | async-start | bytes 8388608
  6.0 4.2 %copy-start.2 = (bf16[2,64,512]{2,1,0:T(8,128)(2,1)S(1)}, bf16[2,64,512]{2,1,0:T(8,128)(2,1)}, u32[]{:S(2)}) copy-start(bf16[2,64,512]{2,1,0:T(8,128)(2,1)} %param.9) | copy-start | bytes 393220
  6.0 6.0 %copy-start.1 = (bf16[2,1024,64]{1,2,0:T(8,128)(2,1)S(1)}, bf16[2,1024,64]{1,2,0:T(8,128)(2,1)}, u32[]{:S(2)}) copy-start(bf16[2,1024,64]{1,2,0:T(8,128)(2,1)} %param.8) | copy-start | bytes 786436
  6.1 13.7 %slice-start.1 = ((s8[8388608]{0:T(1024)(128)(4,1)}), s8[4194304]{0:T(1024)(128)(4,1)S(1)}, s32[]{:S(2)}) async-start(s8[8388608]{0:T(1024)(128)(4,1)} %bitcast.8), calls=%async_computation.1 | async-start | bytes 8388608
  12.2 14.6 %collective-permute-start.4 = (bf16[320,1024]{1,0:T(8,128)(2,1)S(1)}, bf16[320,1024]{1,0:T(8,128)(2,1)S(1)}, u32[]{:S(2)}, u32[]{:S(2)}) collective-permute-start(bf16[320,1024]{1,0:T(8,128)(2,1)S(1)} %get-tuple-element.61), channel_id=1, source_target_pairs={{0,96},{1,25},{2,98},{3,27},{4,100},{5,29},{6,102},{7,31},{8,104},... | collective-permute-start | bytes 1966088 | tf_op jit(solution)/shard_map/ppermute | solution.py:38
  16.3 11.8 %collective-permute-start.3 = (bf16[320,1024]{1,0:T(8,128)(2,1)S(1)}, bf16[320,1024]{1,0:T(8,128)(2,1)S(1)}, u32[]{:S(2)}, u32[]{:S(2)}) collective-permute-start(bf16[320,1024]{1,0:T(8,128)(2,1)S(1)} %get-tuple-element.62), channel_id=1, source_target_pairs={{0,32},{1,9},{2,34},{3,11},{4,36},{5,13},{6,38},{7,15},{8,40},{9,1... | collective-permute-start | bytes 1966088 | tf_op jit(solution)/shard_map/ppermute | solution.py:38
  16.4 17.3 %collective-permute-start.7 = (bf16[256,1024]{1,0:T(8,128)(2,1)S(1)}, bf16[256,1024]{1,0:T(8,128)(2,1)S(1)}, u32[]{:S(2)}, u32[]{:S(2)}) collective-permute-start(bf16[256,1024]{1,0:T(8,128)(2,1)S(1)} %constant_dynamic-update-slice_fusion.refs_1_), channel_id=1, source_target_pairs={{0,32},{1,9},{2,34},{3,11},{4,36},{5,13},{6,38},{7,15},{8,40},{9,1... | collective-permute-start | bytes 1572872 | tf_op jit(solution)/shard_map/ppermute | solution.py:38
  16.5 17.3 %collective-permute-start.8 = (bf16[256,1024]{1,0:T(8,128)(2,1)S(1)}, bf16[256,1024]{1,0:T(8,128)(2,1)S(1)}, u32[]{:S(2)}, u32[]{:S(2)}) collective-permute-start(bf16[256,1024]{1,0:T(8,128)(2,1)S(1)} %pad_maximum_fusion.1.refs_0_), channel_id=1, source_target_pairs={{0,96},{1,25},{2,98},{3,27},{4,100},{5,29},{6,102},{7,31},{8,104},... | collective-permute-start | bytes 1572872 | tf_op jit(solution)/shard_map/ppermute | solution.py:38
  28.1 12.9 %collective-permute-start.5 = (bf16[320,1024]{1,0:T(8,128)(2,1)S(1)}, bf16[320,1024]{1,0:T(8,128)(2,1)S(1)}, u32[]{:S(2)}, u32[]{:S(2)}) collective-permute-start(bf16[320,1024]{1,0:T(8,128)(2,1)S(1)} %collective-permute-done.3), channel_id=1, source_target_pairs={{0,32},{1,9},{2,34},{3,11},{4,36},{5,13},{6,38},{7,15},{8,40},{9,1... | collective-permute-start | bytes 1966088 | tf_op jit(solution)/shard_map/ppermute | solution.py:38
  28.3 11.2 %collective-permute-start.6 = (bf16[256,1024]{1,0:T(8,128)(2,1)S(1)}, bf16[256,1024]{1,0:T(8,128)(2,1)S(1)}, u32[]{:S(2)}, u32[]{:S(2)}) collective-permute-start(bf16[256,1024]{1,0:T(8,128)(2,1)S(1)} %slice.47.refs_5_), channel_id=1, source_target_pairs={{0,96},{1,25},{2,98},{3,27},{4,100},{5,29},{6,102},{7,31},{8,104},... | collective-permute-start | bytes 1572872 | tf_op jit(solution)/shard_map/ppermute | solution.py:38
  37.3 8.3 %collective-permute-start.14 = (bf16[192,1024]{1,0:T(8,128)(2,1)S(1)}, bf16[192,1024]{1,0:T(8,128)(2,1)S(1)}, u32[]{:S(2)}, u32[]{:S(2)}) collective-permute-start(bf16[192,1024]{1,0:T(8,128)(2,1)S(1)} %pad_maximum_fusion.2.refs_0_), channel_id=1, source_target_pairs={{0,24},{1,97},{2,26},{3,99},{4,28},{5,101},{6,30},{7,103},{8,0},{9... | collective-permute-start | bytes 1179656 | tf_op jit(solution)/shard_map/ppermute | solution.py:32
  39.0 9.0 %collective-permute-start.12 = (bf16[192,1024]{1,0:T(8,128)(2,1)S(1)}, bf16[192,1024]{1,0:T(8,128)(2,1)S(1)}, u32[]{:S(2)}, u32[]{:S(2)}) collective-permute-start(bf16[192,1024]{1,0:T(8,128)(2,1)S(1)} %pad_maximum_fusion.2.refs_0_), channel_id=1, source_target_pairs={{0,8},{1,33},{2,10},{3,35},{4,12},{5,37},{6,14},{7,39},{8,16},{9,4... | collective-permute-start | bytes 1179656 | tf_op jit(solution)/shard_map/ppermute | solution.py:32
  42.4 1.4 %collective-permute-start.9 = (f32[256,128]{1,0:T(8,128)S(1)}, f32[256,128]{1,0:T(8,128)S(1)}, u32[]{:S(2)}, u32[]{:S(2)}) collective-permute-start(f32[256,128]{1,0:T(8,128)S(1)} %get-tuple-element.48), channel_id=1, source_target_pairs={{0,1},{1,0},{2,3},{3,2},{4,5},{5,4},{6,7},{7,6},{8,9},{9,8},{10,11... | collective-permute-start | bytes 393224 | tf_op jit(solution)/shard_map/ppermute | solution.py:44
  43.9 6.5 %collective-permute-start.10 = (f32[256,128]{1,0:T(8,128)S(1)}, f32[256,128]{1,0:T(8,128)S(1)}, u32[]{:S(2)}, u32[]{:S(2)}) collective-permute-start(f32[256,128]{1,0:T(8,128)S(1)} %add.9), channel_id=1, source_target_pairs={{0,2},{1,7},{2,0},{3,5},{4,6},{5,3},{6,4},{7,1},{8,10},{9,15},{10,... | collective-permute-start | bytes 393224 | tf_op jit(solution)/shard_map/ppermute | solution.py:51
  48.1 14.3 %collective-permute-start.15 = (bf16[160,1024]{1,0:T(8,128)(2,1)S(1)}, bf16[160,1024]{1,0:T(8,128)(2,1)S(1)}, u32[]{:S(2)}, u32[]{:S(2)}) collective-permute-start(bf16[160,1024]{1,0:T(8,128)(2,1)S(1)} %get-tuple-element.59), channel_id=1, source_target_pairs={{0,24},{1,97},{2,26},{3,99},{4,28},{5,101},{6,30},{7,103},{8,0},{9... | collective-permute-start | bytes 983048 | tf_op jit(solution)/shard_map/ppermute | solution.py:32
  49.1 13.3 %collective-permute-start.13 = (bf16[160,1024]{1,0:T(8,128)(2,1)S(1)}, bf16[160,1024]{1,0:T(8,128)(2,1)S(1)}, u32[]{:S(2)}, u32[]{:S(2)}) collective-permute-start(bf16[160,1024]{1,0:T(8,128)(2,1)S(1)} %get-tuple-element.60), channel_id=1, source_target_pairs={{0,8},{1,33},{2,10},{3,35},{4,12},{5,37},{6,14},{7,39},{8,16},{9,4... | collective-permute-start | bytes 983048 | tf_op jit(solution)/shard_map/ppermute | solution.py:32
  50.4 8.7 %collective-permute-start.11 = (f32[256,128]{1,0:T(8,128)S(1)}, f32[256,128]{1,0:T(8,128)S(1)}, u32[]{:S(2)}, u32[]{:S(2)}) collective-permute-start(f32[256,128]{1,0:T(8,128)S(1)} %add.10), channel_id=1, source_target_pairs={{0,6},{1,3},{2,4},{3,1},{4,2},{5,7},{6,0},{7,5},{8,14},{9,11},{10,... | collective-permute-start | bytes 393224 | tf_op jit(solution)/shard_map/ppermute | solution.py:51
  55.8 6.6 %collective-permute-start.16 = (bf16[64,1024]{1,0:T(8,128)(2,1)S(1)}, bf16[64,1024]{1,0:T(8,128)(2,1)S(1)}, u32[]{:S(2)}, u32[]{:S(2)}) collective-permute-start(bf16[64,1024]{1,0:T(8,128)(2,1)S(1)} %slice.53.refs_5_), channel_id=1, source_target_pairs={{0,16},{1,65},{2,18},{3,67},{4,20},{5,69},{6,22},{7,71},{8,24},{9,... | collective-permute-start | bytes 393224 | tf_op jit(solution)/shard_map/ppermute | solution.py:32
  62.4 1.3 %collective-permute-start.17 = (bf16[256,128]{1,0:T(8,128)(2,1)S(1)}, bf16[256,128]{1,0:T(8,128)(2,1)S(1)}, u32[]{:S(2)}, u32[]{:S(2)}) collective-permute-start(bf16[256,128]{1,0:T(8,128)(2,1)S(1)} %add_convert_fusion.mine_ref), channel_id=1, source_target_pairs={{0,1},{1,0},{2,3},{3,2},{4,5},{5,4},{6,7},{7,6},{8,9},{9,8},{10,11... | collective-permute-start | bytes 196616 | tf_op jit(solution)/shard_map/ppermute | solution.py:44

commit v14 on v10

--- a/solution.py
+++ b/solution.py
@@ -276,15 +276,16 @@
     near = [first(down, d) for d in (1, -1, 2)]
     code = mask_code(token_adapter_index)
     here, half = fetch(tie(activations, code)[0], width)
-    near, here, half, up = tie(near, here, half, up)
-    d_own = jnp.concatenate([down, *near], axis=0)
-    d_before, d_after = second(d_own, 1), second(d_own, -1)
+    before, after, far, here, half = tie(*near, here, half)
+    top, bottom = jnp.concatenate([down, before], axis=0), jnp.concatenate([after, far], axis=0)
+    top_before, bottom_after = second(top, 1), second(bottom, -1)
+    bottom_before, top_after = second(bottom, 1), second(top, -1)
+    base, rest = base_first(half, query_matrix, activations)
+    top_before, bottom_after, base, up = tie(top_before, bottom_after, base, up)
+
+    d_two = [second(top_before, 1), second(bottom_after, -1)]
     u_own = jnp.concatenate([up] + [first(up, d) for d in (1, -1, 2)], axis=0)
-    top, rest = base_first(half, query_matrix, activations)
-    d_before, d_after, top = tie(d_before, d_after, top)
-
-    d_two = [second(d_before[:256], 1), second(d_after[256:], -1)]
-    groups = [([d_own], row(0)), ([d_before], row(-1)), ([d_after], row(1))]
+    groups = [([top, bottom], row(0)), ([top_before, bottom_before], row(-1)), ([top_after, bottom_after], row(1))]
     total = shrink(code, here, groups, None, False, "shrink_near", 5000000000)
     total, u_own = tie(total, u_own)
     u_before, u_after = second(u_own, 1), second(u_own, -1)
@@ -293,12 +294,12 @@
     keep = keep + other_core(give)
     u_two = [second(u_before[:256], 1), second(u_after[256:], -1)]
     keep = keep + pair(keep, 0)
-    there, bottom, *u_two = tie(pair(keep, 1), base_second(rest, query_matrix), *u_two)
+    there, last, *u_two = tie(pair(keep, 1), base_second(rest, query_matrix), *u_two)
     keep = keep + there
     mine = keep.astype(BF)
     parts = [(u_own, row(0), 0, 0), (u_before, row(-1), 0, 0), (u_after, row(1), 0, 0)]
     parts += [(a, row(2, hops), 0, 0) for a, hops in zip(u_two, (HOPS[:2], HOPS[2:]))]
-    return expand(code, mine, other_core(mine), [top, bottom], parts)
+    return expand(code, mine, other_core(mine), [base, last], parts)
 
 
 def solution(mesh):

time: 65 us -> 64.5 us (level)
  waiting for transfers between devices: 11.8 us -> 7.88 us
  starting transfers between devices: 28.6 us -> 32.1 us
    ppermute x8 -> x10, waiting for transfers between devices: 6.42 us -> 2.52 us  [second(): lax.ppermute(a, AXES, every(lambda x, y, z, c: (x + d, y, z, c) if c else...]
    ppermute x8 -> x10, starting transfers between devices: 14.4 us -> 17.7 us  [second(): lax.ppermute(a, AXES, every(lambda x, y, z, c: (x + d, y, z, c) if c else...]
  transfers between devices with their start and end apart: 18 -> 20, of which waited for: 9 -> 6; matrix products, arithmetic and copies ran while one was open for 0% -> 0% of each run, Pallas kernels for 29% -> 29%
where the time goes in v14:
time: 64.5 us; the launch traced here: 63.3 us
  starting transfers between devices  32.1 us (50%)
  Pallas kernels  22.2 us (34%)
  waiting for transfers between devices  7.88 us (12%)
  local copies, waits for them, and re-layouts  0.78 us (1%)
    ppermute x10, starting transfers between devices, second(): lax.ppermute(a, AXES, every(lambda x, y, z, c: (x + d, y, z, c) if c else...  17.7 us
    ppermute x6, starting transfers between devices, first(): lax.ppermute(a, AXES, every(lambda x, y, z, c: (x, y, z + d, c) if c else...  9.31 us
    pallas_call x1, Pallas kernels, base_first(): pl.pallas_call(base_kernel, in_specs=[VMEM, VMEM, HBM], out_specs=[VMEM,...  6.99 us
    pallas_call x2, Pallas kernels, shrink(): pl.pallas_call(functools.partial(shrink_kernel, [(len(parts), places) for...  4.81 us
    ppermute x2, starting transfers between devices, pair(): return lax.ppermute(a, AXES, every(to))  4.75 us
    pallas_call x1, Pallas kernels, fetch(): pl.pallas_call(fetch_kernel, in_specs=[HBM], out_specs=[VMEM] * 2, out_sh...  4.22 us
    pallas_call x1, Pallas kernels, expand(): pl.pallas_call(functools.partial(expand_kernel, [part[1:] for part in par...  3.67 us
    ppermute x2, waiting for transfers between devices, other_core(): return lax.ppermute(a, AXES, every(lambda x, y, z, c: (x, y, z, 1 - c)))  2.58 us
  transfers between devices with their start and end apart: 20, of which 6 were waited for; matrix products, arithmetic and copies ran while one was open for 0% of the time, Pallas kernels for 29%

profile of v14, /device:TPU:0, one launch (start us, length us, event | category | flops | bytes accessed | tf_op | source)
XLA Modules:
  0.0 63.3 jit_solution(15273693932993981009)
XLA Ops:
  0.0 1.6 %collective-permute-start = (bf16[128,1024]{1,0:T(8,128)(2,1)}, bf16[128,1024]{1,0:T(8,128)(2,1)S(1)}, u32[]{:S(2)}, u32[]{:S(2)}) collective-permute-start(bf16[128,1024]{1,0:T(8,128)(2,1)} %bitcast.8), channel_id=1, source_target_pairs={{0,8},{1,33},{2,10},{3,35},{4,12},{5,37},{6,14},{7,39},{8,16},{9,4... | collective-permute-start | bytes 786440 | tf_op jit(solution)/shard_map/ppermute | solution.py:32
  1.6 1.7 %collective-permute-start.1 = (bf16[128,1024]{1,0:T(8,128)(2,1)}, bf16[128,1024]{1,0:T(8,128)(2,1)S(1)}, u32[]{:S(2)}, u32[]{:S(2)}) collective-permute-start(bf16[128,1024]{1,0:T(8,128)(2,1)} %bitcast.9), channel_id=1, source_target_pairs={{0,24},{1,97},{2,26},{3,99},{4,28},{5,101},{6,30},{7,103},{8,0},{9... | collective-permute-start | bytes 786440 | tf_op jit(solution)/shard_map/ppermute | solution.py:32
  3.2 1.9 %collective-permute-start.2 = (bf16[128,1024]{1,0:T(8,128)(2,1)}, bf16[128,1024]{1,0:T(8,128)(2,1)S(1)}, u32[]{:S(2)}, u32[]{:S(2)}) collective-permute-start(bf16[128,1024]{1,0:T(8,128)(2,1)} %bitcast.10), channel_id=1, source_target_pairs={{0,16},{1,65},{2,18},{3,67},{4,20},{5,69},{6,22},{7,71},{8,24},{9,... | collective-permute-start | bytes 786440 | tf_op jit(solution)/shard_map/ppermute | solution.py:32
  5.1 0.0 copy-start
  5.1 0.7 %copy-done = s32[1024,1]{0,1:T(1,128)S(1)} copy-done((s32[1024,1]{0,1:T(1,128)S(1)}, s32[1024,1]{0,1:T(1,128)}, u32[]{:S(2)}) %copy-start) | copy-done | bytes 4120
  5.8 0.0 slice-start
  5.8 0.2 mask_code.1.code_ref
  6.0 0.0 copy-start.1
  6.0 0.0 slice-start.1
  6.1 4.2 %fetch.1 = (bf16[1024,1024]{1,0:T(8,128)(2,1)S(1)}, bf16[512,8192]{1,0:T(8,128)(2,1)S(1)}) custom-call(bf16[1024,8192]{1,0:T(8,128)(2,1)} %x_ref.2), custom_call_target="tpu_custom_call" | custom-call | flops 1000000 | bytes 1048576 | tf_op jit(solution)/shard_map/fetch/pallas_call | solution.py:105
  10.3 0.0 collective-permute-done
  10.3 0.0 collective-permute-done.1
  10.3 1.4 %collective-permute-done.2 = bf16[128,1024]{1,0:T(8,128)(2,1)S(1)} collective-permute-done((bf16[128,1024]{1,0:T(8,128)(2,1)}, bf16[128,1024]{1,0:T(8,128)(2,1)S(1)}, u32[]{:S(2)}, u32[]{:S(2)}) %collective-permute-start.2) | collective-permute-done | bytes 262176 | tf_op jit(solution)/shard_map/ppermute | solution.py:32
  11.7 0.0 copy-done.1
  11.7 2.0 %collective-permute-start.3 = (bf16[256,1024]{1,0:T(8,128)(2,1)S(1)}, bf16[256,1024]{1,0:T(8,128)(2,1)S(1)}, u32[]{:S(2)}, u32[]{:S(2)}) collective-permute-start(bf16[256,1024]{1,0:T(8,128)(2,1)S(1)} %pad_maximum_fusion.refs_0_), channel_id=1, source_target_pairs={{0,32},{1,9},{2,34},{3,11},{4,36},{5,13},{6,38},{7,15},{8,40},{9,1... | collective-permute-start | bytes 1572872 | tf_op jit(solution)/shard_map/ppermute | solution.py:38
  13.7 0.0 copy-start.2
  13.8 2.2 %collective-permute-start.4 = (bf16[256,1024]{1,0:T(8,128)(2,1)S(1)}, bf16[256,1024]{1,0:T(8,128)(2,1)S(1)}, u32[]{:S(2)}, u32[]{:S(2)}) collective-permute-start(bf16[256,1024]{1,0:T(8,128)(2,1)S(1)} %constant_dynamic-update-slice_fusion.refs_1_), channel_id=1, source_target_pairs={{0,96},{1,25},{2,98},{3,27},{4,100},{5,29},{6,102},{7,31},{8,104},... | collective-permute-start | bytes 1572872 | tf_op jit(solution)/shard_map/ppermute | solution.py:38
  16.0 0.0 collective-permute-start.7
  16.0 3.2 %collective-permute-start.8 = (bf16[256,1024]{1,0:T(8,128)(2,1)S(1)}, bf16[256,1024]{1,0:T(8,128)(2,1)S(1)}, u32[]{:S(2)}, u32[]{:S(2)}) collective-permute-start(bf16[256,1024]{1,0:T(8,128)(2,1)S(1)} %pad_maximum_fusion.refs_0_), channel_id=1, source_target_pairs={{0,96},{1,25},{2,98},{3,27},{4,100},{5,29},{6,102},{7,31},{8,104},... | collective-permute-start | bytes 1572872 | tf_op jit(solution)/shard_map/ppermute | solution.py:38
  19.2 0.0 slice-done
  19.2 0.0 slice-done.1
  19.2 7.0 %base_first.1 = (f32[768,512]{1,0:T(8,128)S(1)}, bf16[256,8192]{1,0:T(8,128)(2,1)S(1)}) custom-call(bf16[512,8192]{1,0:T(8,128)(2,1)S(1)} %get-tuple-element.37.half_ref, bf16[8192,512]{1,0:T(8,128)(2,1)S(1)} %bitcast.6, bf16[1024,8192]{1,0:T(8,128)(2,1)} %x_ref.2), custom_call_target="tpu_custom_call" | custom-call | flops 5000000000 | bytes 1048576 | tf_op jit(solution)/shard_map/base_first/pallas_call | solution.py:143
  26.2 0.0 collective-permute-done.3.refs_2_
  26.2 0.0 collective-permute-done.4.refs_5_
  26.2 0.0 copy-done.2
  26.2 1.6 %collective-permute-start.11 = (bf16[128,512]{1,0:T(8,128)(2,1)S(1)}, bf16[128,512]{1,0:T(8,128)(2,1)S(1)}, u32[]{:S(2)}, u32[]{:S(2)}) collective-permute-start(bf16[128,512]{1,0:T(8,128)(2,1)S(1)} %bitcast.12), channel_id=1, source_target_pairs={{0,16},{1,65},{2,18},{3,67},{4,20},{5,69},{6,22},{7,71},{8,24},{9,... | collective-permute-start | bytes 393224 | tf_op jit(solution)/shard_map/ppermute | solution.py:32
  27.9 2.5 %collective-permute-start.10 = (bf16[128,512]{1,0:T(8,128)(2,1)S(1)}, bf16[128,512]{1,0:T(8,128)(2,1)S(1)}, u32[]{:S(2)}, u32[]{:S(2)}) collective-permute-start(bf16[128,512]{1,0:T(8,128)(2,1)S(1)} %bitcast.13), channel_id=1, source_target_pairs={{0,24},{1,97},{2,26},{3,99},{4,28},{5,101},{6,30},{7,103},{8,0},{9... | collective-permute-start | bytes 393224 | tf_op jit(solution)/shard_map/ppermute | solution.py:32
  30.4 0.0 collective-permute-start.9
  30.4 0.0 collective-permute-done.7.refs_3_
  30.4 0.0 collective-permute-start.5
  30.4 0.0 collective-permute-done.8.refs_4_
  30.4 3.6 %collective-permute-start.6 = (bf16[256,1024]{1,0:T(8,128)(2,1)S(1)}, bf16[256,1024]{1,0:T(8,128)(2,1)S(1)}, u32[]{:S(2)}, u32[]{:S(2)}) collective-permute-start(bf16[256,1024]{1,0:T(8,128)(2,1)S(1)} %collective-permute-done.4.refs_5_), channel_id=1, source_target_pairs={{0,96},{1,25},{2,98},{3,27},{4,100},{5,29},{6,102},{7,31},{8,104},... | collective-permute-start | bytes 1572872 | tf_op jit(solution)/shard_map/ppermute | solution.py:38
  34.0 3.5 %shrink_near.1.refs_2_ = f32[1024,128]{1,0:T(8,128)S(1)} custom-call(s32[1024,128]{1,0:T(8,128)S(1)} %mask_code.1.code_ref, bf16[1024,1024]{1,0:T(8,128)(2,1)S(1)} %get-tuple-element.33.x_ref, bf16[256,1024]{1,0:T(8,128)(2,1)S(1)} %pad_maximum_fusion.refs_0_, bf16[256,1024]{1,0:T(8,128)(2,1)S(1)} %constant_dynamic-update-slice_fusion.refs_1_, ...), custom_call_target="tpu_custom_call" | custom-call | flops 5000000000 | bytes 1048576 | tf_op jit(solution)/shard_map/shrink_near/pallas_call | solution.py:203
  37.5 0.0 collective-permute-done.11
  37.5 0.0 collective-permute-done.10
  37.5 0.6 collective-permute-done.9
  38.1 0.1 collective-permute-start.15
  38.2 3.2 %collective-permute-start.17 = (bf16[512,512]{1,0:T(8,128)(2,1)S(1)}, bf16[512,512]{1,0:T(8,128)(2,1)S(1)}, u32[]{:S(2)}, u32[]{:S(2)}) collective-permute-start(bf16[512,512]{1,0:T(8,128)(2,1)S(1)} %pad_maximum_fusion.1.refs_0_), channel_id=1, source_target_pairs={{0,96},{1,25},{2,98},{3,27},{4,100},{5,29},{6,102},{7,31},{8,104},... | collective-permute-start | bytes 1572872 | tf_op jit(solution)/shard_map/ppermute | solution.py:38
  41.4 0.0 collective-permute-done.5.refs_0_
  41.4 0.0 collective-permute-done.6.refs_1_
  41.4 1.4 %shrink_far.1 = (f32[256,128]{1,0:T(8,128)S(1)}, f32[256,128]{1,0:T(8,128)S(1)}) custom-call(s32[1024,128]{1,0:T(8,128)S(1)} %mask_code.1.code_ref, bf16[1024,1024]{1,0:T(8,128)(2,1)S(1)} %get-tuple-element.33.x_ref, bf16[256,1024]{1,0:T(8,128)(2,1)S(1)} %collective-permute-done.5.refs_0_, bf16[256,1024]{1,0:T(8,128)(2,1)S(1)} %collective-permute-done.6.refs_1_, ...), custom_call_target="tpu_custom_call" | custom-call | flops 1048576 | bytes 1048576 | tf_op jit(solution)/shard_map/shrink_far/pallas_call | solution.py:203
  42.8 0.3 collective-permute-start.12
  43.0 1.3 %collective-permute-done.12 = f32[256,128]{1,0:T(8,128)S(1)} collective-permute-done((f32[256,128]{1,0:T(8,128)S(1)}, f32[256,128]{1,0:T(8,128)S(1)}, u32[]{:S(2)}, u32[]{:S(2)}) %collective-permute-start.12) | collective-permute-done | bytes 131104 | tf_op jit(solution)/shard_map/ppermute | solution.py:44
  44.4 1.7 %collective-permute-start.13 = (f32[256,128]{1,0:T(8,128)S(1)}, f32[256,128]{1,0:T(8,128)S(1)}, u32[]{:S(2)}, u32[]{:S(2)}) collective-permute-start(f32[256,128]{1,0:T(8,128)S(1)} %add.9), channel_id=1, source_target_pairs={{0,2},{1,7},{2,0},{3,5},{4,6},{5,3},{6,4},{7,1},{8,10},{9,15},{10,... | collective-permute-start | bytes 393224 | tf_op jit(solution)/shard_map/ppermute | solution.py:51
  46.1 2.5 %collective-permute-done.15.refs_1_ = bf16[512,512]{1,0:T(8,128)(2,1)S(1)} collective-permute-done((bf16[512,512]{1,0:T(8,128)(2,1)S(1)}, bf16[512,512]{1,0:T(8,128)(2,1)S(1)}, u32[]{:S(2)}, u32[]{:S(2)}) %collective-permute-start.15) | collective-permute-done | bytes 524320 | tf_op jit(solution)/shard_map/ppermute | solution.py:38
  48.6 0.1 collective-permute-start.16
  48.7 0.0 collective-permute-done.17.refs_2_
  48.7 3.3 %collective-permute-start.18 = (bf16[256,512]{1,0:T(8,128)(2,1)S(1)}, bf16[256,512]{1,0:T(8,128)(2,1)S(1)}, u32[]{:S(2)}, u32[]{:S(2)}) collective-permute-start(bf16[256,512]{1,0:T(8,128)(2,1)S(1)} %slice.9), channel_id=1, source_target_pairs={{0,96},{1,25},{2,98},{3,27},{4,100},{5,29},{6,102},{7,31},{8,104},... | collective-permute-start | bytes 786440 | tf_op jit(solution)/shard_map/ppermute | solution.py:38
  52.0 0.0 collective-permute-done.13
  52.0 3.1 %collective-permute-start.14 = (f32[256,128]{1,0:T(8,128)S(1)}, f32[256,128]{1,0:T(8,128)S(1)}, u32[]{:S(2)}, u32[]{:S(2)}) collective-permute-start(f32[256,128]{1,0:T(8,128)S(1)} %add.10), channel_id=1, source_target_pairs={{0,6},{1,3},{2,4},{3,1},{4,2},{5,7},{6,0},{7,5},{8,14},{9,11},{10,... | collective-permute-start | bytes 393224 | tf_op jit(solution)/shard_map/ppermute | solution.py:51
  55.1 2.3 %base_second.1.bottom_ref = f32[256,512]{1,0:T(8,128)S(1)} custom-call(bf16[256,8192]{1,0:T(8,128)(2,1)S(1)} %get-tuple-element.48.x_ref, bf16[8192,512]{1,0:T(8,128)(2,1)S(1)} %bitcast.6), custom_call_target="tpu_custom_call" | custom-call | flops 5000000000 | bytes 1048576 | tf_op jit(solution)/shard_map/base_second/pallas_call | solution.py:160
  57.4 0.0 collective-permute-done.16.refs_3_
  57.4 0.0 collective-permute-done.18.refs_4_
  57.4 0.8 %collective-permute-done.14 = f32[256,128]{1,0:T(8,128)S(1)} collective-permute-done((f32[256,128]{1,0:T(8,128)S(1)}, f32[256,128]{1,0:T(8,128)S(1)}, u32[]{:S(2)}, u32[]{:S(2)}) %collective-permute-start.14) | collective-permute-done | bytes 131104 | tf_op jit(solution)/shard_map/ppermute | solution.py:51
  58.3 0.1 collective-permute-start.19
  58.4 1.2 %collective-permute-done.19.other_ref = bf16[256,128]{1,0:T(8,128)(2,1)S(1)} collective-permute-done((bf16[256,128]{1,0:T(8,128)(2,1)S(1)}, bf16[256,128]{1,0:T(8,128)(2,1)S(1)}, u32[]{:S(2)}, u32[]{:S(2)}) %collective-permute-start.19) | collective-permute-done | bytes 65568 | tf_op jit(solution)/shard_map/ppermute | solution.py:44
  59.6 3.7 %expand.1 = bf16[1024,512]{1,0:T(8,128)(2,1)} custom-call(s32[1024,128]{1,0:T(8,128)S(1)} %mask_code.1.code_ref, bf16[256,128]{1,0:T(8,128)(2,1)S(1)} %add_convert_fusion.mine_ref, bf16[256,128]{1,0:T(8,128)(2,1)S(1)} %collective-permute-done.19.other_ref, f32[768,512]{1,0:T(8,128)S(1)} %get-tuple-element.51.top_ref, f32[256,512]{1,0:T(8,128)S(1)} %base_second.1.bottom_ref, ...), custom_call_target="tpu_custom_call" | custom-call | flops 2147483648 | bytes 3145728 | tf_op jit(solution)/shard_map/expand/pallas_call | solution.py:254
  (10 shorter events, 0.2 us)
Async XLA Ops:
  0.0 10.3 %collective-permute-start = (bf16[128,1024]{1,0:T(8,128)(2,1)}, bf16[128,1024]{1,0:T(8,128)(2,1)S(1)}, u32[]{:S(2)}, u32[]{:S(2)}) collective-permute-start(bf16[128,1024]{1,0:T(8,128)(2,1)} %bitcast.8), channel_id=1, source_target_pairs={{0,8},{1,33},{2,10},{3,35},{4,12},{5,37},{6,14},{7,39},{8,16},{9,4... | collective-permute-start | bytes 786440 | tf_op jit(solution)/shard_map/ppermute | solution.py:32
  1.6 8.7 %collective-permute-start.1 = (bf16[128,1024]{1,0:T(8,128)(2,1)}, bf16[128,1024]{1,0:T(8,128)(2,1)S(1)}, u32[]{:S(2)}, u32[]{:S(2)}) collective-permute-start(bf16[128,1024]{1,0:T(8,128)(2,1)} %bitcast.9), channel_id=1, source_target_pairs={{0,24},{1,97},{2,26},{3,99},{4,28},{5,101},{6,30},{7,103},{8,0},{9... | collective-permute-start | bytes 786440 | tf_op jit(solution)/shard_map/ppermute | solution.py:32
  3.2 8.4 %collective-permute-start.2 = (bf16[128,1024]{1,0:T(8,128)(2,1)}, bf16[128,1024]{1,0:T(8,128)(2,1)S(1)}, u32[]{:S(2)}, u32[]{:S(2)}) collective-permute-start(bf16[128,1024]{1,0:T(8,128)(2,1)} %bitcast.10), channel_id=1, source_target_pairs={{0,16},{1,65},{2,18},{3,67},{4,20},{5,69},{6,22},{7,71},{8,24},{9,... | collective-permute-start | bytes 786440 | tf_op jit(solution)/shard_map/ppermute | solution.py:32
  5.1 0.7 %copy-start = (s32[1024,1]{0,1:T(1,128)S(1)}, s32[1024,1]{0,1:T(1,128)}, u32[]{:S(2)}) copy-start(s32[1024,1]{0,1:T(1,128)} %param.6) | copy-start | bytes 12292
  5.8 13.4 %slice-start = ((s8[8388608]{0:T(1024)(128)(4,1)}), s8[4194304]{0:T(1024)(128)(4,1)S(1)}, s32[]{:S(2)}) async-start(s8[8388608]{0:T(1024)(128)(4,1)} %bitcast.5), calls=%async_computation | async-start | bytes 8388608
  6.0 5.6 %copy-start.1 = (bf16[2,1024,64]{1,2,0:T(8,128)(2,1)S(1)}, bf16[2,1024,64]{1,2,0:T(8,128)(2,1)}, u32[]{:S(2)}) copy-start(bf16[2,1024,64]{1,2,0:T(8,128)(2,1)} %param.8) | copy-start | bytes 786436
  6.0 13.2 %slice-start.1 = ((s8[8388608]{0:T(1024)(128)(4,1)}), s8[4194304]{0:T(1024)(128)(4,1)S(1)}, s32[]{:S(2)}) async-start(s8[8388608]{0:T(1024)(128)(4,1)} %bitcast.5), calls=%async_computation.1 | async-start | bytes 8388608
  11.7 14.5 %collective-permute-start.3 = (bf16[256,1024]{1,0:T(8,128)(2,1)S(1)}, bf16[256,1024]{1,0:T(8,128)(2,1)S(1)}, u32[]{:S(2)}, u32[]{:S(2)}) collective-permute-start(bf16[256,1024]{1,0:T(8,128)(2,1)S(1)} %pad_maximum_fusion.refs_0_), channel_id=1, source_target_pairs={{0,32},{1,9},{2,34},{3,11},{4,36},{5,13},{6,38},{7,15},{8,40},{9,1... | collective-permute-start | bytes 1572872 | tf_op jit(solution)/shard_map/ppermute | solution.py:38
  13.7 12.5 %copy-start.2 = (bf16[2,64,512]{2,1,0:T(8,128)(2,1)S(1)}, bf16[2,64,512]{2,1,0:T(8,128)(2,1)}, u32[]{:S(2)}) copy-start(bf16[2,64,512]{2,1,0:T(8,128)(2,1)} %param.9) | copy-start | bytes 393220
  13.8 12.5 %collective-permute-start.4 = (bf16[256,1024]{1,0:T(8,128)(2,1)S(1)}, bf16[256,1024]{1,0:T(8,128)(2,1)S(1)}, u32[]{:S(2)}, u32[]{:S(2)}) collective-permute-start(bf16[256,1024]{1,0:T(8,128)(2,1)S(1)} %constant_dynamic-update-slice_fusion.refs_1_), channel_id=1, source_target_pairs={{0,96},{1,25},{2,98},{3,27},{4,100},{5,29},{6,102},{7,31},{8,104},... | collective-permute-start | bytes 1572872 | tf_op jit(solution)/shard_map/ppermute | solution.py:38
  16.0 14.5 %collective-permute-start.7 = (bf16[256,1024]{1,0:T(8,128)(2,1)S(1)}, bf16[256,1024]{1,0:T(8,128)(2,1)S(1)}, u32[]{:S(2)}, u32[]{:S(2)}) collective-permute-start(bf16[256,1024]{1,0:T(8,128)(2,1)S(1)} %constant_dynamic-update-slice_fusion.refs_1_), channel_id=1, source_target_pairs={{0,32},{1,9},{2,34},{3,11},{4,36},{5,13},{6,38},{7,15},{8,40},{9,1... | collective-permute-start | bytes 1572872 | tf_op jit(solution)/shard_map/ppermute | solution.py:38
  16.0 14.5 %collective-permute-start.8 = (bf16[256,1024]{1,0:T(8,128)(2,1)S(1)}, bf16[256,1024]{1,0:T(8,128)(2,1)S(1)}, u32[]{:S(2)}, u32[]{:S(2)}) collective-permute-start(bf16[256,1024]{1,0:T(8,128)(2,1)S(1)} %pad_maximum_fusion.refs_0_), channel_id=1, source_target_pairs={{0,96},{1,25},{2,98},{3,27},{4,100},{5,29},{6,102},{7,31},{8,104},... | collective-permute-start | bytes 1572872 | tf_op jit(solution)/shard_map/ppermute | solution.py:38
  26.2 11.2 %collective-permute-start.11 = (bf16[128,512]{1,0:T(8,128)(2,1)S(1)}, bf16[128,512]{1,0:T(8,128)(2,1)S(1)}, u32[]{:S(2)}, u32[]{:S(2)}) collective-permute-start(bf16[128,512]{1,0:T(8,128)(2,1)S(1)} %bitcast.12), channel_id=1, source_target_pairs={{0,16},{1,65},{2,18},{3,67},{4,20},{5,69},{6,22},{7,71},{8,24},{9,... | collective-permute-start | bytes 393224 | tf_op jit(solution)/shard_map/ppermute | solution.py:32
  27.9 9.6 %collective-permute-start.10 = (bf16[128,512]{1,0:T(8,128)(2,1)S(1)}, bf16[128,512]{1,0:T(8,128)(2,1)S(1)}, u32[]{:S(2)}, u32[]{:S(2)}) collective-permute-start(bf16[128,512]{1,0:T(8,128)(2,1)S(1)} %bitcast.13), channel_id=1, source_target_pairs={{0,24},{1,97},{2,26},{3,99},{4,28},{5,101},{6,30},{7,103},{8,0},{9... | collective-permute-start | bytes 393224 | tf_op jit(solution)/shard_map/ppermute | solution.py:32
  30.4 7.6 %collective-permute-start.9 = (bf16[128,512]{1,0:T(8,128)(2,1)S(1)}, bf16[128,512]{1,0:T(8,128)(2,1)S(1)}, u32[]{:S(2)}, u32[]{:S(2)}) collective-permute-start(bf16[128,512]{1,0:T(8,128)(2,1)S(1)} %bitcast.14), channel_id=1, source_target_pairs={{0,8},{1,33},{2,10},{3,35},{4,12},{5,37},{6,14},{7,39},{8,16},{9,4... | collective-permute-start | bytes 393224 | tf_op jit(solution)/shard_map/ppermute | solution.py:32
  30.4 11.0 %collective-permute-start.5 = (bf16[256,1024]{1,0:T(8,128)(2,1)S(1)}, bf16[256,1024]{1,0:T(8,128)(2,1)S(1)}, u32[]{:S(2)}, u32[]{:S(2)}) collective-permute-start(bf16[256,1024]{1,0:T(8,128)(2,1)S(1)} %collective-permute-done.3.refs_2_), channel_id=1, source_target_pairs={{0,32},{1,9},{2,34},{3,11},{4,36},{5,13},{6,38},{7,15},{8,40},{9,1... | collective-permute-start | bytes 1572872 | tf_op jit(solution)/shard_map/ppermute | solution.py:38
  30.4 11.0 %collective-permute-start.6 = (bf16[256,1024]{1,0:T(8,128)(2,1)S(1)}, bf16[256,1024]{1,0:T(8,128)(2,1)S(1)}, u32[]{:S(2)}, u32[]{:S(2)}) collective-permute-start(bf16[256,1024]{1,0:T(8,128)(2,1)S(1)} %collective-permute-done.4.refs_5_), channel_id=1, source_target_pairs={{0,96},{1,25},{2,98},{3,27},{4,100},{5,29},{6,102},{7,31},{8,104},... | collective-permute-start | bytes 1572872 | tf_op jit(solution)/shard_map/ppermute | solution.py:38
  38.1 10.5 %collective-permute-start.15 = (bf16[512,512]{1,0:T(8,128)(2,1)S(1)}, bf16[512,512]{1,0:T(8,128)(2,1)S(1)}, u32[]{:S(2)}, u32[]{:S(2)}) collective-permute-start(bf16[512,512]{1,0:T(8,128)(2,1)S(1)} %pad_maximum_fusion.1.refs_0_), channel_id=1, source_target_pairs={{0,32},{1,9},{2,34},{3,11},{4,36},{5,13},{6,38},{7,15},{8,40},{9,1... | collective-permute-start | bytes 1572872 | tf_op jit(solution)/shard_map/ppermute | solution.py:38
  38.2 10.5 %collective-permute-start.17 = (bf16[512,512]{1,0:T(8,128)(2,1)S(1)}, bf16[512,512]{1,0:T(8,128)(2,1)S(1)}, u32[]{:S(2)}, u32[]{:S(2)}) collective-permute-start(bf16[512,512]{1,0:T(8,128)(2,1)S(1)} %pad_maximum_fusion.1.refs_0_), channel_id=1, source_target_pairs={{0,96},{1,25},{2,98},{3,27},{4,100},{5,29},{6,102},{7,31},{8,104},... | collective-permute-start | bytes 1572872 | tf_op jit(solution)/shard_map/ppermute | solution.py:38
  42.8 1.6 %collective-permute-start.12 = (f32[256,128]{1,0:T(8,128)S(1)}, f32[256,128]{1,0:T(8,128)S(1)}, u32[]{:S(2)}, u32[]{:S(2)}) collective-permute-start(f32[256,128]{1,0:T(8,128)S(1)} %get-tuple-element.47), channel_id=1, source_target_pairs={{0,1},{1,0},{2,3},{3,2},{4,5},{5,4},{6,7},{7,6},{8,9},{9,8},{10,11... | collective-permute-start | bytes 393224 | tf_op jit(solution)/shard_map/ppermute | solution.py:44
  44.4 7.6 %collective-permute-start.13 = (f32[256,128]{1,0:T(8,128)S(1)}, f32[256,128]{1,0:T(8,128)S(1)}, u32[]{:S(2)}, u32[]{:S(2)}) collective-permute-start(f32[256,128]{1,0:T(8,128)S(1)} %add.9), channel_id=1, source_target_pairs={{0,2},{1,7},{2,0},{3,5},{4,6},{5,3},{6,4},{7,1},{8,10},{9,15},{10,... | collective-permute-start | bytes 393224 | tf_op jit(solution)/shard_map/ppermute | solution.py:51
  48.6 8.8 %collective-permute-start.16 = (bf16[256,512]{1,0:T(8,128)(2,1)S(1)}, bf16[256,512]{1,0:T(8,128)(2,1)S(1)}, u32[]{:S(2)}, u32[]{:S(2)}) collective-permute-start(bf16[256,512]{1,0:T(8,128)(2,1)S(1)} %slice.8), channel_id=1, source_target_pairs={{0,32},{1,9},{2,34},{3,11},{4,36},{5,13},{6,38},{7,15},{8,40},{9,1... | collective-permute-start | bytes 786440 | tf_op jit(solution)/shard_map/ppermute | solution.py:38
  48.7 8.7 %collective-permute-start.18 = (bf16[256,512]{1,0:T(8,128)(2,1)S(1)}, bf16[256,512]{1,0:T(8,128)(2,1)S(1)}, u32[]{:S(2)}, u32[]{:S(2)}) collective-permute-start(bf16[256,512]{1,0:T(8,128)(2,1)S(1)} %slice.9), channel_id=1, source_target_pairs={{0,96},{1,25},{2,98},{3,27},{4,100},{5,29},{6,102},{7,31},{8,104},... | collective-permute-start | bytes 786440 | tf_op jit(solution)/shard_map/ppermute | solution.py:38
  52.0 6.3 %collective-permute-start.14 = (f32[256,128]{1,0:T(8,128)S(1)}, f32[256,128]{1,0:T(8,128)S(1)}, u32[]{:S(2)}, u32[]{:S(2)}) collective-permute-start(f32[256,128]{1,0:T(8,128)S(1)} %add.10), channel_id=1, source_target_pairs={{0,6},{1,3},{2,4},{3,1},{4,2},{5,7},{6,0},{7,5},{8,14},{9,11},{10,... | collective-permute-start | bytes 393224 | tf_op jit(solution)/shard_map/ppermute | solution.py:51
  58.3 1.3 %collective-permute-start.19 = (bf16[256,128]{1,0:T(8,128)(2,1)S(1)}, bf16[256,128]{1,0:T(8,128)(2,1)S(1)}, u32[]{:S(2)}, u32[]{:S(2)}) collective-permute-start(bf16[256,128]{1,0:T(8,128)(2,1)S(1)} %add_convert_fusion.mine_ref), channel_id=1, source_target_pairs={{0,1},{1,0},{2,3},{3,2},{4,5},{5,4},{6,7},{7,6},{8,9},{9,8},{10,11... | collective-permute-start | bytes 196616 | tf_op jit(solution)/shard_map/ppermute | solution.py:44
